TPU v7x, 32 devices: a whole 2x2x4 slice. The times are simulated.
32 devices in a mesh: ctx: 8 (over z, y), head: 4 (over x, core).
Axes of the slice: x: 2, y: 2, z: 4, core: 2. Of those that a mesh axis runs over, the one named last changes fastest.
Arguments:
- q_rows: bfloat16 [2048, 2048], P(('ctx', 'head')), may hold values from -6 to 6
- k_rows: bfloat16 [2048, 2048], P(('ctx', 'head')), may hold values from -6 to 6
- v_rows: bfloat16 [2048, 4096], P(('ctx', 'head')), may hold values from -6 to 6
- z_rows: bfloat16 [2048, 4096], P(('ctx', 'head')), may hold values from -6 to 6
- a_rows: bfloat16 [2048, 32], P(('ctx', 'head')), may hold values from -5 to 5
- b_rows: bfloat16 [2048, 32], P(('ctx', 'head')), may hold values from -11 to 5
- conv_q: float32 [4, 2048], P(None, 'head'), may hold values from -3 to 3
- conv_k: float32 [4, 2048], P(None, 'head'), may hold values from -3 to 3
- conv_v: float32 [4, 4096], P(None, 'head'), may hold values from -3 to 3
- a_log: float32 [32], P('head'), may hold values from -11 to -1
- dt_bias: float32 [32], P('head'), may hold values from -2 to 1
- norm_gain: float32 [128], replicated, may hold values from 0.5 to 1.5
Outputs:
- gated_out: bfloat16 [2048, 4096], P(('ctx', 'head'))
All inputs are finite; a program needn't handle non-finite values.
Results may differ from a plain program's by a relative error of at most 0.0075.
Values may be sent and summed in bfloat16 or wider, within the bound.
No kernel may reach another device: no remote copies, remote signals or barrier semaphores. Data moves between devices by JAX's collectives and lax.ppermute only.
A program may use at most 128 MiB of HBM per device.

v0:
```python
import jax
import jax.numpy as jnp
from jax import lax
from jax.sharding import PartitionSpec as P

DK = 128
DV = 128
CONV = 4
SPAN = 64


HIGHEST = lax.Precision.HIGHEST


def shifted(block, axis, distance):
    devices = range(lax.axis_size(axis))
    route = [(i - distance, i) for i in devices if i - distance in devices]
    return lax.ppermute(block, axis, route)


def entering(shard, axis, combine, identity):
    peers, here = (lax.axis_size(axis), lax.axis_index(axis))
    everything = jax.tree.map(lambda part: lax.all_gather(part, axis), shard)
    start = jax.tree.map(
        lambda part, zero: jnp.broadcast_to(jnp.asarray(zero, part.dtype), part.shape),
        shard,
        identity,
    )

    def step(k, before):
        reached = k < here
        new = combine(before, jax.tree.map(lambda part: part[k], everything))
        return jax.tree.map(lambda a, b: jnp.where(reached, a, b), new, before)

    return lax.fori_loop(0, peers, step, start)


def conv_silu(seq_rows, rim_rows, weight):
    padded = jnp.concatenate([rim_rows, seq_rows], axis=0).astype(jnp.float32)
    length_rows = seq_rows.shape[0]
    summed = weight[0] * padded[0:length_rows]
    for offset in range(1, weight.shape[0]):
        summed = summed + weight[offset] * padded[offset : offset + length_rows]
    return jax.nn.silu(summed)


def unit_norm(conv_out, head_width, factor):
    shaped = conv_out.reshape(conv_out.shape[0], -1, head_width)
    scaled = shaped * lax.rsqrt(jnp.sum(shaped * shaped, axis=-1, keepdims=True) + 1e-06) * factor
    return scaled.astype(jnp.bfloat16)


def span_parts(q_block, k_block, v_block, g_block, b_block):
    length_rows = g_block.shape[1]
    cum_decay = jnp.cumsum(g_block, axis=1)
    row_ids = lax.broadcasted_iota(jnp.int32, (length_rows, length_rows), 0)
    col_ids = lax.broadcasted_iota(jnp.int32, (length_rows, length_rows), 1)
    lower_mask = row_ids >= col_ids
    gap_log = cum_decay[:, :, None] - cum_decay[:, None, :]
    within = jnp.where(lower_mask, jnp.exp(jnp.where(lower_mask, gap_log, 0.0)), 0.0)
    k_gram = jnp.einsum("hid,hjd->hij", k_block, k_block, precision=HIGHEST)
    strict_part = jnp.where(row_ids > col_ids, b_block[:, :, None] * within * k_gram, 0.0)
    system_mat = strict_part + jnp.eye(length_rows, dtype=jnp.float32)
    growth = jnp.exp(cum_decay)
    right_side = jnp.concatenate(
        [(b_block * growth)[:, :, None] * k_block, b_block[:, :, None] * v_block], axis=2
    )
    solved = jax.scipy.linalg.solve_triangular(
        system_mat, right_side, lower=True, unit_diagonal=True
    )
    key_width = k_block.shape[2]
    w_mat = solved[:, :, :key_width]
    u_mat = solved[:, :, key_width:]
    scores = jnp.einsum("hid,hjd->hij", q_block, k_block, precision=HIGHEST) * within
    q_decay = growth[:, :, None] * q_block
    end_decay = growth[:, -1]
    k_decay = jnp.exp(cum_decay[:, -1:] - cum_decay)[:, :, None] * k_block
    return (q_decay, scores, w_mat, u_mat, k_decay, end_decay)


def combine(earlier, later_map):
    lin_part = jnp.einsum("hde,hef->hdf", later_map[0], earlier[0], precision=HIGHEST)
    add_part = (
        jnp.einsum("hde,hef->hdf", later_map[0], earlier[1], precision=HIGHEST) + later_map[1]
    )
    return (lin_part, add_part)


def local(
    q_rows,
    k_rows,
    v_rows,
    z_rows,
    a_rows,
    b_rows,
    conv_q,
    conv_k,
    conv_v,
    a_log,
    dt_bias,
    norm_gain,
):
    q_grid, k_grid, v_grid, z_grid, a_grid, b_grid = (
        lax.all_to_all(q_rows, "head", split_axis=1, concat_axis=0, tiled=True),
        lax.all_to_all(k_rows, "head", split_axis=1, concat_axis=0, tiled=True),
        lax.all_to_all(v_rows, "head", split_axis=1, concat_axis=0, tiled=True),
        lax.all_to_all(z_rows, "head", split_axis=1, concat_axis=0, tiled=True),
        lax.all_to_all(a_rows, "head", split_axis=1, concat_axis=0, tiled=True),
        lax.all_to_all(b_rows, "head", split_axis=1, concat_axis=0, tiled=True),
    )
    row_count = q_grid.shape[0]
    width_keys = q_grid.shape[1]
    edge_rows = CONV - 1
    tail_rows = jnp.concatenate(
        [
            q_grid[row_count - edge_rows :],
            k_grid[row_count - edge_rows :],
            v_grid[row_count - edge_rows :],
        ],
        axis=1,
    )
    rim_rows = shifted(tail_rows, "ctx", 1)
    queries = unit_norm(conv_silu(q_grid, rim_rows[:, :width_keys], conv_q), DK, DK ** (-0.5))
    keys_unit = unit_norm(
        conv_silu(k_grid, rim_rows[:, width_keys : 2 * width_keys], conv_k), DK, 1.0
    )
    values = conv_silu(v_grid, rim_rows[:, 2 * width_keys :], conv_v).astype(jnp.bfloat16)
    key_heads = width_keys // DK
    value_heads = v_grid.shape[1] // DV
    share_ratio = value_heads // key_heads
    write_rate = jax.nn.sigmoid(b_grid.astype(jnp.float32))
    log_decay = -jnp.exp(a_log)[None, :] * jax.nn.softplus(
        a_grid.astype(jnp.float32) + dt_bias[None, :]
    )
    span_count = row_count // SPAN
    q_all = queries.reshape(span_count, SPAN, key_heads, DK).transpose(0, 2, 1, 3)
    k_all = keys_unit.reshape(span_count, SPAN, key_heads, DK).transpose(0, 2, 1, 3)
    v_all = values.reshape(span_count, SPAN, value_heads, DV).transpose(0, 2, 1, 3)
    g_all = log_decay.reshape(span_count, SPAN, value_heads).transpose(0, 2, 1)
    b_all = write_rate.reshape(span_count, SPAN, value_heads).transpose(0, 2, 1)

    def block_parts(q_block, k_block, v_block, g_block, b_block):
        q_full = jnp.repeat(q_block.astype(jnp.float32), share_ratio, axis=0)
        k_full = jnp.repeat(k_block.astype(jnp.float32), share_ratio, axis=0)
        return span_parts(q_full, k_full, v_block.astype(jnp.float32), g_block, b_block)

    q_decay, scores, w_mat, u_mat, k_decay, end_decay = jax.vmap(block_parts)(
        q_all, k_all, v_all, g_all, b_all
    )
    identity = jnp.broadcast_to(jnp.eye(DK, dtype=jnp.float32), (value_heads, DK, DK))
    zero_add = jnp.zeros((value_heads, DK, DV), jnp.float32)
    step_lin = end_decay[:, :, None, None] * identity[None] - jnp.einsum(
        "nhcd,nhce->nhde", k_decay, w_mat, precision=HIGHEST
    )
    step_add = jnp.einsum("nhcd,nhce->nhde", k_decay, u_mat, precision=HIGHEST)

    def compose(carried, maps):
        lin_now, add_now = carried
        lin_step, add_step = maps
        lin_next = jnp.einsum("hde,hef->hdf", lin_step, lin_now, precision=HIGHEST)
        add_next = jnp.einsum("hde,hef->hdf", lin_step, add_now, precision=HIGHEST) + add_step
        return ((lin_next, add_next), None)

    (lin_local, add_local), _ = lax.scan(compose, (identity, zero_add), (step_lin, step_add))
    prefix = entering((lin_local, add_local), "ctx", combine, (identity, zero_add))
    state_in = prefix[1]

    def advance(state_now, parts):
        q_dec, score_blk, w_blk, u_blk, k_dec, end_dec = parts
        fresh_vals = u_blk - jnp.einsum("hcd,hde->hce", w_blk, state_now, precision=HIGHEST)
        output = jnp.einsum("hcd,hde->hce", q_dec, state_now, precision=HIGHEST) + jnp.einsum(
            "hij,hje->hie", score_blk, fresh_vals, precision=HIGHEST
        )
        state_next = end_dec[:, None, None] * state_now + jnp.einsum(
            "hcd,hce->hde", k_dec, fresh_vals, precision=HIGHEST
        )
        return (state_next, output)

    _, outputs = lax.scan(advance, state_in, (q_decay, scores, w_mat, u_mat, k_decay, end_decay))
    core_out = outputs.transpose(0, 2, 1, 3).reshape(row_count, value_heads, DV)
    normed = (
        core_out
        * lax.rsqrt(jnp.mean(core_out * core_out, axis=-1, keepdims=True) + 1e-06)
        * norm_gain
    ).astype(jnp.bfloat16)
    normed = lax.optimization_barrier(normed)
    outgoing = (
        normed.astype(jnp.float32).reshape(row_count, value_heads * DV)
        * jax.nn.silu(z_grid.astype(jnp.float32))
    ).astype(jnp.bfloat16)
    returned = lax.all_to_all(outgoing, "head", split_axis=0, concat_axis=1, tiled=True)
    return returned


def solution(mesh):
    placed = (
        P(("ctx", "head"), None),
        P(("ctx", "head"), None),
        P(("ctx", "head"), None),
        P(("ctx", "head"), None),
        P(("ctx", "head"), None),
        P(("ctx", "head"), None),
        P(None, "head"),
        P(None, "head"),
        P(None, "head"),
        P("head"),
        P("head"),
        P(),
    )
    return jax.shard_map(
        local, mesh=mesh, in_specs=placed, out_specs=P(("ctx", "head"), None), check_vma=False
    )
```

profile of v0, /device:TPU:0, one launch (start us, length us, event | category | flops | bytes accessed | tf_op | source)
XLA Modules:
  0.0 457.6 jit_solution(3284165974971476676)
XLA Ops:
  6.5 0.7 copy-done
  7.2 0.7 reshape.151
  7.9 4.2 all-to-all-start
  12.1 0.9 fusion.79
  13.0 0.7 bitcast_bitcast_fusion
  13.8 0.9 fusion.77
  14.7 0.7 reshape.153
  15.9 3.2 all-to-all-start.4
  19.2 1.9 copy.85
  21.1 1.7 copy.87
  22.7 1.7 copy.86
  24.4 3.4 all-to-all-start.1
  28.0 5.8 %all-to-all-done.1 = bf16[64,4,512]{2,0,1:T(8,128)(2,1)S(1)} async-done(((bf16[64,4,512]{2,0,1:T(8,128)(2,1)}), bf16[64,4,512]{2,0,1:T(8,128)(2,1)S(1)}, u32[]{:S(2)}, u32[]{:S(2)}) %all-to-all-start.1) | async-done | bytes 262176 | tf_op jit(solution)/shard_map/all_to_all | solution.py:104
  33.8 3.4 all-to-all-start.2
  37.4 5.9 %all-to-all-done.2 = bf16[64,4,512]{2,0,1:T(8,128)(2,1)S(1)} async-done(((bf16[64,4,512]{2,0,1:T(8,128)(2,1)}), bf16[64,4,512]{2,0,1:T(8,128)(2,1)S(1)}, u32[]{:S(2)}, u32[]{:S(2)}) %all-to-all-start.2) | async-done | bytes 262176 | tf_op jit(solution)/shard_map/all_to_all | solution.py:105
  43.3 3.5 all-to-all-start.3
  46.8 0.9 reduce_window_sum.11
  48.0 7.6 %all-to-all-done.3 = bf16[64,4,1024]{2,0,1:T(8,128)(2,1)S(1)} async-done(((bf16[64,4,1024]{2,0,1:T(8,128)(2,1)}), bf16[64,4,1024]{2,0,1:T(8,128)(2,1)S(1)}, u32[]{:S(2)}, u32[]{:S(2)}) %all-to-all-start.3) | async-done | bytes 524320 | tf_op jit(solution)/shard_map/all_to_all | solution.py:106
  55.6 3.9 collective-permute-start
  59.6 1.3 collective-permute-done
  60.9 0.9 maximum_convert_fusion.1
  63.4 2.9 fusion.42
  66.3 158.7 %custom-call.4 = f32[4,8,1,64,64]{3,4,2,1,0:T(8,128)} custom-call(f32[4,8,1,64,64]{4,3,2,1,0:T(8,128)} %fusion.42), custom_call_target="InvertDiagBlocksLowerTriangular" | custom-call | tf_op jit(solution)/shard_map/vmap(jit(_solve_triangular))/vmap()/triangular_solve | solution.py:68
  227.5 2.0 fusion.34
  229.6 4.9 %fusion.70 = f32[4,8,128,128]{3,2,1,0:T(8,128)} fusion(f32[4,8,64,128]{3,2,1,0:T(8,128)S(1)} %get-tuple-element.446, f32[4,8,64,256]{3,2,1,0:T(8,128)S(1)} %fusion.34), kind=kOutput, calls=%fused_computation.136 | convolution fusion | flops 402653184 | bytes 4194304 | tf_op jit(solution)/shard_map/nhcd,nhce->nhde/dot_general | solution.py:155
  234.4 3.8 multiply_subtract_fusion
  238.3 10.2 %while.40 = (s32[]{:T(128)}, f32[8,128,128]{2,1,0:T(8,128)S(1)}, f32[8,128,128]{2,1,0:T(8,128)S(1)}, f32[4,8,128,128]{3,2,1,0:T(8,128)S(1)}, f32[4,8,128,128]{3,2,1,0:T(8,128)}, /*index=5*/s32[]{:T(128)}, s32[]{:T(128)}) while((s32[]{:T(128)}, f32[8,128,128]{2,1,0:T(8,128)S(1)}, f32[8,128,128]{2,1,0:T(8,128)S(1)}, ...), condition=%wide.region_3.4_spmd.clone, body=%wide.region_2.3_spmd.clone.sunk | while | flops 402915328 | bytes 5768283 | solution.py:164
  238.5 1.7 convolution_add_fusion.7
  241.0 1.7 convolution_add_fusion.7
  243.5 1.7 convolution_add_fusion.7
  246.0 1.7 convolution_add_fusion.7
  248.5 0.8 copy-done.1
  250.0 1.9 copy.84
  251.9 3.5 all-to-all-start.5
  257.4 1.3 copy-done.5
  258.7 1.7 fusion.75
  260.4 1.8 convolution_multiply_fusion
  262.2 61.7 %all-gather.5.cloned.1.call-done = f32[64,128,128]{2,1,0:T(8,128)} async-done(((f32[8,128,128]{2,1,0:T(8,128)}), f32[64,128,128]{2,1,0:T(8,128)}) %all-gather.5.cloned.1.call-update) | async-done | bytes 4194320 | tf_op jit(solution)/shard_map/all_gather | solution.py:23
  323.9 73.8 %all-gather.7.cloned.1.call-done = f32[64,128,128]{2,1,0:T(8,128)} async-done(((f32[8,128,128]{2,1,0:T(8,128)}), f32[64,128,128]{2,1,0:T(8,128)}) %all-gather.7.cloned.1.call-update) | async-done | bytes 4194320 | tf_op jit(solution)/shard_map/all_gather | solution.py:23
  397.7 15.7 %while.41 = (s32[]{:T(128)}, f32[8,128,128]{2,1,0:T(8,128)S(1)}, s32[]{:T(128)}, f32[8,8,128,128]{3,2,1,0:T(8,128)}, f32[8,8,128,128]{3,2,1,0:T(8,128)}, /*index=5*/s32[]{:T(128)}, s32[]{:T(128)}) while((s32[]{:T(128)}, f32[8,128,128]{2,1,0:T(8,128)S(1)}, s32[]{:T(128)}, f32[8,8,128,128]{3,2,1,0:T(8,128)}, ...), condition=%wide.region_5.6_spmd.clone, body=%wide.region_4.5_spmd.clone.sunk | while | flops 201850880 | bytes 3672671 | solution.py:35
  397.8 1.9 fusion.128
  399.7 1.9 fusion.128
  401.7 1.9 fusion.128
  403.6 1.9 fusion.128
  405.6 1.9 fusion.128
  407.6 1.9 fusion.128
  409.5 1.9 fusion.128
  411.5 1.9 fusion.128
  413.4 22.5 %while.39 = (s32[]{:T(128)}, f32[8,128,128]{2,1,0:T(8,128)S(1)}, f32[4,8,64,128]{3,1,2,0:T(8,128)}, f32[4,8]{1,0:T(4,128)S(1)}, f32[4,8,64,128]{3,2,1,0:T(8,128)...) while((s32[]{:T(128)}, f32[8,128,128]{2,1,0:T(8,128)S(1)}, ...), condition=%wide.region_8.9_spmd, body=%wide.region_7.8_spmd.sunk | while | flops 352714752 | bytes 5507281 | solution.py:179
  413.4 1.6 convolution_subtract_fusion.2
  416.1 0.9 copy_dynamic-update-slice_fusion.2
  417.0 2.1 convolution_add_fusion.6
  419.1 1.6 convolution_subtract_fusion.2
  421.7 0.9 copy_dynamic-update-slice_fusion.2
  422.6 2.1 convolution_add_fusion.6
  424.7 1.6 convolution_subtract_fusion.2
  427.4 0.9 copy_dynamic-update-slice_fusion.2
  428.2 2.1 convolution_add_fusion.6
  430.3 1.6 convolution_subtract_fusion.2
  433.0 0.8 copy_dynamic-update-slice_fusion.2
  433.8 2.1 convolution_add_fusion.6
  435.9 1.7 fusion.52
  438.5 11.4 %all_to_all.112 = bf16[4,64,1024]{2,1,0:T(8,128)(2,1)S(1)} all-to-all(bf16[4,64,1024]{2,1,0:T(8,128)(2,1)S(1)} %fusion.54), channel_id=1, replica_groups=mesh['ctx'=8,'head'=4] {'head'}, dimensions={0} | all-to-all | bytes 1048576 | tf_op jit(solution)/shard_map/all_to_all | solution.py:191
  449.9 0.8 copy.74
  (117 shorter events, 16.4 us)
Async XLA Ops:
  6.5 0.7 copy-start
  6.5 21.3 %copy-start.14 = (f32[8]{0:T(128)S(1)}, f32[8]{0:T(128)}, u32[]{:S(2)}) copy-start(f32[8]{0:T(128)} %param.27) | copy-start | bytes 100
  6.5 30.7 %copy-start.13 = (f32[8]{0:T(128)S(1)}, f32[8]{0:T(128)}, u32[]{:S(2)}) copy-start(f32[8]{0:T(128)} %param.28) | copy-start | bytes 100
  7.9 8.0 %all-to-all-start = ((bf16[4,2,256]{2,1,0:T(2,128)(2,1)}), bf16[4,2,256]{2,1,0:T(2,128)(2,1)S(1)}, u32[]{:S(2)}, u32[]{:S(2)}) async-start(bf16[4,2,256]{2,1,0:T(2,128)(2,1)} %reshape.151), calls=%async_computation | async-start | bytes 8192 | tf_op jit(solution)/shard_map/all_to_all | solution.py:108
  15.9 8.5 %all-to-all-start.4 = ((bf16[4,2,256]{2,1,0:T(2,128)(2,1)}), bf16[4,2,256]{2,1,0:T(2,128)(2,1)S(1)}, u32[]{:S(2)}, u32[]{:S(2)}) async-start(bf16[4,2,256]{2,1,0:T(2,128)(2,1)} %reshape.153), calls=%async_computation.4 | async-start | bytes 8192 | tf_op jit(solution)/shard_map/all_to_all | solution.py:109
  24.4 9.4 %all-to-all-start.1 = ((bf16[64,4,512]{2,0,1:T(8,128)(2,1)}), bf16[64,4,512]{2,0,1:T(8,128)(2,1)S(1)}, u32[]{:S(2)}, u32[]{:S(2)}) async-start(bf16[64,4,512]{2,0,1:T(8,128)(2,1)} %bitcast.161), calls=%async_computation.1 | async-start | bytes 524288 | tf_op jit(solution)/shard_map/all_to_all | solution.py:104
  33.8 9.4 %all-to-all-start.2 = ((bf16[64,4,512]{2,0,1:T(8,128)(2,1)}), bf16[64,4,512]{2,0,1:T(8,128)(2,1)S(1)}, u32[]{:S(2)}, u32[]{:S(2)}) async-start(bf16[64,4,512]{2,0,1:T(8,128)(2,1)} %bitcast.160), calls=%async_computation.2 | async-start | bytes 524288 | tf_op jit(solution)/shard_map/all_to_all | solution.py:105
  43.3 12.3 %all-to-all-start.3 = ((bf16[64,4,1024]{2,0,1:T(8,128)(2,1)}), bf16[64,4,1024]{2,0,1:T(8,128)(2,1)S(1)}, u32[]{:S(2)}, u32[]{:S(2)}) async-start(bf16[64,4,1024]{2,0,1:T(8,128)(2,1)} %bitcast.159), calls=%async_computation.3 | async-start | bytes 1048576 | tf_op jit(solution)/shard_map/all_to_all | solution.py:106
  46.7 277.2 %all-gather.5.cloned.1.call-start = ((), (), s32[]{:S(2)}) async-start(), calls=%async_computation.7 | async-start | bytes 4718592 | tf_op jit(solution)/shard_map/all_gather | solution.py:23
  55.6 5.3 %collective-permute-start = (bf16[3,2048]{1,0:T(4,128)(2,1)S(1)}, bf16[3,2048]{1,0:T(4,128)(2,1)S(1)}, u32[]{:S(2)}, u32[]{:S(2)}) collective-permute-start(bf16[3,2048]{1,0:T(4,128)(2,1)S(1)} %pad_maximum_fusion), channel_id=1, source_target_pairs={{0,4},{4,8},{8,12},{12,16},{16,20},{20,24},{24,28},{1,5},{5,9},{9,... | collective-permute-start | bytes 36872 | tf_op jit(solution)/shard_map/ppermute | solution.py:18
  63.4 162.9 %copy-start.7 = (f32[4,4,2,64,128]{4,3,2,1,0:T(8,128)}, f32[4,4,2,64,128]{4,3,2,1,0:T(8,128)S(1)}, u32[]{:S(2)}) copy-start(f32[4,4,2,64,128]{4,3,2,1,0:T(8,128)S(1)} %broadcast_in_dim.52) | copy-start | bytes 3145732
  226.3 1.2 copy-start.10
  226.9 7.5 %copy-start.2 = (f32[4,8,64,128]{3,2,1,0:T(8,128)}, f32[4,8,64,128]{3,2,1,0:T(8,128)S(1)}, u32[]{:S(2)}) copy-start(f32[4,8,64,128]{3,2,1,0:T(8,128)S(1)} %get-tuple-element.446) | copy-start | bytes 3145732
  229.6 4.9 %copy-start.4 = (f32[4,8,64,256]{3,2,1,0:T(8,128)}, f32[4,8,64,256]{3,2,1,0:T(8,128)S(1)}, u32[]{:S(2)}) copy-start(f32[4,8,64,256]{3,2,1,0:T(8,128)S(1)} %fusion.34) | copy-start | bytes 6291460
  248.4 0.8 copy-start.1
  248.4 1.0 copy-start.3
  248.4 7.0 %copy-start.11 = (f32[4,512]{1,0:T(4,128)S(1)}, f32[4,512]{1,0:T(4,128)}, u32[]{:S(2)}) copy-start(f32[4,512]{1,0:T(4,128)} %param.24) | copy-start | bytes 24580
  248.5 7.0 %copy-start.6 = (f32[259,512]{1,0:T(8,128)S(1)}, f32[259,512]{1,0:T(8,128)}, u32[]{:S(2)}) copy-start(f32[259,512]{1,0:T(8,128)} %get-tuple-element.278) | copy-start | bytes 1591300
  249.2 148.5 %all-gather.7.cloned.1.call-start = ((), (), s32[]{:S(2)}) async-start(), calls=%async_computation.8 | async-start | bytes 4718592 | tf_op jit(solution)/shard_map/all_gather | solution.py:23
  251.9 186.3 %all-to-all-start.5 = ((bf16[64,4,1024]{2,0,1:T(8,128)(2,1)}), bf16[64,4,1024]{2,0,1:T(8,128)(2,1)S(1)}, u32[]{:S(2)}, u32[]{:S(2)}) async-start(bf16[64,4,1024]{2,0,1:T(8,128)(2,1)} %bitcast.158), calls=%async_computation.5 | async-start | bytes 1048576 | tf_op jit(solution)/shard_map/all_to_all | solution.py:107
  257.0 1.7 copy-start.5
  258.7 1.7 copy-start.8
  413.4 24.2 %copy-start.12 = (f32[128]{0:T(128)S(1)}, f32[128]{0:T(128)}, u32[]{:S(2)}) copy-start(f32[128]{0:T(128)} %param.29) | copy-start | bytes 1540
  435.9 1.7 copy-start.9
Sparse Core Ops, SparseCore 0:
  249.4 74.4 all-gather.4
  326.0 71.6 all-gather.6
where the time goes:
time: 459 us; the launch traced here: 458 us
  other arithmetic  167 us (36%)
  waiting for transfers between devices  157 us (34%)
  matrix products  58.7 us (13%)
  starting transfers between devices  25.2 us (5%)
  local copies, waits for them, and re-layouts  23 us (5%)
  between operations  14 us (3%)
  blocking collectives  11.4 us (2%)
    another operation x4, other arithmetic, span_parts(): jax.scipy.linalg.solve_triangular(system_mat, right_side, lower=True, uni...  159 us
    all_gather x2, waiting for transfers between devices, entering(): everything = jax.tree.map(lambda part: lax.all_gather(part, axis), shard)  136 us
    dot_general x8, matrix products, combine(): jnp.einsum('hde,hef->hdf', later_map[0], earlier[1], precision=HIGHEST)  15.1 us
    all_to_all x1, blocking collectives, local(): lax.all_to_all(outgoing, 'head', split_axis=0, concat_axis=1, tiled=True)  11.4 us
  transfers between devices with their start and end apart: 9, of which 7 were waited for; matrix products, arithmetic and copies ran while one was open for 13% of the time, Pallas kernels for 0%

commit v1 on v0

v1 whole, which is shorter than its diff:
```python
import jax
import jax.numpy as jnp
from jax import lax
from jax.experimental import pallas as pl
from jax.experimental.pallas import tpu as pltpu
from jax.sharding import Mesh, PartitionSpec as P

DK = 128
DV = 128
CONV = 4
SUB = 8
KH = 16
EPS = 1e-06
F32 = jnp.float32
BF16 = jnp.bfloat16
VMEM_BYTES = 56 * 1024 * 1024


def dot(a, b, dims=((1,), (0,))):
    return lax.dot_general(a, b, (dims, ((), ())), preferred_element_type=F32)


def halves(x):
    high = x.astype(BF16)
    return high, (x - high.astype(F32)).astype(BF16)


def mm_left(a, b):
    return dot(jnp.concatenate(halves(a), axis=1), jnp.concatenate([b, b], axis=0))


def mm_right(a, b):
    return dot(jnp.concatenate([a, a], axis=1), jnp.concatenate(halves(b), axis=0))


def mm(a, b):
    a_high, a_low = halves(a)
    b_high, b_low = halves(b)
    both = jnp.concatenate([a_high, a_low], axis=1)
    return dot(both, jnp.concatenate([b_high, b_high], axis=0)) + dot(a_high, b_low)


def silu(x):
    return x / (1.0 + jnp.exp(-x))


def iota(shape, dim):
    return lax.broadcasted_iota(jnp.int32, shape, dim)


def pack_kernel(heads_axis, q_ref, k_ref, v_ref, a_ref, b_ref, out_ref):
    peers, tokens = out_ref.shape[0], q_ref.shape[0]
    heads = peers // (q_ref.shape[1] // DK // heads_axis)
    subs = peers // heads_axis
    for sub in range(subs):
        for head in range(heads_axis):
            dest, key_head = sub * heads_axis + head, head * subs + sub
            out_ref[dest, 0:tokens, :] = q_ref[:, key_head * DK : (key_head + 1) * DK]
            out_ref[dest, tokens : 2 * tokens, :] = k_ref[:, key_head * DK : (key_head + 1) * DK]
            for r in range(2):
                value_head = 2 * key_head + r
                out_ref[dest, (2 + r) * tokens : (3 + r) * tokens, :] = v_ref[
                    :, value_head * DV : (value_head + 1) * DV
                ]
    del heads
    value_heads = a_ref.shape[1]
    row = iota((value_heads, peers * 16), 0)
    col = iota((value_heads, peers * 16), 1)
    dest, entry = col // 16, col % 16
    first = 2 * ((dest % heads_axis) * subs + dest // heads_axis)
    pick_a = jnp.where((entry < 2) & (row == first + entry), 1.0, 0.0).astype(BF16)
    pick_b = jnp.where(
        (entry >= 2) & (entry < 4) & (row == first + entry - 2), 1.0, 0.0
    ).astype(BF16)
    picked = (dot(a_ref[...], pick_a) + dot(b_ref[...], pick_b)).astype(BF16)
    lane_shift = tokens * lax.rem(lax.axis_index("head"), 2)
    place = jnp.where(
        iota((tokens, 128), 1) == iota((tokens, 128), 0) + lane_shift, 1.0, 0.0
    ).astype(BF16)
    gates = dot(picked, place, ((0,), (0,))).astype(BF16)
    for d in range(peers):
        out_ref[d, 4 * tokens :, :] = gates[16 * d : 16 * (d + 1), :]


def invert(systems):
    size = systems[0].shape[0]
    blocks = size // SUB
    row, col = iota((size, size), 0), iota((size, size), 1)
    diagonal = (row // SUB) == (col // SUB)
    compact = jnp.concatenate(
        [
            jnp.sum(jnp.where(diagonal, n, 0.0).reshape(blocks, SUB, size), axis=0)
            for n in systems
        ],
        axis=0,
    )
    count = len(systems)
    lane, line = iota(compact.shape, 1), iota(compact.shape, 0)
    solved = jnp.where(lane % SUB == line % SUB, 1.0, 0.0).reshape(count, SUB, size)
    for m in range(SUB - 1):
        spread = jnp.take_along_axis(compact, (lane // SUB) * SUB + m, axis=1)
        solved = solved - spread.reshape(count, SUB, size) * solved[:, m : m + 1, :]
    inverses = [
        jnp.where(
            diagonal.reshape(blocks, SUB, size), solved[i : i + 1, :, :], 0.0
        ).reshape(size, size)
        for i in range(count)
    ]
    width = SUB
    while width < size:
        odd = [(j, j + width) for j in range(width, size, 2 * width)]

        def rows_of(x):
            return jnp.concatenate([x[lo:hi] for lo, hi in odd], axis=0)

        below = rows_of(
            ((row // (2 * width)) == (col // (2 * width))) & ((col // width) % 2 == 0)
        )
        firsts = [
            mm(jnp.where(below, rows_of(n), 0.0), inv) for n, inv in zip(systems, inverses)
        ]
        zero = jnp.zeros((width, size), F32)
        spreads = []
        for first in firsts:
            parts = []
            for j in range(len(odd)):
                parts += [zero, first[j * width : (j + 1) * width]]
            spreads.append(jnp.concatenate(parts, axis=0))
        seconds = [mm(rows_of(inv), spread) for inv, spread in zip(inverses, spreads)]
        grown = []
        for inv, second in zip(inverses, seconds):
            parts = []
            for j, (lo, hi) in enumerate(odd):
                parts += [inv[lo - width : lo], inv[lo:hi] - second[j * width : (j + 1) * width]]
            grown.append(jnp.concatenate(parts, axis=0))
        inverses = grown
        width *= 2
    return inverses


def core_kernel(
    recv_ref, rim_ref, cq_ref, ck_ref, cv_ref, alog_ref, dt_ref, o_ref, x_ref, rows, qs, ks, vs
):
    sub = lax.axis_index("sub")
    peers = recv_ref.shape[0]
    tokens = (recv_ref.shape[1] - 16) // 4
    total = peers * tokens
    span = 128
    spans = total // span
    for g in range(4):
        rows[0:8, g * 128 : (g + 1) * 128] = rim_ref[16 * g : 16 * (g + 1), :].astype(F32)[8:]

    def widen(s, carry):
        start = pl.multiple_of(8 + s * tokens, 8)
        for g in range(4):
            rows[pl.ds(start, tokens), g * 128 : (g + 1) * 128] = recv_ref[
                s, g * tokens : (g + 1) * tokens, :
            ].astype(F32)
        return carry

    lax.fori_loop(0, peers, widen, 0)
    key_lane = pl.multiple_of(sub * DK, 128)
    value_lane = pl.multiple_of(sub * 2 * DV, 128)
    taps = [
        cq_ref[:, pl.ds(key_lane, DK)],
        ck_ref[:, pl.ds(key_lane, DK)],
        cv_ref[:, pl.ds(value_lane, DV)],
        cv_ref[:, pl.ds(pl.multiple_of(value_lane + DV, 128), DV)],
    ]
    for n in range(spans):
        at = n * span
        results = []
        for g in range(4):
            lanes = slice(g * 128, (g + 1) * 128)
            tap = taps[g]
            summed = tap[0:1] * rows[at + 5 : at + 5 + span, lanes]
            for j in range(1, CONV):
                summed = summed + tap[j : j + 1] * rows[at + 5 + j : at + 5 + j + span, lanes]
            results.append(silu(summed))
        for ref, y, factor in ((qs, results[0], DK**-0.5), (ks, results[1], 1.0)):
            scale = lax.rsqrt(jnp.sum(y * y, axis=-1, keepdims=True) + EPS)
            ref[at : at + span, :] = (y * scale * factor).astype(BF16)
        vs[at : at + span, 0:128] = results[2].astype(BF16)
        vs[at : at + span, 128:256] = results[3].astype(BF16)
    gates = jnp.concatenate(
        [
            recv_ref[2 * n, 4 * tokens :, :].astype(F32)
            + recv_ref[2 * n + 1, 4 * tokens :, :].astype(F32)
            for n in range(spans)
        ],
        axis=0,
    )
    second = iota(gates.shape, 0) % 16 == 1
    a_log = jnp.where(second, alog_ref[2 * sub + 1], alog_ref[2 * sub])
    dt_bias = jnp.where(second, dt_ref[2 * sub + 1], dt_ref[2 * sub])
    shifted = gates + dt_bias
    soft = jnp.maximum(shifted, 0.0) + jnp.log1p(jnp.exp(-jnp.abs(shifted)))
    decay = -jnp.exp(a_log) * soft
    rate = 1.0 / (1.0 + jnp.exp(-gates))
    lane_r, lane_c = iota((span, span), 0), iota((span, span), 1)
    upto = jnp.where(lane_r <= lane_c, 1.0, 0.0).astype(BF16)
    d_high, d_rest = halves(decay)
    d_mid, d_low = halves(decay - d_high.astype(F32))
    cum = dot(d_high, upto) + (dot(d_mid, upto) + dot(d_low, upto))
    growth = jnp.exp(cum)
    mixed = jnp.where(iota(gates.shape, 0) % 16 < 2, cum, rate)
    columns = jnp.transpose(mixed)
    lower = lane_r >= lane_c
    strict = lane_r > lane_c
    keys, keys_t, queries, scores, systems = [], [], [], [], []
    for n in range(spans):
        q_n = qs[n * span : (n + 1) * span, :]
        k_n = ks[n * span : (n + 1) * span, :]
        kt_n = jnp.transpose(k_n.astype(F32)).astype(BF16)
        grams = dot(jnp.concatenate([k_n, q_n], axis=0), kt_n)
        keys.append(k_n)
        keys_t.append(kt_n)
        queries.append(q_n)
        for r in range(2):
            c_col = columns[:, 16 * n + r : 16 * n + r + 1]
            c_row = cum[16 * n + r : 16 * n + r + 1, :]
            b_col = columns[:, 16 * n + 2 + r : 16 * n + 3 + r]
            within = jnp.where(lower, jnp.exp(jnp.where(lower, c_col - c_row, 0.0)), 0.0)
            systems.append(jnp.where(strict, b_col * within * grams[:span], 0.0))
            scores.append(within * grams[span:])
    inverses = invert(systems)
    states = [
        jnp.concatenate([jnp.zeros((DK, DV), F32), jnp.where(lane_r == lane_c, 1.0, 0.0)], axis=1)
        for r in range(2)
    ]
    zero_half = jnp.zeros((span, DV), F32)
    for n in range(spans):
        for r in range(2):
            at = 16 * n + r
            b_row = rate[at + 2 : at + 3, :]
            c_col = columns[:, at : at + 1]
            t_b = inverses[2 * n + r] * b_row
            w_mat = mm_left(t_b * growth[at : at + 1, :], keys[n])
            u_mat = mm_left(t_b, vs[n * span : (n + 1) * span, r * DV : (r + 1) * DV])
            x = states[r]
            fresh = jnp.concatenate([u_mat, zero_half], axis=1) - mm(w_mat, x)
            out = jnp.exp(c_col) * mm_right(queries[n], x) + mm(scores[2 * n + r], fresh)
            o_ref[r, n * span : (n + 1) * span, :] = out
            c_end = c_col[span - 1 : span, :]
            states[r] = jnp.exp(c_end) * x + mm_right(
                keys_t[n], jnp.exp(c_end - c_col) * fresh
            )
    for r in range(2):
        x_ref[r] = states[r]


def finish_kernel(o_ref, s_ref, gain_ref, out_ref):
    peers, tokens = out_ref.shape[0], out_ref.shape[1]
    gain = gain_ref[...]
    group = 2
    for r in range(2):
        s_in = s_ref[r].astype(F32)
        for i in range(0, peers, group):
            at = i * tokens
            ext = o_ref[r, at : at + group * tokens, :]
            core = ext[:, :DV] + mm(ext[:, DV:], s_in)
            scale = lax.rsqrt(jnp.mean(core * core, axis=-1, keepdims=True) + EPS)
            normed = (core * scale * gain).astype(BF16)
            out_ref[i : i + group, :, r * DV : (r + 1) * DV] = normed.reshape(group, tokens, DV)


def gate_kernel(heads_axis, normed_ref, z_ref, out_ref):
    peers = normed_ref.shape[0]
    subs = peers // heads_axis
    for sub in range(subs):
        for head in range(heads_axis):
            key_head = head * subs + sub
            lanes = slice(key_head * 2 * DV, (key_head + 1) * 2 * DV)
            gate = silu(z_ref[:, lanes].astype(F32))
            value = normed_ref[sub * heads_axis + head].astype(F32)
            out_ref[:, lanes] = (value * gate).astype(BF16)


def call(kernel, outs, n_in, scratch=(), smem=()):
    specs = [
        pl.BlockSpec(memory_space=pltpu.SMEM if i in smem else pltpu.VMEM) for i in range(n_in)
    ]
    return pl.pallas_call(
        kernel,
        out_shape=outs,
        in_specs=specs,
        out_specs=jax.tree.map(lambda _: pl.BlockSpec(memory_space=pltpu.VMEM), outs),
        scratch_shapes=list(scratch),
        compiler_params=pltpu.CompilerParams(vmem_limit_bytes=VMEM_BYTES),
    )


def local(
    q_rows,
    k_rows,
    v_rows,
    z_rows,
    a_rows,
    b_rows,
    conv_q,
    conv_k,
    conv_v,
    a_log,
    dt_bias,
    norm_gain,
):
    shards, subs, heads_axis = (lax.axis_size(a) for a in ("half", "sub", "head"))
    peers, tokens = subs * heads_axis, q_rows.shape[0]
    total = peers * tokens
    group = ("sub", "head")
    route = [(i, i + 1) for i in range(shards - 1)]
    shape = jax.ShapeDtypeStruct
    packed = call(
        lambda *refs: pack_kernel(heads_axis, *refs),
        shape((peers, 4 * tokens + 16, 128), BF16),
        5,
    )(q_rows, k_rows, v_rows, a_rows, b_rows)
    received = lax.all_to_all(packed, group, 0, 0, tiled=True)
    tail = jnp.concatenate(
        [received[peers - 1, (g + 1) * tokens - 16 : (g + 1) * tokens] for g in range(4)], axis=0
    )
    rim = lax.ppermute(tail, "half", route)
    partial, state = call(
        core_kernel,
        (shape((2, total, 2 * DV), F32), shape((2, DK, 2 * DV), F32)),
        7,
        scratch=(
            pltpu.VMEM((8 + total, 512), F32),
            pltpu.VMEM((total, DK), BF16),
            pltpu.VMEM((total, DK), BF16),
            pltpu.VMEM((total, 2 * DV), BF16),
        ),
        smem=(5, 6),
    )(received, rim, conv_q, conv_k, conv_v, a_log, dt_bias)
    add, lin = state[:, :, :DV], state[:, :, DV:]
    entering = lax.ppermute(add, "half", route)
    for _ in range(shards - 2):
        moved = jnp.einsum("hde,hef->hdf", lin, entering, precision=lax.Precision.HIGHEST) + add
        entering = lax.ppermute(moved, "half", route)
    normed = call(finish_kernel, shape((peers, tokens, 2 * DV), BF16), 3)(
        partial, entering, norm_gain.reshape(1, DV)
    )
    returned = lax.all_to_all(normed, group, 0, 0, tiled=True)
    return call(
        lambda *refs: gate_kernel(heads_axis, *refs),
        shape((tokens, z_rows.shape[1]), BF16),
        2,
    )(returned, z_rows)


def solution(mesh):
    heads_axis = mesh.shape["head"]
    subs = KH // heads_axis
    regrouped = Mesh(
        mesh.devices.reshape(mesh.shape["ctx"] // subs, subs, heads_axis), ("half", "sub", "head")
    )
    row = P(("half", "sub", "head"), None)
    placed = (row,) * 6 + (P(None, "head"),) * 3 + (P("head"),) * 2 + (P(),)
    return jax.shard_map(local, mesh=regrouped, in_specs=placed, out_specs=row, check_vma=False)
```

time: 459 us -> 79.2 us (0.17)
  other arithmetic: 167 us -> 0.01 us
  waiting for transfers between devices: 157 us -> 3.93 us
  matrix products: 58.7 us -> 0 us
  blocking collectives: 11.4 us -> 37.9 us
  Pallas kernels: 0 us -> 22.2 us
  local copies, waits for them, and re-layouts: 23 us -> 4.94 us
  starting transfers between devices: 25.2 us -> 9.6 us
  between operations: 14 us -> 0.03 us
    another operation x5 -> x0, other arithmetic: 160 us -> none  [the longest x4 159 us: span_parts(): jax.scipy.linalg.solve_triangular(system_mat, right_side, lower=True, uni...]
    all_gather x2 -> x0, waiting for transfers between devices: 136 us -> none  [entering(): everything = jax.tree.map(lambda part: lax.all_gather(part, axis), shard)]
    dot_general x36 -> x0, matrix products: 56.7 us -> none  [the longest x8 15.1 us: combine(): jnp.einsum('hde,hef->hdf', later_map[0], earlier[1], precision=HIGHEST)]
    all_to_all x1 -> x2, blocking collectives: 11.4 us -> 37.9 us  [the longest x1 23.2 us: local(): received = lax.all_to_all(packed, group, 0, 0, tiled=True)]
    pallas_call x0 -> x4, Pallas kernels: none -> 22.2 us  [the longest x1 14.1 us: local(): call(core_kernel, (shape((2, total, 2 * DV), F32), shape((2, DK, 2 * DV),...]
    all_to_all x6 -> x0, starting transfers between devices: 21.2 us -> none  [the longest x1 4.21 us: local(): lax.all_to_all(a_rows, 'head', split_axis=1, concat_axis=0, tiled=True)]
    all_to_all x6 -> x0, waiting for transfers between devices: 19.9 us -> none  [the longest x1 7.58 us: local(): lax.all_to_all(v_rows, 'head', split_axis=1, concat_axis=0, tiled=True)]
    all_to_all x5 -> x0, local copies, waits for them, and re-layouts: 7.98 us -> none  [the longest x1 1.91 us: local(): lax.all_to_all(z_rows, 'head', split_axis=1, concat_axis=0, tiled=True)]
  transfers between devices with their start and end apart: 9 -> 2, of which waited for: 7 -> 2; matrix products, arithmetic and copies ran while one was open for 13% -> 0% of each run, Pallas kernels for 0% -> 0%
where the time goes in v1:
time: 79.2 us; the launch traced here: 78.7 us
  blocking collectives  37.9 us (48%)
  Pallas kernels  22.2 us (28%)
  starting transfers between devices  9.6 us (12%)
  local copies, waits for them, and re-layouts  4.94 us (6%)
  waiting for transfers between devices  3.93 us (5%)
    all_to_all x1, blocking collectives, local(): received = lax.all_to_all(packed, group, 0, 0, tiled=True)  23.2 us
    all_to_all x1, blocking collectives, local(): returned = lax.all_to_all(normed, group, 0, 0, tiled=True)  14.8 us
    pallas_call x1, Pallas kernels, local(): call(core_kernel, (shape((2, total, 2 * DV), F32), shape((2, DK, 2 * DV),...  14.1 us
    ppermute x1, starting transfers between devices, local(): entering = lax.ppermute(add, 'half', route)  5.1 us
    ppermute x1, starting transfers between devices, local(): rim = lax.ppermute(tail, 'half', route)  4.49 us
    unnamed x8, local copies, waits for them, and re-layouts  4.02 us
    pallas_call x1, Pallas kernels, local(): call(finish_kernel, shape((peers, tokens, 2 * DV), BF16), 3)  3.17 us
    pallas_call x1, Pallas kernels, local(): call(lambda *refs: pack_kernel(heads_axis, *refs), shape((peers, 4 * toke...  2.63 us
  transfers between devices with their start and end apart: 2, of which 2 were waited for; matrix products, arithmetic and copies ran while one was open for 0% of the time, Pallas kernels for 0%

profile of v1, /device:TPU:0, one launch (start us, length us, event | category | flops | bytes accessed | tf_op | source)
XLA Modules:
  0.0 78.7 jit_solution(2173747356804266736)
XLA Ops:
  0.0 1.4 %copy.13.refs_3_ = bf16[64,32]{1,0:T(8,128)(2,1)} copy(bf16[64,32]{0,1:T(8,128)(2,1)} %param.16) | data formatting | bytes 8192 | tf_op args[4]
  1.4 1.4 %copy.14.refs_4_ = bf16[64,32]{1,0:T(8,128)(2,1)} copy(bf16[64,32]{0,1:T(8,128)(2,1)} %param.17) | data formatting | bytes 8192 | tf_op args[5]
  2.8 2.6 %shard_map.118 = bf16[16,272,128]{2,1,0:T(8,128)(2,1)} custom-call(bf16[64,2048]{1,0:T(8,128)(2,1)} %refs_0_.1, bf16[64,2048]{1,0:T(8,128)(2,1)} %refs_1_.2, bf16[64,4096]{1,0:T(8,128)(2,1)} %refs_2_.1, bf16[64,32]{1,0:T(8,128)(2,1)} %copy.13.refs_3_, bf16[64,32]{1,0:T(8,128)(2,1)} %copy.14.refs_4_), custom_call_target="tpu_custom_call" | custom-call | tf_op jit(solution)/shard_map/pallas_call | solution.py:313
  5.4 23.2 %all_to_all.10.recv_ref = bf16[16,272,128]{2,1,0:T(8,128)(2,1)S(1)} all-to-all(bf16[16,272,128]{2,1,0:T(8,128)(2,1)} %shard_map.118), channel_id=1, replica_groups=mesh['half'=2,'sub'=4,'head'=4] {'sub','head'}, dimensions={0} | all-to-all | bytes 2228224 | tf_op jit(solution)/shard_map/all_to_all | solution.py:318
  28.6 0.0 copy-start
  28.6 4.5 %collective-permute-start = (bf16[64,128]{1,0:T(8,128)(2,1)S(1)}, bf16[64,128]{1,0:T(8,128)(2,1)S(1)}, u32[]{:S(2)}, u32[]{:S(2)}) collective-permute-start(bf16[64,128]{1,0:T(8,128)(2,1)S(1)} %pad_maximum_fusion), channel_id=1, source_target_pairs={{0,16},{1,17},{2,18},{3,19},{4,20},{5,21},{6,22},{7,23},{8,24},{9,... | collective-permute-start | bytes 49160 | tf_op jit(solution)/shard_map/ppermute | solution.py:322
  33.1 1.4 %collective-permute-done.rim_ref = bf16[64,128]{1,0:T(8,128)(2,1)S(1)} collective-permute-done((bf16[64,128]{1,0:T(8,128)(2,1)S(1)}, bf16[64,128]{1,0:T(8,128)(2,1)S(1)}, u32[]{:S(2)}, u32[]{:S(2)}) %collective-permute-start) | collective-permute-done | bytes 16416 | tf_op jit(solution)/shard_map/ppermute | solution.py:322
  34.5 0.0 copy-done
  34.5 0.0 copy-start.2
  34.5 0.6 copy-done.2
  35.1 14.1 %shard_map.119 = (f32[2,1024,256]{2,1,0:T(8,128)}, f32[2,128,256]{2,1,0:T(8,128)}) custom-call(bf16[16,272,128]{2,1,0:T(8,128)(2,1)} %copy-done, bf16[64,128]{1,0:T(8,128)(2,1)} %copy-done.2, f32[4,512]{1,0:T(4,128)} %cq_ref.1, f32[4,512]{1,0:T(4,128)} %ck_ref.1, f32[4,1024]{1,0:T(4,128)} %cv_ref.1, f32[8]{0:T(128)} %alog_ref.1, f32[8]{0:T(128)} %dt_ref.1), custom_call_target="tpu_custom_call" | custom-call | tf_op jit(solution)/shard_map/pallas_call | solution.py:323
  49.2 0.9 %slice.19 = f32[2,128,128]{2,1,0:T(8,128)S(1)} slice(f32[2,128,256]{2,1,0:T(8,128)} %get-tuple-element.8), slice={[0:2], [0:128], [0:128]} | slice | bytes 262144 | tf_op jit(solution)/shard_map/slice | solution.py:335
  50.1 5.1 %collective-permute-start.1 = (f32[2,128,128]{2,1,0:T(8,128)S(1)}, f32[2,128,128]{2,1,0:T(8,128)S(1)}, u32[]{:S(2)}, u32[]{:S(2)}) collective-permute-start(f32[2,128,128]{2,1,0:T(8,128)S(1)} %slice.19), channel_id=1, source_target_pairs={{0,16},{1,17},{2,18},{3,19},{4,20},{5,21},{6,22},{7,23},{8,24},{9,... | collective-permute-start | bytes 393224 | tf_op jit(solution)/shard_map/ppermute | solution.py:336
  55.2 2.5 %collective-permute-done.1.s_ref = f32[2,128,128]{2,1,0:T(8,128)S(1)} collective-permute-done((f32[2,128,128]{2,1,0:T(8,128)S(1)}, f32[2,128,128]{2,1,0:T(8,128)S(1)}, u32[]{:S(2)}, u32[]{:S(2)}) %collective-permute-start.1) | collective-permute-done | bytes 131104 | tf_op jit(solution)/shard_map/ppermute | solution.py:336
  57.7 0.0 copy-start.1
  57.7 0.6 copy-done.1
  58.4 3.2 %shard_map.120 = bf16[16,64,256]{2,1,0:T(8,128)(2,1)} custom-call(f32[2,1024,256]{2,1,0:T(8,128)} %get-tuple-element.7.o_ref, f32[2,128,128]{2,1,0:T(8,128)} %copy-done.1, f32[1,128]{1,0:T(1,128)} %bitcast.9), custom_call_target="tpu_custom_call" | custom-call | tf_op jit(solution)/shard_map/pallas_call | solution.py:340
  61.5 14.8 %all_to_all.11.refs_0_ = bf16[16,64,256]{2,1,0:T(8,128)(2,1)} all-to-all(bf16[16,64,256]{2,1,0:T(8,128)(2,1)} %shard_map.120), channel_id=1, replica_groups=mesh['half'=2,'sub'=4,'head'=4] {'sub','head'}, dimensions={0} | all-to-all | bytes 1048576 | tf_op jit(solution)/shard_map/all_to_all | solution.py:343
  76.3 2.3 %shard_map.121 = bf16[64,4096]{1,0:T(8,128)(2,1)} custom-call(bf16[16,64,256]{2,1,0:T(8,128)(2,1)} %all_to_all.11.refs_0_, bf16[64,4096]{1,0:T(8,128)(2,1)} %refs_1_.3), custom_call_target="tpu_custom_call" | custom-call | tf_op jit(solution)/shard_map/pallas_call | solution.py:344
  (2 shorter events, 0.0 us)
Async XLA Ops:
  28.6 5.9 %copy-start = (bf16[16,272,128]{2,1,0:T(8,128)(2,1)}, bf16[16,272,128]{2,1,0:T(8,128)(2,1)S(1)}, u32[]{:S(2)}) copy-start(bf16[16,272,128]{2,1,0:T(8,128)(2,1)S(1)} %all_to_all.10.recv_ref) | copy-start | bytes 3342340
  28.6 5.9 %collective-permute-start = (bf16[64,128]{1,0:T(8,128)(2,1)S(1)}, bf16[64,128]{1,0:T(8,128)(2,1)S(1)}, u32[]{:S(2)}, u32[]{:S(2)}) collective-permute-start(bf16[64,128]{1,0:T(8,128)(2,1)S(1)} %pad_maximum_fusion), channel_id=1, source_target_pairs={{0,16},{1,17},{2,18},{3,19},{4,20},{5,21},{6,22},{7,23},{8,24},{9,... | collective-permute-start | bytes 49160 | tf_op jit(solution)/shard_map/ppermute | solution.py:322
  34.5 0.6 copy-start.2
  50.1 7.6 %collective-permute-start.1 = (f32[2,128,128]{2,1,0:T(8,128)S(1)}, f32[2,128,128]{2,1,0:T(8,128)S(1)}, u32[]{:S(2)}, u32[]{:S(2)}) collective-permute-start(f32[2,128,128]{2,1,0:T(8,128)S(1)} %slice.19), channel_id=1, source_target_pairs={{0,16},{1,17},{2,18},{3,19},{4,20},{5,21},{6,22},{7,23},{8,24},{9,... | collective-permute-start | bytes 393224 | tf_op jit(solution)/shard_map/ppermute | solution.py:336
  57.7 0.6 copy-start.1

commit v2 on v1

v2 whole, which is shorter than its diff:
```python
import jax
import jax.numpy as jnp
from jax import lax
from jax.experimental import pallas as pl
from jax.experimental.pallas import tpu as pltpu
from jax.sharding import Mesh, PartitionSpec as P

DK = 128
DV = 128
CONV = 4
KH = 16
SUB = 8
SPAN = 128
EDGE = CONV - 1
EPS = 1e-06
F32 = jnp.float32
BF16 = jnp.bfloat16
VMEM_BYTES = 56 * 1024 * 1024
GATES = 16


def dot(a, b, dims=((1,), (0,))):
    return lax.dot_general(a, b, (dims, ((), ())), preferred_element_type=F32)


def halves(x):
    high = x.astype(BF16)
    return high, (x - high.astype(F32)).astype(BF16)


def mm_left(a, b):
    return dot(jnp.concatenate(halves(a), axis=1), jnp.concatenate([b, b], axis=0))


def mm_right(a, b):
    return dot(jnp.concatenate([a, a], axis=1), jnp.concatenate(halves(b), axis=0))


def mm(a, b):
    a_high, a_low = halves(a)
    b_high, b_low = halves(b)
    both = jnp.concatenate([a_high, a_low], axis=1)
    return dot(both, jnp.concatenate([b_high, b_high], axis=0)) + dot(a_high, b_low)


def silu(x):
    return x / (1.0 + jnp.exp(-x))


def unit(y, factor):
    scale = lax.rsqrt(jnp.sum(y * y, axis=-1, keepdims=True) + EPS)
    return (y * scale * factor).astype(BF16)


def iota(shape, dim):
    return lax.broadcasted_iota(jnp.int32, shape, dim)


def pack_kernel(q_ref, k_ref, v_ref, at_ref, bt_ref, out_ref):
    head = pl.program_id(0)
    subs, tokens = out_ref.shape[0], q_ref.shape[0]
    for sub in range(subs):
        lanes = slice(sub * DK, (sub + 1) * DK)
        out_ref[sub, 0, GATES : GATES + tokens, :] = k_ref[:, lanes]
        for r in range(2):
            value_head = 2 * sub + r
            out_ref[sub, 0, GATES + (1 + r) * tokens : GATES + (2 + r) * tokens, :] = v_ref[
                :, value_head * DV : (value_head + 1) * DV
            ]
        out_ref[sub, 0, GATES + 3 * tokens :, :] = q_ref[:, lanes]
    value_heads = at_ref.shape[0]
    row, entry = iota((subs * GATES, value_heads), 0), iota((subs * GATES, value_heads), 1)
    sub, which = row // GATES, row % GATES
    first = 2 * (head * subs + sub)
    pick_a = jnp.where((which < 2) & (entry == first + which), 1.0, 0.0).astype(BF16)
    pick_b = jnp.where(
        (which >= 2) & (which < 4) & (entry == first + which - 2), 1.0, 0.0
    ).astype(BF16)
    picked = (dot(pick_a, at_ref[...]) + dot(pick_b, bt_ref[...])).astype(BF16)
    lane_shift = tokens * lax.rem(lax.axis_index("head"), SPAN // tokens)
    place = jnp.where(
        iota((tokens, SPAN), 1) == iota((tokens, SPAN), 0) + lane_shift, 1.0, 0.0
    ).astype(BF16)
    gates = dot(picked, place).astype(BF16)
    for sub in range(subs):
        out_ref[sub, 0, 0:GATES, :] = gates[GATES * sub : GATES * (sub + 1), :]


def invert(systems):
    size = systems[0].shape[0]
    blocks = size // SUB
    row, col = iota((size, size), 0), iota((size, size), 1)
    diagonal = (row // SUB) == (col // SUB)
    compact = jnp.concatenate(
        [
            jnp.sum(jnp.where(diagonal, n, 0.0).reshape(blocks, SUB, size), axis=0)
            for n in systems
        ],
        axis=0,
    )
    count = len(systems)
    lane, line = iota(compact.shape, 1), iota(compact.shape, 0)
    solved = jnp.where(lane % SUB == line % SUB, 1.0, 0.0).reshape(count, SUB, size)
    for m in range(SUB - 1):
        spread = jnp.take_along_axis(compact, (lane // SUB) * SUB + m, axis=1)
        solved = solved - spread.reshape(count, SUB, size) * solved[:, m : m + 1, :]
    inverses = [
        jnp.where(
            diagonal.reshape(blocks, SUB, size), solved[i : i + 1, :, :], 0.0
        ).reshape(size, size)
        for i in range(count)
    ]
    width = SUB
    while width < size:
        odd = [(j, j + width) for j in range(width, size, 2 * width)]

        def rows_of(x):
            return jnp.concatenate([x[lo:hi] for lo, hi in odd], axis=0)

        below = rows_of(
            ((row // (2 * width)) == (col // (2 * width))) & ((col // width) % 2 == 0)
        )
        firsts = [
            mm(jnp.where(below, rows_of(n), 0.0), inv) for n, inv in zip(systems, inverses)
        ]
        zero = jnp.zeros((width, size), F32)
        spreads = []
        for first in firsts:
            parts = []
            for j in range(len(odd)):
                parts += [zero, first[j * width : (j + 1) * width]]
            spreads.append(jnp.concatenate(parts, axis=0))
        seconds = [mm(rows_of(inv), spread) for inv, spread in zip(inverses, spreads)]
        grown = []
        for inv, second in zip(inverses, seconds):
            parts = []
            for j, (lo, hi) in enumerate(odd):
                parts += [inv[lo - width : lo], inv[lo:hi] - second[j * width : (j + 1) * width]]
            grown.append(jnp.concatenate(parts, axis=0))
        inverses = grown
        width *= 2
    return inverses


def gate_values(gates, sub, alog_ref, dt_ref):
    second = iota(gates.shape, 0) % GATES == 1
    a_log = jnp.where(second, alog_ref[2 * sub + 1], alog_ref[2 * sub])
    dt_bias = jnp.where(second, dt_ref[2 * sub + 1], dt_ref[2 * sub])
    shifted = gates + dt_bias
    soft = jnp.maximum(shifted, 0.0) + jnp.log1p(jnp.exp(-jnp.abs(shifted)))
    return -jnp.exp(a_log) * soft, 1.0 / (1.0 + jnp.exp(-gates))


def convolved(rows, at, count, lanes, tap):
    summed = tap[0:1] * rows[at : at + count, lanes]
    for j in range(1, CONV):
        summed = summed + tap[j : j + 1] * rows[at + j : at + j + count, lanes]
    return silu(summed)


def taps_of(sub, ck_ref, cv_ref):
    key_lane = pl.multiple_of(sub * DK, 128)
    value_lane = pl.multiple_of(sub * 2 * DV, 128)
    return [
        ck_ref[:, pl.ds(key_lane, DK)],
        cv_ref[:, pl.ds(value_lane, DV)],
        cv_ref[:, pl.ds(pl.multiple_of(value_lane + DV, 128), DV)],
    ]


def state_kernel(
    recv_ref,
    ck_ref,
    cv_ref,
    alog_ref,
    dt_ref,
    hop_ref,
    keys_ref,
    wu_ref,
    xs_ref,
    cols_ref,
    cum_ref,
    early_ref,
    last_ref,
    raw,
    edge,
    rows,
    vs,
    sems,
):
    sub = lax.axis_index("sub")
    later = lax.axis_index("half") > 0
    peers = recv_ref.shape[0]
    tokens = (recv_ref.shape[1] - GATES) // 4
    total = peers * tokens
    spans = total // SPAN
    width = GATES + 3 * tokens
    fetch = pltpu.make_async_copy(recv_ref.at[:, pl.ds(0, width), :], raw, sems.at[0])
    fetch_edge = pltpu.make_async_copy(
        recv_ref.at[peers - 1, pl.ds(GATES + 4 * tokens - 16, 16), :], edge, sems.at[1]
    )
    fetch.start()
    fetch_edge.start()
    taps = taps_of(sub, ck_ref, cv_ref)
    rows[0:8, :] = jnp.zeros((8, 3 * 128), F32)
    fetch.wait()
    fetch_edge.wait()
    hop_ref[2 * DK : 2 * DK + 16, :] = edge[...]
    for g in range(3):
        hop_ref[2 * DK + 16 * (g + 1) : 2 * DK + 16 * (g + 2), :] = raw[
            peers - 1, GATES + (g + 1) * tokens - 16 : GATES + (g + 1) * tokens, :
        ]

    def widen(s, carry):
        start = pl.multiple_of(8 + s * tokens, 8)
        for g in range(3):
            rows[pl.ds(start, tokens), g * 128 : (g + 1) * 128] = raw[
                s, GATES + g * tokens : GATES + (g + 1) * tokens, :
            ].astype(F32)
        return carry

    lax.fori_loop(0, peers, widen, 0)
    for n in range(spans):
        at = n * SPAN
        results = [
            convolved(rows, at + 8 - EDGE, SPAN, slice(g * 128, (g + 1) * 128), taps[g])
            for g in range(3)
        ]
        keys_ref[at : at + SPAN, :] = unit(results[0], 1.0)
        vs[at : at + SPAN, 0:DV] = results[1].astype(BF16)
        vs[at : at + SPAN, DV : 2 * DV] = results[2].astype(BF16)
    gates = jnp.concatenate(
        [
            sum(raw[s, 0:GATES, :].astype(F32) for s in range(n, n + SPAN // tokens))
            for n in range(0, peers, SPAN // tokens)
        ],
        axis=0,
    )
    decay, rate = gate_values(gates, sub, alog_ref, dt_ref)
    early_ref[...] = jnp.where(iota((8, SPAN), 0) < 2, decay[0:8], rate[0:8])
    skipped = later & (iota(gates.shape, 0) < GATES) & (iota(gates.shape, 1) < EDGE)
    decay = jnp.where(skipped, 0.0, decay)
    rate = jnp.where(skipped, 0.0, rate)
    lane_r, lane_c = iota((SPAN, SPAN), 0), iota((SPAN, SPAN), 1)
    upto = jnp.where(lane_r <= lane_c, 1.0, 0.0).astype(BF16)
    d_high, d_rest = halves(decay)
    d_mid, d_low = halves(decay - d_high.astype(F32))
    cum = dot(d_high, upto) + (dot(d_mid, upto) + dot(d_low, upto))
    growth = jnp.exp(cum)
    columns = jnp.transpose(jnp.where(iota(gates.shape, 0) % GATES < 2, cum, rate))
    cum_ref[...] = cum
    cols_ref[...] = columns
    lower = lane_r >= lane_c
    strict = lane_r > lane_c
    keys, keys_t, systems = [], [], []
    for n in range(spans):
        k_n = keys_ref[n * SPAN : (n + 1) * SPAN, :]
        kt_n = jnp.transpose(k_n.astype(F32)).astype(BF16)
        gram = dot(k_n, kt_n)
        keys.append(k_n)
        keys_t.append(kt_n)
        for r in range(2):
            at = GATES * n + r
            gap = columns[:, at : at + 1] - cum[at : at + 1, :]
            within = jnp.exp(jnp.where(lower, gap, 0.0))
            systems.append(jnp.where(strict, columns[:, at + 2 : at + 3] * within * gram, 0.0))
    inverses = invert(systems)
    identity = jnp.where(lane_r == lane_c, 1.0, 0.0)
    maps = []
    for n in range(spans):
        for r in range(2):
            at = GATES * n + r
            c_col = columns[:, at : at + 1]
            t_b = inverses[2 * n + r] * rate[at + 2 : at + 3, :]
            w_mat = mm_left(t_b * growth[at : at + 1, :], keys[n])
            u_mat = mm_left(t_b, vs[n * SPAN : (n + 1) * SPAN, r * DV : (r + 1) * DV])
            both = jnp.concatenate([w_mat, u_mat], axis=1)
            wu_ref[r, n * SPAN : (n + 1) * SPAN, :] = both.astype(BF16)
            c_end = c_col[SPAN - 1 : SPAN, :]
            moved = mm_right(keys_t[n], jnp.exp(c_end - c_col) * both)
            maps.append((jnp.exp(c_end) * identity - moved[:, :DK], moved[:, DK:]))
    states = [jnp.concatenate([jnp.zeros((DK, DV), F32), identity], axis=1) for r in range(2)]
    zero_half = jnp.zeros((DK, DV), F32)
    for n in range(spans):
        for r in range(2):
            xs_ref[r, n] = states[r].astype(BF16)
            lin, add = maps[2 * n + r]
            if n == 0:
                states[r] = jnp.concatenate([add, lin], axis=1)
            else:
                states[r] = mm(lin, states[r]) + jnp.concatenate([add, zero_half], axis=1)
    for r in range(2):
        last_ref[r] = states[r]
        hop_ref[r * DK : (r + 1) * DK, :] = states[r][:, :DV].astype(BF16)


def output_kernel(
    recv_ref, cq_ref, keys_ref, wu_ref, xs_ref, cols_ref, cum_ref, oa_ref, om_ref, raw, rows, sem
):
    sub = lax.axis_index("sub")
    peers = recv_ref.shape[0]
    tokens = (recv_ref.shape[1] - GATES) // 4
    total = peers * tokens
    spans = total // SPAN
    fetch = pltpu.make_async_copy(
        recv_ref.at[:, pl.ds(GATES + 3 * tokens, tokens), :], raw, sem.at[0]
    )
    fetch.start()
    tap = cq_ref[:, pl.ds(pl.multiple_of(sub * DK, 128), DK)]
    rows[0:8, :] = jnp.zeros((8, DK), F32)
    fetch.wait()
    rows[8 : 8 + total, :] = raw[...].astype(F32).reshape(total, DK)
    lane_r, lane_c = iota((SPAN, SPAN), 0), iota((SPAN, SPAN), 1)
    lower = lane_r >= lane_c
    for n in range(spans):
        at = n * SPAN
        q_n = unit(convolved(rows, at + 8 - EDGE, SPAN, slice(0, DK), tap), DK**-0.5)
        k_n = keys_ref[at : at + SPAN, :]
        scores = dot(q_n, k_n, ((1,), (1,)))
        for r in range(2):
            c_col = cols_ref[:, GATES * n + r : GATES * n + r + 1]
            c_row = cum_ref[GATES * n + r : GATES * n + r + 1, :]
            within = jnp.exp(jnp.where(lower, c_col - c_row, 0.0))
            inner = jnp.where(lower, within * scores, 0.0).astype(BF16)
            x_n = xs_ref[r, n]
            both = wu_ref[r, at : at + SPAN, :]
            held = dot(both[:, :DK], x_n)
            fresh_a = (both[:, DK:].astype(F32) - held[:, :DV]).astype(BF16)
            fresh_m = (-held[:, DV:]).astype(BF16)
            out = jnp.exp(c_col) * dot(q_n, x_n) + dot(
                inner, jnp.concatenate([fresh_a, fresh_m], axis=1)
            )
            oa_ref[r, at : at + SPAN, :] = out[:, :DV]
            om_ref[r, at : at + SPAN, :] = out[:, DV:].astype(BF16)


def first_tokens(hop_ref, head_ref, early_ref, cq_ref, ck_ref, cv_ref, rows):
    sub = lax.axis_index("sub")
    later = lax.axis_index("half") > 0
    tokens = (head_ref.shape[0] - GATES) // 4
    starts = [GATES + 3 * tokens, GATES, GATES + tokens, GATES + 2 * tokens]
    taps = [cq_ref[:, pl.ds(pl.multiple_of(sub * DK, 128), DK)]] + taps_of(sub, ck_ref, cv_ref)
    results = []
    for g in range(4):
        lanes = slice(g * 128, (g + 1) * 128)
        rows[0:16, lanes] = hop_ref[2 * DK + 16 * g : 2 * DK + 16 * (g + 1), :].astype(F32)
        rows[16:32, lanes] = head_ref[starts[g] : starts[g] + 16, :].astype(F32)
        results.append(convolved(rows, 16 - EDGE, 8, lanes, taps[g]))
    q_cols = jnp.transpose(unit(results[0], DK**-0.5).astype(F32))
    k_cols = jnp.transpose(unit(results[1], 1.0).astype(F32))
    gates = early_ref[...]
    line = iota((8, DV), 0)
    finals, outputs = [], []
    for r in range(2):
        values = results[2 + r].astype(BF16).astype(F32)
        entering = hop_ref[r * DK : (r + 1) * DK, :].astype(F32)
        state, out = entering, jnp.zeros((8, DV), F32)
        for t in range(EDGE):
            k_t, q_t = k_cols[:, t : t + 1], q_cols[:, t : t + 1]
            state = jnp.exp(gates[r : r + 1, t : t + 1]) * state
            held = jnp.sum(k_t * state, axis=0, keepdims=True)
            state = state + k_t * (
                gates[2 + r : 3 + r, t : t + 1] * (values[t : t + 1, :] - held)
            )
            out = jnp.where(line == t, jnp.sum(q_t * state, axis=0, keepdims=True), out)
        finals.append(jnp.where(later, state, entering))
        outputs.append(out)
    return finals, outputs, later


def finish_kernel(
    hop_ref,
    head_ref,
    early_ref,
    cq_ref,
    ck_ref,
    cv_ref,
    gain_ref,
    oa_ref,
    om_ref,
    out_ref,
    rows,
    states,
    starts,
):
    step = pl.program_id(0)

    @pl.when(step == 0)
    def _():
        finals, outputs, _ = first_tokens(
            hop_ref, head_ref, early_ref, cq_ref, ck_ref, cv_ref, rows
        )
        for r in range(2):
            states[r] = finals[r].astype(BF16)
            starts[r] = outputs[r]

    gain = gain_ref[...]
    peers, tokens = out_ref.shape[0], out_ref.shape[1]
    opening = (step == 0) & (lax.axis_index("half") > 0)
    for r in range(2):
        core = oa_ref[r] + dot(om_ref[r], states[r])
        replaced = opening & (iota((8, DV), 0) < EDGE)
        core = jnp.concatenate([jnp.where(replaced, starts[r], core[0:8]), core[8:]], axis=0)
        scale = lax.rsqrt(jnp.mean(core * core, axis=-1, keepdims=True) + EPS)
        normed = (core * scale * gain).astype(BF16)
        out_ref[:, :, r * DV : (r + 1) * DV] = normed.reshape(peers, tokens, DV)


def advance_kernel(
    hop_ref, head_ref, early_ref, cq_ref, ck_ref, cv_ref, last_ref, next_ref, rows
):
    finals, _, _ = first_tokens(hop_ref, head_ref, early_ref, cq_ref, ck_ref, cv_ref, rows)
    for r in range(2):
        x = last_ref[r]
        next_ref[r * DK : (r + 1) * DK, :] = (mm(x[:, DV:], finals[r]) + x[:, :DV]).astype(BF16)
    next_ref[2 * DK :, :] = hop_ref[2 * DK :, :]


def gate_kernel(normed_ref, z_ref, out_ref):
    subs = normed_ref.shape[0]
    for sub in range(subs):
        lanes = slice(sub * 2 * DV, (sub + 1) * 2 * DV)
        gate = silu(z_ref[:, lanes].astype(F32))
        out_ref[:, lanes] = (normed_ref[sub, 0].astype(F32) * gate).astype(BF16)


VMEM = pl.BlockSpec(memory_space=pltpu.VMEM)
SMEM = pl.BlockSpec(memory_space=pltpu.SMEM)
ANY = pl.BlockSpec(memory_space=pl.ANY)


def call(kernel, outs, in_specs, out_specs=None, grid=(), scratch=(), flops=1 << 26, moved=1 << 21):
    return pl.pallas_call(
        kernel,
        grid=grid,
        out_shape=outs,
        in_specs=in_specs,
        out_specs=jax.tree.map(lambda _: VMEM, outs) if out_specs is None else out_specs,
        scratch_shapes=list(scratch),
        compiler_params=pltpu.CompilerParams(vmem_limit_bytes=VMEM_BYTES),
        cost_estimate=pl.CostEstimate(flops=flops, bytes_accessed=moved, transcendentals=0),
    )


def whole(shape):
    return pl.BlockSpec(shape, lambda i: (0,) * len(shape))


def local(
    q_rows,
    k_rows,
    v_rows,
    z_rows,
    a_rows,
    b_rows,
    conv_q,
    conv_k,
    conv_v,
    a_log,
    dt_bias,
    norm_gain,
):
    shards, subs, heads_axis = (lax.axis_size(a) for a in ("half", "sub", "head"))
    peers, tokens = subs * heads_axis, q_rows.shape[0]
    total = peers * tokens
    spans = total // SPAN
    block = GATES + 4 * tokens
    group = ("sub", "head")
    route = [(i, i + 1) for i in range(shards - 1)]
    shape = jax.ShapeDtypeStruct
    heads_in_all = a_rows.shape[1]
    columns = lambda width: pl.BlockSpec((tokens, width), lambda i: (0, i))
    packed = call(
        pack_kernel,
        shape((subs, heads_axis, block, 128), BF16),
        [columns(subs * DK), columns(subs * DK), columns(2 * subs * DV)]
        + [whole((heads_in_all, tokens))] * 2,
        pl.BlockSpec((subs, 1, block, 128), lambda i: (0, i, 0, 0)),
        (heads_axis,),
    )(q_rows, k_rows, v_rows, a_rows.T, b_rows.T)
    received = lax.all_to_all(
        packed.reshape(peers, block, 128), group, 0, 0, tiled=True
    )
    hop, keys, both, starts, cols, cum, early, last = call(
        state_kernel,
        (
            shape((2 * DK + 64, 128), BF16),
            shape((total, DK), BF16),
            shape((2, total, 2 * DV), BF16),
            shape((2, spans, DK, 2 * DV), BF16),
            shape((SPAN, spans * GATES), F32),
            shape((spans * GATES, SPAN), F32),
            shape((8, SPAN), F32),
            shape((2, DK, 2 * DV), F32),
        ),
        [ANY, VMEM, VMEM, SMEM, SMEM],
        scratch=(
            pltpu.VMEM((peers, GATES + 3 * tokens, 128), BF16),
            pltpu.VMEM((16, 128), BF16),
            pltpu.VMEM((8 + total, 384), F32),
            pltpu.VMEM((total, 2 * DV), BF16),
            pltpu.SemaphoreType.DMA((2,)),
        ),
    )(received, conv_k, conv_v, a_log, dt_bias)
    entering = lax.ppermute(hop, "half", route)
    out_a, out_m = call(
        output_kernel,
        (shape((2, total, DV), F32), shape((2, total, DV), BF16)),
        [ANY] + [VMEM] * 6,
        scratch=(
            pltpu.VMEM((peers, tokens, 128), BF16),
            pltpu.VMEM((8 + total, DK), F32),
            pltpu.SemaphoreType.DMA((1,)),
        ),
    )(received, conv_q, keys, both, starts, cols, cum)
    head_rows = pl.BlockSpec((None, block, 128), lambda i: (0, 0, 0))
    fixed = [
        whole(entering.shape),
        head_rows,
        whole(early.shape),
        whole(conv_q.shape),
        whole(conv_k.shape),
        whole(conv_v.shape),
    ]
    fixed_values = (received, early, conv_q, conv_k, conv_v)
    for _ in range(shards - 2):
        moved = call(
            advance_kernel,
            shape(hop.shape, BF16),
            fixed + [whole(last.shape)],
            whole(hop.shape),
            (1,),
            (pltpu.VMEM((32, 512), F32),),
        )(entering, *fixed_values, last)
        fresh_hop = jnp.concatenate([moved[: 2 * DK], hop[2 * DK :]], axis=0)
        entering = lax.ppermute(fresh_hop, "half", route)
    steps = 4
    normed = call(
        finish_kernel,
        shape((peers, tokens, 2 * DV), BF16),
        fixed
        + [whole((1, DV))]
        + [pl.BlockSpec((2, total // steps, DV), lambda i: (0, i, 0))] * 2,
        pl.BlockSpec((peers // steps, tokens, 2 * DV), lambda i: (i, 0, 0)),
        (steps,),
        (
            pltpu.VMEM((32, 512), F32),
            pltpu.VMEM((2, DK, DV), BF16),
            pltpu.VMEM((2, 8, DV), F32),
        ),
    )(entering, *fixed_values, norm_gain.reshape(1, DV), out_a, out_m)
    returned = lax.all_to_all(normed, group, 0, 0, tiled=True)
    return call(
        gate_kernel,
        shape((tokens, z_rows.shape[1]), BF16),
        [
            pl.BlockSpec((subs, 1, tokens, 2 * DV), lambda i: (0, i, 0, 0)),
            columns(2 * subs * DV),
        ],
        columns(2 * subs * DV),
        (heads_axis,),
    )(returned.reshape(subs, heads_axis, tokens, 2 * DV), z_rows)


def solution(mesh):
    heads_axis = mesh.shape["head"]
    subs = KH // heads_axis
    regrouped = Mesh(
        mesh.devices.reshape(mesh.shape["ctx"] // subs, subs, heads_axis), ("half", "sub", "head")
    )
    row = P(("half", "sub", "head"), None)
    placed = (row,) * 6 + (P(None, "head"),) * 3 + (P("head"),) * 2 + (P(),)
    return jax.shard_map(local, mesh=regrouped, in_specs=placed, out_specs=row, check_vma=False)
```

time: 79.2 us -> 73.8 us (0.932)
  Pallas kernels: 22.2 us -> 30 us
  starting transfers between devices: 9.6 us -> 4.48 us
  local copies, waits for them, and re-layouts: 4.94 us -> 0.62 us
  waiting for transfers between devices: 3.93 us -> 0.01 us
    pallas_call x4 -> x5, Pallas kernels: 22.2 us -> 30 us  [the longest x1 12.2 us: local(): call(state_kernel, (shape((2 * DK + 64, 128), BF16), shape((total, DK), B...]
    ppermute x2 -> x1, starting transfers between devices: 9.6 us -> 4.48 us  [local(): entering = lax.ppermute(hop, 'half', route)]
    ppermute x2 -> x1, waiting for transfers between devices: 3.93 us -> 0.01 us  [local(): entering = lax.ppermute(hop, 'half', route)]
    unnamed x8 -> x2, local copies, waits for them, and re-layouts: 4.02 us -> 0.62 us
    slice x1 -> x0, local copies, waits for them, and re-layouts: 0.91 us -> none  [local(): add, lin = (state[:, :, :DV], state[:, :, DV:])]
  transfers between devices with their start and end apart: 2 -> 1, of which waited for: 2 -> 0; matrix products, arithmetic and copies ran while one was open for 0% -> 0% of each run, Pallas kernels for 0% -> 8%
where the time goes in v2:
time: 73.8 us; the launch traced here: 73.2 us
  blocking collectives  38 us (51%)
  Pallas kernels  30 us (41%)
  starting transfers between devices  4.48 us (6%)
    all_to_all x1, blocking collectives, local(): lax.all_to_all(packed.reshape(peers, block, 128), group, 0, 0, tiled=True)  23.3 us
    all_to_all x1, blocking collectives, local(): returned = lax.all_to_all(normed, group, 0, 0, tiled=True)  14.8 us
    pallas_call x1, Pallas kernels, local(): call(state_kernel, (shape((2 * DK + 64, 128), BF16), shape((total, DK), B...  12.2 us
    pallas_call x1, Pallas kernels, local(): call(output_kernel, (shape((2, total, DV), F32), shape((2, total, DV), BF...  5.86 us
    pallas_call x1, Pallas kernels, local(): call(finish_kernel, shape((peers, tokens, 2 * DV), BF16), fixed + [whole(...  4.51 us
    ppermute x1, starting transfers between devices, local(): entering = lax.ppermute(hop, 'half', route)  4.48 us
    pallas_call x1, Pallas kernels, local(): call(pack_kernel, shape((subs, heads_axis, block, 128), BF16), [columns(s...  3.97 us
    pallas_call x1, Pallas kernels, local(): call(gate_kernel, shape((tokens, z_rows.shape[1]), BF16), [pl.BlockSpec((...  3.47 us
  transfers between devices with their start and end apart: 1, of which 0 were waited for; matrix products, arithmetic and copies ran while one was open for 0% of the time, Pallas kernels for 8%

profile of v2, /device:TPU:0, one launch (start us, length us, event | category | flops | bytes accessed | tf_op | source)
XLA Modules:
  0.0 73.2 jit_solution(5533186054451501826)
XLA Ops:
  0.0 4.0 %shard_map.118 = bf16[4,4,272,128]{3,2,1,0:T(8,128)(2,1)} custom-call(bf16[64,2048]{1,0:T(8,128)(2,1)} %q_ref.1, bf16[64,2048]{1,0:T(8,128)(2,1)} %k_ref.1, bf16[64,4096]{1,0:T(8,128)(2,1)} %v_ref.1, bf16[32,64]{1,0:T(8,128)(2,1)} %bitcast.7, bf16[32,64]{1,0:T(8,128)(2,1)} %bitcast.8), custom_call_target="tpu_custom_call" | custom-call | flops 67108864 | bytes 2097152 | tf_op jit(solution)/shard_map/pallas_call | solution.py:473
  4.0 23.3 %all_to_all.10.recv_ref.head_ref = bf16[16,272,128]{2,1,0:T(8,128)(2,1)} all-to-all(bf16[16,272,128]{2,1,0:T(8,128)(2,1)} %bitcast.5), channel_id=1, replica_groups=mesh['half'=2,'sub'=4,'head'=4] {'sub','head'}, dimensions={0} | all-to-all | bytes 2228224 | tf_op jit(solution)/shard_map/all_to_all | solution.py:481
  27.2 12.2 %shard_map.119 = (bf16[320,128]{1,0:T(8,128)(2,1)}, bf16[1024,128]{1,0:T(8,128)(2,1)}, bf16[2,1024,256]{2,1,0:T(8,128)(2,1)}, bf16[2,8,128,256]{3,2,1,0:T(8,128)...) custom-call(bf16[16,272,128]{2,1,0:T(8,128)(2,1)} %all_to_all.10.recv_ref.head_ref, ...), custom_call_target="tpu_custom_call" | custom-call | flops 67108864 | bytes 2097152 | tf_op jit(solution)/shard_map/pallas_call | solution.py:484
  39.4 4.5 %collective-permute-start = (bf16[320,128]{1,0:T(8,128)(2,1)}, bf16[320,128]{1,0:T(8,128)(2,1)S(1)}, u32[]{:S(2)}, u32[]{:S(2)}) collective-permute-start(bf16[320,128]{1,0:T(8,128)(2,1)} %get-tuple-element.14), channel_id=1, source_target_pairs={{0,16},{1,17},{2,18},{3,19},{4,20},{5,21},{6,22},{7,23},{8,24},{9,... | collective-permute-start | bytes 245768 | tf_op jit(solution)/shard_map/ppermute | solution.py:505
  43.9 5.9 %shard_map.120 = (f32[2,1024,128]{2,1,0:T(8,128)}, bf16[2,1024,128]{2,1,0:T(8,128)(2,1)}) custom-call(bf16[16,272,128]{2,1,0:T(8,128)(2,1)} %all_to_all.10.recv_ref.head_ref, f32[4,512]{1,0:T(4,128)} %cq_ref.3, bf16[1024,128]{1,0:T(8,128)(2,1)} %get-tuple-element.16.keys_ref, bf16[2,1024,256]{2,1,0:T(8,128)(2,1)} %get-tuple-element.17.wu_ref, ...), custom_call_target="tpu_custom_call" | custom-call | flops 67108864 | bytes 2097152 | tf_op jit(solution)/shard_map/pallas_call | solution.py:506
  49.8 0.0 collective-permute-done.hop_ref
  49.8 0.0 copy-start
  49.8 0.6 copy-done
  50.4 4.5 %shard_map.121 = bf16[16,64,256]{2,1,0:T(8,128)(2,1)} custom-call(bf16[320,128]{1,0:T(8,128)(2,1)} %copy-done, bf16[16,272,128]{2,1,0:T(8,128)(2,1)} %all_to_all.10.recv_ref.head_ref, f32[8,128]{1,0:T(8,128)} %get-tuple-element.15.early_ref, f32[4,512]{1,0:T(4,128)} %cq_ref.3, f32[4,512]{1,0:T(4,128)} %ck_ref.3, f32[4,1024]{1,0:T(4,128)} %cv_ref.3, ...), custom_call_target="tpu_custom_call" | custom-call | flops 67108864 | bytes 2097152 | tf_op jit(solution)/shard_map/pallas_call | solution.py:538
  55.0 14.8 %all_to_all.11 = bf16[16,64,256]{2,1,0:T(8,128)(2,1)} all-to-all(bf16[16,64,256]{2,1,0:T(8,128)(2,1)} %shard_map.121), channel_id=1, replica_groups=mesh['half'=2,'sub'=4,'head'=4] {'sub','head'}, dimensions={0} | all-to-all | bytes 1048576 | tf_op jit(solution)/shard_map/all_to_all | solution.py:552
  69.7 3.5 %shard_map.122 = bf16[64,4096]{1,0:T(8,128)(2,1)} custom-call(bf16[4,4,64,256]{3,2,1,0:T(8,128)(2,1)} %bitcast.6, bf16[64,4096]{1,0:T(8,128)(2,1)} %z_ref.1), custom_call_target="tpu_custom_call" | custom-call | flops 67108864 | bytes 2097152 | tf_op jit(solution)/shard_map/pallas_call | solution.py:553
Async XLA Ops:
  39.4 10.4 %collective-permute-start = (bf16[320,128]{1,0:T(8,128)(2,1)}, bf16[320,128]{1,0:T(8,128)(2,1)S(1)}, u32[]{:S(2)}, u32[]{:S(2)}) collective-permute-start(bf16[320,128]{1,0:T(8,128)(2,1)} %get-tuple-element.14), channel_id=1, source_target_pairs={{0,16},{1,17},{2,18},{3,19},{4,20},{5,21},{6,22},{7,23},{8,24},{9,... | collective-permute-start | bytes 245768 | tf_op jit(solution)/shard_map/ppermute | solution.py:505
  49.8 0.6 copy-start

commit v3 on v2

v3 whole, which is shorter than its diff:
```python
import functools

import jax
import jax.numpy as jnp
from jax import lax
from jax.experimental import pallas as pl
from jax.experimental.pallas import tpu as pltpu
from jax.sharding import Mesh, PartitionSpec as P

DK = 128
DV = 128
CONV = 4
KH = 16
SUB = 8
SPAN = 128
EDGE = CONV - 1
EPS = 1e-06
F32 = jnp.float32
BF16 = jnp.bfloat16
VMEM_BYTES = 56 * 1024 * 1024
GATES = 16


def dot(a, b, dims=((1,), (0,))):
    return lax.dot_general(a, b, (dims, ((), ())), preferred_element_type=F32)


def halves(x):
    high = x.astype(BF16)
    return high, (x - high.astype(F32)).astype(BF16)


def mm_left(a, b):
    return dot(jnp.concatenate(halves(a), axis=1), jnp.concatenate([b, b], axis=0))


def mm_right(a, b):
    return dot(jnp.concatenate([a, a], axis=1), jnp.concatenate(halves(b), axis=0))


def mm(a, b):
    a_high, a_low = halves(a)
    b_high, b_low = halves(b)
    both = jnp.concatenate([a_high, a_low], axis=1)
    return dot(both, jnp.concatenate([b_high, b_high], axis=0)) + dot(a_high, b_low)


def silu(x):
    return x / (1.0 + jnp.exp(-x))


def unit(y, factor):
    scale = lax.rsqrt(jnp.sum(y * y, axis=-1, keepdims=True) + EPS)
    return (y * scale * factor).astype(BF16)


def iota(shape, dim):
    return lax.broadcasted_iota(jnp.int32, shape, dim)


def pack_keys_kernel(heads_axis, k_ref, at_ref, bt_ref, out_ref):
    peers, tokens = out_ref.shape[0], k_ref.shape[0]
    subs = peers // heads_axis
    for dest in range(peers):
        key_head = (dest % heads_axis) * subs + dest // heads_axis
        out_ref[dest, GATES:, :] = k_ref[:, key_head * DK : (key_head + 1) * DK]
    value_heads = at_ref.shape[0]
    row, entry = iota((peers * GATES, value_heads), 0), iota((peers * GATES, value_heads), 1)
    dest, which = row // GATES, row % GATES
    first = 2 * ((dest % heads_axis) * subs + dest // heads_axis)
    pick_a = jnp.where((which < 2) & (entry == first + which), 1.0, 0.0).astype(BF16)
    pick_b = jnp.where(
        (which >= 2) & (which < 4) & (entry == first + which - 2), 1.0, 0.0
    ).astype(BF16)
    picked = (dot(pick_a, at_ref[...]) + dot(pick_b, bt_ref[...])).astype(BF16)
    lane_shift = tokens * lax.rem(lax.axis_index("head"), SPAN // tokens)
    place = jnp.where(
        iota((tokens, SPAN), 1) == iota((tokens, SPAN), 0) + lane_shift, 1.0, 0.0
    ).astype(BF16)
    gates = dot(picked, place).astype(BF16)
    for dest in range(peers):
        out_ref[dest, 0:GATES, :] = gates[GATES * dest : GATES * (dest + 1), :]


def pack_values_kernel(heads_axis, v_ref, q_ref, out_ref):
    peers, tokens = out_ref.shape[0], q_ref.shape[0]
    subs = peers // heads_axis
    for dest in range(peers):
        key_head = (dest % heads_axis) * subs + dest // heads_axis
        for r in range(2):
            lanes = slice((2 * key_head + r) * DV, (2 * key_head + r + 1) * DV)
            out_ref[dest, r * tokens : (r + 1) * tokens, :] = v_ref[:, lanes]
        out_ref[dest, 2 * tokens :, :] = q_ref[:, key_head * DK : (key_head + 1) * DK]


def invert(systems):
    size = systems[0].shape[0]
    blocks = size // SUB
    row, col = iota((size, size), 0), iota((size, size), 1)
    diagonal = (row // SUB) == (col // SUB)
    compact = jnp.concatenate(
        [
            jnp.sum(jnp.where(diagonal, n, 0.0).reshape(blocks, SUB, size), axis=0)
            for n in systems
        ],
        axis=0,
    )
    count = len(systems)
    lane, line = iota(compact.shape, 1), iota(compact.shape, 0)
    solved = jnp.where(lane % SUB == line % SUB, 1.0, 0.0).reshape(count, SUB, size)
    for m in range(SUB - 1):
        spread = jnp.take_along_axis(compact, (lane // SUB) * SUB + m, axis=1)
        solved = solved - spread.reshape(count, SUB, size) * solved[:, m : m + 1, :]
    inverses = [
        jnp.where(
            diagonal.reshape(blocks, SUB, size), solved[i : i + 1, :, :], 0.0
        ).reshape(size, size)
        for i in range(count)
    ]
    width = SUB
    while width < size:
        odd = [(j, j + width) for j in range(width, size, 2 * width)]

        def rows_of(x):
            return jnp.concatenate([x[lo:hi] for lo, hi in odd], axis=0)

        below = rows_of(
            ((row // (2 * width)) == (col // (2 * width))) & ((col // width) % 2 == 0)
        )
        firsts = [
            mm(jnp.where(below, rows_of(n), 0.0), inv) for n, inv in zip(systems, inverses)
        ]
        zero = jnp.zeros((width, size), F32)
        spreads = []
        for first in firsts:
            parts = []
            for j in range(len(odd)):
                parts += [zero, first[j * width : (j + 1) * width]]
            spreads.append(jnp.concatenate(parts, axis=0))
        seconds = [mm(rows_of(inv), spread) for inv, spread in zip(inverses, spreads)]
        grown = []
        for inv, second in zip(inverses, seconds):
            parts = []
            for j, (lo, hi) in enumerate(odd):
                parts += [inv[lo - width : lo], inv[lo:hi] - second[j * width : (j + 1) * width]]
            grown.append(jnp.concatenate(parts, axis=0))
        inverses = grown
        width *= 2
    return inverses


def gate_values(gates, sub, alog_ref, dt_ref):
    second = iota(gates.shape, 0) % GATES == 1
    a_log = jnp.where(second, alog_ref[2 * sub + 1], alog_ref[2 * sub])
    dt_bias = jnp.where(second, dt_ref[2 * sub + 1], dt_ref[2 * sub])
    shifted = gates + dt_bias
    soft = jnp.maximum(shifted, 0.0) + jnp.log1p(jnp.exp(-jnp.abs(shifted)))
    return -jnp.exp(a_log) * soft, 1.0 / (1.0 + jnp.exp(-gates))


def convolved(rows, at, count, lanes, tap):
    summed = tap[0:1] * rows[at : at + count, lanes]
    for j in range(1, CONV):
        summed = summed + tap[j : j + 1] * rows[at + j : at + j + count, lanes]
    return silu(summed)


def key_tap(sub, tap_ref):
    return tap_ref[:, pl.ds(pl.multiple_of(sub * DK, 128), DK)]


def value_taps(sub, cv_ref):
    lane = pl.multiple_of(sub * 2 * DV, 128)
    return [cv_ref[:, pl.ds(pl.multiple_of(lane + r * DV, 128), DV)] for r in range(2)]


def inverse_kernel(
    recv_ref,
    ck_ref,
    alog_ref,
    dt_ref,
    keys_ref,
    tb_ref,
    w_ref,
    lin_ref,
    ms_ref,
    cols_ref,
    cum_ref,
    early_ref,
    edge_ref,
    rows,
):
    sub = lax.axis_index("sub")
    later = lax.axis_index("half") > 0
    peers = recv_ref.shape[0]
    tokens = recv_ref.shape[1] - GATES
    total = peers * tokens
    spans = total // SPAN
    edge_ref[...] = recv_ref[peers - 1, GATES + tokens - 16 :, :]
    tap = key_tap(sub, ck_ref)
    rows[0:8, :] = jnp.zeros((8, DK), F32)
    for s in range(peers):
        rows[8 + s * tokens : 8 + (s + 1) * tokens, :] = recv_ref[s, GATES:, :].astype(F32)
    gates = jnp.concatenate(
        [
            sum(recv_ref[s, 0:GATES, :].astype(F32) for s in range(n, n + SPAN // tokens))
            for n in range(0, peers, SPAN // tokens)
        ],
        axis=0,
    )
    decay, rate = gate_values(gates, sub, alog_ref, dt_ref)
    early_ref[...] = jnp.where(iota((8, SPAN), 0) < 2, decay[0:8], rate[0:8])
    skipped = later & (iota(gates.shape, 0) < GATES) & (iota(gates.shape, 1) < EDGE)
    decay = jnp.where(skipped, 0.0, decay)
    rate = jnp.where(skipped, 0.0, rate)
    lane_r, lane_c = iota((SPAN, SPAN), 0), iota((SPAN, SPAN), 1)
    upto = jnp.where(lane_r <= lane_c, 1.0, 0.0).astype(BF16)
    d_high, d_rest = halves(decay)
    d_mid, d_low = halves(decay - d_high.astype(F32))
    cum = dot(d_high, upto) + (dot(d_mid, upto) + dot(d_low, upto))
    growth = jnp.exp(cum)
    columns = jnp.transpose(jnp.where(iota(gates.shape, 0) % GATES < 2, cum, rate))
    cum_ref[...] = cum
    cols_ref[...] = columns
    lower = lane_r >= lane_c
    strict = lane_r > lane_c
    keys, keys_t, systems = [], [], []
    for n in range(spans):
        k_n = unit(convolved(rows, n * SPAN + 8 - EDGE, SPAN, slice(0, DK), tap), 1.0)
        keys_ref[n * SPAN : (n + 1) * SPAN, :] = k_n
        kt_n = jnp.transpose(k_n.astype(F32)).astype(BF16)
        gram = dot(k_n, kt_n)
        keys.append(k_n)
        keys_t.append(kt_n)
        for r in range(2):
            at = GATES * n + r
            gap = columns[:, at : at + 1] - cum[at : at + 1, :]
            within = jnp.exp(jnp.where(lower, gap, 0.0))
            systems.append(jnp.where(strict, columns[:, at + 2 : at + 3] * within * gram, 0.0))
    inverses = invert(systems)
    identity = jnp.where(lane_r == lane_c, 1.0, 0.0)
    lins = []
    for n in range(spans):
        for r in range(2):
            at = GATES * n + r
            c_col = columns[:, at : at + 1]
            t_b = inverses[2 * n + r] * rate[at + 2 : at + 3, :]
            tb_ref[r, n] = jnp.concatenate(halves(t_b), axis=1)
            w_mat = mm_left(t_b * growth[at : at + 1, :], keys[n])
            w_ref[r, n * SPAN : (n + 1) * SPAN, :] = w_mat.astype(BF16)
            c_end = c_col[SPAN - 1 : SPAN, :]
            lin = jnp.exp(c_end) * identity - mm_right(keys_t[n], jnp.exp(c_end - c_col) * w_mat)
            lin_ref[r, n] = jnp.concatenate(halves(lin), axis=1)
            lins.append(lin)
    states = [identity, identity]
    for n in range(spans):
        for r in range(2):
            ms_ref[r, n] = states[r].astype(BF16)
            states[r] = lins[r] if n == 0 else mm(lins[2 * n + r], states[r])
    for r in range(2):
        ms_ref[r, spans] = states[r].astype(BF16)


def state_kernel(
    recv_ref, cv_ref, keys_ref, tb_ref, lin_ref, cols_ref, edge_ref, hop_ref, u_ref, xs_ref, raw, rows, sem
):
    sub = lax.axis_index("sub")
    peers = recv_ref.shape[0]
    tokens = recv_ref.shape[1] // 3
    total = peers * tokens
    spans = total // SPAN
    fetch = pltpu.make_async_copy(recv_ref, raw, sem.at[0])
    fetch.start()
    taps = value_taps(sub, cv_ref)
    rows[0:8, :] = jnp.zeros((8, 2 * DV), F32)
    hop_ref[2 * DK + 16 : 2 * DK + 32, :] = edge_ref[...]
    fetch.wait()
    for at, first in ((0, 2 * tokens), (32, 0), (48, tokens)):
        hop_ref[2 * DK + at : 2 * DK + at + 16, :] = raw[
            peers - 1, first + tokens - 16 : first + tokens, :
        ]
    for s in range(peers):
        for r in range(2):
            rows[8 + s * tokens : 8 + (s + 1) * tokens, r * DV : (r + 1) * DV] = raw[
                s, r * tokens : (r + 1) * tokens, :
            ].astype(F32)
    adds = []
    for n in range(spans):
        at = n * SPAN
        kt_n = jnp.transpose(keys_ref[at : at + SPAN, :].astype(F32)).astype(BF16)
        for r in range(2):
            v_n = convolved(
                rows, at + 8 - EDGE, SPAN, slice(r * DV, (r + 1) * DV), taps[r]
            ).astype(BF16)
            u_mat = dot(tb_ref[r, n], jnp.concatenate([v_n, v_n], axis=0))
            u_ref[r, at : at + SPAN, :] = u_mat.astype(BF16)
            c_col = cols_ref[:, GATES * n + r : GATES * n + r + 1]
            adds.append(mm_right(kt_n, jnp.exp(c_col[SPAN - 1 : SPAN, :] - c_col) * u_mat))
    states = [None, None]
    for r in range(2):
        xs_ref[r, 0] = jnp.zeros((DK, DV), BF16)
    for n in range(spans):
        for r in range(2):
            if n == 0:
                states[r] = adds[r]
            else:
                high, low = halves(states[r])
                xs_ref[r, n] = high
                lin = lin_ref[r, n]
                states[r] = (
                    dot(lin, jnp.concatenate([high, high], axis=0))
                    + dot(lin[:, :DK], low)
                    + adds[2 * n + r]
                )
    for r in range(2):
        hop_ref[r * DK : (r + 1) * DK, :] = states[r].astype(BF16)


def output_kernel(
    recv_ref,
    cq_ref,
    keys_ref,
    w_ref,
    u_ref,
    xs_ref,
    ms_ref,
    cols_ref,
    cum_ref,
    oa_ref,
    om_ref,
    raw,
    rows,
    sem,
):
    sub = lax.axis_index("sub")
    peers = recv_ref.shape[0]
    tokens = recv_ref.shape[1] // 3
    total = peers * tokens
    spans = total // SPAN
    fetch = pltpu.make_async_copy(
        recv_ref.at[:, pl.ds(2 * tokens, tokens), :], raw, sem.at[0]
    )
    fetch.start()
    tap = key_tap(sub, cq_ref)
    rows[0:8, :] = jnp.zeros((8, DK), F32)
    fetch.wait()
    rows[8 : 8 + total, :] = raw[...].astype(F32).reshape(total, DK)
    lane_r, lane_c = iota((SPAN, SPAN), 0), iota((SPAN, SPAN), 1)
    lower = lane_r >= lane_c
    for n in range(spans):
        at = n * SPAN
        q_n = unit(convolved(rows, at + 8 - EDGE, SPAN, slice(0, DK), tap), DK**-0.5)
        k_n = keys_ref[at : at + SPAN, :]
        scores = dot(q_n, k_n, ((1,), (1,)))
        for r in range(2):
            c_col = cols_ref[:, GATES * n + r : GATES * n + r + 1]
            c_row = cum_ref[GATES * n + r : GATES * n + r + 1, :]
            within = jnp.exp(jnp.where(lower, c_col - c_row, 0.0))
            inner = jnp.where(lower, within * scores, 0.0).astype(BF16)
            x_n = jnp.concatenate([xs_ref[r, n], ms_ref[r, n]], axis=1)
            held = dot(w_ref[r, at : at + SPAN, :], x_n)
            fresh_a = (u_ref[r, at : at + SPAN, :].astype(F32) - held[:, :DV]).astype(BF16)
            fresh_m = (-held[:, DV:]).astype(BF16)
            out = jnp.exp(c_col) * dot(q_n, x_n) + dot(
                inner, jnp.concatenate([fresh_a, fresh_m], axis=1)
            )
            oa_ref[r, at : at + SPAN, :] = out[:, :DV]
            om_ref[r, at : at + SPAN, :] = out[:, DV:].astype(BF16)


def first_tokens(hop_ref, keys_head, values_head, early_ref, cq_ref, ck_ref, cv_ref, rows):
    sub = lax.axis_index("sub")
    later = lax.axis_index("half") > 0
    tokens = values_head.shape[0] // 3
    opening = [values_head[2 * tokens : 2 * tokens + 16, :], keys_head[GATES : GATES + 16, :]]
    opening += [values_head[r * tokens : r * tokens + 16, :] for r in range(2)]
    taps = [key_tap(sub, cq_ref), key_tap(sub, ck_ref)] + value_taps(sub, cv_ref)
    results = []
    for g in range(4):
        lanes = slice(g * 128, (g + 1) * 128)
        rows[0:16, lanes] = hop_ref[2 * DK + 16 * g : 2 * DK + 16 * (g + 1), :].astype(F32)
        rows[16:32, lanes] = opening[g].astype(F32)
        results.append(convolved(rows, 16 - EDGE, 8, lanes, taps[g]))
    q_cols = jnp.transpose(unit(results[0], DK**-0.5).astype(F32))
    k_cols = jnp.transpose(unit(results[1], 1.0).astype(F32))
    gates = early_ref[...]
    line = iota((8, DV), 0)
    finals, outputs = [], []
    for r in range(2):
        values = results[2 + r].astype(BF16).astype(F32)
        entering = hop_ref[r * DK : (r + 1) * DK, :].astype(F32)
        state, out = entering, jnp.zeros((8, DV), F32)
        for t in range(EDGE):
            k_t, q_t = k_cols[:, t : t + 1], q_cols[:, t : t + 1]
            state = jnp.exp(gates[r : r + 1, t : t + 1]) * state
            held = jnp.sum(k_t * state, axis=0, keepdims=True)
            state = state + k_t * (
                gates[2 + r : 3 + r, t : t + 1] * (values[t : t + 1, :] - held)
            )
            out = jnp.where(line == t, jnp.sum(q_t * state, axis=0, keepdims=True), out)
        finals.append(jnp.where(later, state, entering))
        outputs.append(out)
    return finals, outputs, later


def finish_kernel(
    hop_in,
    keys_head,
    values_head,
    early_ref,
    cq_ref,
    ck_ref,
    cv_ref,
    gain_ref,
    oa_ref,
    om_ref,
    out_ref,
    hop,
    heads_k,
    heads_v,
    oa,
    om,
    made,
    rows,
    sems,
):
    peers, tokens = out_ref.shape[0], out_ref.shape[1]
    total = peers * tokens
    chunks = 4
    part, peer_part = total // chunks, peers // chunks
    first = [
        pltpu.make_async_copy(hop_in, hop, sems.at[0]),
        pltpu.make_async_copy(keys_head.at[0], heads_k, sems.at[1]),
        pltpu.make_async_copy(values_head.at[0], heads_v, sems.at[2]),
    ]
    fetches = []
    for c in range(chunks):
        here = pl.ds(c * part, part)
        fetches.append(
            [
                pltpu.make_async_copy(oa_ref.at[:, here, :], oa.at[:, here, :], sems.at[3 + 2 * c]),
                pltpu.make_async_copy(om_ref.at[:, here, :], om.at[:, here, :], sems.at[4 + 2 * c]),
            ]
        )
    for copy in first:
        copy.start()
    for pair in fetches:
        for copy in pair:
            copy.start()
    for copy in first:
        copy.wait()
    finals, outputs, later = first_tokens(
        hop, heads_k, heads_v, early_ref, cq_ref, ck_ref, cv_ref, rows
    )
    states = [x.astype(BF16) for x in finals]
    gain = gain_ref[...]
    replaced = later & (iota((8, DV), 0) < EDGE)
    stores = []
    for c in range(chunks):
        for copy in fetches[c]:
            copy.wait()
        at = c * part
        for r in range(2):
            core = oa[r, at : at + part, :] + dot(om[r, at : at + part, :], states[r])
            if c == 0:
                core = jnp.concatenate(
                    [jnp.where(replaced, outputs[r], core[0:8]), core[8:]], axis=0
                )
            scale = lax.rsqrt(jnp.mean(core * core, axis=-1, keepdims=True) + EPS)
            normed = (core * scale * gain).astype(BF16)
            made[c * peer_part : (c + 1) * peer_part, :, r * DV : (r + 1) * DV] = normed.reshape(
                peer_part, tokens, DV
            )
        here = pl.ds(c * peer_part, peer_part)
        store = pltpu.make_async_copy(made.at[here], out_ref.at[here], sems.at[3 + 2 * chunks + c])
        store.start()
        stores.append(store)
    for store in stores:
        store.wait()


def advance_kernel(
    hop_in,
    keys_head,
    values_head,
    early_ref,
    cq_ref,
    ck_ref,
    cv_ref,
    hop_own,
    ms_ref,
    next_ref,
    rows,
):
    finals, _, _ = first_tokens(
        hop_in, keys_head.at[0], values_head.at[0], early_ref, cq_ref, ck_ref, cv_ref, rows
    )
    last = ms_ref.shape[1] - 1
    for r in range(2):
        own = hop_own[r * DK : (r + 1) * DK, :].astype(F32)
        next_ref[r * DK : (r + 1) * DK, :] = (mm_right(ms_ref[r, last], finals[r]) + own).astype(
            BF16
        )
    next_ref[2 * DK :, :] = hop_own[2 * DK :, :]


def gate_kernel(heads_axis, normed_ref, z_ref, out_ref, normed, z, made, sems):
    peers, tokens = normed_ref.shape[0], normed_ref.shape[1]
    subs = peers // heads_axis
    width = subs * 2 * DV
    fetches, stores = [], []
    for head in range(heads_axis):
        lanes = pl.ds(head * width, width)
        fetches.append([pltpu.make_async_copy(z_ref.at[:, lanes], z.at[:, lanes], sems.at[0, head])])
    for sub in range(subs):
        here = pl.ds(sub * heads_axis, heads_axis)
        fetches[sub % heads_axis].append(
            pltpu.make_async_copy(normed_ref.at[here], normed.at[here], sems.at[1, sub])
        )
    for copies in fetches:
        for copy in copies:
            copy.start()
    for copies in fetches:
        for copy in copies:
            copy.wait()
    for head in range(heads_axis):
        for sub in range(subs):
            at = (head * subs + sub) * 2 * DV
            gate = silu(z[:, at : at + 2 * DV].astype(F32))
            value = normed[sub * heads_axis + head].astype(F32)
            made[:, at : at + 2 * DV] = (value * gate).astype(BF16)
        lanes = pl.ds(head * width, width)
        store = pltpu.make_async_copy(made.at[:, lanes], out_ref.at[:, lanes], sems.at[2, head])
        store.start()
        stores.append(store)
    for store in stores:
        store.wait()


VMEM = pl.BlockSpec(memory_space=pltpu.VMEM)
SMEM = pl.BlockSpec(memory_space=pltpu.SMEM)
ANY = pl.BlockSpec(memory_space=pl.ANY)


def call(kernel, outs, in_specs, out_specs=None, scratch=(), flops=1 << 26, moved=1 << 21):
    return pl.pallas_call(
        kernel,
        out_shape=outs,
        in_specs=in_specs,
        out_specs=jax.tree.map(lambda _: VMEM, outs) if out_specs is None else out_specs,
        scratch_shapes=list(scratch),
        compiler_params=pltpu.CompilerParams(vmem_limit_bytes=VMEM_BYTES),
        cost_estimate=pl.CostEstimate(flops=flops, bytes_accessed=moved, transcendentals=0),
    )


def local(
    q_rows,
    k_rows,
    v_rows,
    z_rows,
    a_rows,
    b_rows,
    conv_q,
    conv_k,
    conv_v,
    a_log,
    dt_bias,
    norm_gain,
):
    shards, subs, heads_axis = (lax.axis_size(a) for a in ("half", "sub", "head"))
    peers, tokens = subs * heads_axis, q_rows.shape[0]
    total = peers * tokens
    spans = total // SPAN
    group = ("sub", "head")
    route = [(i, i + 1) for i in range(shards - 1)]
    shape = jax.ShapeDtypeStruct
    key_block, value_block = GATES + tokens, 3 * tokens
    packed_keys = call(
        functools.partial(pack_keys_kernel, heads_axis),
        shape((peers, key_block, 128), BF16),
        [VMEM] * 3,
        flops=1 << 20,
    )(k_rows, a_rows.T, b_rows.T)
    key_blocks = lax.all_to_all(packed_keys, group, 0, 0, tiled=True)
    packed_values = call(
        functools.partial(pack_values_kernel, heads_axis),
        shape((peers, value_block, 128), BF16),
        [VMEM] * 2,
        flops=1 << 20,
    )(v_rows, q_rows)
    value_blocks = lax.all_to_all(packed_values, group, 0, 0, tiled=True)
    keys, t_b, w_mats, lins, ms, cols, cum, early, edge = call(
        inverse_kernel,
        (
            shape((total, DK), BF16),
            shape((2, spans, SPAN, 2 * SPAN), BF16),
            shape((2, total, DK), BF16),
            shape((2, spans, DK, 2 * DK), BF16),
            shape((2, spans + 1, DK, DK), BF16),
            shape((SPAN, spans * GATES), F32),
            shape((spans * GATES, SPAN), F32),
            shape((8, SPAN), F32),
            shape((16, 128), BF16),
        ),
        [VMEM, VMEM, SMEM, SMEM],
        scratch=(pltpu.VMEM((8 + total, DK), F32),),
        flops=1 << 32,
    )(key_blocks, conv_k, a_log, dt_bias)
    hop, u_mats, starts = call(
        state_kernel,
        (
            shape((2 * DK + 64, 128), BF16),
            shape((2, total, DV), BF16),
            shape((2, spans, DK, DV), BF16),
        ),
        [ANY] + [VMEM] * 6,
        scratch=(
            pltpu.VMEM((peers, value_block, 128), BF16),
            pltpu.VMEM((8 + total, 2 * DV), F32),
            pltpu.SemaphoreType.DMA((1,)),
        ),
    )(value_blocks, conv_v, keys, t_b, lins, cols, edge)
    entering = lax.ppermute(hop, "half", route)
    out_a, out_m = call(
        output_kernel,
        (shape((2, total, DV), F32), shape((2, total, DV), BF16)),
        [ANY] + [VMEM] * 8,
        scratch=(
            pltpu.VMEM((peers, tokens, 128), BF16),
            pltpu.VMEM((8 + total, DK), F32),
            pltpu.SemaphoreType.DMA((1,)),
        ),
        flops=1 << 32,
    )(value_blocks, conv_q, keys, w_mats, u_mats, starts, ms, cols, cum)
    for _ in range(shards - 2):
        moved = call(
            advance_kernel,
            shape(hop.shape, BF16),
            [VMEM] * 9,
            scratch=(pltpu.VMEM((32, 512), F32),),
        )(entering, key_blocks[:1], value_blocks[:1], early, conv_q, conv_k, conv_v, hop, ms)
        entering = lax.ppermute(moved, "half", route)
    chunks = 4
    normed = call(
        finish_kernel,
        shape((peers, tokens, 2 * DV), BF16),
        [ANY] * 3 + [VMEM] * 5 + [ANY] * 2,
        ANY,
        (
            pltpu.VMEM(hop.shape, BF16),
            pltpu.VMEM((key_block, 128), BF16),
            pltpu.VMEM((value_block, 128), BF16),
            pltpu.VMEM((2, total, DV), F32),
            pltpu.VMEM((2, total, DV), BF16),
            pltpu.VMEM((peers, tokens, 2 * DV), BF16),
            pltpu.VMEM((32, 512), F32),
            pltpu.SemaphoreType.DMA((3 + 3 * chunks,)),
        ),
    )(
        entering,
        key_blocks,
        value_blocks,
        early,
        conv_q,
        conv_k,
        conv_v,
        norm_gain.reshape(1, DV),
        out_a,
        out_m,
    )
    returned = lax.all_to_all(normed, group, 0, 0, tiled=True)
    return call(
        functools.partial(gate_kernel, heads_axis),
        shape(z_rows.shape, BF16),
        [ANY] * 2,
        ANY,
        (
            pltpu.VMEM(normed.shape, BF16),
            pltpu.VMEM(z_rows.shape, BF16),
            pltpu.VMEM(z_rows.shape, BF16),
            pltpu.SemaphoreType.DMA((3, max(heads_axis, subs))),
        ),
    )(returned, z_rows)


def solution(mesh):
    heads_axis = mesh.shape["head"]
    subs = KH // heads_axis
    regrouped = Mesh(
        mesh.devices.reshape(mesh.shape["ctx"] // subs, subs, heads_axis), ("half", "sub", "head")
    )
    row = P(("half", "sub", "head"), None)
    placed = (row,) * 6 + (P(None, "head"),) * 3 + (P("head"),) * 2 + (P(),)
    return jax.shard_map(local, mesh=regrouped, in_specs=placed, out_specs=row, check_vma=False)
```

time: 73.8 us -> 74.4 us (level)
  blocking collectives: 38 us -> 14.8 us
  waiting for transfers between devices: 0.01 us -> 11.6 us
  starting transfers between devices: 4.48 us -> 14.4 us
  local copies, waits for them, and re-layouts: 0.62 us -> 2.23 us
    all_to_all x1 -> x0, blocking collectives: 23.3 us -> none  [local(): lax.all_to_all(packed.reshape(peers, block, 128), group, 0, 0, tiled=True)]
    all_to_all x0 -> x2, waiting for transfers between devices: none -> 11.6 us  [the longest x1 6.31 us: local(): key_blocks = lax.all_to_all(packed_keys, group, 0, 0, tiled=True)]
    all_to_all x0 -> x2, starting transfers between devices: none -> 9.9 us  [the longest x1 6.29 us: local(): key_blocks = lax.all_to_all(packed_keys, group, 0, 0, tiled=True)]
    unnamed x2 -> x6, local copies, waits for them, and re-layouts: 0.62 us -> 2.23 us
    pallas_call x4 -> x6, Pallas kernels: 24.1 us -> 24.7 us  [the longest x1 7.99 us: local(): call(inverse_kernel, (shape((total, DK), BF16), shape((2, spans, SPAN, 2...]
  transfers between devices with their start and end apart: 1 -> 3, of which waited for: 0 -> 2; matrix products, arithmetic and copies ran while one was open for 0% -> 0% of each run, Pallas kernels for 8% -> 22%
where the time goes in v3:
time: 74.4 us; the launch traced here: 73.7 us
  Pallas kernels  30.6 us (41%)
  blocking collectives  14.8 us (20%)
  starting transfers between devices  14.4 us (19%)
  waiting for transfers between devices  11.6 us (16%)
  local copies, waits for them, and re-layouts  2.23 us (3%)
    all_to_all x1, blocking collectives, local(): returned = lax.all_to_all(normed, group, 0, 0, tiled=True)  14.8 us
    pallas_call x1, Pallas kernels, local(): call(inverse_kernel, (shape((total, DK), BF16), shape((2, spans, SPAN, 2...  7.99 us
    all_to_all x1, waiting for transfers between devices, local(): key_blocks = lax.all_to_all(packed_keys, group, 0, 0, tiled=True)  6.31 us
    all_to_all x1, starting transfers between devices, local(): key_blocks = lax.all_to_all(packed_keys, group, 0, 0, tiled=True)  6.29 us
    pallas_call x1, Pallas kernels, local(): call(state_kernel, (shape((2 * DK + 64, 128), BF16), shape((2, total, DV)...  6.11 us
    pallas_call x1, Pallas kernels, local(): call(output_kernel, (shape((2, total, DV), F32), shape((2, total, DV), BF...  5.87 us
    all_to_all x1, waiting for transfers between devices, local(): value_blocks = lax.all_to_all(packed_values, group, 0, 0, tiled=True)  5.33 us
    ppermute x1, starting transfers between devices, local(): entering = lax.ppermute(hop, 'half', route)  4.49 us
  transfers between devices with their start and end apart: 3, of which 2 were waited for; matrix products, arithmetic and copies ran while one was open for 0% of the time, Pallas kernels for 22%

profile of v3, /device:TPU:0, one launch (start us, length us, event | category | flops | bytes accessed | tf_op | source)
XLA Modules:
  0.0 73.7 jit_solution(8915230987623388768)
XLA Ops:
  0.0 2.0 %shard_map.119 = bf16[16,80,128]{2,1,0:T(8,128)(2,1)} custom-call(bf16[64,2048]{1,0:T(8,128)(2,1)} %k_ref.1, bf16[32,64]{1,0:T(8,128)(2,1)} %bitcast.3, bf16[32,64]{1,0:T(8,128)(2,1)} %bitcast.4), custom_call_target="tpu_custom_call" | custom-call | flops 1048576 | bytes 2097152 | tf_op jit(solution)/shard_map/pallas_call | solution.py:579
  2.0 6.3 %all-to-all-start.1 = ((bf16[16,80,128]{2,1,0:T(8,128)(2,1)}), bf16[16,80,128]{2,1,0:T(8,128)(2,1)S(1)}, u32[]{:S(2)}, u32[]{:S(2)}) async-start(bf16[16,80,128]{2,1,0:T(8,128)(2,1)} %shard_map.119), calls=%async_computation.1 | async-start | bytes 655360 | tf_op jit(solution)/shard_map/all_to_all | solution.py:585
  8.3 2.1 %shard_map.118 = bf16[16,192,128]{2,1,0:T(8,128)(2,1)} custom-call(bf16[64,4096]{1,0:T(8,128)(2,1)} %v_ref.1, bf16[64,2048]{1,0:T(8,128)(2,1)} %q_ref.1), custom_call_target="tpu_custom_call" | custom-call | flops 1048576 | bytes 2097152 | tf_op jit(solution)/shard_map/pallas_call | solution.py:586
  10.4 6.3 %all-to-all-done.1.recv_ref.keys_head = bf16[16,80,128]{2,1,0:T(8,128)(2,1)S(1)} async-done(((bf16[16,80,128]{2,1,0:T(8,128)(2,1)}), bf16[16,80,128]{2,1,0:T(8,128)(2,1)S(1)}, u32[]{:S(2)}, u32[]{:S(2)}) %all-to-all-start.1) | async-done | bytes 327712 | tf_op jit(solution)/shard_map/all_to_all | solution.py:585
  16.7 0.0 copy-start.1
  16.7 0.7 copy-done.1
  17.5 3.6 %all-to-all-start = ((bf16[16,192,128]{2,1,0:T(8,128)(2,1)}), bf16[16,192,128]{2,1,0:T(8,128)(2,1)S(1)}, u32[]{:S(2)}, u32[]{:S(2)}) async-start(bf16[16,192,128]{2,1,0:T(8,128)(2,1)} %shard_map.118), calls=%async_computation | async-start | bytes 1572864 | tf_op jit(solution)/shard_map/all_to_all | solution.py:592
  21.1 8.0 %shard_map.120 = (bf16[1024,128]{1,0:T(8,128)(2,1)}, bf16[2,8,128,256]{3,2,1,0:T(8,128)(2,1)}, bf16[2,1024,128]{2,1,0:T(8,128)(2,1)}, bf16[2,8,128,256]{3,2,1,0:...) custom-call(bf16[16,80,128]{2,1,0:T(8,128)(2,1)} %copy-done.1, ...), custom_call_target="tpu_custom_call" | custom-call | flops 4294967296 | bytes 2097152 | tf_op jit(solution)/shard_map/pallas_call | solution.py:593
  29.1 5.3 %all-to-all-done.recv_ref.values_head = bf16[16,192,128]{2,1,0:T(8,128)(2,1)S(1)} async-done(((bf16[16,192,128]{2,1,0:T(8,128)(2,1)}), bf16[16,192,128]{2,1,0:T(8,128)(2,1)S(1)}, u32[]{:S(2)}, u32[]{:S(2)}) %all-to-all-start) | async-done | bytes 786464 | tf_op jit(solution)/shard_map/all_to_all | solution.py:592
  34.4 0.0 copy-start
  34.4 0.9 %copy-done = bf16[16,192,128]{2,1,0:T(8,128)(2,1)} copy-done((bf16[16,192,128]{2,1,0:T(8,128)(2,1)}, bf16[16,192,128]{2,1,0:T(8,128)(2,1)S(1)}, u32[]{:S(2)}) %copy-start) | copy-done | bytes 786456
  35.3 6.1 %shard_map.121 = (bf16[320,128]{1,0:T(8,128)(2,1)}, bf16[2,1024,128]{2,1,0:T(8,128)(2,1)}, bf16[2,8,128,128]{3,2,1,0:T(8,128)(2,1)}) custom-call(bf16[16,192,128]{2,1,0:T(8,128)(2,1)} %copy-done, f32[4,1024]{1,0:T(4,128)} %cv_ref.3, bf16[1024,128]{1,0:T(8,128)(2,1)} %get-tuple-element.19.keys_ref, bf16[2,8,128,256]{3,2,1,0:T(8,128)(2,1)} %get-tuple-element.20.tb_ref, ...), custom_call_target="tpu_custom_call" | custom-call | flops 67108864 | bytes 2097152 | tf_op jit(solution)/shard_map/pallas_call | solution.py:610
  41.4 4.5 %collective-permute-start = (bf16[320,128]{1,0:T(8,128)(2,1)}, bf16[320,128]{1,0:T(8,128)(2,1)S(1)}, u32[]{:S(2)}, u32[]{:S(2)}) collective-permute-start(bf16[320,128]{1,0:T(8,128)(2,1)} %get-tuple-element.24), channel_id=1, source_target_pairs={{0,16},{1,17},{2,18},{3,19},{4,20},{5,21},{6,22},{7,23},{8,24},{9,... | collective-permute-start | bytes 245768 | tf_op jit(solution)/shard_map/ppermute | solution.py:624
  45.9 5.9 %shard_map.122 = (f32[2,1024,128]{2,1,0:T(8,128)}, bf16[2,1024,128]{2,1,0:T(8,128)(2,1)}) custom-call(bf16[16,192,128]{2,1,0:T(8,128)(2,1)} %copy-done, f32[4,512]{1,0:T(4,128)} %cq_ref.3, bf16[1024,128]{1,0:T(8,128)(2,1)} %get-tuple-element.19.keys_ref, bf16[2,1024,128]{2,1,0:T(8,128)(2,1)} %get-tuple-element.26.w_ref, ...), custom_call_target="tpu_custom_call" | custom-call | flops 4294967296 | bytes 2097152 | tf_op jit(solution)/shard_map/pallas_call | solution.py:625
  51.8 0.0 collective-permute-done.hop_in
  51.8 0.0 copy-start.2
  51.8 0.6 copy-done.2
  52.4 4.1 %shard_map.123 = bf16[16,64,256]{2,1,0:T(8,128)(2,1)} custom-call(bf16[320,128]{1,0:T(8,128)(2,1)} %copy-done.2, bf16[16,80,128]{2,1,0:T(8,128)(2,1)} %copy-done.1, bf16[16,192,128]{2,1,0:T(8,128)(2,1)} %copy-done, f32[8,128]{1,0:T(8,128)} %get-tuple-element.25.early_ref, f32[4,512]{1,0:T(4,128)} %cq_ref.3, f32[4,512]{1,0:T(4,128)} %ck_ref.3, ...), custom_call_target="tpu_custom_call" | custom-call | flops 67108864 | bytes 2097152 | tf_op jit(solution)/shard_map/pallas_call | solution.py:645
  56.5 14.8 %all_to_all.15.normed_ref = bf16[16,64,256]{2,1,0:T(8,128)(2,1)} all-to-all(bf16[16,64,256]{2,1,0:T(8,128)(2,1)} %shard_map.123), channel_id=1, replica_groups=mesh['half'=2,'sub'=4,'head'=4] {'sub','head'}, dimensions={0} | all-to-all | bytes 1048576 | tf_op jit(solution)/shard_map/all_to_all | solution.py:672
  71.3 2.4 %shard_map.124 = bf16[64,4096]{1,0:T(8,128)(2,1)} custom-call(bf16[16,64,256]{2,1,0:T(8,128)(2,1)} %all_to_all.15.normed_ref, bf16[64,4096]{1,0:T(8,128)(2,1)} %z_ref.1), custom_call_target="tpu_custom_call" | custom-call | flops 67108864 | bytes 2097152 | tf_op jit(solution)/shard_map/pallas_call | solution.py:673
Async XLA Ops:
  2.0 14.7 %all-to-all-start.1 = ((bf16[16,80,128]{2,1,0:T(8,128)(2,1)}), bf16[16,80,128]{2,1,0:T(8,128)(2,1)S(1)}, u32[]{:S(2)}, u32[]{:S(2)}) async-start(bf16[16,80,128]{2,1,0:T(8,128)(2,1)} %shard_map.119), calls=%async_computation.1 | async-start | bytes 655360 | tf_op jit(solution)/shard_map/all_to_all | solution.py:585
  16.7 0.7 copy-start.1
  17.5 16.9 %all-to-all-start = ((bf16[16,192,128]{2,1,0:T(8,128)(2,1)}), bf16[16,192,128]{2,1,0:T(8,128)(2,1)S(1)}, u32[]{:S(2)}, u32[]{:S(2)}) async-start(bf16[16,192,128]{2,1,0:T(8,128)(2,1)} %shard_map.118), calls=%async_computation | async-start | bytes 1572864 | tf_op jit(solution)/shard_map/all_to_all | solution.py:592
  34.4 0.9 %copy-start = (bf16[16,192,128]{2,1,0:T(8,128)(2,1)}, bf16[16,192,128]{2,1,0:T(8,128)(2,1)S(1)}, u32[]{:S(2)}) copy-start(bf16[16,192,128]{2,1,0:T(8,128)(2,1)S(1)} %all-to-all-done.recv_ref.values_head) | copy-start | bytes 2359300
  41.4 10.4 %collective-permute-start = (bf16[320,128]{1,0:T(8,128)(2,1)}, bf16[320,128]{1,0:T(8,128)(2,1)S(1)}, u32[]{:S(2)}, u32[]{:S(2)}) collective-permute-start(bf16[320,128]{1,0:T(8,128)(2,1)} %get-tuple-element.24), channel_id=1, source_target_pairs={{0,16},{1,17},{2,18},{3,19},{4,20},{5,21},{6,22},{7,23},{8,24},{9,... | collective-permute-start | bytes 245768 | tf_op jit(solution)/shard_map/ppermute | solution.py:624
  51.8 0.6 copy-start.2

commit v4 on v2

v4 whole, which is shorter than its diff:
```python
import functools

import jax
import jax.numpy as jnp
from jax import lax
from jax.experimental import pallas as pl
from jax.experimental.pallas import tpu as pltpu
from jax.sharding import Mesh, PartitionSpec as P

DK = 128
DV = 128
CONV = 4
KH = 16
SUB = 16
SPAN = 128
EDGE = CONV - 1
EPS = 1e-06
F32 = jnp.float32
BF16 = jnp.bfloat16
VMEM_BYTES = 24 * 1024 * 1024
GATES = 16


def dot(a, b, dims=((1,), (0,))):
    return lax.dot_general(a, b, (dims, ((), ())), preferred_element_type=F32)


def halves(x):
    high = x.astype(BF16)
    return high, (x - high.astype(F32)).astype(BF16)


def mm_left(a, b):
    return dot(jnp.concatenate(halves(a), axis=1), jnp.concatenate([b, b], axis=0))


def mm_right(a, b):
    return dot(jnp.concatenate([a, a], axis=1), jnp.concatenate(halves(b), axis=0))


def mm(a, b):
    a_high, a_low = halves(a)
    b_high, b_low = halves(b)
    both = jnp.concatenate([a_high, a_low], axis=1)
    return dot(both, jnp.concatenate([b_high, b_high], axis=0)) + dot(a_high, b_low)


def silu(x):
    return x / (1.0 + jnp.exp(-x))


def unit(y, factor):
    scale = lax.rsqrt(jnp.sum(y * y, axis=-1, keepdims=True) + EPS)
    return (y * scale * factor).astype(BF16)


def iota(shape, dim):
    return lax.broadcasted_iota(jnp.int32, shape, dim)


def pack_kernel(heads_axis, q_ref, k_ref, v_ref, at_ref, bt_ref, out_ref):
    peers, tokens = out_ref.shape[0], q_ref.shape[0]
    subs = peers // heads_axis
    for dest in range(peers):
        key_head = (dest % heads_axis) * subs + dest // heads_axis
        lanes = slice(key_head * DK, (key_head + 1) * DK)
        out_ref[dest, GATES : GATES + tokens, :] = k_ref[:, lanes]
        for r in range(2):
            value_lanes = slice((2 * key_head + r) * DV, (2 * key_head + r + 1) * DV)
            out_ref[dest, GATES + (1 + r) * tokens : GATES + (2 + r) * tokens, :] = v_ref[
                :, value_lanes
            ]
        out_ref[dest, GATES + 3 * tokens :, :] = q_ref[:, lanes]
    value_heads = at_ref.shape[0]
    row, entry = iota((peers * GATES, value_heads), 0), iota((peers * GATES, value_heads), 1)
    dest, which = row // GATES, row % GATES
    first = 2 * ((dest % heads_axis) * subs + dest // heads_axis)
    pick_a = jnp.where((which < 2) & (entry == first + which), 1.0, 0.0).astype(BF16)
    pick_b = jnp.where(
        (which >= 2) & (which < 4) & (entry == first + which - 2), 1.0, 0.0
    ).astype(BF16)
    picked = (dot(pick_a, at_ref[...]) + dot(pick_b, bt_ref[...])).astype(BF16)
    lane_shift = tokens * lax.rem(lax.axis_index("head"), SPAN // tokens)
    place = jnp.where(
        iota((tokens, SPAN), 1) == iota((tokens, SPAN), 0) + lane_shift, 1.0, 0.0
    ).astype(BF16)
    gates = dot(picked, place).astype(BF16)
    for dest in range(peers):
        out_ref[dest, 0:GATES, :] = gates[GATES * dest : GATES * (dest + 1), :]


def invert(systems):
    size = systems[0].shape[0]
    blocks = size // SUB
    row, col = iota((size, size), 0), iota((size, size), 1)
    diagonal = (row // SUB) == (col // SUB)
    compact = jnp.concatenate(
        [
            jnp.sum(jnp.where(diagonal, n, 0.0).reshape(blocks, SUB, size), axis=0)
            for n in systems
        ],
        axis=0,
    )
    count = len(systems)
    lane, line = iota(compact.shape, 1), iota(compact.shape, 0)
    solved = jnp.where(lane % SUB == line % SUB, 1.0, 0.0).reshape(count, SUB, size)
    for m in range(SUB - 1):
        spread = jnp.take_along_axis(compact, (lane // SUB) * SUB + m, axis=1)
        solved = solved - spread.reshape(count, SUB, size) * solved[:, m : m + 1, :]
    inverses = [
        jnp.where(
            diagonal.reshape(blocks, SUB, size), solved[i : i + 1, :, :], 0.0
        ).reshape(size, size)
        for i in range(count)
    ]
    width = SUB
    while width < size:
        odd = [(j, j + width) for j in range(width, size, 2 * width)]

        def rows_of(x):
            return jnp.concatenate([x[lo:hi] for lo, hi in odd], axis=0)

        below = rows_of(
            ((row // (2 * width)) == (col // (2 * width))) & ((col // width) % 2 == 0)
        )
        firsts = [
            mm(jnp.where(below, rows_of(n), 0.0), inv) for n, inv in zip(systems, inverses)
        ]
        zero = jnp.zeros((width, size), F32)
        spreads = []
        for first in firsts:
            parts = []
            for j in range(len(odd)):
                parts += [zero, first[j * width : (j + 1) * width]]
            spreads.append(jnp.concatenate(parts, axis=0))
        seconds = [mm(rows_of(inv), spread) for inv, spread in zip(inverses, spreads)]
        grown = []
        for inv, second in zip(inverses, seconds):
            parts = []
            for j, (lo, hi) in enumerate(odd):
                parts += [inv[lo - width : lo], inv[lo:hi] - second[j * width : (j + 1) * width]]
            grown.append(jnp.concatenate(parts, axis=0))
        inverses = grown
        width *= 2
    return inverses


def gate_values(gates, sub, alog_ref, dt_ref):
    second = iota(gates.shape, 0) % GATES == 1
    a_log = jnp.where(second, alog_ref[2 * sub + 1], alog_ref[2 * sub])
    dt_bias = jnp.where(second, dt_ref[2 * sub + 1], dt_ref[2 * sub])
    shifted = gates + dt_bias
    soft = jnp.maximum(shifted, 0.0) + jnp.log1p(jnp.exp(-jnp.abs(shifted)))
    return -jnp.exp(a_log) * soft, 1.0 / (1.0 + jnp.exp(-gates))


def convolved(rows, at, count, lanes, tap):
    summed = tap[0:1] * rows[at : at + count, lanes]
    for j in range(1, CONV):
        summed = summed + tap[j : j + 1] * rows[at + j : at + j + count, lanes]
    return silu(summed)


def key_tap(sub, tap_ref):
    return tap_ref[:, pl.ds(pl.multiple_of(sub * DK, 128), DK)]


def value_taps(sub, cv_ref):
    lane = pl.multiple_of(sub * 2 * DV, 128)
    return [cv_ref[:, pl.ds(pl.multiple_of(lane + r * DV, 128), DV)] for r in range(2)]


def state_kernel(
    recv_ref,
    ck_ref,
    cv_ref,
    alog_ref,
    dt_ref,
    hop_ref,
    keys_ref,
    w_ref,
    u_ref,
    within_ref,
    xs_ref,
    cols_ref,
    early_ref,
    rows,
):
    sub = lax.axis_index("sub")
    later = lax.axis_index("half") > 0
    peers = recv_ref.shape[0]
    tokens = (recv_ref.shape[1] - GATES) // 4
    total = peers * tokens
    spans = total // SPAN
    starts = [GATES + i * tokens for i in range(4)]
    for at, first in ((0, 3), (16, 0), (32, 1), (48, 2)):
        hop_ref[2 * DK + at : 2 * DK + at + 16, :] = recv_ref[
            peers - 1, starts[first] + tokens - 16 : starts[first] + tokens, :
        ]
    taps = [key_tap(sub, ck_ref)] + value_taps(sub, cv_ref)
    rows[0:8, :] = jnp.zeros((8, 384), F32)
    for s in range(peers):
        for g in range(3):
            rows[8 + s * tokens : 8 + (s + 1) * tokens, g * 128 : (g + 1) * 128] = recv_ref[
                s, starts[g] : starts[g] + tokens, :
            ].astype(F32)
    gates = jnp.concatenate(
        [
            sum(recv_ref[s, 0:GATES, :].astype(F32) for s in range(n, n + SPAN // tokens))
            for n in range(0, peers, SPAN // tokens)
        ],
        axis=0,
    )
    decay, rate = gate_values(gates, sub, alog_ref, dt_ref)
    early_ref[...] = jnp.where(iota((8, SPAN), 0) < 2, decay[0:8], rate[0:8])
    skipped = later & (iota(gates.shape, 0) < GATES) & (iota(gates.shape, 1) < EDGE)
    decay = jnp.where(skipped, 0.0, decay)
    rate = jnp.where(skipped, 0.0, rate)
    lane_r, lane_c = iota((SPAN, SPAN), 0), iota((SPAN, SPAN), 1)
    upto = jnp.where(lane_r <= lane_c, 1.0, 0.0).astype(BF16)
    d_high, d_rest = halves(decay)
    d_mid, d_low = halves(decay - d_high.astype(F32))
    cum = dot(d_high, upto) + (dot(d_mid, upto) + dot(d_low, upto))
    growth = jnp.exp(cum)
    columns = jnp.transpose(jnp.where(iota(gates.shape, 0) % GATES < 2, cum, rate))
    cols_ref[...] = columns
    lower = lane_r >= lane_c
    strict = lane_r > lane_c
    keys, keys_t, systems = [], [], []
    for n in range(spans):
        k_n = unit(convolved(rows, n * SPAN + 8 - EDGE, SPAN, slice(0, DK), taps[0]), 1.0)
        keys_ref[n * SPAN : (n + 1) * SPAN, :] = k_n
        kt_n = jnp.transpose(k_n.astype(F32)).astype(BF16)
        gram = dot(k_n, kt_n)
        keys.append(k_n)
        keys_t.append(kt_n)
        for r in range(2):
            at = GATES * n + r
            gap = columns[:, at : at + 1] - cum[at : at + 1, :]
            within = jnp.where(lower, jnp.exp(jnp.where(lower, gap, 0.0)), 0.0)
            within_ref[r, n * SPAN : (n + 1) * SPAN, :] = within.astype(BF16)
            systems.append(jnp.where(strict, columns[:, at + 2 : at + 3] * within * gram, 0.0))
    inverses = invert(systems)
    identity = jnp.where(lane_r == lane_c, 1.0, 0.0)
    maps = []
    for n in range(spans):
        at_rows = slice(n * SPAN, (n + 1) * SPAN)
        for r in range(2):
            at = GATES * n + r
            c_col = columns[:, at : at + 1]
            v_n = convolved(
                rows, n * SPAN + 8 - EDGE, SPAN, slice((1 + r) * DV, (2 + r) * DV), taps[1 + r]
            ).astype(BF16)
            t_b = inverses[2 * n + r] * rate[at + 2 : at + 3, :]
            w_mat = mm_left(t_b * growth[at : at + 1, :], keys[n])
            u_mat = mm_left(t_b, v_n)
            w_ref[r, at_rows, :] = w_mat.astype(BF16)
            u_ref[r, at_rows, :] = u_mat.astype(BF16)
            c_end = c_col[SPAN - 1 : SPAN, :]
            both = jnp.concatenate([w_mat, u_mat], axis=1)
            moved = mm_right(keys_t[n], jnp.exp(c_end - c_col) * both)
            maps.append((jnp.exp(c_end) * identity - moved[:, :DK], moved[:, DK:]))
    zero_half = jnp.zeros((DK, DV), F32)
    states = [jnp.concatenate([zero_half, identity], axis=1) for r in range(2)]
    for n in range(spans):
        for r in range(2):
            xs_ref[r, n] = states[r].astype(BF16)
            lin, add = maps[2 * n + r]
            if n == 0:
                states[r] = jnp.concatenate([add, lin], axis=1)
            else:
                states[r] = mm(lin, states[r]) + jnp.concatenate([add, zero_half], axis=1)
    for r in range(2):
        xs_ref[r, spans] = states[r].astype(BF16)
        hop_ref[r * DK : (r + 1) * DK, :] = states[r][:, :DV].astype(BF16)


def output_kernel(
    recv_ref, cq_ref, keys_ref, w_ref, u_ref, within_ref, xs_ref, cols_ref, oa_ref, om_ref, rows
):
    sub = lax.axis_index("sub")
    peers = recv_ref.shape[0]
    tokens = (recv_ref.shape[1] - GATES) // 4
    total = peers * tokens
    spans = total // SPAN
    tap = key_tap(sub, cq_ref)
    rows[0:8, :] = jnp.zeros((8, DK), F32)
    for s in range(peers):
        rows[8 + s * tokens : 8 + (s + 1) * tokens, :] = recv_ref[
            s, GATES + 3 * tokens :, :
        ].astype(F32)
    for n in range(spans):
        at = n * SPAN
        q_n = unit(convolved(rows, at + 8 - EDGE, SPAN, slice(0, DK), tap), DK**-0.5)
        scores = dot(q_n, keys_ref[at : at + SPAN, :], ((1,), (1,)))
        for r in range(2):
            c_col = cols_ref[:, GATES * n + r : GATES * n + r + 1]
            inner = (within_ref[r, at : at + SPAN, :].astype(F32) * scores).astype(BF16)
            x_n = xs_ref[r, n]
            held = dot(w_ref[r, at : at + SPAN, :], x_n)
            fresh_a = (u_ref[r, at : at + SPAN, :].astype(F32) - held[:, :DV]).astype(BF16)
            fresh_m = (-held[:, DV:]).astype(BF16)
            out = jnp.exp(c_col) * dot(q_n, x_n) + dot(
                inner, jnp.concatenate([fresh_a, fresh_m], axis=1)
            )
            oa_ref[r, at : at + SPAN, :] = out[:, :DV]
            om_ref[r, at : at + SPAN, :] = out[:, DV:].astype(BF16)


def first_tokens(hop_ref, recv_ref, early_ref, cq_ref, ck_ref, cv_ref, rows):
    sub = lax.axis_index("sub")
    later = lax.axis_index("half") > 0
    tokens = (recv_ref.shape[1] - GATES) // 4
    taps = [key_tap(sub, cq_ref), key_tap(sub, ck_ref)] + value_taps(sub, cv_ref)
    results = []
    for g, first in enumerate((3, 0, 1, 2)):
        lanes = slice(g * 128, (g + 1) * 128)
        start = GATES + first * tokens
        rows[0:16, lanes] = hop_ref[2 * DK + 16 * g : 2 * DK + 16 * (g + 1), :].astype(F32)
        rows[16:32, lanes] = recv_ref[0, start : start + 16, :].astype(F32)
        results.append(convolved(rows, 16 - EDGE, 8, lanes, taps[g]))
    q_cols = jnp.transpose(unit(results[0], DK**-0.5).astype(F32))
    k_cols = jnp.transpose(unit(results[1], 1.0).astype(F32))
    gates = early_ref[...]
    line = iota((8, DV), 0)
    finals, outputs = [], []
    for r in range(2):
        values = results[2 + r].astype(BF16).astype(F32)
        entering = hop_ref[r * DK : (r + 1) * DK, :].astype(F32)
        state, out = entering, jnp.zeros((8, DV), F32)
        for t in range(EDGE):
            k_t, q_t = k_cols[:, t : t + 1], q_cols[:, t : t + 1]
            state = jnp.exp(gates[r : r + 1, t : t + 1]) * state
            held = jnp.sum(k_t * state, axis=0, keepdims=True)
            state = state + k_t * (
                gates[2 + r : 3 + r, t : t + 1] * (values[t : t + 1, :] - held)
            )
            out = jnp.where(line == t, jnp.sum(q_t * state, axis=0, keepdims=True), out)
        finals.append(jnp.where(later, state, entering))
        outputs.append(out)
    return finals, outputs, later


def finish_kernel(
    hop_ref, recv_ref, early_ref, cq_ref, ck_ref, cv_ref, gain_ref, oa_ref, om_ref, out_ref, rows
):
    peers, tokens = out_ref.shape[0], out_ref.shape[1]
    finals, outputs, later = first_tokens(
        hop_ref, recv_ref, early_ref, cq_ref, ck_ref, cv_ref, rows
    )
    states = [x.astype(BF16) for x in finals]
    gain = gain_ref[...]
    replaced = later & (iota((8, DV), 0) < EDGE)
    chunks = 4
    part, peer_part = peers * tokens // chunks, peers // chunks
    for c in range(chunks):
        at = c * part
        for r in range(2):
            core = oa_ref[r, at : at + part, :] + dot(om_ref[r, at : at + part, :], states[r])
            if c == 0:
                core = jnp.concatenate(
                    [jnp.where(replaced, outputs[r], core[0:8]), core[8:]], axis=0
                )
            scale = lax.rsqrt(jnp.mean(core * core, axis=-1, keepdims=True) + EPS)
            normed = (core * scale * gain).astype(BF16)
            out_ref[c * peer_part : (c + 1) * peer_part, :, r * DV : (r + 1) * DV] = (
                normed.reshape(peer_part, tokens, DV)
            )


def advance_kernel(
    hop_ref, recv_ref, early_ref, cq_ref, ck_ref, cv_ref, hop_own, xs_ref, next_ref, rows
):
    finals, _, _ = first_tokens(hop_ref, recv_ref, early_ref, cq_ref, ck_ref, cv_ref, rows)
    last = xs_ref.shape[1] - 1
    for r in range(2):
        own = hop_own[r * DK : (r + 1) * DK, :].astype(F32)
        through = mm_right(xs_ref[r, last][:, DV:], finals[r])
        next_ref[r * DK : (r + 1) * DK, :] = (through + own).astype(BF16)
    next_ref[2 * DK :, :] = hop_own[2 * DK :, :]


def gate_kernel(heads_axis, normed_ref, z_ref, out_ref):
    subs = normed_ref.shape[0] // heads_axis
    for sub in range(subs):
        for head in range(heads_axis):
            at = (head * subs + sub) * 2 * DV
            gate = silu(z_ref[:, at : at + 2 * DV].astype(F32))
            value = normed_ref[sub * heads_axis + head].astype(F32)
            out_ref[:, at : at + 2 * DV] = (value * gate).astype(BF16)


VMEM = pl.BlockSpec(memory_space=pltpu.VMEM)
SMEM = pl.BlockSpec(memory_space=pltpu.SMEM)


def near(x):
    return pltpu.with_memory_space_constraint(x, pltpu.VMEM)


def call(kernel, outs, in_specs, scratch=(), flops=1 << 26, moved=1 << 21):
    return pl.pallas_call(
        kernel,
        out_shape=outs,
        in_specs=in_specs,
        out_specs=jax.tree.map(lambda _: VMEM, outs),
        scratch_shapes=list(scratch),
        compiler_params=pltpu.CompilerParams(vmem_limit_bytes=VMEM_BYTES),
        cost_estimate=pl.CostEstimate(flops=flops, bytes_accessed=moved, transcendentals=0),
    )


def local(
    q_rows,
    k_rows,
    v_rows,
    z_rows,
    a_rows,
    b_rows,
    conv_q,
    conv_k,
    conv_v,
    a_log,
    dt_bias,
    norm_gain,
):
    shards, subs, heads_axis = (lax.axis_size(a) for a in ("half", "sub", "head"))
    peers, tokens = subs * heads_axis, q_rows.shape[0]
    total = peers * tokens
    spans = total // SPAN
    group = ("sub", "head")
    route = [(i, i + 1) for i in range(shards - 1)]
    packed = call(
        functools.partial(pack_kernel, heads_axis),
        pltpu.VMEM((peers, GATES + 4 * tokens, 128), BF16),
        [VMEM] * 5,
        flops=1 << 20,
    )(q_rows, k_rows, v_rows, a_rows.T, b_rows.T)
    blocks = lax.all_to_all(packed, group, 0, 0, tiled=True)
    hop, keys, w_mats, u_mats, within, starts, cols, early = call(
        state_kernel,
        (
            pltpu.VMEM((2 * DK + 64, 128), BF16),
            pltpu.VMEM((total, DK), BF16),
            pltpu.VMEM((2, total, DK), BF16),
            pltpu.VMEM((2, total, DV), BF16),
            pltpu.VMEM((2, total, SPAN), BF16),
            pltpu.VMEM((2, spans + 1, DK, 2 * DV), BF16),
            pltpu.VMEM((SPAN, spans * GATES), F32),
            pltpu.VMEM((8, SPAN), F32),
        ),
        [VMEM, VMEM, VMEM, SMEM, SMEM],
        scratch=(pltpu.VMEM((8 + total, 384), F32),),
        flops=1 << 32,
    )(near(blocks), conv_k, conv_v, a_log, dt_bias)
    entering = lax.ppermute(hop, "half", route)
    out_a, out_m = call(
        output_kernel,
        (pltpu.VMEM((2, total, DV), F32), pltpu.VMEM((2, total, DV), BF16)),
        [VMEM] * 8,
        scratch=(pltpu.VMEM((8 + total, DK), F32),),
        flops=1 << 32,
    )(
        near(blocks),
        conv_q,
        near(keys),
        near(w_mats),
        near(u_mats),
        near(within),
        near(starts),
        near(cols),
    )
    for _ in range(shards - 2):
        moved = call(
            advance_kernel,
            pltpu.VMEM(hop.shape, BF16),
            [VMEM] * 8,
            scratch=(pltpu.VMEM((32, 512), F32),),
        )(near(entering), near(blocks), near(early), conv_q, conv_k, conv_v, near(hop), near(starts))
        entering = lax.ppermute(moved, "half", route)
    normed = call(
        finish_kernel,
        pltpu.VMEM((peers, tokens, 2 * DV), BF16),
        [VMEM] * 9,
        scratch=(pltpu.VMEM((32, 512), F32),),
    )(
        near(entering),
        near(blocks),
        near(early),
        conv_q,
        conv_k,
        conv_v,
        norm_gain.reshape(1, DV),
        near(out_a),
        near(out_m),
    )
    returned = lax.all_to_all(normed, group, 0, 0, tiled=True)
    return call(
        functools.partial(gate_kernel, heads_axis),
        jax.ShapeDtypeStruct(z_rows.shape, BF16),
        [VMEM] * 2,
    )(near(returned), z_rows)


def solution(mesh):
    heads_axis = mesh.shape["head"]
    subs = KH // heads_axis
    regrouped = Mesh(
        mesh.devices.reshape(mesh.shape["ctx"] // subs, subs, heads_axis), ("half", "sub", "head")
    )
    row = P(("half", "sub", "head"), None)
    placed = (row,) * 6 + (P(None, "head"),) * 3 + (P("head"),) * 2 + (P(),)
    return jax.shard_map(local, mesh=regrouped, in_specs=placed, out_specs=row, check_vma=False)
```

time: 73.8 us -> 61.1 us (0.83)
  Pallas kernels: 30 us -> 14.8 us
  local copies, waits for them, and re-layouts: 0.62 us -> 4.38 us
  blocking collectives: 38 us -> 36.9 us
    pallas_call x5, Pallas kernels: 30 us -> 14.8 us  [the longest x1 10 us: local(): call(state_kernel, (pltpu.VMEM((2 * DK + 64, 128), BF16), pltpu.VMEM((tot...]
    unnamed x2 -> x24, local copies, waits for them, and re-layouts: 0.62 us -> 4.38 us
    all_to_all x1, blocking collectives: 14.8 us -> 13.8 us  [local(): returned = lax.all_to_all(normed, group, 0, 0, tiled=True)]
  transfers between devices with their start and end apart: 1 -> 1, of which waited for: 0 -> 0; matrix products, arithmetic and copies ran while one was open for 0% -> 0% of each run, Pallas kernels for 8% -> 4%
where the time goes in v4:
time: 61.1 us; the launch traced here: 60.7 us
  blocking collectives  36.9 us (60%)
  Pallas kernels  14.8 us (24%)
  starting transfers between devices  4.5 us (7%)
  local copies, waits for them, and re-layouts  4.38 us (7%)
    all_to_all x1, blocking collectives, local(): blocks = lax.all_to_all(packed, group, 0, 0, tiled=True)  23.1 us
    all_to_all x1, blocking collectives, local(): returned = lax.all_to_all(normed, group, 0, 0, tiled=True)  13.8 us
    pallas_call x1, Pallas kernels, local(): call(state_kernel, (pltpu.VMEM((2 * DK + 64, 128), BF16), pltpu.VMEM((tot...  10 us
    ppermute x1, starting transfers between devices, local(): entering = lax.ppermute(hop, 'half', route)  4.5 us
    unnamed x24, local copies, waits for them, and re-layouts  4.38 us
    pallas_call x1, Pallas kernels, local(): call(output_kernel, (pltpu.VMEM((2, total, DV), F32), pltpu.VMEM((2, tota...  2.25 us
  transfers between devices with their start and end apart: 1, of which 0 were waited for; matrix products, arithmetic and copies ran while one was open for 0% of the time, Pallas kernels for 4%

profile of v4, /device:TPU:0, one launch (start us, length us, event | category | flops | bytes accessed | tf_op | source)
XLA Modules:
  0.0 60.7 jit_solution(2185390796094329235)
XLA Ops:
  0.0 0.0 copy-start.1
  0.0 1.0 %copy-done.1 = bf16[64,4096]{1,0:T(8,128)(2,1)S(1)} copy-done((bf16[64,4096]{1,0:T(8,128)(2,1)S(1)}, bf16[64,4096]{1,0:T(8,128)(2,1)}, u32[]{:S(2)}) %copy-start.1) | copy-done | bytes 524312
  1.0 0.0 copy-start.2
  1.0 0.9 %copy-done.2 = bf16[64,2048]{1,0:T(8,128)(2,1)S(1)} copy-done((bf16[64,2048]{1,0:T(8,128)(2,1)S(1)}, bf16[64,2048]{1,0:T(8,128)(2,1)}, u32[]{:S(2)}) %copy-start.2) | copy-done | bytes 262168
  2.0 0.0 copy-start.3
  2.0 0.9 %copy-done.3 = bf16[64,2048]{1,0:T(8,128)(2,1)S(1)} copy-done((bf16[64,2048]{1,0:T(8,128)(2,1)S(1)}, bf16[64,2048]{1,0:T(8,128)(2,1)}, u32[]{:S(2)}) %copy-start.3) | copy-done | bytes 262168
  2.9 0.0 copy-start.5
  2.9 0.7 %copy-done.5 = bf16[64,32]{0,1:T(8,128)(2,1)S(1)} copy-done((bf16[64,32]{0,1:T(8,128)(2,1)S(1)}, bf16[64,32]{0,1:T(8,128)(2,1)}, u32[]{:S(2)}) %copy-start.5) | copy-done | bytes 4120
  3.6 0.0 copy-start.6
  3.6 0.7 %copy-done.6 = bf16[64,32]{0,1:T(8,128)(2,1)S(1)} copy-done((bf16[64,32]{0,1:T(8,128)(2,1)S(1)}, bf16[64,32]{0,1:T(8,128)(2,1)}, u32[]{:S(2)}) %copy-start.6) | copy-done | bytes 4120
  4.3 0.4 shard_map.118
  4.7 0.0 copy-start.4
  4.7 0.0 copy-start.7
  4.7 0.0 copy-start.10
  4.7 0.0 copy-start.11
  4.8 23.1 %all_to_all.10.recv_ref = bf16[16,272,128]{2,1,0:T(8,128)(2,1)S(1)} all-to-all(bf16[16,272,128]{2,1,0:T(8,128)(2,1)S(1)} %shard_map.118), channel_id=1, replica_groups=mesh['half'=2,'sub'=4,'head'=4] {'sub','head'}, dimensions={0} | all-to-all | bytes 2228224 | tf_op jit(solution)/shard_map/all_to_all | solution.py:439
  27.8 0.0 copy-done.4
  27.8 0.0 copy-done.7
  27.9 0.0 copy-done.10
  27.9 0.0 copy-done.11
  27.9 0.0 copy-start.8
  27.9 10.0 %shard_map.119 = (bf16[320,128]{1,0:T(8,128)(2,1)S(1)}, bf16[1024,128]{1,0:T(8,128)(2,1)S(1)}, bf16[2,1024,128]{2,1,0:T(8,128)(2,1)S(1)}, bf16[2,1024,128]{2,1,0...) custom-call(bf16[16,272,128]{2,1,0:T(8,128)(2,1)S(1)} %all_to_all.10, ...), custom_call_target="tpu_custom_call" | custom-call | flops 4294967296 | bytes 2097152 | tf_op jit(solution)/shard_map/pallas_call | solution.py:440
  37.9 4.5 %collective-permute-start = (bf16[320,128]{1,0:T(8,128)(2,1)S(1)}, bf16[320,128]{1,0:T(8,128)(2,1)S(1)}, u32[]{:S(2)}, u32[]{:S(2)}) collective-permute-start(bf16[320,128]{1,0:T(8,128)(2,1)S(1)} %get-tuple-element.15), channel_id=1, source_target_pairs={{0,16},{1,17},{2,18},{3,19},{4,20},{5,21},{6,22},{7,23},{8,24},{9,... | collective-permute-start | bytes 245768 | tf_op jit(solution)/shard_map/ppermute | solution.py:456
  42.4 0.0 copy-done.8
  42.4 0.0 copy-start.9
  42.5 2.2 %shard_map.120 = (f32[2,1024,128]{2,1,0:T(8,128)S(1)}, bf16[2,1024,128]{2,1,0:T(8,128)(2,1)S(1)}) custom-call(bf16[16,272,128]{2,1,0:T(8,128)(2,1)S(1)} %all_to_all.10.recv_ref, f32[4,512]{1,0:T(4,128)S(1)} %copy-done.8, bf16[1024,128]{1,0:T(8,128)(2,1)S(1)} %get-tuple-element.17.keys_ref, bf16[2,1024,128]{2,1,0:T(8,128)(2,1)S(1)} %get-tuple-element.18.w_ref, ...), custom_call_target="tpu_custom_call" | custom-call | flops 4294967296 | bytes 2097152 | tf_op jit(solution)/shard_map/pallas_call | solution.py:457
  44.7 0.0 collective-permute-done.hop_ref
  44.7 0.0 copy-done.9
  44.7 1.0 %shard_map.121 = bf16[16,64,256]{2,1,0:T(8,128)(2,1)S(1)} custom-call(bf16[320,128]{1,0:T(8,128)(2,1)S(1)} %collective-permute-done.hop_ref, bf16[16,272,128]{2,1,0:T(8,128)(2,1)S(1)} %all_to_all.10.recv_ref, f32[8,128]{1,0:T(8,128)S(1)} %get-tuple-element.16.early_ref, f32[4,512]{1,0:T(4,128)S(1)} %copy-done.8, f32[4,512]{1,0:T(4,128)S(1)} %copy-done.7, ...), custom_call_target="tpu_custom_call" | custom-call | flops 67108864 | bytes 2097152 | tf_op jit(solution)/shard_map/pallas_call | solution.py:481
  45.7 0.0 copy-start
  45.7 13.8 %all_to_all.11.normed_ref = bf16[16,64,256]{2,1,0:T(8,128)(2,1)S(1)} all-to-all(bf16[16,64,256]{2,1,0:T(8,128)(2,1)S(1)} %shard_map.121), channel_id=1, replica_groups=mesh['half'=2,'sub'=4,'head'=4] {'sub','head'}, dimensions={0} | all-to-all | bytes 1048576 | tf_op jit(solution)/shard_map/all_to_all | solution.py:497
  59.5 0.0 copy-done
  59.6 1.1 %shard_map.122 = bf16[64,4096]{1,0:T(8,128)(2,1)} custom-call(bf16[16,64,256]{2,1,0:T(8,128)(2,1)S(1)} %all_to_all.11.normed_ref, bf16[64,4096]{1,0:T(8,128)(2,1)S(1)} %copy-done), custom_call_target="tpu_custom_call" | custom-call | flops 67108864 | bytes 2097152 | tf_op jit(solution)/shard_map/pallas_call | solution.py:498
Async XLA Ops:
  0.0 1.0 %copy-start.1 = (bf16[64,4096]{1,0:T(8,128)(2,1)S(1)}, bf16[64,4096]{1,0:T(8,128)(2,1)}, u32[]{:S(2)}) copy-start(bf16[64,4096]{1,0:T(8,128)(2,1)} %v_ref.1) | copy-start | bytes 1572868
  1.0 0.9 %copy-start.2 = (bf16[64,2048]{1,0:T(8,128)(2,1)S(1)}, bf16[64,2048]{1,0:T(8,128)(2,1)}, u32[]{:S(2)}) copy-start(bf16[64,2048]{1,0:T(8,128)(2,1)} %q_ref.1) | copy-start | bytes 786436
  2.0 0.9 %copy-start.3 = (bf16[64,2048]{1,0:T(8,128)(2,1)S(1)}, bf16[64,2048]{1,0:T(8,128)(2,1)}, u32[]{:S(2)}) copy-start(bf16[64,2048]{1,0:T(8,128)(2,1)} %k_ref.1) | copy-start | bytes 786436
  2.9 0.7 %copy-start.5 = (bf16[64,32]{0,1:T(8,128)(2,1)S(1)}, bf16[64,32]{0,1:T(8,128)(2,1)}, u32[]{:S(2)}) copy-start(bf16[64,32]{0,1:T(8,128)(2,1)} %param.16) | copy-start | bytes 12292
  3.6 0.7 %copy-start.6 = (bf16[64,32]{0,1:T(8,128)(2,1)S(1)}, bf16[64,32]{0,1:T(8,128)(2,1)}, u32[]{:S(2)}) copy-start(bf16[64,32]{0,1:T(8,128)(2,1)} %param.17) | copy-start | bytes 12292
  4.7 23.1 %copy-start.4 = (f32[4,1024]{1,0:T(4,128)S(1)}, f32[4,1024]{1,0:T(4,128)}, u32[]{:S(2)}) copy-start(f32[4,1024]{1,0:T(4,128)} %cv_ref.3) | copy-start | bytes 49156
  4.7 23.1 %copy-start.7 = (f32[4,512]{1,0:T(4,128)S(1)}, f32[4,512]{1,0:T(4,128)}, u32[]{:S(2)}) copy-start(f32[4,512]{1,0:T(4,128)} %ck_ref.3) | copy-start | bytes 24580
  4.7 23.1 %copy-start.10 = (f32[8]{0:T(128)S(1)}, f32[8]{0:T(128)}, u32[]{:S(2)}) copy-start(f32[8]{0:T(128)} %alog_ref.1) | copy-start | bytes 100
  4.7 23.1 %copy-start.11 = (f32[8]{0:T(128)S(1)}, f32[8]{0:T(128)}, u32[]{:S(2)}) copy-start(f32[8]{0:T(128)} %dt_ref.1) | copy-start | bytes 100
  27.9 14.6 %copy-start.8 = (f32[4,512]{1,0:T(4,128)S(1)}, f32[4,512]{1,0:T(4,128)}, u32[]{:S(2)}) copy-start(f32[4,512]{1,0:T(4,128)} %cq_ref.3) | copy-start | bytes 24580
  37.9 6.8 %collective-permute-start = (bf16[320,128]{1,0:T(8,128)(2,1)S(1)}, bf16[320,128]{1,0:T(8,128)(2,1)S(1)}, u32[]{:S(2)}, u32[]{:S(2)}) collective-permute-start(bf16[320,128]{1,0:T(8,128)(2,1)S(1)} %get-tuple-element.15), channel_id=1, source_target_pairs={{0,16},{1,17},{2,18},{3,19},{4,20},{5,21},{6,22},{7,23},{8,24},{9,... | collective-permute-start | bytes 245768 | tf_op jit(solution)/shard_map/ppermute | solution.py:456
  42.4 2.3 %copy-start.9 = (f32[128]{0:T(128)S(1)}, f32[128]{0:T(128)}, u32[]{:S(2)}) copy-start(f32[128]{0:T(128)} %param.23) | copy-start | bytes 1540
  45.7 13.8 %copy-start = (bf16[64,4096]{1,0:T(8,128)(2,1)S(1)}, bf16[64,4096]{1,0:T(8,128)(2,1)}, u32[]{:S(2)}) copy-start(bf16[64,4096]{1,0:T(8,128)(2,1)} %z_ref.1) | copy-start | bytes 1572868

commit v5 on v4

v5 whole, which is shorter than its diff:
```python
import functools

import jax
import jax.numpy as jnp
from jax import lax
from jax.experimental import pallas as pl
from jax.experimental.pallas import tpu as pltpu
from jax.sharding import Mesh, PartitionSpec as P

DK = 128
DV = 128
CONV = 4
KH = 16
SUB = 16
SPAN = 128
EDGE = CONV - 1
EPS = 1e-06
F32 = jnp.float32
BF16 = jnp.bfloat16
VMEM_BYTES = 24 * 1024 * 1024
GATES = 16


def dot(a, b, dims=((1,), (0,))):
    return lax.dot_general(a, b, (dims, ((), ())), preferred_element_type=F32)


def halves(x):
    high = x.astype(BF16)
    return high, (x - high.astype(F32)).astype(BF16)


def mm_right(a, b):
    return dot(jnp.concatenate([a, a], axis=1), jnp.concatenate(halves(b), axis=0))


def mm_parts(a, b):
    both = jnp.concatenate(a, axis=1)
    return dot(both, jnp.concatenate([b[0], b[0]], axis=0)) + dot(a[0], b[1])


def silu(x):
    half = 0.5 * x
    return half + half * jnp.tanh(half)


def unit(y, factor):
    scale = lax.rsqrt(jnp.sum(y * y, axis=-1, keepdims=True) + EPS)
    return (y * scale * factor).astype(BF16)


def iota(shape, dim):
    return lax.broadcasted_iota(jnp.int32, shape, dim)


def pack_kernel(
    heads_axis, q_in, k_in, v_in, at_in, bt_in, out_ref, q_ref, k_ref, v_ref, at_ref, bt_ref, sems
):
    peers, tokens = out_ref.shape[0], q_ref.shape[0]
    pairs = ((at_in, at_ref), (bt_in, bt_ref), (k_in, k_ref), (v_in, v_ref), (q_in, q_ref))
    copies = [pltpu.make_async_copy(a, b, sems.at[i]) for i, (a, b) in enumerate(pairs)]
    for copy in copies:
        copy.start()
    for copy in copies:
        copy.wait()
    subs = peers // heads_axis
    for dest in range(peers):
        key_head = (dest % heads_axis) * subs + dest // heads_axis
        lanes = slice(key_head * DK, (key_head + 1) * DK)
        out_ref[dest, GATES : GATES + tokens, :] = k_ref[:, lanes]
        for r in range(2):
            value_lanes = slice((2 * key_head + r) * DV, (2 * key_head + r + 1) * DV)
            out_ref[dest, GATES + (1 + r) * tokens : GATES + (2 + r) * tokens, :] = v_ref[
                :, value_lanes
            ]
        out_ref[dest, GATES + 3 * tokens :, :] = q_ref[:, lanes]
    value_heads = at_ref.shape[0]
    row, entry = iota((peers * GATES, value_heads), 0), iota((peers * GATES, value_heads), 1)
    dest, which = row // GATES, row % GATES
    first = 2 * ((dest % heads_axis) * subs + dest // heads_axis)
    pick_a = jnp.where((which < 2) & (entry == first + which), 1.0, 0.0).astype(BF16)
    pick_b = jnp.where(
        (which >= 2) & (which < 4) & (entry == first + which - 2), 1.0, 0.0
    ).astype(BF16)
    picked = (dot(pick_a, at_ref[...]) + dot(pick_b, bt_ref[...])).astype(BF16)
    lane_shift = tokens * lax.rem(lax.axis_index("head"), SPAN // tokens)
    place = jnp.where(
        iota((tokens, SPAN), 1) == iota((tokens, SPAN), 0) + lane_shift, 1.0, 0.0
    ).astype(BF16)
    gates = dot(picked, place).astype(BF16)
    for dest in range(peers):
        out_ref[dest, 0:GATES, :] = gates[GATES * dest : GATES * (dest + 1), :]


def invert(systems):
    size = systems[0].shape[0]
    blocks = size // SUB
    row, col = iota((size, size), 0), iota((size, size), 1)
    diagonal = (row // SUB) == (col // SUB)
    compact = jnp.concatenate(
        [
            jnp.sum(jnp.where(diagonal, n, 0.0).reshape(blocks, SUB, size), axis=0)
            for n in systems
        ],
        axis=0,
    )
    count = len(systems)
    lane, line = iota(compact.shape, 1), iota(compact.shape, 0)
    solved = jnp.where(lane % SUB == line % SUB, 1.0, 0.0).reshape(count, SUB, size)
    for m in range(SUB - 1):
        spread = jnp.take_along_axis(compact, (lane // SUB) * SUB + m, axis=1)
        solved = solved - spread.reshape(count, SUB, size) * solved[:, m : m + 1, :]
    inverses = [
        jnp.where(
            diagonal.reshape(blocks, SUB, size), solved[i : i + 1, :, :], 0.0
        ).reshape(size, size)
        for i in range(count)
    ]
    lows = [halves(n) for n in systems]
    parts = [halves(inv) for inv in inverses]
    width = SUB
    while width < size:
        odd = [(j, j + width) for j in range(width, size, 2 * width)]

        def rows_of(x):
            return jnp.concatenate([x[lo:hi] for lo, hi in odd], axis=0)

        def woven(even, x):
            pieces = []
            for j, (lo, hi) in enumerate(odd):
                pieces += [even[lo - width : lo], x[j * width : (j + 1) * width]]
            return jnp.concatenate(pieces, axis=0)

        below = ((row // (2 * width)) == (col // (2 * width))) & ((col // width) % 2 == 0)
        mask = rows_of(jnp.where(below, 1.0, 0.0).astype(BF16))
        blank = jnp.zeros((size, size), BF16)
        firsts = [
            mm_parts((rows_of(n[0]) * mask, rows_of(n[1]) * mask), t) for n, t in zip(lows, parts)
        ]
        spreads = [tuple(woven(blank, x) for x in halves(first)) for first in firsts]
        odds = [(rows_of(t[0]), rows_of(t[1])) for t in parts]
        seconds = [halves(-mm_parts(o, spread)) for o, spread in zip(odds, spreads)]
        parts = [
            tuple(woven(t[i], o[i] + second[i]) for i in range(2))
            for t, o, second in zip(parts, odds, seconds)
        ]
        width *= 2
    return parts


def gate_values(gates, sub, alog_ref, dt_ref):
    second = iota(gates.shape, 0) % GATES == 1
    a_log = jnp.where(second, alog_ref[2 * sub + 1], alog_ref[2 * sub])
    dt_bias = jnp.where(second, dt_ref[2 * sub + 1], dt_ref[2 * sub])
    shifted = gates + dt_bias
    soft = jnp.maximum(shifted, 0.0) + jnp.log1p(jnp.exp(-jnp.abs(shifted)))
    return -jnp.exp(a_log) * soft, 1.0 / (1.0 + jnp.exp(-gates))


def convolved(rows, at, count, lanes, tap):
    summed = tap[0:1] * rows[at : at + count, lanes]
    for j in range(1, CONV):
        summed = summed + tap[j : j + 1] * rows[at + j : at + j + count, lanes]
    return silu(summed)


def key_tap(sub, tap_ref):
    return tap_ref[:, pl.ds(pl.multiple_of(sub * DK, 128), DK)]


def value_taps(sub, cv_ref):
    lane = pl.multiple_of(sub * 2 * DV, 128)
    return [cv_ref[:, pl.ds(pl.multiple_of(lane + r * DV, 128), DV)] for r in range(2)]


def widened(rows, recv_ref, starts, tokens):
    rows[0:8, :] = jnp.zeros((8, rows.shape[1]), F32)
    for s in range(recv_ref.shape[0]):
        for g, start in enumerate(starts):
            rows[8 + s * tokens : 8 + (s + 1) * tokens, g * 128 : (g + 1) * 128] = recv_ref[
                s, start : start + tokens, :
            ].astype(F32)


def keys_kernel(
    recv_ref,
    ck_ref,
    alog_ref,
    dt_ref,
    keys_ref,
    keys_t_ref,
    t_ref,
    lin_ref,
    within_ref,
    cols_ref,
    early_ref,
    rows,
):
    sub = lax.axis_index("sub")
    later = lax.axis_index("half") > 0
    peers = recv_ref.shape[0]
    tokens = (recv_ref.shape[1] - GATES) // 4
    spans = peers * tokens // SPAN
    tap = key_tap(sub, ck_ref)
    widened(rows, recv_ref, [GATES], tokens)
    gates = jnp.concatenate(
        [
            sum(recv_ref[s, 0:GATES, :].astype(F32) for s in range(n, n + SPAN // tokens))
            for n in range(0, peers, SPAN // tokens)
        ],
        axis=0,
    )
    decay, rate = gate_values(gates, sub, alog_ref, dt_ref)
    early_ref[...] = jnp.where(iota((8, SPAN), 0) < 2, decay[0:8], rate[0:8])
    skipped = later & (iota(gates.shape, 0) < GATES) & (iota(gates.shape, 1) < EDGE)
    decay = jnp.where(skipped, 0.0, decay)
    rate = jnp.where(skipped, 0.0, rate)
    lane_r, lane_c = iota((SPAN, SPAN), 0), iota((SPAN, SPAN), 1)
    upto = jnp.where(lane_r <= lane_c, 1.0, 0.0).astype(BF16)
    d_high, d_rest = halves(decay)
    d_mid, d_low = halves(decay - d_high.astype(F32))
    cum = dot(d_high, upto) + (dot(d_mid, upto) + dot(d_low, upto))
    columns = jnp.transpose(jnp.where(iota(gates.shape, 0) % GATES < 2, cum, rate))
    cols_ref[...] = columns
    lower = lane_r >= lane_c
    strict = lane_r > lane_c
    keys, keys_t, systems = [], [], []
    for n in range(spans):
        k_n = unit(convolved(rows, n * SPAN + 8 - EDGE, SPAN, slice(0, DK), tap), 1.0)
        kt_n = jnp.transpose(k_n.astype(F32)).astype(BF16)
        keys_ref[n * SPAN : (n + 1) * SPAN, :] = k_n
        keys_t_ref[n] = kt_n
        gram = dot(k_n, kt_n)
        keys.append(k_n)
        keys_t.append(kt_n)
        for r in range(2):
            at = GATES * n + r
            gap = columns[:, at : at + 1] - cum[at : at + 1, :]
            within = jnp.where(lower, jnp.exp(jnp.where(lower, gap, 0.0)), 0.0)
            within_ref[r, n * SPAN : (n + 1) * SPAN, :] = within.astype(BF16)
            systems.append(jnp.where(strict, columns[:, at + 2 : at + 3] * within * gram, 0.0))
    inverses = invert(systems)
    identity = jnp.where(lane_r == lane_c, 1.0, 0.0)
    for n in range(spans):
        for r in range(2):
            at = GATES * n + r
            c_col = columns[:, at : at + 1]
            t_parts = inverses[2 * n + r]
            t_ref[r, n] = jnp.concatenate(t_parts, axis=1)
            scaled = (columns[:, at + 2 : at + 3] * jnp.exp(c_col)) * keys[n].astype(F32)
            w_mat = mm_parts(t_parts, halves(scaled))
            c_end = c_col[SPAN - 1 : SPAN, :]
            moved = mm_right(keys_t[n], jnp.exp(c_end - c_col) * w_mat)
            lin = jnp.exp(c_end) * identity - moved
            lin_ref[r, n] = jnp.concatenate(halves(lin), axis=1)


def step(lin, parts):
    high, low = parts
    return dot(lin, jnp.concatenate([high, high], axis=0)) + dot(lin[:, :DK], low)


def values_part(recv_ref, cv_ref, keys_t_ref, t_ref, cols_ref, rows, vs):
    sub = lax.axis_index("sub")
    tokens = (recv_ref.shape[1] - GATES) // 4
    spans = t_ref.shape[1]
    taps = value_taps(sub, cv_ref)
    widened(rows, recv_ref, [GATES + tokens, GATES + 2 * tokens], tokens)
    adds = []
    for n in range(spans):
        for r in range(2):
            lanes = slice(r * DV, (r + 1) * DV)
            at = GATES * n + r
            v_n = convolved(rows, n * SPAN + 8 - EDGE, SPAN, lanes, taps[r]).astype(BF16)
            vs[n * SPAN : (n + 1) * SPAN, lanes] = v_n
            t_n = t_ref[r, n]
            high, low = halves(cols_ref[:, at + 2 : at + 3] * v_n.astype(F32))
            u_mat = step(t_n, (high, low))
            c_col = cols_ref[:, at : at + 1]
            adds.append(mm_right(keys_t_ref[n], jnp.exp(c_col[SPAN - 1 : SPAN, :] - c_col) * u_mat))
    return adds


def opening_kernel(
    recv_ref, cv_ref, keys_t_ref, t_ref, lin_ref, cols_ref, hop_ref, vs_ref, xs_ref, rows
):
    first = lax.axis_index("half") == 0
    peers = recv_ref.shape[0]
    tokens = (recv_ref.shape[1] - GATES) // 4
    spans = t_ref.shape[1]
    for at, which in ((0, 3), (16, 0), (32, 1), (48, 2)):
        end = GATES + (which + 1) * tokens
        hop_ref[2 * DK + at : 2 * DK + at + 16, :] = recv_ref[peers - 1, end - 16 : end, :]

    @pl.when(first)
    def _():
        adds = values_part(recv_ref, cv_ref, keys_t_ref, t_ref, cols_ref, rows, vs_ref)
        states = [adds[0], adds[1]]
        for n in range(1, spans):
            for r in range(2):
                parts = halves(states[r])
                xs_ref[r, n] = jnp.concatenate(parts, axis=0)
                states[r] = step(lin_ref[r, n], parts) + adds[2 * n + r]
        for r in range(2):
            hop_ref[r * DK : (r + 1) * DK, :] = states[r].astype(BF16)

    @pl.when(jnp.logical_not(first))
    def _():
        hop_ref[0 : 2 * DK, :] = jnp.zeros((2 * DK, DV), BF16)


def output_kernel(
    recv_ref,
    cq_ref,
    cv_ref,
    keys_ref,
    keys_t_ref,
    t_ref,
    lin_ref,
    within_ref,
    cols_ref,
    hop_ref,
    vs_ref,
    xs_ref,
    oa_ref,
    om_ref,
    last_ref,
    rows,
    query_rows,
    values,
):
    sub = lax.axis_index("sub")
    first = lax.axis_index("half") == 0
    tokens = (recv_ref.shape[1] - GATES) // 4
    spans = t_ref.shape[1]
    tap = key_tap(sub, cq_ref)
    widened(query_rows, recv_ref, [GATES + 3 * tokens], tokens)

    def seen(n):
        at = n * SPAN
        q_n = unit(convolved(query_rows, at + 8 - EDGE, SPAN, slice(0, DK), tap), DK**-0.5)
        k_n = keys_ref[at : at + SPAN, :]
        readers = jnp.concatenate([k_n, q_n], axis=0)
        return readers, dot(q_n, keys_t_ref[n])

    def weights(n, r, scores):
        return (within_ref[r, n * SPAN : (n + 1) * SPAN, :].astype(F32) * scores).astype(BF16)

    def spread(t_n, rest, inner):
        rest = rest.astype(BF16)
        fresh = dot(t_n, jnp.concatenate([rest, rest], axis=0))
        return dot(inner, fresh.astype(BF16))

    @pl.when(first)
    def _():
        for n in range(spans):
            at = slice(n * SPAN, (n + 1) * SPAN)
            readers, scores = seen(n)
            readers = jnp.concatenate([readers, readers], axis=1)
            for r in range(2):
                growth = jnp.exp(cols_ref[:, GATES * n + r : GATES * n + r + 1])
                rate = cols_ref[:, GATES * n + 2 + r : GATES * n + 3 + r]
                value = vs_ref[at, r * DV : (r + 1) * DV].astype(F32)
                inner = weights(n, r, scores)
                if n == 0:
                    oa_ref[r, at, :] = spread(t_ref[r, n], rate * value, inner)
                else:
                    read = dot(readers, xs_ref[r, n])
                    rest = rate * (value - growth * read[:SPAN])
                    oa_ref[r, at, :] = growth * read[SPAN:] + spread(t_ref[r, n], rest, inner)
        for r in range(2):
            last_ref[r, :, 0:DV] = hop_ref[r * DK : (r + 1) * DK, :].astype(F32)
            last_ref[r, :, DV:] = jnp.zeros((DK, DV), F32)

    @pl.when(jnp.logical_not(first))
    def _():
        adds = values_part(recv_ref, cv_ref, keys_t_ref, t_ref, cols_ref, rows, values)
        zero_half = jnp.zeros((SPAN, DV), F32)
        identity = jnp.where(iota((DK, DK), 0) == iota((DK, DK), 1), 1.0, 0.0)
        states = [jnp.concatenate([zero_half, identity], axis=1) for r in range(2)]
        for n in range(spans):
            at = slice(n * SPAN, (n + 1) * SPAN)
            readers, scores = seen(n)
            readers = jnp.concatenate([readers, readers], axis=1)
            for r in range(2):
                parts = halves(states[r])
                growth = jnp.exp(cols_ref[:, GATES * n + r : GATES * n + r + 1])
                rate = cols_ref[:, GATES * n + 2 + r : GATES * n + 3 + r]
                value = values[at, r * DV : (r + 1) * DV].astype(F32)
                inner = weights(n, r, scores)
                read = dot(readers, jnp.concatenate(parts, axis=0))
                rest = rate * (jnp.concatenate([value, zero_half], axis=1) - growth * read[:SPAN])
                out = growth * read[SPAN:] + spread(t_ref[r, n], rest, inner)
                oa_ref[r, at, :] = out[:, :DV]
                om_ref[r, at, :] = out[:, DV:].astype(BF16)
                add = jnp.concatenate([adds[2 * n + r], zero_half], axis=1)
                states[r] = step(lin_ref[r, n], parts) + add
        for r in range(2):
            last_ref[r] = states[r]


def first_tokens(hop_ref, recv_ref, early_ref, cq_ref, ck_ref, cv_ref, rows):
    sub = lax.axis_index("sub")
    later = lax.axis_index("half") > 0
    tokens = (recv_ref.shape[1] - GATES) // 4
    taps = [key_tap(sub, cq_ref), key_tap(sub, ck_ref)] + value_taps(sub, cv_ref)
    results = []
    for g, first in enumerate((3, 0, 1, 2)):
        lanes = slice(g * 128, (g + 1) * 128)
        start = GATES + first * tokens
        rows[0:16, lanes] = hop_ref[2 * DK + 16 * g : 2 * DK + 16 * (g + 1), :].astype(F32)
        rows[16:32, lanes] = recv_ref[0, start : start + 16, :].astype(F32)
        results.append(convolved(rows, 16 - EDGE, 8, lanes, taps[g]))
    q_cols = jnp.transpose(unit(results[0], DK**-0.5).astype(F32))
    k_cols = jnp.transpose(unit(results[1], 1.0).astype(F32))
    gates = early_ref[...]
    line = iota((8, DV), 0)
    finals, outputs = [], []
    for r in range(2):
        values = results[2 + r].astype(BF16).astype(F32)
        entering = hop_ref[r * DK : (r + 1) * DK, :].astype(F32)
        state, out = entering, jnp.zeros((8, DV), F32)
        for t in range(EDGE):
            k_t, q_t = k_cols[:, t : t + 1], q_cols[:, t : t + 1]
            state = jnp.exp(gates[r : r + 1, t : t + 1]) * state
            held = jnp.sum(k_t * state, axis=0, keepdims=True)
            state = state + k_t * (
                gates[2 + r : 3 + r, t : t + 1] * (values[t : t + 1, :] - held)
            )
            out = jnp.where(line == t, jnp.sum(q_t * state, axis=0, keepdims=True), out)
        finals.append(jnp.where(later, state, entering))
        outputs.append(out)
    return finals, outputs, later


def finish_kernel(
    hop_ref, recv_ref, early_ref, cq_ref, ck_ref, cv_ref, gain_ref, oa_ref, om_ref, out_ref, rows
):
    peers, tokens = out_ref.shape[0], out_ref.shape[1]
    finals, outputs, later = first_tokens(
        hop_ref, recv_ref, early_ref, cq_ref, ck_ref, cv_ref, rows
    )
    states = [x.astype(BF16) for x in finals]
    gain = gain_ref[...]
    replaced = later & (iota((8, DV), 0) < EDGE)
    chunks = 4
    part, peer_part = peers * tokens // chunks, peers // chunks
    for c in range(chunks):
        at = c * part
        for r in range(2):
            passed = dot(om_ref[r, at : at + part, :], states[r])
            core = oa_ref[r, at : at + part, :] + jnp.where(later, passed, 0.0)
            if c == 0:
                core = jnp.concatenate(
                    [jnp.where(replaced, outputs[r], core[0:8]), core[8:]], axis=0
                )
            scale = lax.rsqrt(jnp.mean(core * core, axis=-1, keepdims=True) + EPS)
            normed = (core * scale * gain).astype(BF16)
            out_ref[c * peer_part : (c + 1) * peer_part, :, r * DV : (r + 1) * DV] = (
                normed.reshape(peer_part, tokens, DV)
            )


def advance_kernel(
    hop_ref, recv_ref, early_ref, cq_ref, ck_ref, cv_ref, hop_own, last_ref, next_ref, rows
):
    finals, _, _ = first_tokens(hop_ref, recv_ref, early_ref, cq_ref, ck_ref, cv_ref, rows)
    for r in range(2):
        last = last_ref[r]
        through = mm_parts(halves(last[:, DV:]), halves(finals[r]))
        next_ref[r * DK : (r + 1) * DK, :] = (through + last[:, :DV]).astype(BF16)
    next_ref[2 * DK :, :] = hop_own[2 * DK :, :]


def gate_kernel(heads_axis, normed_ref, z_ref, out_ref, made, sems):
    subs = normed_ref.shape[0] // heads_axis
    width = subs * 2 * DV
    copies = []
    for head in range(heads_axis):
        for sub in range(subs):
            at = (head * subs + sub) * 2 * DV
            gate = silu(z_ref[:, at : at + 2 * DV].astype(F32))
            value = normed_ref[sub * heads_axis + head].astype(F32)
            made[:, at : at + 2 * DV] = (value * gate).astype(BF16)
        lanes = pl.ds(head * width, width)
        copy = pltpu.make_async_copy(made.at[:, lanes], out_ref.at[:, lanes], sems.at[head])
        copy.start()
        copies.append(copy)
    for copy in copies:
        copy.wait()


VMEM = pl.BlockSpec(memory_space=pltpu.VMEM)
SMEM = pl.BlockSpec(memory_space=pltpu.SMEM)
ANY = pl.BlockSpec(memory_space=pl.ANY)


def near(x):
    return pltpu.with_memory_space_constraint(x, pltpu.VMEM)


def far(x):
    return pltpu.with_memory_space_constraint(x, pltpu.HBM)


def call(kernel, outs, in_specs, scratch=(), out_spec=VMEM, flops=1 << 26, moved=1 << 21):
    return pl.pallas_call(
        kernel,
        out_shape=outs,
        in_specs=in_specs,
        out_specs=jax.tree.map(lambda _: out_spec, outs),
        scratch_shapes=list(scratch),
        compiler_params=pltpu.CompilerParams(vmem_limit_bytes=VMEM_BYTES),
        cost_estimate=pl.CostEstimate(flops=flops, bytes_accessed=moved, transcendentals=0),
    )


def local(
    q_rows,
    k_rows,
    v_rows,
    z_rows,
    a_rows,
    b_rows,
    conv_q,
    conv_k,
    conv_v,
    a_log,
    dt_bias,
    norm_gain,
):
    shards, subs, heads_axis = (lax.axis_size(a) for a in ("half", "sub", "head"))
    peers, tokens = subs * heads_axis, q_rows.shape[0]
    total = peers * tokens
    spans = total // SPAN
    group = ("sub", "head")
    route = [(i, i + 1) for i in range(shards - 1)]
    inputs = [far(x) for x in (q_rows, k_rows, v_rows, a_rows.T, b_rows.T)]
    packed = call(
        functools.partial(pack_kernel, heads_axis),
        pltpu.VMEM((peers, GATES + 4 * tokens, 128), BF16),
        [ANY] * 5,
        [pltpu.VMEM(x.shape, BF16) for x in inputs] + [pltpu.SemaphoreType.DMA((5,))],
        flops=1 << 20,
    )(*inputs)
    blocks = near(lax.all_to_all(packed, group, 0, 0, tiled=True))
    keys, keys_t, inverses, lins, within, cols, early = call(
        keys_kernel,
        (
            pltpu.VMEM((total, DK), BF16),
            pltpu.VMEM((spans, DK, SPAN), BF16),
            pltpu.VMEM((2, spans, SPAN, 2 * SPAN), BF16),
            pltpu.VMEM((2, spans, DK, 2 * DK), BF16),
            pltpu.VMEM((2, total, SPAN), BF16),
            pltpu.VMEM((SPAN, spans * GATES), F32),
            pltpu.VMEM((8, SPAN), F32),
        ),
        [VMEM, VMEM, SMEM, SMEM],
        [pltpu.VMEM((8 + total, DK), F32)],
        flops=1 << 32,
    )(blocks, conv_k, a_log, dt_bias)
    keys, keys_t, inverses, lins, within, cols, early = (
        near(x) for x in (keys, keys_t, inverses, lins, within, cols, early)
    )
    hop, values, starts = call(
        opening_kernel,
        (
            pltpu.VMEM((2 * DK + 64, 128), BF16),
            pltpu.VMEM((total, 2 * DV), BF16),
            pltpu.VMEM((2, spans, 2 * DK, DV), BF16),
        ),
        [VMEM] * 6,
        [pltpu.VMEM((8 + total, 2 * DV), F32)],
        flops=1 << 32,
    )(blocks, conv_v, keys_t, inverses, lins, cols)
    entering = near(lax.ppermute(hop, "half", route))
    hop, values, starts = near(hop), near(values), near(starts)
    out_a, out_m, last = call(
        output_kernel,
        (
            pltpu.VMEM((2, total, DV), F32),
            pltpu.VMEM((2, total, DV), BF16),
            pltpu.VMEM((2, DK, 2 * DV), F32),
        ),
        [VMEM] * 12,
        [
            pltpu.VMEM((8 + total, 2 * DV), F32),
            pltpu.VMEM((8 + total, DK), F32),
            pltpu.VMEM((total, 2 * DV), BF16),
        ],
        flops=1 << 32,
    )(
        blocks,
        conv_q,
        conv_v,
        keys,
        keys_t,
        inverses,
        lins,
        within,
        cols,
        hop,
        values,
        starts,
    )
    for _ in range(shards - 2):
        moved = call(
            advance_kernel,
            pltpu.VMEM(hop.shape, BF16),
            [VMEM] * 8,
            [pltpu.VMEM((32, 512), F32)],
        )(entering, blocks, early, conv_q, conv_k, conv_v, hop, near(last))
        entering = near(lax.ppermute(moved, "half", route))
    normed = call(
        finish_kernel,
        pltpu.VMEM((peers, tokens, 2 * DV), BF16),
        [VMEM] * 9,
        [pltpu.VMEM((32, 512), F32)],
    )(
        entering,
        blocks,
        early,
        conv_q,
        conv_k,
        conv_v,
        norm_gain.reshape(1, DV),
        near(out_a),
        near(out_m),
    )
    returned = near(lax.all_to_all(normed, group, 0, 0, tiled=True))
    return call(
        functools.partial(gate_kernel, heads_axis),
        jax.ShapeDtypeStruct(z_rows.shape, BF16),
        [VMEM] * 2,
        [pltpu.VMEM(z_rows.shape, BF16), pltpu.SemaphoreType.DMA((heads_axis,))],
        ANY,
    )(returned, z_rows)


def solution(mesh):
    heads_axis = mesh.shape["head"]
    subs = KH // heads_axis
    regrouped = Mesh(
        mesh.devices.reshape(mesh.shape["ctx"] // subs, subs, heads_axis), ("half", "sub", "head")
    )
    row = P(("half", "sub", "head"), None)
    placed = (row,) * 6 + (P(None, "head"),) * 3 + (P("head"),) * 2 + (P(),)
    return jax.shard_map(local, mesh=regrouped, in_specs=placed, out_specs=row, check_vma=False)
```

time: 61.1 us -> 59.9 us (0.980)
  Pallas kernels: 14.8 us -> 21.6 us
  local copies, waits for them, and re-layouts: 4.38 us -> 0.04 us
  starting transfers between devices: 4.5 us -> 1.29 us
    unnamed x24 -> x14, local copies, waits for them, and re-layouts: 4.38 us -> 0.04 us
    ppermute x1, starting transfers between devices: 4.5 us -> 1.29 us  [local(): entering = near(lax.ppermute(hop, 'half', route))]
    pallas_call x1, Pallas kernels: 2.25 us -> 5.16 us  [local(): call(output_kernel, (pltpu.VMEM((2, total, DV), F32), pltpu.VMEM((2, tota...]
    pallas_call x1 -> x2, Pallas kernels: 10 us -> 12.8 us  [the longest x1 8.29 us: local(): call(keys_kernel, (pltpu.VMEM((total, DK), BF16), pltpu.VMEM((spans, DK,...]
    pallas_call x1, Pallas kernels: 0.36 us -> 1.75 us  [local(): call(functools.partial(pack_kernel, heads_axis), pltpu.VMEM((peers, GATES...]
  transfers between devices with their start and end apart: 1 -> 1, of which waited for: 0 -> 0; matrix products, arithmetic and copies ran while one was open for 0% -> 0% of each run, Pallas kernels for 4% -> 9%
where the time goes in v5:
time: 59.9 us; the launch traced here: 59.6 us
  blocking collectives  36.4 us (61%)
  Pallas kernels  21.6 us (36%)
  starting transfers between devices  1.29 us (2%)
    all_to_all x1, blocking collectives, local(): blocks = near(lax.all_to_all(packed, group, 0, 0, tiled=True))  23.1 us
    all_to_all x1, blocking collectives, local(): returned = near(lax.all_to_all(normed, group, 0, 0, tiled=True))  13.3 us
    pallas_call x1, Pallas kernels, local(): call(keys_kernel, (pltpu.VMEM((total, DK), BF16), pltpu.VMEM((spans, DK,...  8.29 us
    pallas_call x1, Pallas kernels, local(): call(output_kernel, (pltpu.VMEM((2, total, DV), F32), pltpu.VMEM((2, tota...  5.16 us
    pallas_call x1, Pallas kernels, local(): call(opening_kernel, (pltpu.VMEM((2 * DK + 64, 128), BF16), pltpu.VMEM((t...  4.51 us
    pallas_call x1, Pallas kernels, local(): call(functools.partial(pack_kernel, heads_axis), pltpu.VMEM((peers, GATES...  1.75 us
    ppermute x1, starting transfers between devices, local(): entering = near(lax.ppermute(hop, 'half', route))  1.29 us
  transfers between devices with their start and end apart: 1, of which 0 were waited for; matrix products, arithmetic and copies ran while one was open for 0% of the time, Pallas kernels for 9%

profile of v5, /device:TPU:0, one launch (start us, length us, event | category | flops | bytes accessed | tf_op | source)
XLA Modules:
  0.0 59.6 jit_solution(3627954475933629339)
XLA Ops:
  0.0 1.7 %shard_map.118 = bf16[16,272,128]{2,1,0:T(8,128)(2,1)S(1)} custom-call(bf16[64,2048]{1,0:T(8,128)(2,1)} %q_in.1, bf16[64,2048]{1,0:T(8,128)(2,1)} %k_in.1, bf16[64,4096]{1,0:T(8,128)(2,1)} %v_in.1, bf16[32,64]{1,0:T(8,128)(2,1)} %bitcast.4, bf16[32,64]{1,0:T(8,128)(2,1)} %bitcast.5), custom_call_target="tpu_custom_call" | custom-call | flops 1048576 | bytes 2097152 | tf_op jit(solution)/shard_map/pallas_call | solution.py:539
  1.8 0.0 copy-start.2
  1.8 0.0 copy-start.5
  1.8 0.0 copy-start.6
  1.8 23.1 %all_to_all.10.recv_ref = bf16[16,272,128]{2,1,0:T(8,128)(2,1)S(1)} all-to-all(bf16[16,272,128]{2,1,0:T(8,128)(2,1)S(1)} %shard_map.118), channel_id=1, replica_groups=mesh['half'=2,'sub'=4,'head'=4] {'sub','head'}, dimensions={0} | all-to-all | bytes 2228224 | tf_op jit(solution)/shard_map/all_to_all | solution.py:546
  24.9 0.0 copy-done.2
  24.9 0.0 copy-done.5
  24.9 0.0 copy-done.6
  24.9 0.0 copy-start.1
  24.9 8.3 %shard_map.119 = (bf16[1024,128]{1,0:T(8,128)(2,1)S(1)}, bf16[8,128,128]{2,1,0:T(8,128)(2,1)S(1)}, bf16[2,8,128,256]{3,2,1,0:T(8,128)(2,1)S(1)}, bf16[2,8,128,25...) custom-call(bf16[16,272,128]{2,1,0:T(8,128)(2,1)S(1)} %all_to_all.10.r, ...), custom_call_target="tpu_custom_call" | custom-call | flops 4294967296 | bytes 2097152 | tf_op jit(solution)/shard_map/pallas_call | solution.py:547
  33.2 0.0 copy-done.1
  33.2 0.0 copy-start.3
  33.2 4.5 %shard_map.120 = (bf16[320,128]{1,0:T(8,128)(2,1)S(1)}, bf16[1024,256]{1,0:T(8,128)(2,1)S(1)}, bf16[2,8,256,128]{3,2,1,0:T(8,128)(2,1)S(1)}) custom-call(bf16[16,272,128]{2,1,0:T(8,128)(2,1)S(1)} %all_to_all.10.recv_ref, f32[4,1024]{1,0:T(4,128)S(1)} %copy-done.1, bf16[8,128,128]{2,1,0:T(8,128)(2,1)S(1)} %get-tuple-element.17.keys_t_ref, ...), custom_call_target="tpu_custom_call" | custom-call | flops 4294967296 | bytes 2097152 | tf_op jit(solution)/shard_map/pallas_call | solution.py:565
  37.7 1.3 %collective-permute-start = (bf16[320,128]{1,0:T(8,128)(2,1)S(1)}, bf16[320,128]{1,0:T(8,128)(2,1)S(1)}, u32[]{:S(2)}, u32[]{:S(2)}) collective-permute-start(bf16[320,128]{1,0:T(8,128)(2,1)S(1)} %get-tuple-element.21.hop_ref), channel_id=1, source_target_pairs={{0,16},{1,17},{2,18},{3,19},{4,20},{5,21},{6,22},{7,23},{8,24},{9,... | collective-permute-start | bytes 245768 | tf_op jit(solution)/shard_map/ppermute | solution.py:576
  39.0 0.0 copy-done.3
  39.0 0.0 copy-start.4
  39.1 5.2 %shard_map.121 = (f32[2,1024,128]{2,1,0:T(8,128)S(1)}, bf16[2,1024,128]{2,1,0:T(8,128)(2,1)S(1)}, f32[2,128,256]{2,1,0:T(8,128)}) custom-call(bf16[16,272,128]{2,1,0:T(8,128)(2,1)S(1)} %all_to_all.10.recv_ref, f32[4,512]{1,0:T(4,128)S(1)} %copy-done.3, f32[4,1024]{1,0:T(4,128)S(1)} %copy-done.1, bf16[1024,128]{1,0:T(8,128)(2,1)S(1)} %get-tuple-element.23.keys_ref, ...), custom_call_target="tpu_custom_call" | custom-call | flops 4294967296 | bytes 2097152 | tf_op jit(solution)/shard_map/pallas_call | solution.py:578
  44.2 0.0 collective-permute-done.hop_ref
  44.2 0.0 copy-done.4
  44.2 1.0 %shard_map.122 = bf16[16,64,256]{2,1,0:T(8,128)(2,1)S(1)} custom-call(bf16[320,128]{1,0:T(8,128)(2,1)S(1)} %collective-permute-done.hop_ref, bf16[16,272,128]{2,1,0:T(8,128)(2,1)S(1)} %all_to_all.10.recv_ref, f32[8,128]{1,0:T(8,128)S(1)} %get-tuple-element.22.early_ref, f32[4,512]{1,0:T(4,128)S(1)} %copy-done.3, f32[4,512]{1,0:T(4,128)S(1)} %copy-done.2, ...), custom_call_target="tpu_custom_call" | custom-call | flops 67108864 | bytes 2097152 | tf_op jit(solution)/shard_map/pallas_call | solution.py:614
  45.2 0.0 copy-start
  45.2 13.3 %all_to_all.11.normed_ref = bf16[16,64,256]{2,1,0:T(8,128)(2,1)S(1)} all-to-all(bf16[16,64,256]{2,1,0:T(8,128)(2,1)S(1)} %shard_map.122), channel_id=1, replica_groups=mesh['half'=2,'sub'=4,'head'=4] {'sub','head'}, dimensions={0} | all-to-all | bytes 1048576 | tf_op jit(solution)/shard_map/all_to_all | solution.py:630
  58.5 0.0 copy-done
  58.5 0.9 %shard_map.123 = bf16[64,4096]{1,0:T(8,128)(2,1)} custom-call(bf16[16,64,256]{2,1,0:T(8,128)(2,1)S(1)} %all_to_all.11.normed_ref, bf16[64,4096]{1,0:T(8,128)(2,1)S(1)} %copy-done), custom_call_target="tpu_custom_call" | custom-call | flops 67108864 | bytes 2097152 | tf_op jit(solution)/shard_map/pallas_call | solution.py:631
Async XLA Ops:
  1.8 23.1 %copy-start.2 = (f32[4,512]{1,0:T(4,128)S(1)}, f32[4,512]{1,0:T(4,128)}, u32[]{:S(2)}) copy-start(f32[4,512]{1,0:T(4,128)} %ck_ref.3) | copy-start | bytes 24580
  1.8 23.1 %copy-start.5 = (f32[8]{0:T(128)S(1)}, f32[8]{0:T(128)}, u32[]{:S(2)}) copy-start(f32[8]{0:T(128)} %alog_ref.1) | copy-start | bytes 100
  1.8 23.1 %copy-start.6 = (f32[8]{0:T(128)S(1)}, f32[8]{0:T(128)}, u32[]{:S(2)}) copy-start(f32[8]{0:T(128)} %dt_ref.1) | copy-start | bytes 100
  24.9 8.3 %copy-start.1 = (f32[4,1024]{1,0:T(4,128)S(1)}, f32[4,1024]{1,0:T(4,128)}, u32[]{:S(2)}) copy-start(f32[4,1024]{1,0:T(4,128)} %cv_ref.5) | copy-start | bytes 49156
  33.2 5.8 %copy-start.3 = (f32[4,512]{1,0:T(4,128)S(1)}, f32[4,512]{1,0:T(4,128)}, u32[]{:S(2)}) copy-start(f32[4,512]{1,0:T(4,128)} %cq_ref.3) | copy-start | bytes 24580
  37.7 6.5 %collective-permute-start = (bf16[320,128]{1,0:T(8,128)(2,1)S(1)}, bf16[320,128]{1,0:T(8,128)(2,1)S(1)}, u32[]{:S(2)}, u32[]{:S(2)}) collective-permute-start(bf16[320,128]{1,0:T(8,128)(2,1)S(1)} %get-tuple-element.21.hop_ref), channel_id=1, source_target_pairs={{0,16},{1,17},{2,18},{3,19},{4,20},{5,21},{6,22},{7,23},{8,24},{9,... | collective-permute-start | bytes 245768 | tf_op jit(solution)/shard_map/ppermute | solution.py:576
  39.0 5.2 %copy-start.4 = (f32[128]{0:T(128)S(1)}, f32[128]{0:T(128)}, u32[]{:S(2)}) copy-start(f32[128]{0:T(128)} %param.23) | copy-start | bytes 1540
  45.2 13.3 %copy-start = (bf16[64,4096]{1,0:T(8,128)(2,1)S(1)}, bf16[64,4096]{1,0:T(8,128)(2,1)}, u32[]{:S(2)}) copy-start(bf16[64,4096]{1,0:T(8,128)(2,1)} %z_ref.1) | copy-start | bytes 1572868

commit v6 on v5

--- a/solution.py
+++ b/solution.py
@@ -193,6 +193,7 @@
     lin_ref,
     within_ref,
     cols_ref,
+    rates_ref,
     early_ref,
     rows,
 ):
@@ -217,42 +218,59 @@
     rate = jnp.where(skipped, 0.0, rate)
     lane_r, lane_c = iota((SPAN, SPAN), 0), iota((SPAN, SPAN), 1)
     upto = jnp.where(lane_r <= lane_c, 1.0, 0.0).astype(BF16)
-    d_high, d_rest = halves(decay)
+    d_high, _ = halves(decay)
     d_mid, d_low = halves(decay - d_high.astype(F32))
     cum = dot(d_high, upto) + (dot(d_mid, upto) + dot(d_low, upto))
-    columns = jnp.transpose(jnp.where(iota(gates.shape, 0) % GATES < 2, cum, rate))
+    growth = jnp.exp(cum)
+    here = pltpu.roll(rate, rate.shape[0] - 2, 0)
+    rest = jnp.exp(cum[:, SPAN - 1 :] - cum) * here
+    which = iota(gates.shape, 0) % GATES
+    mixed = jnp.where(which < 2, cum, pltpu.roll(growth, 2, 0))
+    columns = jnp.transpose(jnp.where(which < 4, mixed, pltpu.roll(rest, 4, 0)))
     cols_ref[...] = columns
+    rates_ref[...] = here
     lower = lane_r >= lane_c
     strict = lane_r > lane_c
-    keys, keys_t, systems = [], [], []
+    both = [(n, r) for n in range(spans) for r in range(2)]
+    keys = []
     for n in range(spans):
         k_n = unit(convolved(rows, n * SPAN + 8 - EDGE, SPAN, slice(0, DK), tap), 1.0)
-        kt_n = jnp.transpose(k_n.astype(F32)).astype(BF16)
         keys_ref[n * SPAN : (n + 1) * SPAN, :] = k_n
+        keys.append(k_n)
+    keys_t = []
+    for n in range(spans):
+        kt_n = jnp.transpose(keys[n].astype(F32)).astype(BF16)
         keys_t_ref[n] = kt_n
-        gram = dot(k_n, kt_n)
-        keys.append(k_n)
         keys_t.append(kt_n)
-        for r in range(2):
-            at = GATES * n + r
-            gap = columns[:, at : at + 1] - cum[at : at + 1, :]
-            within = jnp.where(lower, jnp.exp(jnp.where(lower, gap, 0.0)), 0.0)
-            within_ref[r, n * SPAN : (n + 1) * SPAN, :] = within.astype(BF16)
-            systems.append(jnp.where(strict, columns[:, at + 2 : at + 3] * within * gram, 0.0))
+    grams = [dot(keys[n], keys_t[n]) for n in range(spans)]
+    systems = []
+    for n, r in both:
+        at = GATES * n + r
+        gap = columns[:, at : at + 1] - cum[at : at + 1, :]
+        within = jnp.where(lower, jnp.exp(jnp.where(lower, gap, 0.0)), 0.0)
+        within_ref[r, n * SPAN : (n + 1) * SPAN, :] = within.astype(BF16)
+        systems.append(jnp.where(strict, within * grams[n], 0.0) * here[at : at + 1, :])
     inverses = invert(systems)
+    for i, (n, r) in enumerate(both):
+        t_ref[r, n] = jnp.concatenate(inverses[i], axis=1)
+    scaled = []
+    for n, r in both:
+        at = GATES * n + r
+        scaled.append(halves(columns[:, at + 2 : at + 3] * keys[n].astype(F32)))
+    w_mats = [mm_parts(t, x) for t, x in zip(inverses, scaled)]
+    weighed = []
+    for (n, r), w_mat in zip(both, w_mats):
+        at = GATES * n + r
+        weighed.append(columns[:, at + 4 : at + 5] * w_mat)
+    moved = [
+        mm_right(keys_t[n], jnp.concatenate(weighed[2 * n : 2 * n + 2], axis=1))
+        for n in range(spans)
+    ]
     identity = jnp.where(lane_r == lane_c, 1.0, 0.0)
-    for n in range(spans):
-        for r in range(2):
-            at = GATES * n + r
-            c_col = columns[:, at : at + 1]
-            t_parts = inverses[2 * n + r]
-            t_ref[r, n] = jnp.concatenate(t_parts, axis=1)
-            scaled = (columns[:, at + 2 : at + 3] * jnp.exp(c_col)) * keys[n].astype(F32)
-            w_mat = mm_parts(t_parts, halves(scaled))
-            c_end = c_col[SPAN - 1 : SPAN, :]
-            moved = mm_right(keys_t[n], jnp.exp(c_end - c_col) * w_mat)
-            lin = jnp.exp(c_end) * identity - moved
-            lin_ref[r, n] = jnp.concatenate(halves(lin), axis=1)
+    for n, r in both:
+        at = GATES * n + r
+        lin = growth[at : at + 1, SPAN - 1 :] * identity - moved[n][:, r * DK : (r + 1) * DK]
+        lin_ref[r, n] = jnp.concatenate(halves(lin), axis=1)
 
 
 def step(lin, parts):
@@ -266,19 +284,23 @@
     spans = t_ref.shape[1]
     taps = value_taps(sub, cv_ref)
     widened(rows, recv_ref, [GATES + tokens, GATES + 2 * tokens], tokens)
-    adds = []
-    for n in range(spans):
-        for r in range(2):
-            lanes = slice(r * DV, (r + 1) * DV)
-            at = GATES * n + r
-            v_n = convolved(rows, n * SPAN + 8 - EDGE, SPAN, lanes, taps[r]).astype(BF16)
-            vs[n * SPAN : (n + 1) * SPAN, lanes] = v_n
-            t_n = t_ref[r, n]
-            high, low = halves(cols_ref[:, at + 2 : at + 3] * v_n.astype(F32))
-            u_mat = step(t_n, (high, low))
-            c_col = cols_ref[:, at : at + 1]
-            adds.append(mm_right(keys_t_ref[n], jnp.exp(c_col[SPAN - 1 : SPAN, :] - c_col) * u_mat))
-    return adds
+    both = [(n, r) for n in range(spans) for r in range(2)]
+    values = []
+    for n, r in both:
+        lanes = slice(r * DV, (r + 1) * DV)
+        v_n = convolved(rows, n * SPAN + 8 - EDGE, SPAN, lanes, taps[r]).astype(BF16)
+        vs[n * SPAN : (n + 1) * SPAN, lanes] = v_n
+        values.append(jnp.concatenate([v_n, v_n], axis=0))
+    solved = [dot(t_ref[r, n], v) for (n, r), v in zip(both, values)]
+    weighed = []
+    for (n, r), u_mat in zip(both, solved):
+        at = GATES * n + r
+        weighed.append(cols_ref[:, at + 4 : at + 5] * u_mat)
+    moved = [
+        mm_right(keys_t_ref[n], jnp.concatenate(weighed[2 * n : 2 * n + 2], axis=1))
+        for n in range(spans)
+    ]
+    return [moved[n][:, r * DV : (r + 1) * DV] for n, r in both]
 
 
 def opening_kernel(
@@ -299,7 +321,7 @@
         for n in range(1, spans):
             for r in range(2):
                 parts = halves(states[r])
-                xs_ref[r, n] = jnp.concatenate(parts, axis=0)
+                xs_ref[n, :, r * DV : (r + 1) * DV] = jnp.concatenate(parts, axis=0)
                 states[r] = step(lin_ref[r, n], parts) + adds[2 * n + r]
         for r in range(2):
             hop_ref[r * DK : (r + 1) * DK, :] = states[r].astype(BF16)
@@ -319,6 +341,7 @@
     lin_ref,
     within_ref,
     cols_ref,
+    rates_ref,
     hop_ref,
     vs_ref,
     xs_ref,
@@ -328,46 +351,60 @@
     rows,
     query_rows,
     values,
+    inner,
+    readers,
+    states_ref,
 ):
     sub = lax.axis_index("sub")
     first = lax.axis_index("half") == 0
     tokens = (recv_ref.shape[1] - GATES) // 4
     spans = t_ref.shape[1]
+    both = [(n, r) for n in range(spans) for r in range(2)]
     tap = key_tap(sub, cq_ref)
     widened(query_rows, recv_ref, [GATES + 3 * tokens], tokens)
 
-    def seen(n):
-        at = n * SPAN
-        q_n = unit(convolved(query_rows, at + 8 - EDGE, SPAN, slice(0, DK), tap), DK**-0.5)
-        k_n = keys_ref[at : at + SPAN, :]
-        readers = jnp.concatenate([k_n, q_n], axis=0)
-        return readers, dot(q_n, keys_t_ref[n])
-
-    def weights(n, r, scores):
-        return (within_ref[r, n * SPAN : (n + 1) * SPAN, :].astype(F32) * scores).astype(BF16)
-
-    def spread(t_n, rest, inner):
-        rest = rest.astype(BF16)
-        fresh = dot(t_n, jnp.concatenate([rest, rest], axis=0))
-        return dot(inner, fresh.astype(BF16))
+    def span_rows(n):
+        return slice(n * SPAN, (n + 1) * SPAN)
+
+    def growth(n, r):
+        return cols_ref[:, GATES * n + 2 + r : GATES * n + 3 + r]
+
+    def prepare():
+        queries = []
+        for n in range(spans):
+            at = n * SPAN + 8 - EDGE
+            q_n = unit(convolved(query_rows, at, SPAN, slice(0, DK), tap), DK**-0.5)
+            queries.append(q_n)
+            readers[n, 0:SPAN, :] = keys_ref[span_rows(n), :]
+            readers[n, SPAN:, :] = q_n
+        scores = [dot(queries[n], keys_t_ref[n]) for n in range(spans)]
+        for n, r in both:
+            at = GATES * n + r
+            weight = within_ref[r, span_rows(n), :].astype(F32) * rates_ref[at : at + 1, :]
+            inner[r, n] = (weight * scores[n]).astype(BF16)
+
+    def twice(x, axis):
+        return jnp.concatenate([x, x], axis=axis)
 
     @pl.when(first)
     def _():
-        for n in range(spans):
-            at = slice(n * SPAN, (n + 1) * SPAN)
-            readers, scores = seen(n)
-            readers = jnp.concatenate([readers, readers], axis=1)
-            for r in range(2):
-                growth = jnp.exp(cols_ref[:, GATES * n + r : GATES * n + r + 1])
-                rate = cols_ref[:, GATES * n + 2 + r : GATES * n + 3 + r]
-                value = vs_ref[at, r * DV : (r + 1) * DV].astype(F32)
-                inner = weights(n, r, scores)
-                if n == 0:
-                    oa_ref[r, at, :] = spread(t_ref[r, n], rate * value, inner)
-                else:
-                    read = dot(readers, xs_ref[r, n])
-                    rest = rate * (value - growth * read[:SPAN])
-                    oa_ref[r, at, :] = growth * read[SPAN:] + spread(t_ref[r, n], rest, inner)
+        prepare()
+        reads = [dot(twice(readers[n], 1), xs_ref[n]) for n in range(1, spans)]
+        rests, seen = [], []
+        for n, r in both:
+            lanes = slice(r * DV, (r + 1) * DV)
+            value = vs_ref[span_rows(n), lanes]
+            if n == 0:
+                rests.append(value)
+                seen.append(None)
+            else:
+                read = growth(n, r) * reads[n - 1][:SPAN, lanes]
+                rests.append((value.astype(F32) - read).astype(BF16))
+                seen.append(growth(n, r) * reads[n - 1][SPAN:, lanes])
+        fresh = [dot(t_ref[r, n], twice(x, 0)).astype(BF16) for (n, r), x in zip(both, rests)]
+        spreads = [dot(inner[r, n], x) for (n, r), x in zip(both, fresh)]
+        for (n, r), x, y in zip(both, spreads, seen):
+            oa_ref[r, span_rows(n), :] = x if y is None else x + y
         for r in range(2):
             last_ref[r, :, 0:DV] = hop_ref[r * DK : (r + 1) * DK, :].astype(F32)
             last_ref[r, :, DV:] = jnp.zeros((DK, DV), F32)
@@ -375,28 +412,44 @@
     @pl.when(jnp.logical_not(first))
     def _():
         adds = values_part(recv_ref, cv_ref, keys_t_ref, t_ref, cols_ref, rows, values)
-        zero_half = jnp.zeros((SPAN, DV), F32)
-        identity = jnp.where(iota((DK, DK), 0) == iota((DK, DK), 1), 1.0, 0.0)
-        states = [jnp.concatenate([zero_half, identity], axis=1) for r in range(2)]
-        for n in range(spans):
-            at = slice(n * SPAN, (n + 1) * SPAN)
-            readers, scores = seen(n)
-            readers = jnp.concatenate([readers, readers], axis=1)
+        zero_half = jnp.zeros((DK, DV), F32)
+        states = [
+            jnp.concatenate(
+                [adds[r], lin_ref[r, 0, :, :DK].astype(F32) + lin_ref[r, 0, :, DK:].astype(F32)],
+                axis=1,
+            )
+            for r in range(2)
+        ]
+        for n in range(1, spans):
             for r in range(2):
                 parts = halves(states[r])
-                growth = jnp.exp(cols_ref[:, GATES * n + r : GATES * n + r + 1])
-                rate = cols_ref[:, GATES * n + 2 + r : GATES * n + 3 + r]
-                value = values[at, r * DV : (r + 1) * DV].astype(F32)
-                inner = weights(n, r, scores)
-                read = dot(readers, jnp.concatenate(parts, axis=0))
-                rest = rate * (jnp.concatenate([value, zero_half], axis=1) - growth * read[:SPAN])
-                out = growth * read[SPAN:] + spread(t_ref[r, n], rest, inner)
-                oa_ref[r, at, :] = out[:, :DV]
-                om_ref[r, at, :] = out[:, DV:].astype(BF16)
+                states_ref[r, n] = jnp.concatenate(parts, axis=0)
                 add = jnp.concatenate([adds[2 * n + r], zero_half], axis=1)
                 states[r] = step(lin_ref[r, n], parts) + add
         for r in range(2):
             last_ref[r] = states[r]
+        prepare()
+        reads = [
+            dot(twice(readers[n], 1), states_ref[r, n]) if n > 0 else None for n, r in both
+        ]
+        rests, seen = [], []
+        for (n, r), read in zip(both, reads):
+            value = values[span_rows(n), r * DV : (r + 1) * DV].astype(F32)
+            if n == 0:
+                known = growth(n, r) * readers[n].astype(F32)[:SPAN]
+                asked = growth(n, r) * readers[n].astype(F32)[SPAN:]
+                rest = jnp.concatenate([value, -known], axis=1)
+                seen.append(jnp.concatenate([zero_half, asked], axis=1))
+            else:
+                rest = jnp.concatenate([value, zero_half], axis=1) - growth(n, r) * read[:SPAN]
+                seen.append(growth(n, r) * read[SPAN:])
+            rests.append(rest.astype(BF16))
+        fresh = [dot(t_ref[r, n], twice(x, 0)).astype(BF16) for (n, r), x in zip(both, rests)]
+        spreads = [dot(inner[r, n], x) for (n, r), x in zip(both, fresh)]
+        for (n, r), x, y in zip(both, spreads, seen):
+            out = x + y
+            oa_ref[r, span_rows(n), :] = out[:, :DV]
+            om_ref[r, span_rows(n), :] = out[:, DV:].astype(BF16)
 
 
 def first_tokens(hop_ref, recv_ref, early_ref, cq_ref, ck_ref, cv_ref, rows):
@@ -544,7 +597,7 @@
         flops=1 << 20,
     )(*inputs)
     blocks = near(lax.all_to_all(packed, group, 0, 0, tiled=True))
-    keys, keys_t, inverses, lins, within, cols, early = call(
+    keys, keys_t, inverses, lins, within, cols, rates, early = call(
         keys_kernel,
         (
             pltpu.VMEM((total, DK), BF16),
@@ -553,21 +606,22 @@
             pltpu.VMEM((2, spans, DK, 2 * DK), BF16),
             pltpu.VMEM((2, total, SPAN), BF16),
             pltpu.VMEM((SPAN, spans * GATES), F32),
+            pltpu.VMEM((spans * GATES, SPAN), F32),
             pltpu.VMEM((8, SPAN), F32),
         ),
         [VMEM, VMEM, SMEM, SMEM],
         [pltpu.VMEM((8 + total, DK), F32)],
         flops=1 << 32,
     )(blocks, conv_k, a_log, dt_bias)
-    keys, keys_t, inverses, lins, within, cols, early = (
-        near(x) for x in (keys, keys_t, inverses, lins, within, cols, early)
+    keys, keys_t, inverses, lins, within, cols, rates, early = (
+        near(x) for x in (keys, keys_t, inverses, lins, within, cols, rates, early)
     )
     hop, values, starts = call(
         opening_kernel,
         (
             pltpu.VMEM((2 * DK + 64, 128), BF16),
             pltpu.VMEM((total, 2 * DV), BF16),
-            pltpu.VMEM((2, spans, 2 * DK, DV), BF16),
+            pltpu.VMEM((spans, 2 * DK, 2 * DV), BF16),
         ),
         [VMEM] * 6,
         [pltpu.VMEM((8 + total, 2 * DV), F32)],
@@ -582,11 +636,14 @@
             pltpu.VMEM((2, total, DV), BF16),
             pltpu.VMEM((2, DK, 2 * DV), F32),
         ),
-        [VMEM] * 12,
+        [VMEM] * 13,
         [
             pltpu.VMEM((8 + total, 2 * DV), F32),
             pltpu.VMEM((8 + total, DK), F32),
             pltpu.VMEM((total, 2 * DV), BF16),
+            pltpu.VMEM((2, spans, SPAN, SPAN), BF16),
+            pltpu.VMEM((spans, 2 * SPAN, DK), BF16),
+            pltpu.VMEM((2, spans, 2 * DK, 2 * DV), BF16),
         ],
         flops=1 << 32,
     )(
@@ -599,6 +656,7 @@
         lins,
         within,
         cols,
+        rates,
         hop,
         values,
         starts,

time: 59.9 us -> 53.5 us (0.89)
  Pallas kernels: 21.6 us -> 14.3 us
  blocking collectives: 36.4 us -> 37.1 us
    pallas_call x1, Pallas kernels: 5.16 us -> 2.12 us  [local(): call(output_kernel, (pltpu.VMEM((2, total, DV), F32), pltpu.VMEM((2, tota...]
    pallas_call x1, Pallas kernels: 8.29 us -> 5.56 us  [local(): call(keys_kernel, (pltpu.VMEM((total, DK), BF16), pltpu.VMEM((spans, DK,...]
    pallas_call x1, Pallas kernels: 4.51 us -> 2.92 us  [local(): call(opening_kernel, (pltpu.VMEM((2 * DK + 64, 128), BF16), pltpu.VMEM((t...]
    all_to_all x1, blocking collectives: 13.3 us -> 14 us  [local(): returned = near(lax.all_to_all(normed, group, 0, 0, tiled=True))]
  transfers between devices with their start and end apart: 1 -> 1, of which waited for: 0 -> 0; matrix products, arithmetic and copies ran while one was open for 0% -> 0% of each run, Pallas kernels for 9% -> 4%
where the time goes in v6:
time: 53.5 us; the launch traced here: 53.3 us
  blocking collectives  37.1 us (69%)
  Pallas kernels  14.3 us (27%)
  starting transfers between devices  1.61 us (3%)
    all_to_all x1, blocking collectives, local(): blocks = near(lax.all_to_all(packed, group, 0, 0, tiled=True))  23.1 us
    all_to_all x1, blocking collectives, local(): returned = near(lax.all_to_all(normed, group, 0, 0, tiled=True))  14 us
    pallas_call x1, Pallas kernels, local(): call(keys_kernel, (pltpu.VMEM((total, DK), BF16), pltpu.VMEM((spans, DK,...  5.56 us
    pallas_call x1, Pallas kernels, local(): call(opening_kernel, (pltpu.VMEM((2 * DK + 64, 128), BF16), pltpu.VMEM((t...  2.92 us
    pallas_call x1, Pallas kernels, local(): call(output_kernel, (pltpu.VMEM((2, total, DV), F32), pltpu.VMEM((2, tota...  2.12 us
    pallas_call x1, Pallas kernels, local(): call(functools.partial(pack_kernel, heads_axis), pltpu.VMEM((peers, GATES...  1.75 us
    ppermute x1, starting transfers between devices, local(): entering = near(lax.ppermute(hop, 'half', route))  1.61 us
  transfers between devices with their start and end apart: 1, of which 0 were waited for; matrix products, arithmetic and copies ran while one was open for 0% of the time, Pallas kernels for 4%

profile of v6, /device:TPU:0, one launch (start us, length us, event | category | flops | bytes accessed | tf_op | source)
XLA Modules:
  0.0 53.3 jit_solution(15130467933050869759)
XLA Ops:
  0.0 1.7 %shard_map.118 = bf16[16,272,128]{2,1,0:T(8,128)(2,1)S(1)} custom-call(bf16[64,2048]{1,0:T(8,128)(2,1)} %q_in.1, bf16[64,2048]{1,0:T(8,128)(2,1)} %k_in.1, bf16[64,4096]{1,0:T(8,128)(2,1)} %v_in.1, bf16[32,64]{1,0:T(8,128)(2,1)} %bitcast.4, bf16[32,64]{1,0:T(8,128)(2,1)} %bitcast.5), custom_call_target="tpu_custom_call" | custom-call | flops 1048576 | bytes 2097152 | tf_op jit(solution)/shard_map/pallas_call | solution.py:592
  1.8 0.0 copy-start.2
  1.8 0.0 copy-start.5
  1.8 0.0 copy-start.6
  1.8 23.1 %all_to_all.10.recv_ref = bf16[16,272,128]{2,1,0:T(8,128)(2,1)S(1)} all-to-all(bf16[16,272,128]{2,1,0:T(8,128)(2,1)S(1)} %shard_map.118), channel_id=1, replica_groups=mesh['half'=2,'sub'=4,'head'=4] {'sub','head'}, dimensions={0} | all-to-all | bytes 2228224 | tf_op jit(solution)/shard_map/all_to_all | solution.py:599
  24.9 0.0 copy-done.2
  24.9 0.0 copy-done.5
  24.9 0.0 copy-done.6
  24.9 0.0 copy-start.1
  24.9 5.6 %shard_map.119 = (bf16[1024,128]{1,0:T(8,128)(2,1)S(1)}, bf16[8,128,128]{2,1,0:T(8,128)(2,1)S(1)}, bf16[2,8,128,256]{3,2,1,0:T(8,128)(2,1)S(1)}, bf16[2,8,128,25...) custom-call(bf16[16,272,128]{2,1,0:T(8,128)(2,1)S(1)} %all_to_all.10, ...), custom_call_target="tpu_custom_call" | custom-call | flops 4294967296 | bytes 2097152 | tf_op jit(solution)/shard_map/pallas_call | solution.py:600
  30.5 0.0 copy-done.1
  30.5 0.0 copy-start.3
  30.5 2.9 %shard_map.120 = (bf16[320,128]{1,0:T(8,128)(2,1)S(1)}, bf16[1024,256]{1,0:T(8,128)(2,1)S(1)}, bf16[8,256,256]{2,1,0:T(8,128)(2,1)S(1)}) custom-call(bf16[16,272,128]{2,1,0:T(8,128)(2,1)S(1)} %all_to_all.10.recv_ref, f32[4,1024]{1,0:T(4,128)S(1)} %copy-done.1, bf16[8,128,128]{2,1,0:T(8,128)(2,1)S(1)} %get-tuple-element.18.keys_t_ref, ...), custom_call_target="tpu_custom_call" | custom-call | flops 4294967296 | bytes 2097152 | tf_op jit(solution)/shard_map/pallas_call | solution.py:619
  33.4 1.6 %collective-permute-start = (bf16[320,128]{1,0:T(8,128)(2,1)S(1)}, bf16[320,128]{1,0:T(8,128)(2,1)S(1)}, u32[]{:S(2)}, u32[]{:S(2)}) collective-permute-start(bf16[320,128]{1,0:T(8,128)(2,1)S(1)} %get-tuple-element.22.hop_ref), channel_id=1, source_target_pairs={{0,16},{1,17},{2,18},{3,19},{4,20},{5,21},{6,22},{7,23},{8,24},{9,... | collective-permute-start | bytes 245768 | tf_op jit(solution)/shard_map/ppermute | solution.py:630
  35.0 0.0 copy-done.3
  35.0 0.0 copy-start.4
  35.1 2.1 %shard_map.121 = (f32[2,1024,128]{2,1,0:T(8,128)S(1)}, bf16[2,1024,128]{2,1,0:T(8,128)(2,1)S(1)}, f32[2,128,256]{2,1,0:T(8,128)}) custom-call(bf16[16,272,128]{2,1,0:T(8,128)(2,1)S(1)} %all_to_all.10.recv_ref, f32[4,512]{1,0:T(4,128)S(1)} %copy-done.3, f32[4,1024]{1,0:T(4,128)S(1)} %copy-done.1, bf16[1024,128]{1,0:T(8,128)(2,1)S(1)} %get-tuple-element.24.keys_ref, ...), custom_call_target="tpu_custom_call" | custom-call | flops 4294967296 | bytes 2097152 | tf_op jit(solution)/shard_map/pallas_call | solution.py:632
  37.2 0.0 collective-permute-done.hop_ref
  37.2 0.0 copy-done.4
  37.2 1.0 %shard_map.122 = bf16[16,64,256]{2,1,0:T(8,128)(2,1)S(1)} custom-call(bf16[320,128]{1,0:T(8,128)(2,1)S(1)} %collective-permute-done.hop_ref, bf16[16,272,128]{2,1,0:T(8,128)(2,1)S(1)} %all_to_all.10.recv_ref, f32[8,128]{1,0:T(8,128)S(1)} %get-tuple-element.23.early_ref, f32[4,512]{1,0:T(4,128)S(1)} %copy-done.3, f32[4,512]{1,0:T(4,128)S(1)} %copy-done.2, ...), custom_call_target="tpu_custom_call" | custom-call | flops 67108864 | bytes 2097152 | tf_op jit(solution)/shard_map/pallas_call | solution.py:672
  38.2 0.0 copy-start
  38.2 14.0 %all_to_all.11.normed_ref = bf16[16,64,256]{2,1,0:T(8,128)(2,1)S(1)} all-to-all(bf16[16,64,256]{2,1,0:T(8,128)(2,1)S(1)} %shard_map.122), channel_id=1, replica_groups=mesh['half'=2,'sub'=4,'head'=4] {'sub','head'}, dimensions={0} | all-to-all | bytes 1048576 | tf_op jit(solution)/shard_map/all_to_all | solution.py:688
  52.2 0.0 copy-done
  52.2 0.9 %shard_map.123 = bf16[64,4096]{1,0:T(8,128)(2,1)} custom-call(bf16[16,64,256]{2,1,0:T(8,128)(2,1)S(1)} %all_to_all.11.normed_ref, bf16[64,4096]{1,0:T(8,128)(2,1)S(1)} %copy-done), custom_call_target="tpu_custom_call" | custom-call | flops 67108864 | bytes 2097152 | tf_op jit(solution)/shard_map/pallas_call | solution.py:689
Async XLA Ops:
  1.8 23.1 %copy-start.2 = (f32[4,512]{1,0:T(4,128)S(1)}, f32[4,512]{1,0:T(4,128)}, u32[]{:S(2)}) copy-start(f32[4,512]{1,0:T(4,128)} %ck_ref.3) | copy-start | bytes 24580
  1.8 23.1 %copy-start.5 = (f32[8]{0:T(128)S(1)}, f32[8]{0:T(128)}, u32[]{:S(2)}) copy-start(f32[8]{0:T(128)} %alog_ref.1) | copy-start | bytes 100
  1.8 23.1 %copy-start.6 = (f32[8]{0:T(128)S(1)}, f32[8]{0:T(128)}, u32[]{:S(2)}) copy-start(f32[8]{0:T(128)} %dt_ref.1) | copy-start | bytes 100
  24.9 5.6 %copy-start.1 = (f32[4,1024]{1,0:T(4,128)S(1)}, f32[4,1024]{1,0:T(4,128)}, u32[]{:S(2)}) copy-start(f32[4,1024]{1,0:T(4,128)} %cv_ref.5) | copy-start | bytes 49156
  30.5 4.6 %copy-start.3 = (f32[4,512]{1,0:T(4,128)S(1)}, f32[4,512]{1,0:T(4,128)}, u32[]{:S(2)}) copy-start(f32[4,512]{1,0:T(4,128)} %cq_ref.3) | copy-start | bytes 24580
  33.4 3.8 %collective-permute-start = (bf16[320,128]{1,0:T(8,128)(2,1)S(1)}, bf16[320,128]{1,0:T(8,128)(2,1)S(1)}, u32[]{:S(2)}, u32[]{:S(2)}) collective-permute-start(bf16[320,128]{1,0:T(8,128)(2,1)S(1)} %get-tuple-element.22.hop_ref), channel_id=1, source_target_pairs={{0,16},{1,17},{2,18},{3,19},{4,20},{5,21},{6,22},{7,23},{8,24},{9,... | collective-permute-start | bytes 245768 | tf_op jit(solution)/shard_map/ppermute | solution.py:630
  35.0 2.1 %copy-start.4 = (f32[128]{0:T(128)S(1)}, f32[128]{0:T(128)}, u32[]{:S(2)}) copy-start(f32[128]{0:T(128)} %param.23) | copy-start | bytes 1540
  38.2 14.0 %copy-start = (bf16[64,4096]{1,0:T(8,128)(2,1)S(1)}, bf16[64,4096]{1,0:T(8,128)(2,1)}, u32[]{:S(2)}) copy-start(bf16[64,4096]{1,0:T(8,128)(2,1)} %z_ref.1) | copy-start | bytes 1572868

commit v7 on v6

--- a/solution.py
+++ b/solution.py
@@ -61,19 +61,10 @@
     copies = [pltpu.make_async_copy(a, b, sems.at[i]) for i, (a, b) in enumerate(pairs)]
     for copy in copies:
         copy.start()
-    for copy in copies:
+    subs = peers // heads_axis
+    key_heads = [(dest % heads_axis) * subs + dest // heads_axis for dest in range(peers)]
+    for copy in copies[:2]:
         copy.wait()
-    subs = peers // heads_axis
-    for dest in range(peers):
-        key_head = (dest % heads_axis) * subs + dest // heads_axis
-        lanes = slice(key_head * DK, (key_head + 1) * DK)
-        out_ref[dest, GATES : GATES + tokens, :] = k_ref[:, lanes]
-        for r in range(2):
-            value_lanes = slice((2 * key_head + r) * DV, (2 * key_head + r + 1) * DV)
-            out_ref[dest, GATES + (1 + r) * tokens : GATES + (2 + r) * tokens, :] = v_ref[
-                :, value_lanes
-            ]
-        out_ref[dest, GATES + 3 * tokens :, :] = q_ref[:, lanes]
     value_heads = at_ref.shape[0]
     row, entry = iota((peers * GATES, value_heads), 0), iota((peers * GATES, value_heads), 1)
     dest, which = row // GATES, row % GATES
@@ -90,6 +81,21 @@
     gates = dot(picked, place).astype(BF16)
     for dest in range(peers):
         out_ref[dest, 0:GATES, :] = gates[GATES * dest : GATES * (dest + 1), :]
+
+    def laid(ref, lane, start):
+        for dest, key_head in enumerate(key_heads):
+            at = lane(key_head) * 128
+            out_ref[dest, GATES + start * tokens : GATES + (start + 1) * tokens, :] = ref[
+                :, at : at + 128
+            ]
+
+    copies[2].wait()
+    laid(k_ref, lambda key_head: key_head, 0)
+    copies[3].wait()
+    laid(v_ref, lambda key_head: 2 * key_head, 1)
+    laid(v_ref, lambda key_head: 2 * key_head + 1, 2)
+    copies[4].wait()
+    laid(q_ref, lambda key_head: key_head, 3)
 
 
 def invert(systems):
@@ -110,14 +116,12 @@
     for m in range(SUB - 1):
         spread = jnp.take_along_axis(compact, (lane // SUB) * SUB + m, axis=1)
         solved = solved - spread.reshape(count, SUB, size) * solved[:, m : m + 1, :]
-    inverses = [
-        jnp.where(
-            diagonal.reshape(blocks, SUB, size), solved[i : i + 1, :, :], 0.0
-        ).reshape(size, size)
+    lows = [halves(n) for n in systems]
+    placed = jnp.where(diagonal, 1.0, 0.0).astype(BF16)
+    parts = [
+        tuple(jnp.concatenate([x] * blocks, axis=0) * placed for x in halves(solved[i]))
         for i in range(count)
     ]
-    lows = [halves(n) for n in systems]
-    parts = [halves(inv) for inv in inverses]
     width = SUB
     while width < size:
         odd = [(j, j + width) for j in range(width, size, 2 * width)]
@@ -193,7 +197,6 @@
     lin_ref,
     within_ref,
     cols_ref,
-    rates_ref,
     early_ref,
     rows,
 ):
@@ -228,7 +231,6 @@
     mixed = jnp.where(which < 2, cum, pltpu.roll(growth, 2, 0))
     columns = jnp.transpose(jnp.where(which < 4, mixed, pltpu.roll(rest, 4, 0)))
     cols_ref[...] = columns
-    rates_ref[...] = here
     lower = lane_r >= lane_c
     strict = lane_r > lane_c
     both = [(n, r) for n in range(spans) for r in range(2)]
@@ -247,9 +249,9 @@
     for n, r in both:
         at = GATES * n + r
         gap = columns[:, at : at + 1] - cum[at : at + 1, :]
-        within = jnp.where(lower, jnp.exp(jnp.where(lower, gap, 0.0)), 0.0)
-        within_ref[r, n * SPAN : (n + 1) * SPAN, :] = within.astype(BF16)
-        systems.append(jnp.where(strict, within * grams[n], 0.0) * here[at : at + 1, :])
+        within = jnp.exp(jnp.where(lower, gap, 0.0)) * here[at : at + 1, :]
+        within_ref[r, n * SPAN : (n + 1) * SPAN, :] = jnp.where(lower, within, 0.0).astype(BF16)
+        systems.append(jnp.where(strict, within * grams[n], 0.0))
     inverses = invert(systems)
     for i, (n, r) in enumerate(both):
         t_ref[r, n] = jnp.concatenate(inverses[i], axis=1)
@@ -310,9 +312,12 @@
     peers = recv_ref.shape[0]
     tokens = (recv_ref.shape[1] - GATES) // 4
     spans = t_ref.shape[1]
-    for at, which in ((0, 3), (16, 0), (32, 1), (48, 2)):
+    edges = []
+    for which in (3, 0, 1, 2):
         end = GATES + (which + 1) * tokens
-        hop_ref[2 * DK + at : 2 * DK + at + 16, :] = recv_ref[peers - 1, end - 16 : end, :]
+        edges.append(recv_ref[peers - 1, end - 16 : end, :].astype(F32)[16 - EDGE :])
+    edges.append(jnp.zeros((16 - 4 * EDGE, 128), F32))
+    hop_ref[2 * DK :, :] = jnp.concatenate(edges, axis=0).astype(BF16)
 
     @pl.when(first)
     def _():
@@ -341,7 +346,6 @@
     lin_ref,
     within_ref,
     cols_ref,
-    rates_ref,
     hop_ref,
     vs_ref,
     xs_ref,
@@ -379,8 +383,7 @@
             readers[n, SPAN:, :] = q_n
         scores = [dot(queries[n], keys_t_ref[n]) for n in range(spans)]
         for n, r in both:
-            at = GATES * n + r
-            weight = within_ref[r, span_rows(n), :].astype(F32) * rates_ref[at : at + 1, :]
+            weight = within_ref[r, span_rows(n), :].astype(F32)
             inner[r, n] = (weight * scores[n]).astype(BF16)
 
     def twice(x, axis):
@@ -454,14 +457,14 @@
 
 def first_tokens(hop_ref, recv_ref, early_ref, cq_ref, ck_ref, cv_ref, rows):
     sub = lax.axis_index("sub")
-    later = lax.axis_index("half") > 0
     tokens = (recv_ref.shape[1] - GATES) // 4
     taps = [key_tap(sub, cq_ref), key_tap(sub, ck_ref)] + value_taps(sub, cv_ref)
     results = []
+    edges = hop_ref[2 * DK :, :].astype(F32)
     for g, first in enumerate((3, 0, 1, 2)):
         lanes = slice(g * 128, (g + 1) * 128)
         start = GATES + first * tokens
-        rows[0:16, lanes] = hop_ref[2 * DK + 16 * g : 2 * DK + 16 * (g + 1), :].astype(F32)
+        rows[16 - EDGE : 16, lanes] = edges[EDGE * g : EDGE * (g + 1)]
         rows[16:32, lanes] = recv_ref[0, start : start + 16, :].astype(F32)
         results.append(convolved(rows, 16 - EDGE, 8, lanes, taps[g]))
     q_cols = jnp.transpose(unit(results[0], DK**-0.5).astype(F32))
@@ -481,47 +484,59 @@
                 gates[2 + r : 3 + r, t : t + 1] * (values[t : t + 1, :] - held)
             )
             out = jnp.where(line == t, jnp.sum(q_t * state, axis=0, keepdims=True), out)
-        finals.append(jnp.where(later, state, entering))
+        finals.append(state)
         outputs.append(out)
-    return finals, outputs, later
+    return finals, outputs
 
 
 def finish_kernel(
     hop_ref, recv_ref, early_ref, cq_ref, ck_ref, cv_ref, gain_ref, oa_ref, om_ref, out_ref, rows
 ):
     peers, tokens = out_ref.shape[0], out_ref.shape[1]
-    finals, outputs, later = first_tokens(
-        hop_ref, recv_ref, early_ref, cq_ref, ck_ref, cv_ref, rows
-    )
-    states = [x.astype(BF16) for x in finals]
+    first = lax.axis_index("half") == 0
     gain = gain_ref[...]
-    replaced = later & (iota((8, DV), 0) < EDGE)
     chunks = 4
     part, peer_part = peers * tokens // chunks, peers // chunks
-    for c in range(chunks):
-        at = c * part
-        for r in range(2):
-            passed = dot(om_ref[r, at : at + part, :], states[r])
-            core = oa_ref[r, at : at + part, :] + jnp.where(later, passed, 0.0)
-            if c == 0:
-                core = jnp.concatenate(
-                    [jnp.where(replaced, outputs[r], core[0:8]), core[8:]], axis=0
-                )
-            scale = lax.rsqrt(jnp.mean(core * core, axis=-1, keepdims=True) + EPS)
-            normed = (core * scale * gain).astype(BF16)
-            out_ref[c * peer_part : (c + 1) * peer_part, :, r * DV : (r + 1) * DV] = (
-                normed.reshape(peer_part, tokens, DV)
-            )
+
+    def put(c, r, core):
+        scale = lax.rsqrt(jnp.mean(core * core, axis=-1, keepdims=True) + EPS)
+        normed = (core * scale * gain).astype(BF16)
+        out_ref[c * peer_part : (c + 1) * peer_part, :, r * DV : (r + 1) * DV] = normed.reshape(
+            peer_part, tokens, DV
+        )
+
+    @pl.when(first)
+    def _():
+        for c in range(chunks):
+            for r in range(2):
+                put(c, r, oa_ref[r, c * part : (c + 1) * part, :])
+
+    @pl.when(jnp.logical_not(first))
+    def _():
+        finals, outputs = first_tokens(hop_ref, recv_ref, early_ref, cq_ref, ck_ref, cv_ref, rows)
+        replaced = iota((8, DV), 0) < EDGE
+        passed = [dot(om_ref[r], finals[r].astype(BF16)) for r in range(2)]
+        for c in range(chunks):
+            at = c * part
+            for r in range(2):
+                core = oa_ref[r, at : at + part, :] + passed[r][at : at + part]
+                if c == 0:
+                    core = jnp.concatenate(
+                        [jnp.where(replaced, outputs[r], core[0:8]), core[8:]], axis=0
+                    )
+                put(c, r, core)
 
 
 def advance_kernel(
     hop_ref, recv_ref, early_ref, cq_ref, ck_ref, cv_ref, hop_own, last_ref, next_ref, rows
 ):
-    finals, _, _ = first_tokens(hop_ref, recv_ref, early_ref, cq_ref, ck_ref, cv_ref, rows)
+    finals, _ = first_tokens(hop_ref, recv_ref, early_ref, cq_ref, ck_ref, cv_ref, rows)
+    first = lax.axis_index("half") == 0
     for r in range(2):
         last = last_ref[r]
         through = mm_parts(halves(last[:, DV:]), halves(finals[r]))
-        next_ref[r * DK : (r + 1) * DK, :] = (through + last[:, :DV]).astype(BF16)
+        moved = jnp.where(first, 0.0, through) + last[:, :DV]
+        next_ref[r * DK : (r + 1) * DK, :] = moved.astype(BF16)
     next_ref[2 * DK :, :] = hop_own[2 * DK :, :]
 
 
@@ -597,7 +612,7 @@
         flops=1 << 20,
     )(*inputs)
     blocks = near(lax.all_to_all(packed, group, 0, 0, tiled=True))
-    keys, keys_t, inverses, lins, within, cols, rates, early = call(
+    keys, keys_t, inverses, lins, within, cols, early = call(
         keys_kernel,
         (
             pltpu.VMEM((total, DK), BF16),
@@ -606,20 +621,19 @@
             pltpu.VMEM((2, spans, DK, 2 * DK), BF16),
             pltpu.VMEM((2, total, SPAN), BF16),
             pltpu.VMEM((SPAN, spans * GATES), F32),
-            pltpu.VMEM((spans * GATES, SPAN), F32),
             pltpu.VMEM((8, SPAN), F32),
         ),
         [VMEM, VMEM, SMEM, SMEM],
         [pltpu.VMEM((8 + total, DK), F32)],
         flops=1 << 32,
     )(blocks, conv_k, a_log, dt_bias)
-    keys, keys_t, inverses, lins, within, cols, rates, early = (
-        near(x) for x in (keys, keys_t, inverses, lins, within, cols, rates, early)
+    keys, keys_t, inverses, lins, within, cols, early = (
+        near(x) for x in (keys, keys_t, inverses, lins, within, cols, early)
     )
     hop, values, starts = call(
         opening_kernel,
         (
-            pltpu.VMEM((2 * DK + 64, 128), BF16),
+            pltpu.VMEM((2 * DK + 16, 128), BF16),
             pltpu.VMEM((total, 2 * DV), BF16),
             pltpu.VMEM((spans, 2 * DK, 2 * DV), BF16),
         ),
@@ -636,7 +650,7 @@
             pltpu.VMEM((2, total, DV), BF16),
             pltpu.VMEM((2, DK, 2 * DV), F32),
         ),
-        [VMEM] * 13,
+        [VMEM] * 12,
         [
             pltpu.VMEM((8 + total, 2 * DV), F32),
             pltpu.VMEM((8 + total, DK), F32),
@@ -656,7 +670,6 @@
         lins,
         within,
         cols,
-        rates,
         hop,
         values,
         starts,

time: 53.5 us -> 51.9 us (0.970)
  Pallas kernels: 14.3 us -> 13.2 us
  blocking collectives: 37.1 us -> 36.5 us
    pallas_call x1, Pallas kernels: 0.97 us -> 0.36 us  [local(): call(finish_kernel, pltpu.VMEM((peers, tokens, 2 * DV), BF16), [VMEM] * 9...]
    all_to_all x1, blocking collectives: 14 us -> 13.4 us  [local(): returned = near(lax.all_to_all(normed, group, 0, 0, tiled=True))]
where the time goes in v7:
time: 51.9 us; the launch traced here: 51.7 us
  blocking collectives  36.5 us (70%)
  Pallas kernels  13.2 us (25%)
  starting transfers between devices  1.61 us (3%)
    all_to_all x1, blocking collectives, local(): blocks = near(lax.all_to_all(packed, group, 0, 0, tiled=True))  23.1 us
    all_to_all x1, blocking collectives, local(): returned = near(lax.all_to_all(normed, group, 0, 0, tiled=True))  13.4 us
    pallas_call x1, Pallas kernels, local(): call(keys_kernel, (pltpu.VMEM((total, DK), BF16), pltpu.VMEM((spans, DK,...  5.47 us
    pallas_call x1, Pallas kernels, local(): call(opening_kernel, (pltpu.VMEM((2 * DK + 16, 128), BF16), pltpu.VMEM((t...  2.91 us
    pallas_call x1, Pallas kernels, local(): call(output_kernel, (pltpu.VMEM((2, total, DV), F32), pltpu.VMEM((2, tota...  2.17 us
    ppermute x1, starting transfers between devices, local(): entering = near(lax.ppermute(hop, 'half', route))  1.61 us
    pallas_call x1, Pallas kernels, local(): call(functools.partial(pack_kernel, heads_axis), pltpu.VMEM((peers, GATES...  1.34 us
  transfers between devices with their start and end apart: 1, of which 0 were waited for; matrix products, arithmetic and copies ran while one was open for 0% of the time, Pallas kernels for 4%

profile of v7, /device:TPU:0, one launch (start us, length us, event | category | flops | bytes accessed | tf_op | source)
XLA Modules:
  0.0 51.7 jit_solution(1657229055738501531)
XLA Ops:
  0.0 1.3 %shard_map.118 = bf16[16,272,128]{2,1,0:T(8,128)(2,1)S(1)} custom-call(bf16[64,2048]{1,0:T(8,128)(2,1)} %q_in.1, bf16[64,2048]{1,0:T(8,128)(2,1)} %k_in.1, bf16[64,4096]{1,0:T(8,128)(2,1)} %v_in.1, bf16[32,64]{1,0:T(8,128)(2,1)} %bitcast.4, bf16[32,64]{1,0:T(8,128)(2,1)} %bitcast.5), custom_call_target="tpu_custom_call" | custom-call | flops 1048576 | bytes 2097152 | tf_op jit(solution)/shard_map/pallas_call | solution.py:607
  1.3 0.0 copy-start.2
  1.4 0.0 copy-start.5
  1.4 0.0 copy-start.6
  1.4 23.1 %all_to_all.10.recv_ref = bf16[16,272,128]{2,1,0:T(8,128)(2,1)S(1)} all-to-all(bf16[16,272,128]{2,1,0:T(8,128)(2,1)S(1)} %shard_map.118), channel_id=1, replica_groups=mesh['half'=2,'sub'=4,'head'=4] {'sub','head'}, dimensions={0} | all-to-all | bytes 2228224 | tf_op jit(solution)/shard_map/all_to_all | solution.py:614
  24.5 0.0 copy-done.2
  24.5 0.0 copy-done.5
  24.5 0.0 copy-done.6
  24.5 0.0 copy-start.1
  24.5 5.5 %shard_map.119 = (bf16[1024,128]{1,0:T(8,128)(2,1)S(1)}, bf16[8,128,128]{2,1,0:T(8,128)(2,1)S(1)}, bf16[2,8,128,256]{3,2,1,0:T(8,128)(2,1)S(1)}, bf16[2,8,128,25...) custom-call(bf16[16,272,128]{2,1,0:T(8,128)(2,1)S(1)} %all_to_all.10.r, ...), custom_call_target="tpu_custom_call" | custom-call | flops 4294967296 | bytes 2097152 | tf_op jit(solution)/shard_map/pallas_call | solution.py:615
  30.0 0.0 copy-done.1
  30.0 0.0 copy-start.3
  30.0 2.9 %shard_map.120 = (bf16[272,128]{1,0:T(8,128)(2,1)S(1)}, bf16[1024,256]{1,0:T(8,128)(2,1)S(1)}, bf16[8,256,256]{2,1,0:T(8,128)(2,1)S(1)}) custom-call(bf16[16,272,128]{2,1,0:T(8,128)(2,1)S(1)} %all_to_all.10.recv_ref, f32[4,1024]{1,0:T(4,128)S(1)} %copy-done.1, bf16[8,128,128]{2,1,0:T(8,128)(2,1)S(1)} %get-tuple-element.17.keys_t_ref, ...), custom_call_target="tpu_custom_call" | custom-call | flops 4294967296 | bytes 2097152 | tf_op jit(solution)/shard_map/pallas_call | solution.py:633
  32.9 1.6 %collective-permute-start = (bf16[272,128]{1,0:T(8,128)(2,1)S(1)}, bf16[272,128]{1,0:T(8,128)(2,1)S(1)}, u32[]{:S(2)}, u32[]{:S(2)}) collective-permute-start(bf16[272,128]{1,0:T(8,128)(2,1)S(1)} %get-tuple-element.21.hop_ref), channel_id=1, source_target_pairs={{0,16},{1,17},{2,18},{3,19},{4,20},{5,21},{6,22},{7,23},{8,24},{9,... | collective-permute-start | bytes 208904 | tf_op jit(solution)/shard_map/ppermute | solution.py:644
  34.5 0.0 copy-done.3
  34.5 0.0 copy-start.4
  34.5 2.2 %shard_map.121 = (f32[2,1024,128]{2,1,0:T(8,128)S(1)}, bf16[2,1024,128]{2,1,0:T(8,128)(2,1)S(1)}, f32[2,128,256]{2,1,0:T(8,128)}) custom-call(bf16[16,272,128]{2,1,0:T(8,128)(2,1)S(1)} %all_to_all.10.recv_ref, f32[4,512]{1,0:T(4,128)S(1)} %copy-done.3, f32[4,1024]{1,0:T(4,128)S(1)} %copy-done.1, bf16[1024,128]{1,0:T(8,128)(2,1)S(1)} %get-tuple-element.23.keys_ref, ...), custom_call_target="tpu_custom_call" | custom-call | flops 4294967296 | bytes 2097152 | tf_op jit(solution)/shard_map/pallas_call | solution.py:646
  36.7 0.0 collective-permute-done.hop_ref
  36.7 0.0 copy-done.4
  36.7 0.4 shard_map.122
  37.1 0.0 copy-start
  37.1 13.4 %all_to_all.11.normed_ref = bf16[16,64,256]{2,1,0:T(8,128)(2,1)S(1)} all-to-all(bf16[16,64,256]{2,1,0:T(8,128)(2,1)S(1)} %shard_map.122), channel_id=1, replica_groups=mesh['half'=2,'sub'=4,'head'=4] {'sub','head'}, dimensions={0} | all-to-all | bytes 1048576 | tf_op jit(solution)/shard_map/all_to_all | solution.py:701
  50.5 0.0 copy-done
  50.5 0.9 %shard_map.123 = bf16[64,4096]{1,0:T(8,128)(2,1)} custom-call(bf16[16,64,256]{2,1,0:T(8,128)(2,1)S(1)} %all_to_all.11.normed_ref, bf16[64,4096]{1,0:T(8,128)(2,1)S(1)} %copy-done), custom_call_target="tpu_custom_call" | custom-call | flops 67108864 | bytes 2097152 | tf_op jit(solution)/shard_map/pallas_call | solution.py:702
Async XLA Ops:
  1.3 23.1 %copy-start.2 = (f32[4,512]{1,0:T(4,128)S(1)}, f32[4,512]{1,0:T(4,128)}, u32[]{:S(2)}) copy-start(f32[4,512]{1,0:T(4,128)} %ck_ref.3) | copy-start | bytes 24580
  1.4 23.1 %copy-start.5 = (f32[8]{0:T(128)S(1)}, f32[8]{0:T(128)}, u32[]{:S(2)}) copy-start(f32[8]{0:T(128)} %alog_ref.1) | copy-start | bytes 100
  1.4 23.1 %copy-start.6 = (f32[8]{0:T(128)S(1)}, f32[8]{0:T(128)}, u32[]{:S(2)}) copy-start(f32[8]{0:T(128)} %dt_ref.1) | copy-start | bytes 100
  24.5 5.5 %copy-start.1 = (f32[4,1024]{1,0:T(4,128)S(1)}, f32[4,1024]{1,0:T(4,128)}, u32[]{:S(2)}) copy-start(f32[4,1024]{1,0:T(4,128)} %cv_ref.5) | copy-start | bytes 49156
  30.0 4.6 %copy-start.3 = (f32[4,512]{1,0:T(4,128)S(1)}, f32[4,512]{1,0:T(4,128)}, u32[]{:S(2)}) copy-start(f32[4,512]{1,0:T(4,128)} %cq_ref.3) | copy-start | bytes 24580
  32.9 3.8 %collective-permute-start = (bf16[272,128]{1,0:T(8,128)(2,1)S(1)}, bf16[272,128]{1,0:T(8,128)(2,1)S(1)}, u32[]{:S(2)}, u32[]{:S(2)}) collective-permute-start(bf16[272,128]{1,0:T(8,128)(2,1)S(1)} %get-tuple-element.21.hop_ref), channel_id=1, source_target_pairs={{0,16},{1,17},{2,18},{3,19},{4,20},{5,21},{6,22},{7,23},{8,24},{9,... | collective-permute-start | bytes 208904 | tf_op jit(solution)/shard_map/ppermute | solution.py:644
  34.5 2.2 %copy-start.4 = (f32[128]{0:T(128)S(1)}, f32[128]{0:T(128)}, u32[]{:S(2)}) copy-start(f32[128]{0:T(128)} %param.23) | copy-start | bytes 1540
  37.1 13.5 %copy-start = (bf16[64,4096]{1,0:T(8,128)(2,1)S(1)}, bf16[64,4096]{1,0:T(8,128)(2,1)}, u32[]{:S(2)}) copy-start(bf16[64,4096]{1,0:T(8,128)(2,1)} %z_ref.1) | copy-start | bytes 1572868

commit v8 on v7

--- a/solution.py
+++ b/solution.py
@@ -18,7 +18,7 @@
 F32 = jnp.float32
 BF16 = jnp.bfloat16
 VMEM_BYTES = 24 * 1024 * 1024
-GATES = 16
+GATES = 8
 
 
 def dot(a, b, dims=((1,), (0,))):
@@ -35,8 +35,9 @@
 
 
 def mm_parts(a, b):
-    both = jnp.concatenate(a, axis=1)
-    return dot(both, jnp.concatenate([b[0], b[0]], axis=0)) + dot(a[0], b[1])
+    rows, width = a[0].shape[0], b[0].shape[1]
+    terms = dot(jnp.concatenate(a, axis=0), jnp.concatenate(b, axis=1))
+    return terms[:rows, :width] + (terms[:rows, width:] + terms[rows:, :width])
 
 
 def silu(x):
@@ -80,12 +81,12 @@
     ).astype(BF16)
     gates = dot(picked, place).astype(BF16)
     for dest in range(peers):
-        out_ref[dest, 0:GATES, :] = gates[GATES * dest : GATES * (dest + 1), :]
+        out_ref[dest, 4 * tokens :, :] = gates[GATES * dest : GATES * (dest + 1), :]
 
     def laid(ref, lane, start):
         for dest, key_head in enumerate(key_heads):
             at = lane(key_head) * 128
-            out_ref[dest, GATES + start * tokens : GATES + (start + 1) * tokens, :] = ref[
+            out_ref[dest, start * tokens : (start + 1) * tokens, :] = ref[
                 :, at : at + 128
             ]
 
@@ -98,7 +99,7 @@
     laid(q_ref, lambda key_head: key_head, 3)
 
 
-def invert(systems):
+def invert(systems, meanwhile):
     size = systems[0].shape[0]
     blocks = size // SUB
     row, col = iota((size, size), 0), iota((size, size), 1)
@@ -141,9 +142,11 @@
         firsts = [
             mm_parts((rows_of(n[0]) * mask, rows_of(n[1]) * mask), t) for n, t in zip(lows, parts)
         ]
+        meanwhile()
         spreads = [tuple(woven(blank, x) for x in halves(first)) for first in firsts]
         odds = [(rows_of(t[0]), rows_of(t[1])) for t in parts]
         seconds = [halves(-mm_parts(o, spread)) for o, spread in zip(odds, spreads)]
+        meanwhile()
         parts = [
             tuple(woven(t[i], o[i] + second[i]) for i in range(2))
             for t, o, second in zip(parts, odds, seconds)
@@ -189,6 +192,7 @@
 def keys_kernel(
     recv_ref,
     ck_ref,
+    cv_ref,
     alog_ref,
     dt_ref,
     keys_ref,
@@ -198,6 +202,7 @@
     within_ref,
     cols_ref,
     early_ref,
+    values_ref,
     rows,
 ):
     sub = lax.axis_index("sub")
@@ -205,15 +210,14 @@
     peers = recv_ref.shape[0]
     tokens = (recv_ref.shape[1] - GATES) // 4
     spans = peers * tokens // SPAN
-    tap = key_tap(sub, ck_ref)
-    widened(rows, recv_ref, [GATES], tokens)
-    gates = jnp.concatenate(
-        [
-            sum(recv_ref[s, 0:GATES, :].astype(F32) for s in range(n, n + SPAN // tokens))
-            for n in range(0, peers, SPAN // tokens)
-        ],
-        axis=0,
-    )
+    taps = [key_tap(sub, ck_ref)] + value_taps(sub, cv_ref)
+    widened(rows, recv_ref, [0, tokens, 2 * tokens], tokens)
+    stacked = [
+        sum(recv_ref[s, 4 * tokens :, :].astype(F32) for s in range(n, n + SPAN // tokens))
+        for n in range(0, peers, SPAN // tokens)
+    ]
+    stacked.append(jnp.zeros((SPAN - spans * GATES, SPAN), F32))
+    gates = jnp.concatenate(stacked, axis=0)
     decay, rate = gate_values(gates, sub, alog_ref, dt_ref)
     early_ref[...] = jnp.where(iota((8, SPAN), 0) < 2, decay[0:8], rate[0:8])
     skipped = later & (iota(gates.shape, 0) < GATES) & (iota(gates.shape, 1) < EDGE)
@@ -236,7 +240,7 @@
     both = [(n, r) for n in range(spans) for r in range(2)]
     keys = []
     for n in range(spans):
-        k_n = unit(convolved(rows, n * SPAN + 8 - EDGE, SPAN, slice(0, DK), tap), 1.0)
+        k_n = unit(convolved(rows, n * SPAN + 8 - EDGE, SPAN, slice(0, DK), taps[0]), 1.0)
         keys_ref[n * SPAN : (n + 1) * SPAN, :] = k_n
         keys.append(k_n)
     keys_t = []
@@ -252,7 +256,18 @@
         within = jnp.exp(jnp.where(lower, gap, 0.0)) * here[at : at + 1, :]
         within_ref[r, n * SPAN : (n + 1) * SPAN, :] = jnp.where(lower, within, 0.0).astype(BF16)
         systems.append(jnp.where(strict, within * grams[n], 0.0))
-    inverses = invert(systems)
+    waiting = list(both)
+
+    def meanwhile():
+        for n, r in waiting[: 2 * spans // 6 + 1]:
+            lanes = slice((1 + r) * DV, (2 + r) * DV)
+            value = convolved(rows, n * SPAN + 8 - EDGE, SPAN, lanes, taps[1 + r])
+            values_ref[n * SPAN : (n + 1) * SPAN, r * DV : (r + 1) * DV] = value.astype(BF16)
+        del waiting[: 2 * spans // 6 + 1]
+
+    inverses = invert(systems, meanwhile)
+    while waiting:
+        meanwhile()
     for i, (n, r) in enumerate(both):
         t_ref[r, n] = jnp.concatenate(inverses[i], axis=1)
     scaled = []
@@ -280,18 +295,12 @@
     return dot(lin, jnp.concatenate([high, high], axis=0)) + dot(lin[:, :DK], low)
 
 
-def values_part(recv_ref, cv_ref, keys_t_ref, t_ref, cols_ref, rows, vs):
-    sub = lax.axis_index("sub")
-    tokens = (recv_ref.shape[1] - GATES) // 4
+def added(values_ref, keys_t_ref, t_ref, cols_ref):
     spans = t_ref.shape[1]
-    taps = value_taps(sub, cv_ref)
-    widened(rows, recv_ref, [GATES + tokens, GATES + 2 * tokens], tokens)
     both = [(n, r) for n in range(spans) for r in range(2)]
     values = []
     for n, r in both:
-        lanes = slice(r * DV, (r + 1) * DV)
-        v_n = convolved(rows, n * SPAN + 8 - EDGE, SPAN, lanes, taps[r]).astype(BF16)
-        vs[n * SPAN : (n + 1) * SPAN, lanes] = v_n
+        v_n = values_ref[n * SPAN : (n + 1) * SPAN, r * DV : (r + 1) * DV]
         values.append(jnp.concatenate([v_n, v_n], axis=0))
     solved = [dot(t_ref[r, n], v) for (n, r), v in zip(both, values)]
     weighed = []
@@ -306,7 +315,7 @@
 
 
 def opening_kernel(
-    recv_ref, cv_ref, keys_t_ref, t_ref, lin_ref, cols_ref, hop_ref, vs_ref, xs_ref, rows
+    recv_ref, values_ref, keys_t_ref, t_ref, lin_ref, cols_ref, hop_ref, xs_ref
 ):
     first = lax.axis_index("half") == 0
     peers = recv_ref.shape[0]
@@ -314,14 +323,14 @@
     spans = t_ref.shape[1]
     edges = []
     for which in (3, 0, 1, 2):
-        end = GATES + (which + 1) * tokens
+        end = (which + 1) * tokens
         edges.append(recv_ref[peers - 1, end - 16 : end, :].astype(F32)[16 - EDGE :])
     edges.append(jnp.zeros((16 - 4 * EDGE, 128), F32))
     hop_ref[2 * DK :, :] = jnp.concatenate(edges, axis=0).astype(BF16)
 
     @pl.when(first)
     def _():
-        adds = values_part(recv_ref, cv_ref, keys_t_ref, t_ref, cols_ref, rows, vs_ref)
+        adds = added(values_ref, keys_t_ref, t_ref, cols_ref)
         states = [adds[0], adds[1]]
         for n in range(1, spans):
             for r in range(2):
@@ -339,22 +348,19 @@
 def output_kernel(
     recv_ref,
     cq_ref,
-    cv_ref,
     keys_ref,
     keys_t_ref,
     t_ref,
     lin_ref,
     within_ref,
     cols_ref,
+    values_ref,
     hop_ref,
-    vs_ref,
     xs_ref,
     oa_ref,
     om_ref,
     last_ref,
-    rows,
     query_rows,
-    values,
     inner,
     readers,
     states_ref,
@@ -365,7 +371,7 @@
     spans = t_ref.shape[1]
     both = [(n, r) for n in range(spans) for r in range(2)]
     tap = key_tap(sub, cq_ref)
-    widened(query_rows, recv_ref, [GATES + 3 * tokens], tokens)
+    widened(query_rows, recv_ref, [3 * tokens], tokens)
 
     def span_rows(n):
         return slice(n * SPAN, (n + 1) * SPAN)
@@ -396,7 +402,7 @@
         rests, seen = [], []
         for n, r in both:
             lanes = slice(r * DV, (r + 1) * DV)
-            value = vs_ref[span_rows(n), lanes]
+            value = values_ref[span_rows(n), lanes]
             if n == 0:
                 rests.append(value)
                 seen.append(None)
@@ -414,7 +420,7 @@
 
     @pl.when(jnp.logical_not(first))
     def _():
-        adds = values_part(recv_ref, cv_ref, keys_t_ref, t_ref, cols_ref, rows, values)
+        adds = added(values_ref, keys_t_ref, t_ref, cols_ref)
         zero_half = jnp.zeros((DK, DV), F32)
         states = [
             jnp.concatenate(
@@ -437,7 +443,7 @@
         ]
         rests, seen = [], []
         for (n, r), read in zip(both, reads):
-            value = values[span_rows(n), r * DV : (r + 1) * DV].astype(F32)
+            value = values_ref[span_rows(n), r * DV : (r + 1) * DV].astype(F32)
             if n == 0:
                 known = growth(n, r) * readers[n].astype(F32)[:SPAN]
                 asked = growth(n, r) * readers[n].astype(F32)[SPAN:]
@@ -463,7 +469,7 @@
     edges = hop_ref[2 * DK :, :].astype(F32)
     for g, first in enumerate((3, 0, 1, 2)):
         lanes = slice(g * 128, (g + 1) * 128)
-        start = GATES + first * tokens
+        start = first * tokens
         rows[16 - EDGE : 16, lanes] = edges[EDGE * g : EDGE * (g + 1)]
         rows[16:32, lanes] = recv_ref[0, start : start + 16, :].astype(F32)
         results.append(convolved(rows, 16 - EDGE, 8, lanes, taps[g]))
@@ -612,7 +618,7 @@
         flops=1 << 20,
     )(*inputs)
     blocks = near(lax.all_to_all(packed, group, 0, 0, tiled=True))
-    keys, keys_t, inverses, lins, within, cols, early = call(
+    made = call(
         keys_kernel,
         (
             pltpu.VMEM((total, DK), BF16),
@@ -620,29 +626,26 @@
             pltpu.VMEM((2, spans, SPAN, 2 * SPAN), BF16),
             pltpu.VMEM((2, spans, DK, 2 * DK), BF16),
             pltpu.VMEM((2, total, SPAN), BF16),
-            pltpu.VMEM((SPAN, spans * GATES), F32),
+            pltpu.VMEM((SPAN, SPAN), F32),
             pltpu.VMEM((8, SPAN), F32),
+            pltpu.VMEM((total, 2 * DV), BF16),
         ),
-        [VMEM, VMEM, SMEM, SMEM],
-        [pltpu.VMEM((8 + total, DK), F32)],
+        [VMEM, VMEM, VMEM, SMEM, SMEM],
+        [pltpu.VMEM((8 + total, DK + 2 * DV), F32)],
         flops=1 << 32,
-    )(blocks, conv_k, a_log, dt_bias)
-    keys, keys_t, inverses, lins, within, cols, early = (
-        near(x) for x in (keys, keys_t, inverses, lins, within, cols, early)
-    )
-    hop, values, starts = call(
+    )(blocks, conv_k, conv_v, a_log, dt_bias)
+    keys, keys_t, inverses, lins, within, cols, early, values = (near(x) for x in made)
+    hop, starts = call(
         opening_kernel,
         (
             pltpu.VMEM((2 * DK + 16, 128), BF16),
-            pltpu.VMEM((total, 2 * DV), BF16),
             pltpu.VMEM((spans, 2 * DK, 2 * DV), BF16),
         ),
         [VMEM] * 6,
-        [pltpu.VMEM((8 + total, 2 * DV), F32)],
         flops=1 << 32,
-    )(blocks, conv_v, keys_t, inverses, lins, cols)
+    )(blocks, values, keys_t, inverses, lins, cols)
     entering = near(lax.ppermute(hop, "half", route))
-    hop, values, starts = near(hop), near(values), near(starts)
+    hop, starts = near(hop), near(starts)
     out_a, out_m, last = call(
         output_kernel,
         (
@@ -650,30 +653,15 @@
             pltpu.VMEM((2, total, DV), BF16),
             pltpu.VMEM((2, DK, 2 * DV), F32),
         ),
-        [VMEM] * 12,
+        [VMEM] * 11,
         [
-            pltpu.VMEM((8 + total, 2 * DV), F32),
             pltpu.VMEM((8 + total, DK), F32),
-            pltpu.VMEM((total, 2 * DV), BF16),
             pltpu.VMEM((2, spans, SPAN, SPAN), BF16),
             pltpu.VMEM((spans, 2 * SPAN, DK), BF16),
             pltpu.VMEM((2, spans, 2 * DK, 2 * DV), BF16),
         ],
         flops=1 << 32,
-    )(
-        blocks,
-        conv_q,
-        conv_v,
-        keys,
-        keys_t,
-        inverses,
-        lins,
-        within,
-        cols,
-        hop,
-        values,
-        starts,
-    )
+    )(blocks, conv_q, keys, keys_t, inverses, lins, within, cols, values, hop, starts)
     for _ in range(shards - 2):
         moved = call(
             advance_kernel,

time: 51.9 us -> 53 us (1.021)
  starting transfers between devices: 1.61 us -> 2.67 us
    pallas_call x1, Pallas kernels: 5.47 us -> 6.74 us  [local(): call(keys_kernel, (pltpu.VMEM((total, DK), BF16), pltpu.VMEM((spans, DK,...]
    ppermute x1, starting transfers between devices: 1.61 us -> 2.67 us  [local(): entering = near(lax.ppermute(hop, 'half', route))]
    pallas_call x1, Pallas kernels: 2.91 us -> 1.86 us  [local(): call(opening_kernel, (pltpu.VMEM((2 * DK + 16, 128), BF16), pltpu.VMEM((s...]
where the time goes in v8:
time: 53 us; the launch traced here: 52.7 us
  blocking collectives  36.4 us (69%)
  Pallas kernels  13.4 us (25%)
  starting transfers between devices  2.67 us (5%)
    all_to_all x1, blocking collectives, local(): blocks = near(lax.all_to_all(packed, group, 0, 0, tiled=True))  22.7 us
    all_to_all x1, blocking collectives, local(): returned = near(lax.all_to_all(normed, group, 0, 0, tiled=True))  13.6 us
    pallas_call x1, Pallas kernels, local(): call(keys_kernel, (pltpu.VMEM((total, DK), BF16), pltpu.VMEM((spans, DK,...  6.74 us
    ppermute x1, starting transfers between devices, local(): entering = near(lax.ppermute(hop, 'half', route))  2.67 us
    pallas_call x1, Pallas kernels, local(): call(output_kernel, (pltpu.VMEM((2, total, DV), F32), pltpu.VMEM((2, tota...  2.12 us
    pallas_call x1, Pallas kernels, local(): call(opening_kernel, (pltpu.VMEM((2 * DK + 16, 128), BF16), pltpu.VMEM((s...  1.86 us
    pallas_call x1, Pallas kernels, local(): call(functools.partial(pack_kernel, heads_axis), pltpu.VMEM((peers, GATES...  1.34 us
  transfers between devices with their start and end apart: 1, of which 0 were waited for; matrix products, arithmetic and copies ran while one was open for 0% of the time, Pallas kernels for 4%

profile of v8, /device:TPU:0, one launch (start us, length us, event | category | flops | bytes accessed | tf_op | source)
XLA Modules:
  0.0 52.7 jit_solution(2839603858329134718)
XLA Ops:
  0.0 1.3 %shard_map.118 = bf16[16,264,128]{2,1,0:T(8,128)(2,1)S(1)} custom-call(bf16[64,2048]{1,0:T(8,128)(2,1)} %q_in.1, bf16[64,2048]{1,0:T(8,128)(2,1)} %k_in.1, bf16[64,4096]{1,0:T(8,128)(2,1)} %v_in.1, bf16[32,64]{1,0:T(8,128)(2,1)} %bitcast.4, bf16[32,64]{1,0:T(8,128)(2,1)} %bitcast.5), custom_call_target="tpu_custom_call" | custom-call | flops 1048576 | bytes 2097152 | tf_op jit(solution)/shard_map/pallas_call | solution.py:613
  1.3 0.0 copy-start.1
  1.4 0.0 copy-start.2
  1.4 0.0 copy-start.5
  1.4 0.0 copy-start.6
  1.4 22.7 %all_to_all.10.recv_ref = bf16[16,264,128]{2,1,0:T(8,128)(2,1)S(1)} all-to-all(bf16[16,264,128]{2,1,0:T(8,128)(2,1)S(1)} %shard_map.118), channel_id=1, replica_groups=mesh['half'=2,'sub'=4,'head'=4] {'sub','head'}, dimensions={0} | all-to-all | bytes 2162688 | tf_op jit(solution)/shard_map/all_to_all | solution.py:620
  24.1 0.0 copy-done.1
  24.1 0.0 copy-done.2
  24.1 0.0 copy-done.5
  24.1 0.0 copy-done.6
  24.2 6.7 %shard_map.119 = (bf16[1024,128]{1,0:T(8,128)(2,1)S(1)}, bf16[8,128,128]{2,1,0:T(8,128)(2,1)S(1)}, bf16[2,8,128,256]{3,2,1,0:T(8,128)(2,1)S(1)}, bf16[2,8,128,25...) custom-call(bf16[16,264,128]{2,1,0:T(8,128)(2,1)S(1)} %all_to_all.10, ...), custom_call_target="tpu_custom_call" | custom-call | flops 4294967296 | bytes 2097152 | tf_op jit(solution)/shard_map/pallas_call | solution.py:621
  30.9 0.0 copy-start.3
  30.9 1.9 %shard_map.120 = (bf16[272,128]{1,0:T(8,128)(2,1)S(1)}, bf16[8,256,256]{2,1,0:T(8,128)(2,1)S(1)}) custom-call(bf16[16,264,128]{2,1,0:T(8,128)(2,1)S(1)} %all_to_all.10.recv_ref, bf16[1024,256]{1,0:T(8,128)(2,1)S(1)} %get-tuple-element.17.values_ref, bf16[8,128,128]{2,1,0:T(8,128)(2,1)S(1)} %get-tuple-element.18.keys_t_ref, ...), custom_call_target="tpu_custom_call" | custom-call | flops 4294967296 | bytes 2097152 | tf_op jit(solution)/shard_map/pallas_call | solution.py:638
  32.8 2.7 %collective-permute-start = (bf16[272,128]{1,0:T(8,128)(2,1)S(1)}, bf16[272,128]{1,0:T(8,128)(2,1)S(1)}, u32[]{:S(2)}, u32[]{:S(2)}) collective-permute-start(bf16[272,128]{1,0:T(8,128)(2,1)S(1)} %get-tuple-element.22.hop_ref), channel_id=1, source_target_pairs={{0,16},{1,17},{2,18},{3,19},{4,20},{5,21},{6,22},{7,23},{8,24},{9,... | collective-permute-start | bytes 208904 | tf_op jit(solution)/shard_map/ppermute | solution.py:647
  35.5 0.0 copy-done.3
  35.5 0.0 copy-start.4
  35.5 2.1 %shard_map.121 = (f32[2,1024,128]{2,1,0:T(8,128)S(1)}, bf16[2,1024,128]{2,1,0:T(8,128)(2,1)S(1)}, f32[2,128,256]{2,1,0:T(8,128)}) custom-call(bf16[16,264,128]{2,1,0:T(8,128)(2,1)S(1)} %all_to_all.10.recv_ref, f32[4,512]{1,0:T(4,128)S(1)} %copy-done.3, bf16[1024,128]{1,0:T(8,128)(2,1)S(1)} %get-tuple-element.24.keys_ref, ...), custom_call_target="tpu_custom_call" | custom-call | flops 4294967296 | bytes 2097152 | tf_op jit(solution)/shard_map/pallas_call | solution.py:649
  37.6 0.0 collective-permute-done.hop_ref
  37.6 0.0 copy-done.4
  37.6 0.4 shard_map.122
  38.0 0.0 copy-start
  38.0 13.6 %all_to_all.11.normed_ref = bf16[16,64,256]{2,1,0:T(8,128)(2,1)S(1)} all-to-all(bf16[16,64,256]{2,1,0:T(8,128)(2,1)S(1)} %shard_map.122), channel_id=1, replica_groups=mesh['half'=2,'sub'=4,'head'=4] {'sub','head'}, dimensions={0} | all-to-all | bytes 1048576 | tf_op jit(solution)/shard_map/all_to_all | solution.py:689
  51.6 0.0 copy-done
  51.6 0.9 %shard_map.123 = bf16[64,4096]{1,0:T(8,128)(2,1)} custom-call(bf16[16,64,256]{2,1,0:T(8,128)(2,1)S(1)} %all_to_all.11.normed_ref, bf16[64,4096]{1,0:T(8,128)(2,1)S(1)} %copy-done), custom_call_target="tpu_custom_call" | custom-call | flops 67108864 | bytes 2097152 | tf_op jit(solution)/shard_map/pallas_call | solution.py:690
Async XLA Ops:
  1.3 22.8 %copy-start.1 = (f32[4,1024]{1,0:T(4,128)S(1)}, f32[4,1024]{1,0:T(4,128)}, u32[]{:S(2)}) copy-start(f32[4,1024]{1,0:T(4,128)} %cv_ref.3) | copy-start | bytes 49156
  1.4 22.8 %copy-start.2 = (f32[4,512]{1,0:T(4,128)S(1)}, f32[4,512]{1,0:T(4,128)}, u32[]{:S(2)}) copy-start(f32[4,512]{1,0:T(4,128)} %ck_ref.3) | copy-start | bytes 24580
  1.4 22.8 %copy-start.5 = (f32[8]{0:T(128)S(1)}, f32[8]{0:T(128)}, u32[]{:S(2)}) copy-start(f32[8]{0:T(128)} %alog_ref.1) | copy-start | bytes 100
  1.4 22.8 %copy-start.6 = (f32[8]{0:T(128)S(1)}, f32[8]{0:T(128)}, u32[]{:S(2)}) copy-start(f32[8]{0:T(128)} %dt_ref.1) | copy-start | bytes 100
  30.9 4.6 %copy-start.3 = (f32[4,512]{1,0:T(4,128)S(1)}, f32[4,512]{1,0:T(4,128)}, u32[]{:S(2)}) copy-start(f32[4,512]{1,0:T(4,128)} %cq_ref.3) | copy-start | bytes 24580
  32.8 4.8 %collective-permute-start = (bf16[272,128]{1,0:T(8,128)(2,1)S(1)}, bf16[272,128]{1,0:T(8,128)(2,1)S(1)}, u32[]{:S(2)}, u32[]{:S(2)}) collective-permute-start(bf16[272,128]{1,0:T(8,128)(2,1)S(1)} %get-tuple-element.22.hop_ref), channel_id=1, source_target_pairs={{0,16},{1,17},{2,18},{3,19},{4,20},{5,21},{6,22},{7,23},{8,24},{9,... | collective-permute-start | bytes 208904 | tf_op jit(solution)/shard_map/ppermute | solution.py:647
  35.5 2.1 %copy-start.4 = (f32[128]{0:T(128)S(1)}, f32[128]{0:T(128)}, u32[]{:S(2)}) copy-start(f32[128]{0:T(128)} %param.23) | copy-start | bytes 1540
  38.0 13.6 %copy-start = (bf16[64,4096]{1,0:T(8,128)(2,1)S(1)}, bf16[64,4096]{1,0:T(8,128)(2,1)}, u32[]{:S(2)}) copy-start(bf16[64,4096]{1,0:T(8,128)(2,1)} %z_ref.1) | copy-start | bytes 1572868

commit v9 on v7

--- a/solution.py
+++ b/solution.py
@@ -18,7 +18,7 @@
 F32 = jnp.float32
 BF16 = jnp.bfloat16
 VMEM_BYTES = 24 * 1024 * 1024
-GATES = 16
+GATES = 8
 
 
 def dot(a, b, dims=((1,), (0,))):
@@ -28,10 +28,6 @@
 def halves(x):
     high = x.astype(BF16)
     return high, (x - high.astype(F32)).astype(BF16)
-
-
-def mm_right(a, b):
-    return dot(jnp.concatenate([a, a], axis=1), jnp.concatenate(halves(b), axis=0))
 
 
 def mm_parts(a, b):
@@ -80,12 +76,12 @@
     ).astype(BF16)
     gates = dot(picked, place).astype(BF16)
     for dest in range(peers):
-        out_ref[dest, 0:GATES, :] = gates[GATES * dest : GATES * (dest + 1), :]
+        out_ref[dest, 4 * tokens :, :] = gates[GATES * dest : GATES * (dest + 1), :]
 
     def laid(ref, lane, start):
         for dest, key_head in enumerate(key_heads):
             at = lane(key_head) * 128
-            out_ref[dest, GATES + start * tokens : GATES + (start + 1) * tokens, :] = ref[
+            out_ref[dest, start * tokens : (start + 1) * tokens, :] = ref[
                 :, at : at + 128
             ]
 
@@ -195,6 +191,7 @@
     keys_t_ref,
     t_ref,
     lin_ref,
+    ends_ref,
     within_ref,
     cols_ref,
     early_ref,
@@ -206,14 +203,13 @@
     tokens = (recv_ref.shape[1] - GATES) // 4
     spans = peers * tokens // SPAN
     tap = key_tap(sub, ck_ref)
-    widened(rows, recv_ref, [GATES], tokens)
-    gates = jnp.concatenate(
-        [
-            sum(recv_ref[s, 0:GATES, :].astype(F32) for s in range(n, n + SPAN // tokens))
-            for n in range(0, peers, SPAN // tokens)
-        ],
-        axis=0,
-    )
+    widened(rows, recv_ref, [0], tokens)
+    stacked = [
+        sum(recv_ref[s, 4 * tokens :, :].astype(F32) for s in range(n, n + SPAN // tokens))
+        for n in range(0, peers, SPAN // tokens)
+    ]
+    stacked.append(jnp.zeros((SPAN - spans * GATES, SPAN), F32))
+    gates = jnp.concatenate(stacked, axis=0)
     decay, rate = gate_values(gates, sub, alog_ref, dt_ref)
     early_ref[...] = jnp.where(iota((8, SPAN), 0) < 2, decay[0:8], rate[0:8])
     skipped = later & (iota(gates.shape, 0) < GATES) & (iota(gates.shape, 1) < EDGE)
@@ -258,26 +254,24 @@
     scaled = []
     for n, r in both:
         at = GATES * n + r
-        scaled.append(halves(columns[:, at + 2 : at + 3] * keys[n].astype(F32)))
-    w_mats = [mm_parts(t, x) for t, x in zip(inverses, scaled)]
+        right = (columns[:, at + 2 : at + 3] * keys[n].astype(F32)).astype(BF16)
+        scaled.append(jnp.concatenate([right, right], axis=0))
+    w_mats = [dot(jnp.concatenate(t, axis=1), x) for t, x in zip(inverses, scaled)]
     weighed = []
     for (n, r), w_mat in zip(both, w_mats):
         at = GATES * n + r
-        weighed.append(columns[:, at + 4 : at + 5] * w_mat)
+        weighed.append((columns[:, at + 4 : at + 5] * w_mat).astype(BF16))
     moved = [
-        mm_right(keys_t[n], jnp.concatenate(weighed[2 * n : 2 * n + 2], axis=1))
-        for n in range(spans)
+        dot(keys_t[n], jnp.concatenate(weighed[2 * n : 2 * n + 2], axis=1)) for n in range(spans)
     ]
-    identity = jnp.where(lane_r == lane_c, 1.0, 0.0)
+    ends_ref[...] = jnp.broadcast_to(growth[:, SPAN - 1 :], ends_ref.shape)
     for n, r in both:
-        at = GATES * n + r
-        lin = growth[at : at + 1, SPAN - 1 :] * identity - moved[n][:, r * DK : (r + 1) * DK]
-        lin_ref[r, n] = jnp.concatenate(halves(lin), axis=1)
-
-
-def step(lin, parts):
-    high, low = parts
-    return dot(lin, jnp.concatenate([high, high], axis=0)) + dot(lin[:, :DK], low)
+        lin_ref[r, n] = moved[n][:, r * DK : (r + 1) * DK].astype(BF16)
+
+
+def step(end, moved, state, parts):
+    both = jnp.concatenate([moved, moved], axis=1)
+    return end * state - dot(both, jnp.concatenate(parts, axis=0))
 
 
 def values_part(recv_ref, cv_ref, keys_t_ref, t_ref, cols_ref, rows, vs):
@@ -285,7 +279,7 @@
     tokens = (recv_ref.shape[1] - GATES) // 4
     spans = t_ref.shape[1]
     taps = value_taps(sub, cv_ref)
-    widened(rows, recv_ref, [GATES + tokens, GATES + 2 * tokens], tokens)
+    widened(rows, recv_ref, [tokens, 2 * tokens], tokens)
     both = [(n, r) for n in range(spans) for r in range(2)]
     values = []
     for n, r in both:
@@ -297,16 +291,16 @@
     weighed = []
     for (n, r), u_mat in zip(both, solved):
         at = GATES * n + r
-        weighed.append(cols_ref[:, at + 4 : at + 5] * u_mat)
+        weighed.append((cols_ref[:, at + 4 : at + 5] * u_mat).astype(BF16))
     moved = [
-        mm_right(keys_t_ref[n], jnp.concatenate(weighed[2 * n : 2 * n + 2], axis=1))
+        dot(keys_t_ref[n], jnp.concatenate(weighed[2 * n : 2 * n + 2], axis=1))
         for n in range(spans)
     ]
     return [moved[n][:, r * DV : (r + 1) * DV] for n, r in both]
 
 
 def opening_kernel(
-    recv_ref, cv_ref, keys_t_ref, t_ref, lin_ref, cols_ref, hop_ref, vs_ref, xs_ref, rows
+    recv_ref, cv_ref, keys_t_ref, t_ref, lin_ref, ends_ref, cols_ref, hop_ref, vs_ref, xs_ref, rows
 ):
     first = lax.axis_index("half") == 0
     peers = recv_ref.shape[0]
@@ -314,7 +308,7 @@
     spans = t_ref.shape[1]
     edges = []
     for which in (3, 0, 1, 2):
-        end = GATES + (which + 1) * tokens
+        end = (which + 1) * tokens
         edges.append(recv_ref[peers - 1, end - 16 : end, :].astype(F32)[16 - EDGE :])
     edges.append(jnp.zeros((16 - 4 * EDGE, 128), F32))
     hop_ref[2 * DK :, :] = jnp.concatenate(edges, axis=0).astype(BF16)
@@ -327,7 +321,8 @@
             for r in range(2):
                 parts = halves(states[r])
                 xs_ref[n, :, r * DV : (r + 1) * DV] = jnp.concatenate(parts, axis=0)
-                states[r] = step(lin_ref[r, n], parts) + adds[2 * n + r]
+                end = ends_ref[GATES * n + r : GATES * n + r + 1, :]
+                states[r] = step(end, lin_ref[r, n], states[r], parts) + adds[2 * n + r]
         for r in range(2):
             hop_ref[r * DK : (r + 1) * DK, :] = states[r].astype(BF16)
 
@@ -344,6 +339,7 @@
     keys_t_ref,
     t_ref,
     lin_ref,
+    ends_ref,
     within_ref,
     cols_ref,
     hop_ref,
@@ -365,7 +361,7 @@
     spans = t_ref.shape[1]
     both = [(n, r) for n in range(spans) for r in range(2)]
     tap = key_tap(sub, cq_ref)
-    widened(query_rows, recv_ref, [GATES + 3 * tokens], tokens)
+    widened(query_rows, recv_ref, [3 * tokens], tokens)
 
     def span_rows(n):
         return slice(n * SPAN, (n + 1) * SPAN)
@@ -416,10 +412,10 @@
     def _():
         adds = values_part(recv_ref, cv_ref, keys_t_ref, t_ref, cols_ref, rows, values)
         zero_half = jnp.zeros((DK, DV), F32)
+        identity = jnp.where(iota((DK, DK), 0) == iota((DK, DK), 1), 1.0, 0.0)
         states = [
             jnp.concatenate(
-                [adds[r], lin_ref[r, 0, :, :DK].astype(F32) + lin_ref[r, 0, :, DK:].astype(F32)],
-                axis=1,
+                [adds[r], ends_ref[r : r + 1, :] * identity - lin_ref[r, 0].astype(F32)], axis=1
             )
             for r in range(2)
         ]
@@ -428,7 +424,9 @@
                 parts = halves(states[r])
                 states_ref[r, n] = jnp.concatenate(parts, axis=0)
                 add = jnp.concatenate([adds[2 * n + r], zero_half], axis=1)
-                states[r] = step(lin_ref[r, n], parts) + add
+                end = ends_ref[GATES * n + r : GATES * n + r + 1, :]
+                end = jnp.concatenate([end, end], axis=1)
+                states[r] = step(end, lin_ref[r, n], states[r], parts) + add
         for r in range(2):
             last_ref[r] = states[r]
         prepare()
@@ -463,7 +461,7 @@
     edges = hop_ref[2 * DK :, :].astype(F32)
     for g, first in enumerate((3, 0, 1, 2)):
         lanes = slice(g * 128, (g + 1) * 128)
-        start = GATES + first * tokens
+        start = first * tokens
         rows[16 - EDGE : 16, lanes] = edges[EDGE * g : EDGE * (g + 1)]
         rows[16:32, lanes] = recv_ref[0, start : start + 16, :].astype(F32)
         results.append(convolved(rows, 16 - EDGE, 8, lanes, taps[g]))
@@ -612,23 +610,24 @@
         flops=1 << 20,
     )(*inputs)
     blocks = near(lax.all_to_all(packed, group, 0, 0, tiled=True))
-    keys, keys_t, inverses, lins, within, cols, early = call(
+    keys, keys_t, inverses, lins, ends, within, cols, early = call(
         keys_kernel,
         (
             pltpu.VMEM((total, DK), BF16),
             pltpu.VMEM((spans, DK, SPAN), BF16),
             pltpu.VMEM((2, spans, SPAN, 2 * SPAN), BF16),
-            pltpu.VMEM((2, spans, DK, 2 * DK), BF16),
+            pltpu.VMEM((2, spans, DK, DK), BF16),
+            pltpu.VMEM((SPAN, DK), F32),
             pltpu.VMEM((2, total, SPAN), BF16),
-            pltpu.VMEM((SPAN, spans * GATES), F32),
+            pltpu.VMEM((SPAN, SPAN), F32),
             pltpu.VMEM((8, SPAN), F32),
         ),
         [VMEM, VMEM, SMEM, SMEM],
         [pltpu.VMEM((8 + total, DK), F32)],
         flops=1 << 32,
     )(blocks, conv_k, a_log, dt_bias)
-    keys, keys_t, inverses, lins, within, cols, early = (
-        near(x) for x in (keys, keys_t, inverses, lins, within, cols, early)
+    keys, keys_t, inverses, lins, ends, within, cols, early = (
+        near(x) for x in (keys, keys_t, inverses, lins, ends, within, cols, early)
     )
     hop, values, starts = call(
         opening_kernel,
@@ -637,10 +636,10 @@
             pltpu.VMEM((total, 2 * DV), BF16),
             pltpu.VMEM((spans, 2 * DK, 2 * DV), BF16),
         ),
-        [VMEM] * 6,
+        [VMEM] * 7,
         [pltpu.VMEM((8 + total, 2 * DV), F32)],
         flops=1 << 32,
-    )(blocks, conv_v, keys_t, inverses, lins, cols)
+    )(blocks, conv_v, keys_t, inverses, lins, ends, cols)
     entering = near(lax.ppermute(hop, "half", route))
     hop, values, starts = near(hop), near(values), near(starts)
     out_a, out_m, last = call(
@@ -650,7 +649,7 @@
             pltpu.VMEM((2, total, DV), BF16),
             pltpu.VMEM((2, DK, 2 * DV), F32),
         ),
-        [VMEM] * 12,
+        [VMEM] * 13,
         [
             pltpu.VMEM((8 + total, 2 * DV), F32),
             pltpu.VMEM((8 + total, DK), F32),
@@ -668,6 +667,7 @@
         keys_t,
         inverses,
         lins,
+        ends,
         within,
         cols,
         hop,

time: 51.9 us -> 51.3 us (0.988)
  Pallas kernels: 13.2 us -> 12.6 us
where the time goes in v9:
time: 51.3 us; the launch traced here: 51 us
  blocking collectives  36.5 us (71%)
  Pallas kernels  12.6 us (25%)
  starting transfers between devices  1.73 us (3%)
    all_to_all x1, blocking collectives, local(): blocks = near(lax.all_to_all(packed, group, 0, 0, tiled=True))  22.7 us
    all_to_all x1, blocking collectives, local(): returned = near(lax.all_to_all(normed, group, 0, 0, tiled=True))  13.8 us
    pallas_call x1, Pallas kernels, local(): call(keys_kernel, (pltpu.VMEM((total, DK), BF16), pltpu.VMEM((spans, DK,...  5.24 us
    pallas_call x1, Pallas kernels, local(): call(opening_kernel, (pltpu.VMEM((2 * DK + 16, 128), BF16), pltpu.VMEM((t...  2.8 us
    pallas_call x1, Pallas kernels, local(): call(output_kernel, (pltpu.VMEM((2, total, DV), F32), pltpu.VMEM((2, tota...  1.96 us
    ppermute x1, starting transfers between devices, local(): entering = near(lax.ppermute(hop, 'half', route))  1.73 us
    pallas_call x1, Pallas kernels, local(): call(functools.partial(pack_kernel, heads_axis), pltpu.VMEM((peers, GATES...  1.34 us
  transfers between devices with their start and end apart: 1, of which 0 were waited for; matrix products, arithmetic and copies ran while one was open for 0% of the time, Pallas kernels for 4%

profile of v9, /device:TPU:0, one launch (start us, length us, event | category | flops | bytes accessed | tf_op | source)
XLA Modules:
  0.0 51.0 jit_solution(1610519094450281423)
XLA Ops:
  0.0 1.3 %shard_map.118 = bf16[16,264,128]{2,1,0:T(8,128)(2,1)S(1)} custom-call(bf16[64,2048]{1,0:T(8,128)(2,1)} %q_in.1, bf16[64,2048]{1,0:T(8,128)(2,1)} %k_in.1, bf16[64,4096]{1,0:T(8,128)(2,1)} %v_in.1, bf16[32,64]{1,0:T(8,128)(2,1)} %bitcast.4, bf16[32,64]{1,0:T(8,128)(2,1)} %bitcast.5), custom_call_target="tpu_custom_call" | custom-call | flops 1048576 | bytes 2097152 | tf_op jit(solution)/shard_map/pallas_call | solution.py:605
  1.3 0.0 copy-start.2
  1.4 0.0 copy-start.5
  1.4 0.0 copy-start.6
  1.4 22.7 %all_to_all.10.recv_ref = bf16[16,264,128]{2,1,0:T(8,128)(2,1)S(1)} all-to-all(bf16[16,264,128]{2,1,0:T(8,128)(2,1)S(1)} %shard_map.118), channel_id=1, replica_groups=mesh['half'=2,'sub'=4,'head'=4] {'sub','head'}, dimensions={0} | all-to-all | bytes 2162688 | tf_op jit(solution)/shard_map/all_to_all | solution.py:612
  24.1 0.0 copy-done.2
  24.1 0.0 copy-done.5
  24.1 0.0 copy-done.6
  24.1 0.0 copy-start.1
  24.1 5.2 %shard_map.119 = (bf16[1024,128]{1,0:T(8,128)(2,1)S(1)}, bf16[8,128,128]{2,1,0:T(8,128)(2,1)S(1)}, bf16[2,8,128,256]{3,2,1,0:T(8,128)(2,1)S(1)}, bf16[2,8,128,12...) custom-call(bf16[16,264,128]{2,1,0:T(8,128)(2,1)S(1)} %all_to_all.10, ...), custom_call_target="tpu_custom_call" | custom-call | flops 4294967296 | bytes 2097152 | tf_op jit(solution)/shard_map/pallas_call | solution.py:613
  29.4 0.0 copy-done.1
  29.4 0.0 copy-start.3
  29.4 2.8 %shard_map.120 = (bf16[272,128]{1,0:T(8,128)(2,1)S(1)}, bf16[1024,256]{1,0:T(8,128)(2,1)S(1)}, bf16[8,256,256]{2,1,0:T(8,128)(2,1)S(1)}) custom-call(bf16[16,264,128]{2,1,0:T(8,128)(2,1)S(1)} %all_to_all.10.recv_ref, f32[4,1024]{1,0:T(4,128)S(1)} %copy-done.1, bf16[8,128,128]{2,1,0:T(8,128)(2,1)S(1)} %get-tuple-element.18.keys_t_ref, ...), custom_call_target="tpu_custom_call" | custom-call | flops 4294967296 | bytes 2097152 | tf_op jit(solution)/shard_map/pallas_call | solution.py:632
  32.2 1.7 %collective-permute-start = (bf16[272,128]{1,0:T(8,128)(2,1)S(1)}, bf16[272,128]{1,0:T(8,128)(2,1)S(1)}, u32[]{:S(2)}, u32[]{:S(2)}) collective-permute-start(bf16[272,128]{1,0:T(8,128)(2,1)S(1)} %get-tuple-element.23.hop_ref), channel_id=1, source_target_pairs={{0,16},{1,17},{2,18},{3,19},{4,20},{5,21},{6,22},{7,23},{8,24},{9,... | collective-permute-start | bytes 208904 | tf_op jit(solution)/shard_map/ppermute | solution.py:643
  33.9 0.0 copy-done.3
  34.0 0.0 copy-start.4
  34.0 2.0 %shard_map.121 = (f32[2,1024,128]{2,1,0:T(8,128)S(1)}, bf16[2,1024,128]{2,1,0:T(8,128)(2,1)S(1)}, f32[2,128,256]{2,1,0:T(8,128)}) custom-call(bf16[16,264,128]{2,1,0:T(8,128)(2,1)S(1)} %all_to_all.10.recv_ref, f32[4,512]{1,0:T(4,128)S(1)} %copy-done.3, f32[4,1024]{1,0:T(4,128)S(1)} %copy-done.1, bf16[1024,128]{1,0:T(8,128)(2,1)S(1)} %get-tuple-element.25.keys_ref, ...), custom_call_target="tpu_custom_call" | custom-call | flops 4294967296 | bytes 2097152 | tf_op jit(solution)/shard_map/pallas_call | solution.py:645
  35.9 0.0 collective-permute-done.hop_ref
  35.9 0.0 copy-done.4
  35.9 0.4 shard_map.122
  36.3 0.0 copy-start
  36.3 13.8 %all_to_all.11.normed_ref = bf16[16,64,256]{2,1,0:T(8,128)(2,1)S(1)} all-to-all(bf16[16,64,256]{2,1,0:T(8,128)(2,1)S(1)} %shard_map.122), channel_id=1, replica_groups=mesh['half'=2,'sub'=4,'head'=4] {'sub','head'}, dimensions={0} | all-to-all | bytes 1048576 | tf_op jit(solution)/shard_map/all_to_all | solution.py:701
  50.1 0.0 copy-done
  50.1 0.9 %shard_map.123 = bf16[64,4096]{1,0:T(8,128)(2,1)} custom-call(bf16[16,64,256]{2,1,0:T(8,128)(2,1)S(1)} %all_to_all.11.normed_ref, bf16[64,4096]{1,0:T(8,128)(2,1)S(1)} %copy-done), custom_call_target="tpu_custom_call" | custom-call | flops 67108864 | bytes 2097152 | tf_op jit(solution)/shard_map/pallas_call | solution.py:702
Async XLA Ops:
  1.3 22.8 %copy-start.2 = (f32[4,512]{1,0:T(4,128)S(1)}, f32[4,512]{1,0:T(4,128)}, u32[]{:S(2)}) copy-start(f32[4,512]{1,0:T(4,128)} %ck_ref.3) | copy-start | bytes 24580
  1.4 22.8 %copy-start.5 = (f32[8]{0:T(128)S(1)}, f32[8]{0:T(128)}, u32[]{:S(2)}) copy-start(f32[8]{0:T(128)} %alog_ref.1) | copy-start | bytes 100
  1.4 22.8 %copy-start.6 = (f32[8]{0:T(128)S(1)}, f32[8]{0:T(128)}, u32[]{:S(2)}) copy-start(f32[8]{0:T(128)} %dt_ref.1) | copy-start | bytes 100
  24.1 5.3 %copy-start.1 = (f32[4,1024]{1,0:T(4,128)S(1)}, f32[4,1024]{1,0:T(4,128)}, u32[]{:S(2)}) copy-start(f32[4,1024]{1,0:T(4,128)} %cv_ref.5) | copy-start | bytes 49156
  29.4 4.6 %copy-start.3 = (f32[4,512]{1,0:T(4,128)S(1)}, f32[4,512]{1,0:T(4,128)}, u32[]{:S(2)}) copy-start(f32[4,512]{1,0:T(4,128)} %cq_ref.3) | copy-start | bytes 24580
  32.2 3.7 %collective-permute-start = (bf16[272,128]{1,0:T(8,128)(2,1)S(1)}, bf16[272,128]{1,0:T(8,128)(2,1)S(1)}, u32[]{:S(2)}, u32[]{:S(2)}) collective-permute-start(bf16[272,128]{1,0:T(8,128)(2,1)S(1)} %get-tuple-element.23.hop_ref), channel_id=1, source_target_pairs={{0,16},{1,17},{2,18},{3,19},{4,20},{5,21},{6,22},{7,23},{8,24},{9,... | collective-permute-start | bytes 208904 | tf_op jit(solution)/shard_map/ppermute | solution.py:643
  34.0 2.0 %copy-start.4 = (f32[128]{0:T(128)S(1)}, f32[128]{0:T(128)}, u32[]{:S(2)}) copy-start(f32[128]{0:T(128)} %param.23) | copy-start | bytes 1540
  36.3 13.8 %copy-start = (bf16[64,4096]{1,0:T(8,128)(2,1)S(1)}, bf16[64,4096]{1,0:T(8,128)(2,1)}, u32[]{:S(2)}) copy-start(bf16[64,4096]{1,0:T(8,128)(2,1)} %z_ref.1) | copy-start | bytes 1572868

commit v10 on v9

--- a/solution.py
+++ b/solution.py
@@ -47,6 +47,14 @@
 
 def iota(shape, dim):
     return lax.broadcasted_iota(jnp.int32, shape, dim)
+
+
+def block_of(x, size):
+    return lax.shift_right_logical(x, jnp.full(x.shape, size.bit_length() - 1, jnp.int32))
+
+
+def place_in(x, size):
+    return x & (size - 1)
 
 
 def pack_kernel(
@@ -63,8 +71,8 @@
         copy.wait()
     value_heads = at_ref.shape[0]
     row, entry = iota((peers * GATES, value_heads), 0), iota((peers * GATES, value_heads), 1)
-    dest, which = row // GATES, row % GATES
-    first = 2 * ((dest % heads_axis) * subs + dest // heads_axis)
+    dest, which = block_of(row, GATES), place_in(row, GATES)
+    first = 2 * (place_in(dest, heads_axis) * subs + block_of(dest, heads_axis))
     pick_a = jnp.where((which < 2) & (entry == first + which), 1.0, 0.0).astype(BF16)
     pick_b = jnp.where(
         (which >= 2) & (which < 4) & (entry == first + which - 2), 1.0, 0.0
@@ -98,7 +106,7 @@
     size = systems[0].shape[0]
     blocks = size // SUB
     row, col = iota((size, size), 0), iota((size, size), 1)
-    diagonal = (row // SUB) == (col // SUB)
+    diagonal = block_of(row, SUB) == block_of(col, SUB)
     compact = jnp.concatenate(
         [
             jnp.sum(jnp.where(diagonal, n, 0.0).reshape(blocks, SUB, size), axis=0)
@@ -108,9 +116,10 @@
     )
     count = len(systems)
     lane, line = iota(compact.shape, 1), iota(compact.shape, 0)
-    solved = jnp.where(lane % SUB == line % SUB, 1.0, 0.0).reshape(count, SUB, size)
+    solved = jnp.where(place_in(lane ^ line, SUB) == 0, 1.0, 0.0).reshape(count, SUB, size)
     for m in range(SUB - 1):
-        spread = jnp.take_along_axis(compact, (lane // SUB) * SUB + m, axis=1)
+        source = (lane & ~(SUB - 1)) | m
+        spread = jnp.take_along_axis(compact, source, axis=1, mode="promise_in_bounds")
         solved = solved - spread.reshape(count, SUB, size) * solved[:, m : m + 1, :]
     lows = [halves(n) for n in systems]
     placed = jnp.where(diagonal, 1.0, 0.0).astype(BF16)
@@ -131,7 +140,7 @@
                 pieces += [even[lo - width : lo], x[j * width : (j + 1) * width]]
             return jnp.concatenate(pieces, axis=0)
 
-        below = ((row // (2 * width)) == (col // (2 * width))) & ((col // width) % 2 == 0)
+        below = (block_of(row ^ col, 2 * width) == 0) & ((col & width) == 0)
         mask = rows_of(jnp.where(below, 1.0, 0.0).astype(BF16))
         blank = jnp.zeros((size, size), BF16)
         firsts = [
@@ -149,7 +158,7 @@
 
 
 def gate_values(gates, sub, alog_ref, dt_ref):
-    second = iota(gates.shape, 0) % GATES == 1
+    second = place_in(iota(gates.shape, 0), GATES) == 1
     a_log = jnp.where(second, alog_ref[2 * sub + 1], alog_ref[2 * sub])
     dt_bias = jnp.where(second, dt_ref[2 * sub + 1], dt_ref[2 * sub])
     shifted = gates + dt_bias
@@ -223,7 +232,7 @@
     growth = jnp.exp(cum)
     here = pltpu.roll(rate, rate.shape[0] - 2, 0)
     rest = jnp.exp(cum[:, SPAN - 1 :] - cum) * here
-    which = iota(gates.shape, 0) % GATES
+    which = place_in(iota(gates.shape, 0), GATES)
     mixed = jnp.where(which < 2, cum, pltpu.roll(growth, 2, 0))
     columns = jnp.transpose(jnp.where(which < 4, mixed, pltpu.roll(rest, 4, 0)))
     cols_ref[...] = columns

time: 51.3 us -> 51.3 us (level)
  no operation moved by 1% of the time
where the time goes in v10:
time: 51.3 us; the launch traced here: 51 us
  blocking collectives  36.5 us (71%)
  Pallas kernels  12.6 us (25%)
  starting transfers between devices  1.73 us (3%)
    all_to_all x1, blocking collectives, local(): blocks = near(lax.all_to_all(packed, group, 0, 0, tiled=True))  22.7 us
    all_to_all x1, blocking collectives, local(): returned = near(lax.all_to_all(normed, group, 0, 0, tiled=True))  13.8 us
    pallas_call x1, Pallas kernels, local(): call(keys_kernel, (pltpu.VMEM((total, DK), BF16), pltpu.VMEM((spans, DK,...  5.19 us
    pallas_call x1, Pallas kernels, local(): call(opening_kernel, (pltpu.VMEM((2 * DK + 16, 128), BF16), pltpu.VMEM((t...  2.8 us
    pallas_call x1, Pallas kernels, local(): call(output_kernel, (pltpu.VMEM((2, total, DV), F32), pltpu.VMEM((2, tota...  1.96 us
    ppermute x1, starting transfers between devices, local(): entering = near(lax.ppermute(hop, 'half', route))  1.73 us
    pallas_call x1, Pallas kernels, local(): call(functools.partial(pack_kernel, heads_axis), pltpu.VMEM((peers, GATES...  1.34 us
  transfers between devices with their start and end apart: 1, of which 0 were waited for; matrix products, arithmetic and copies ran while one was open for 0% of the time, Pallas kernels for 4%

profile of v10, /device:TPU:0, one launch (start us, length us, event | category | flops | bytes accessed | tf_op | source)
XLA Modules:
  0.0 51.0 jit_solution(6009770701910029238)
XLA Ops:
  0.0 1.3 %shard_map.118 = bf16[16,264,128]{2,1,0:T(8,128)(2,1)S(1)} custom-call(bf16[64,2048]{1,0:T(8,128)(2,1)} %q_in.1, bf16[64,2048]{1,0:T(8,128)(2,1)} %k_in.1, bf16[64,4096]{1,0:T(8,128)(2,1)} %v_in.1, bf16[32,64]{1,0:T(8,128)(2,1)} %bitcast.4, bf16[32,64]{1,0:T(8,128)(2,1)} %bitcast.5), custom_call_target="tpu_custom_call" | custom-call | flops 1048576 | bytes 2097152 | tf_op jit(solution)/shard_map/pallas_call | solution.py:614
  1.3 0.0 copy-start.2
  1.4 0.0 copy-start.5
  1.4 0.0 copy-start.6
  1.4 22.7 %all_to_all.10.recv_ref = bf16[16,264,128]{2,1,0:T(8,128)(2,1)S(1)} all-to-all(bf16[16,264,128]{2,1,0:T(8,128)(2,1)S(1)} %shard_map.118), channel_id=1, replica_groups=mesh['half'=2,'sub'=4,'head'=4] {'sub','head'}, dimensions={0} | all-to-all | bytes 2162688 | tf_op jit(solution)/shard_map/all_to_all | solution.py:621
  24.1 0.0 copy-done.2
  24.1 0.0 copy-done.5
  24.1 0.0 copy-done.6
  24.1 0.0 copy-start.1
  24.1 5.2 %shard_map.119 = (bf16[1024,128]{1,0:T(8,128)(2,1)S(1)}, bf16[8,128,128]{2,1,0:T(8,128)(2,1)S(1)}, bf16[2,8,128,256]{3,2,1,0:T(8,128)(2,1)S(1)}, bf16[2,8,128,12...) custom-call(bf16[16,264,128]{2,1,0:T(8,128)(2,1)S(1)} %all_to_all.10, ...), custom_call_target="tpu_custom_call" | custom-call | flops 4294967296 | bytes 2097152 | tf_op jit(solution)/shard_map/pallas_call | solution.py:622
  29.3 0.0 copy-done.1
  29.3 0.0 copy-start.3
  29.4 2.8 %shard_map.120 = (bf16[272,128]{1,0:T(8,128)(2,1)S(1)}, bf16[1024,256]{1,0:T(8,128)(2,1)S(1)}, bf16[8,256,256]{2,1,0:T(8,128)(2,1)S(1)}) custom-call(bf16[16,264,128]{2,1,0:T(8,128)(2,1)S(1)} %all_to_all.10.recv_ref, f32[4,1024]{1,0:T(4,128)S(1)} %copy-done.1, bf16[8,128,128]{2,1,0:T(8,128)(2,1)S(1)} %get-tuple-element.18.keys_t_ref, ...), custom_call_target="tpu_custom_call" | custom-call | flops 4294967296 | bytes 2097152 | tf_op jit(solution)/shard_map/pallas_call | solution.py:641
  32.2 1.7 %collective-permute-start = (bf16[272,128]{1,0:T(8,128)(2,1)S(1)}, bf16[272,128]{1,0:T(8,128)(2,1)S(1)}, u32[]{:S(2)}, u32[]{:S(2)}) collective-permute-start(bf16[272,128]{1,0:T(8,128)(2,1)S(1)} %get-tuple-element.23.hop_ref), channel_id=1, source_target_pairs={{0,16},{1,17},{2,18},{3,19},{4,20},{5,21},{6,22},{7,23},{8,24},{9,... | collective-permute-start | bytes 208904 | tf_op jit(solution)/shard_map/ppermute | solution.py:652
  33.9 0.0 copy-done.3
  33.9 0.0 copy-start.4
  33.9 2.0 %shard_map.121 = (f32[2,1024,128]{2,1,0:T(8,128)S(1)}, bf16[2,1024,128]{2,1,0:T(8,128)(2,1)S(1)}, f32[2,128,256]{2,1,0:T(8,128)}) custom-call(bf16[16,264,128]{2,1,0:T(8,128)(2,1)S(1)} %all_to_all.10.recv_ref, f32[4,512]{1,0:T(4,128)S(1)} %copy-done.3, f32[4,1024]{1,0:T(4,128)S(1)} %copy-done.1, bf16[1024,128]{1,0:T(8,128)(2,1)S(1)} %get-tuple-element.25.keys_ref, ...), custom_call_target="tpu_custom_call" | custom-call | flops 4294967296 | bytes 2097152 | tf_op jit(solution)/shard_map/pallas_call | solution.py:654
  35.9 0.0 collective-permute-done.hop_ref
  35.9 0.0 copy-done.4
  35.9 0.4 shard_map.122
  36.3 0.0 copy-start
  36.3 13.8 %all_to_all.11.normed_ref = bf16[16,64,256]{2,1,0:T(8,128)(2,1)S(1)} all-to-all(bf16[16,64,256]{2,1,0:T(8,128)(2,1)S(1)} %shard_map.122), channel_id=1, replica_groups=mesh['half'=2,'sub'=4,'head'=4] {'sub','head'}, dimensions={0} | all-to-all | bytes 1048576 | tf_op jit(solution)/shard_map/all_to_all | solution.py:710
  50.0 0.0 copy-done
  50.0 0.9 %shard_map.123 = bf16[64,4096]{1,0:T(8,128)(2,1)} custom-call(bf16[16,64,256]{2,1,0:T(8,128)(2,1)S(1)} %all_to_all.11.normed_ref, bf16[64,4096]{1,0:T(8,128)(2,1)S(1)} %copy-done), custom_call_target="tpu_custom_call" | custom-call | flops 67108864 | bytes 2097152 | tf_op jit(solution)/shard_map/pallas_call | solution.py:711
Async XLA Ops:
  1.3 22.8 %copy-start.2 = (f32[4,512]{1,0:T(4,128)S(1)}, f32[4,512]{1,0:T(4,128)}, u32[]{:S(2)}) copy-start(f32[4,512]{1,0:T(4,128)} %ck_ref.3) | copy-start | bytes 24580
  1.4 22.8 %copy-start.5 = (f32[8]{0:T(128)S(1)}, f32[8]{0:T(128)}, u32[]{:S(2)}) copy-start(f32[8]{0:T(128)} %alog_ref.1) | copy-start | bytes 100
  1.4 22.8 %copy-start.6 = (f32[8]{0:T(128)S(1)}, f32[8]{0:T(128)}, u32[]{:S(2)}) copy-start(f32[8]{0:T(128)} %dt_ref.1) | copy-start | bytes 100
  24.1 5.2 %copy-start.1 = (f32[4,1024]{1,0:T(4,128)S(1)}, f32[4,1024]{1,0:T(4,128)}, u32[]{:S(2)}) copy-start(f32[4,1024]{1,0:T(4,128)} %cv_ref.5) | copy-start | bytes 49156
  29.3 4.6 %copy-start.3 = (f32[4,512]{1,0:T(4,128)S(1)}, f32[4,512]{1,0:T(4,128)}, u32[]{:S(2)}) copy-start(f32[4,512]{1,0:T(4,128)} %cq_ref.3) | copy-start | bytes 24580
  32.2 3.7 %collective-permute-start = (bf16[272,128]{1,0:T(8,128)(2,1)S(1)}, bf16[272,128]{1,0:T(8,128)(2,1)S(1)}, u32[]{:S(2)}, u32[]{:S(2)}) collective-permute-start(bf16[272,128]{1,0:T(8,128)(2,1)S(1)} %get-tuple-element.23.hop_ref), channel_id=1, source_target_pairs={{0,16},{1,17},{2,18},{3,19},{4,20},{5,21},{6,22},{7,23},{8,24},{9,... | collective-permute-start | bytes 208904 | tf_op jit(solution)/shard_map/ppermute | solution.py:652
  33.9 2.0 %copy-start.4 = (f32[128]{0:T(128)S(1)}, f32[128]{0:T(128)}, u32[]{:S(2)}) copy-start(f32[128]{0:T(128)} %param.23) | copy-start | bytes 1540
  36.3 13.8 %copy-start = (bf16[64,4096]{1,0:T(8,128)(2,1)S(1)}, bf16[64,4096]{1,0:T(8,128)(2,1)}, u32[]{:S(2)}) copy-start(bf16[64,4096]{1,0:T(8,128)(2,1)} %z_ref.1) | copy-start | bytes 1572868

commit v11 on v10

--- a/solution.py
+++ b/solution.py
@@ -13,6 +13,7 @@
 KH = 16
 SUB = 16
 SPAN = 128
+GROUP = 4
 EDGE = CONV - 1
 EPS = 1e-06
 F32 = jnp.float32
@@ -127,8 +128,22 @@
         tuple(jnp.concatenate([x] * blocks, axis=0) * placed for x in halves(solved[i]))
         for i in range(count)
     ]
+    levels = []
     width = SUB
     while width < size:
+        below = (block_of(row ^ col, 2 * width) == 0) & ((col & width) == 0)
+        levels.append((width, jnp.where(below, 1.0, 0.0).astype(BF16)))
+        width *= 2
+    grown = []
+    for i in range(0, count, GROUP):
+        grown += doubled(lows[i : i + GROUP], parts[i : i + GROUP], levels)
+    return grown
+
+
+def doubled(lows, parts, levels):
+    size = levels[0][1].shape[0]
+    blank = jnp.zeros((size, size), BF16)
+    for width, below in levels:
         odd = [(j, j + width) for j in range(width, size, 2 * width)]
 
         def rows_of(x):
@@ -140,9 +155,7 @@
                 pieces += [even[lo - width : lo], x[j * width : (j + 1) * width]]
             return jnp.concatenate(pieces, axis=0)
 
-        below = (block_of(row ^ col, 2 * width) == 0) & ((col & width) == 0)
-        mask = rows_of(jnp.where(below, 1.0, 0.0).astype(BF16))
-        blank = jnp.zeros((size, size), BF16)
+        mask = rows_of(below)
         firsts = [
             mm_parts((rows_of(n[0]) * mask, rows_of(n[1]) * mask), t) for n, t in zip(lows, parts)
         ]
@@ -153,7 +166,6 @@
             tuple(woven(t[i], o[i] + second[i]) for i in range(2))
             for t, o, second in zip(parts, odds, seconds)
         ]
-        width *= 2
     return parts
 
 
@@ -259,7 +271,7 @@
         systems.append(jnp.where(strict, within * grams[n], 0.0))
     inverses = invert(systems)
     for i, (n, r) in enumerate(both):
-        t_ref[r, n] = jnp.concatenate(inverses[i], axis=1)
+        t_ref[r, n, 0], t_ref[r, n, 1] = inverses[i]
     scaled = []
     for n, r in both:
         at = GATES * n + r
@@ -278,6 +290,40 @@
         lin_ref[r, n] = moved[n][:, r * DK : (r + 1) * DK].astype(BF16)
 
 
+def unwound(t_ref, n, r, x):
+    both = jnp.concatenate([t_ref[r, n, 0], t_ref[r, n, 1]], axis=1)
+    return dot(both, jnp.concatenate([x, x], axis=0))
+
+
+def end_of(ends_ref, n, r):
+    return ends_ref[GATES * n + r : GATES * n + r + 1, :]
+
+
+def followed(span_map, state):
+    end, moved, add = span_map
+    return step(end, moved, state, halves(state)) + add
+
+
+def composed(maps):
+    if len(maps) == 1:
+        return maps[0]
+    half = len(maps) // 2
+    end_a, moved_a, add_a = composed(maps[:half])
+    end_b, moved_b, add_b = composed(maps[half:])
+    high, low = halves(add_a)
+    rights = jnp.concatenate(
+        [
+            jnp.concatenate([moved_a, high], axis=1),
+            jnp.concatenate([jnp.zeros_like(moved_a), low], axis=1),
+        ],
+        axis=0,
+    )
+    passed = dot(jnp.concatenate([moved_b, moved_b], axis=1), rights)
+    moved = end_b * moved_a.astype(F32) + end_a * moved_b.astype(F32) - passed[:, :DK]
+    add = end_b * add_a - passed[:, DK:] + add_b
+    return end_a * end_b, moved.astype(BF16), add
+
+
 def step(end, moved, state, parts):
     both = jnp.concatenate([moved, moved], axis=1)
     return end * state - dot(both, jnp.concatenate(parts, axis=0))
@@ -294,9 +340,9 @@
     for n, r in both:
         lanes = slice(r * DV, (r + 1) * DV)
         v_n = convolved(rows, n * SPAN + 8 - EDGE, SPAN, lanes, taps[r]).astype(BF16)
-        vs[n * SPAN : (n + 1) * SPAN, lanes] = v_n
-        values.append(jnp.concatenate([v_n, v_n], axis=0))
-    solved = [dot(t_ref[r, n], v) for (n, r), v in zip(both, values)]
+        vs[r, n * SPAN : (n + 1) * SPAN, :] = v_n
+        values.append(v_n)
+    solved = [unwound(t_ref, n, r, v) for (n, r), v in zip(both, values)]
     weighed = []
     for (n, r), u_mat in zip(both, solved):
         at = GATES * n + r
@@ -309,7 +355,7 @@
 
 
 def opening_kernel(
-    recv_ref, cv_ref, keys_t_ref, t_ref, lin_ref, ends_ref, cols_ref, hop_ref, vs_ref, xs_ref, rows
+    recv_ref, cv_ref, keys_t_ref, t_ref, lin_ref, ends_ref, cols_ref, hop_ref, vs_ref, xs_ref, adds_ref, rows
 ):
     first = lax.axis_index("half") == 0
     peers = recv_ref.shape[0]
@@ -325,13 +371,22 @@
     @pl.when(first)
     def _():
         adds = values_part(recv_ref, cv_ref, keys_t_ref, t_ref, cols_ref, rows, vs_ref)
-        states = [adds[0], adds[1]]
-        for n in range(1, spans):
+        for n in range(spans):
             for r in range(2):
-                parts = halves(states[r])
-                xs_ref[n, :, r * DV : (r + 1) * DV] = jnp.concatenate(parts, axis=0)
-                end = ends_ref[GATES * n + r : GATES * n + r + 1, :]
-                states[r] = step(end, lin_ref[r, n], states[r], parts) + adds[2 * n + r]
+                adds_ref[r, n] = adds[2 * n + r]
+        maps = [
+            [(end_of(ends_ref, n, r), lin_ref[r, n], adds[2 * n + r]) for n in range(spans)]
+            for r in range(2)
+        ]
+        states = [m[0][2] for m in maps]
+        done = 1
+        while done < spans:
+            for r in range(2):
+                if done > 1:
+                    xs_ref[r, done] = jnp.concatenate(halves(states[r]), axis=0)
+            later = [composed(m[done : 2 * done]) for m in maps]
+            states = [followed(m, x) for m, x in zip(later, states)]
+            done *= 2
         for r in range(2):
             hop_ref[r * DK : (r + 1) * DK, :] = states[r].astype(BF16)
 
@@ -354,6 +409,7 @@
     hop_ref,
     vs_ref,
     xs_ref,
+    adds_ref,
     oa_ref,
     om_ref,
     last_ref,
@@ -397,11 +453,29 @@
     @pl.when(first)
     def _():
         prepare()
-        reads = [dot(twice(readers[n], 1), xs_ref[n]) for n in range(1, spans)]
+        stacks, states = [], []
+        for n in range(1, spans):
+            if n == 1:
+                states = [adds_ref[r, 0] for r in range(2)]
+                stack = [jnp.concatenate(halves(x), axis=0) for x in states]
+            elif n & (n - 1) == 0:
+                stack = [xs_ref[r, n] for r in range(2)]
+                states = [x[:DK].astype(F32) + x[DK:].astype(F32) for x in stack]
+            else:
+                states = [
+                    followed(
+                        (end_of(ends_ref, n - 1, r), lin_ref[r, n - 1], adds_ref[r, n - 1]),
+                        states[r],
+                    )
+                    for r in range(2)
+                ]
+                stack = [jnp.concatenate(halves(x), axis=0) for x in states]
+            stacks.append(jnp.concatenate(stack, axis=1))
+        reads = [dot(twice(readers[n], 1), stacks[n - 1]) for n in range(1, spans)]
         rests, seen = [], []
         for n, r in both:
             lanes = slice(r * DV, (r + 1) * DV)
-            value = vs_ref[span_rows(n), lanes]
+            value = vs_ref[r, span_rows(n), :]
             if n == 0:
                 rests.append(value)
                 seen.append(None)
@@ -409,7 +483,7 @@
                 read = growth(n, r) * reads[n - 1][:SPAN, lanes]
                 rests.append((value.astype(F32) - read).astype(BF16))
                 seen.append(growth(n, r) * reads[n - 1][SPAN:, lanes])
-        fresh = [dot(t_ref[r, n], twice(x, 0)).astype(BF16) for (n, r), x in zip(both, rests)]
+        fresh = [unwound(t_ref, n, r, x).astype(BF16) for (n, r), x in zip(both, rests)]
         spreads = [dot(inner[r, n], x) for (n, r), x in zip(both, fresh)]
         for (n, r), x, y in zip(both, spreads, seen):
             oa_ref[r, span_rows(n), :] = x if y is None else x + y
@@ -431,20 +505,27 @@
         for n in range(1, spans):
             for r in range(2):
                 parts = halves(states[r])
-                states_ref[r, n] = jnp.concatenate(parts, axis=0)
+                for i in range(2):
+                    both_parts = [x[:, i * DV : (i + 1) * DV] for x in parts]
+                    states_ref[i, r, n] = jnp.concatenate(both_parts, axis=0)
                 add = jnp.concatenate([adds[2 * n + r], zero_half], axis=1)
-                end = ends_ref[GATES * n + r : GATES * n + r + 1, :]
-                end = jnp.concatenate([end, end], axis=1)
+                end = jnp.concatenate([end_of(ends_ref, n, r)] * 2, axis=1)
                 states[r] = step(end, lin_ref[r, n], states[r], parts) + add
         for r in range(2):
             last_ref[r] = states[r]
         prepare()
         reads = [
-            dot(twice(readers[n], 1), states_ref[r, n]) if n > 0 else None for n, r in both
+            dot(
+                twice(readers[n], 1),
+                jnp.concatenate([states_ref[0, r, n], states_ref[1, r, n]], axis=1),
+            )
+            if n > 0
+            else None
+            for n, r in both
         ]
         rests, seen = [], []
         for (n, r), read in zip(both, reads):
-            value = values[span_rows(n), r * DV : (r + 1) * DV].astype(F32)
+            value = values[r, span_rows(n), :].astype(F32)
             if n == 0:
                 known = growth(n, r) * readers[n].astype(F32)[:SPAN]
                 asked = growth(n, r) * readers[n].astype(F32)[SPAN:]
@@ -454,7 +535,7 @@
                 rest = jnp.concatenate([value, zero_half], axis=1) - growth(n, r) * read[:SPAN]
                 seen.append(growth(n, r) * read[SPAN:])
             rests.append(rest.astype(BF16))
-        fresh = [dot(t_ref[r, n], twice(x, 0)).astype(BF16) for (n, r), x in zip(both, rests)]
+        fresh = [unwound(t_ref, n, r, x).astype(BF16) for (n, r), x in zip(both, rests)]
         spreads = [dot(inner[r, n], x) for (n, r), x in zip(both, fresh)]
         for (n, r), x, y in zip(both, spreads, seen):
             out = x + y
@@ -499,7 +580,7 @@
 def finish_kernel(
     hop_ref, recv_ref, early_ref, cq_ref, ck_ref, cv_ref, gain_ref, oa_ref, om_ref, out_ref, rows
 ):
-    peers, tokens = out_ref.shape[0], out_ref.shape[1]
+    peers, tokens = out_ref.shape[0], out_ref.shape[1] // 2
     first = lax.axis_index("half") == 0
     gain = gain_ref[...]
     chunks = 4
@@ -508,9 +589,8 @@
     def put(c, r, core):
         scale = lax.rsqrt(jnp.mean(core * core, axis=-1, keepdims=True) + EPS)
         normed = (core * scale * gain).astype(BF16)
-        out_ref[c * peer_part : (c + 1) * peer_part, :, r * DV : (r + 1) * DV] = normed.reshape(
-            peer_part, tokens, DV
-        )
+        here = slice(c * peer_part, (c + 1) * peer_part)
+        out_ref[here, r * tokens : (r + 1) * tokens, :] = normed.reshape(peer_part, tokens, DV)
 
     @pl.when(first)
     def _():
@@ -548,15 +628,17 @@
 
 
 def gate_kernel(heads_axis, normed_ref, z_ref, out_ref, made, sems):
-    subs = normed_ref.shape[0] // heads_axis
+    subs, tokens = normed_ref.shape[0] // heads_axis, z_ref.shape[0]
     width = subs * 2 * DV
     copies = []
     for head in range(heads_axis):
         for sub in range(subs):
-            at = (head * subs + sub) * 2 * DV
-            gate = silu(z_ref[:, at : at + 2 * DV].astype(F32))
-            value = normed_ref[sub * heads_axis + head].astype(F32)
-            made[:, at : at + 2 * DV] = (value * gate).astype(BF16)
+            for r in range(2):
+                at = (2 * (head * subs + sub) + r) * DV
+                gate = silu(z_ref[:, at : at + DV].astype(F32))
+                here = slice(r * tokens, (r + 1) * tokens)
+                value = normed_ref[sub * heads_axis + head, here, :].astype(F32)
+                made[:, at : at + DV] = (value * gate).astype(BF16)
         lanes = pl.ds(head * width, width)
         copy = pltpu.make_async_copy(made.at[:, lanes], out_ref.at[:, lanes], sems.at[head])
         copy.start()
@@ -624,7 +706,7 @@
         (
             pltpu.VMEM((total, DK), BF16),
             pltpu.VMEM((spans, DK, SPAN), BF16),
-            pltpu.VMEM((2, spans, SPAN, 2 * SPAN), BF16),
+            pltpu.VMEM((2, spans, 2, SPAN, SPAN), BF16),
             pltpu.VMEM((2, spans, DK, DK), BF16),
             pltpu.VMEM((SPAN, DK), F32),
             pltpu.VMEM((2, total, SPAN), BF16),
@@ -638,19 +720,20 @@
     keys, keys_t, inverses, lins, ends, within, cols, early = (
         near(x) for x in (keys, keys_t, inverses, lins, ends, within, cols, early)
     )
-    hop, values, starts = call(
+    hop, values, starts, adds = call(
         opening_kernel,
         (
             pltpu.VMEM((2 * DK + 16, 128), BF16),
-            pltpu.VMEM((total, 2 * DV), BF16),
-            pltpu.VMEM((spans, 2 * DK, 2 * DV), BF16),
+            pltpu.VMEM((2, total, DV), BF16),
+            pltpu.VMEM((2, spans, 2 * DK, DV), BF16),
+            pltpu.VMEM((2, spans, DK, DV), F32),
         ),
         [VMEM] * 7,
         [pltpu.VMEM((8 + total, 2 * DV), F32)],
         flops=1 << 32,
     )(blocks, conv_v, keys_t, inverses, lins, ends, cols)
     entering = near(lax.ppermute(hop, "half", route))
-    hop, values, starts = near(hop), near(values), near(starts)
+    hop, values, starts, adds = (near(x) for x in (hop, values, starts, adds))
     out_a, out_m, last = call(
         output_kernel,
         (
@@ -658,14 +741,14 @@
             pltpu.VMEM((2, total, DV), BF16),
             pltpu.VMEM((2, DK, 2 * DV), F32),
         ),
-        [VMEM] * 13,
+        [VMEM] * 14,
         [
             pltpu.VMEM((8 + total, 2 * DV), F32),
             pltpu.VMEM((8 + total, DK), F32),
-            pltpu.VMEM((total, 2 * DV), BF16),
+            pltpu.VMEM((2, total, DV), BF16),
             pltpu.VMEM((2, spans, SPAN, SPAN), BF16),
             pltpu.VMEM((spans, 2 * SPAN, DK), BF16),
-            pltpu.VMEM((2, spans, 2 * DK, 2 * DV), BF16),
+            pltpu.VMEM((2, 2, spans, 2 * DK, DV), BF16),
         ],
         flops=1 << 32,
     )(
@@ -682,6 +765,7 @@
         hop,
         values,
         starts,
+        adds,
     )
     for _ in range(shards - 2):
         moved = call(
@@ -693,7 +777,7 @@
         entering = near(lax.ppermute(moved, "half", route))
     normed = call(
         finish_kernel,
-        pltpu.VMEM((peers, tokens, 2 * DV), BF16),
+        pltpu.VMEM((peers, 2 * tokens, DV), BF16),
         [VMEM] * 9,
         [pltpu.VMEM((32, 512), F32)],
     )(

time: 51.3 us -> 52.3 us (1.019)
  Pallas kernels: 12.6 us -> 13.5 us
    pallas_call x1, Pallas kernels: 5.19 us -> 5.93 us  [local(): call(keys_kernel, (pltpu.VMEM((total, DK), BF16), pltpu.VMEM((spans, DK,...]
    pallas_call x1, Pallas kernels: 1.96 us -> 2.53 us  [local(): call(output_kernel, (pltpu.VMEM((2, total, DV), F32), pltpu.VMEM((2, tota...]
  transfers between devices with their start and end apart: 1 -> 1, of which waited for: 0 -> 0; matrix products, arithmetic and copies ran while one was open for 0% -> 0% of each run, Pallas kernels for 4% -> 5%
where the time goes in v11:
time: 52.3 us; the launch traced here: 52 us
  blocking collectives  36 us (69%)
  Pallas kernels  13.5 us (26%)
  starting transfers between devices  2.18 us (4%)
    all_to_all x1, blocking collectives, local(): blocks = near(lax.all_to_all(packed, group, 0, 0, tiled=True))  22.7 us
    all_to_all x1, blocking collectives, local(): returned = near(lax.all_to_all(normed, group, 0, 0, tiled=True))  13.3 us
    pallas_call x1, Pallas kernels, local(): call(keys_kernel, (pltpu.VMEM((total, DK), BF16), pltpu.VMEM((spans, DK,...  5.93 us
    pallas_call x1, Pallas kernels, local(): call(output_kernel, (pltpu.VMEM((2, total, DV), F32), pltpu.VMEM((2, tota...  2.53 us
    pallas_call x1, Pallas kernels, local(): call(opening_kernel, (pltpu.VMEM((2 * DK + 16, 128), BF16), pltpu.VMEM((2...  2.35 us
    ppermute x1, starting transfers between devices, local(): entering = near(lax.ppermute(hop, 'half', route))  2.18 us
    pallas_call x1, Pallas kernels, local(): call(functools.partial(pack_kernel, heads_axis), pltpu.VMEM((peers, GATES...  1.34 us
  transfers between devices with their start and end apart: 1, of which 0 were waited for; matrix products, arithmetic and copies ran while one was open for 0% of the time, Pallas kernels for 5%

profile of v11, /device:TPU:0, one launch (start us, length us, event | category | flops | bytes accessed | tf_op | source)
XLA Modules:
  0.0 52.0 jit_solution(6748033185705356698)
XLA Ops:
  0.0 1.3 %shard_map.118 = bf16[16,264,128]{2,1,0:T(8,128)(2,1)S(1)} custom-call(bf16[64,2048]{1,0:T(8,128)(2,1)} %q_in.1, bf16[64,2048]{1,0:T(8,128)(2,1)} %k_in.1, bf16[64,4096]{1,0:T(8,128)(2,1)} %v_in.1, bf16[32,64]{1,0:T(8,128)(2,1)} %bitcast.4, bf16[32,64]{1,0:T(8,128)(2,1)} %bitcast.5), custom_call_target="tpu_custom_call" | custom-call | flops 1048576 | bytes 2097152 | tf_op jit(solution)/shard_map/pallas_call | solution.py:696
  1.3 0.0 copy-start.2
  1.4 0.0 copy-start.5
  1.4 0.0 copy-start.6
  1.4 22.7 %all_to_all.10.recv_ref = bf16[16,264,128]{2,1,0:T(8,128)(2,1)S(1)} all-to-all(bf16[16,264,128]{2,1,0:T(8,128)(2,1)S(1)} %shard_map.118), channel_id=1, replica_groups=mesh['half'=2,'sub'=4,'head'=4] {'sub','head'}, dimensions={0} | all-to-all | bytes 2162688 | tf_op jit(solution)/shard_map/all_to_all | solution.py:703
  24.1 0.0 copy-done.2
  24.1 0.0 copy-done.5
  24.1 0.0 copy-done.6
  24.1 0.0 copy-start.1
  24.1 5.9 %shard_map.119 = (bf16[1024,128]{1,0:T(8,128)(2,1)S(1)}, bf16[8,128,128]{2,1,0:T(8,128)(2,1)S(1)}, bf16[2,8,2,128,128]{4,3,2,1,0:T(8,128)(2,1)S(1)}, bf16[2,8,12...) custom-call(bf16[16,264,128]{2,1,0:T(8,128)(2,1)S(1)} %all_to_all.10, ...), custom_call_target="tpu_custom_call" | custom-call | flops 4294967296 | bytes 2097152 | tf_op jit(solution)/shard_map/pallas_call | solution.py:704
  30.1 0.0 copy-done.1
  30.1 0.0 copy-start.3
  30.1 2.3 %shard_map.120 = (bf16[272,128]{1,0:T(8,128)(2,1)S(1)}, bf16[2,1024,128]{2,1,0:T(8,128)(2,1)S(1)}, bf16[2,8,256,128]{3,2,1,0:T(8,128)(2,1)S(1)}, f32[2,8,128,128]{3,2,1,0:T(8,128)S(1)}) custom-call(bf16[16,264,128]{2,1,0:T(8,128)(2,1)S(1)} %all_to_all.10.recv_ref, f32[4,1024]{1,0:T(4,128)S(1)} %copy-done.1, ...), custom_call_target="tpu_custom_call" | custom-call | flops 4294967296 | bytes 2097152 | tf_op jit(solution)/shard_map/pallas_call | solution.py:723
  32.5 2.2 %collective-permute-start = (bf16[272,128]{1,0:T(8,128)(2,1)S(1)}, bf16[272,128]{1,0:T(8,128)(2,1)S(1)}, u32[]{:S(2)}, u32[]{:S(2)}) collective-permute-start(bf16[272,128]{1,0:T(8,128)(2,1)S(1)} %get-tuple-element.24.hop_ref), channel_id=1, source_target_pairs={{0,16},{1,17},{2,18},{3,19},{4,20},{5,21},{6,22},{7,23},{8,24},{9,... | collective-permute-start | bytes 208904 | tf_op jit(solution)/shard_map/ppermute | solution.py:735
  34.6 0.0 copy-done.3
  34.6 0.0 copy-start.4
  34.7 2.5 %shard_map.121 = (f32[2,1024,128]{2,1,0:T(8,128)S(1)}, bf16[2,1024,128]{2,1,0:T(8,128)(2,1)S(1)}, f32[2,128,256]{2,1,0:T(8,128)}) custom-call(bf16[16,264,128]{2,1,0:T(8,128)(2,1)S(1)} %all_to_all.10.recv_ref, f32[4,512]{1,0:T(4,128)S(1)} %copy-done.3, f32[4,1024]{1,0:T(4,128)S(1)} %copy-done.1, bf16[1024,128]{1,0:T(8,128)(2,1)S(1)} %get-tuple-element.26.keys_ref, ...), custom_call_target="tpu_custom_call" | custom-call | flops 4294967296 | bytes 2097152 | tf_op jit(solution)/shard_map/pallas_call | solution.py:737
  37.2 0.0 collective-permute-done.hop_ref
  37.2 0.0 copy-done.4
  37.2 0.4 shard_map.122
  37.6 0.0 copy-start
  37.6 13.3 %all_to_all.11.normed_ref = bf16[16,128,128]{2,1,0:T(8,128)(2,1)S(1)} all-to-all(bf16[16,128,128]{2,1,0:T(8,128)(2,1)S(1)} %shard_map.122), channel_id=1, replica_groups=mesh['half'=2,'sub'=4,'head'=4] {'sub','head'}, dimensions={0} | all-to-all | bytes 1048576 | tf_op jit(solution)/shard_map/all_to_all | solution.py:794
  50.9 0.0 copy-done
  50.9 1.0 %shard_map.123 = bf16[64,4096]{1,0:T(8,128)(2,1)} custom-call(bf16[16,128,128]{2,1,0:T(8,128)(2,1)S(1)} %all_to_all.11.normed_ref, bf16[64,4096]{1,0:T(8,128)(2,1)S(1)} %copy-done), custom_call_target="tpu_custom_call" | custom-call | flops 67108864 | bytes 2097152 | tf_op jit(solution)/shard_map/pallas_call | solution.py:795
Async XLA Ops:
  1.3 22.8 %copy-start.2 = (f32[4,512]{1,0:T(4,128)S(1)}, f32[4,512]{1,0:T(4,128)}, u32[]{:S(2)}) copy-start(f32[4,512]{1,0:T(4,128)} %ck_ref.3) | copy-start | bytes 24580
  1.4 22.8 %copy-start.5 = (f32[8]{0:T(128)S(1)}, f32[8]{0:T(128)}, u32[]{:S(2)}) copy-start(f32[8]{0:T(128)} %alog_ref.1) | copy-start | bytes 100
  1.4 22.8 %copy-start.6 = (f32[8]{0:T(128)S(1)}, f32[8]{0:T(128)}, u32[]{:S(2)}) copy-start(f32[8]{0:T(128)} %dt_ref.1) | copy-start | bytes 100
  24.1 5.9 %copy-start.1 = (f32[4,1024]{1,0:T(4,128)S(1)}, f32[4,1024]{1,0:T(4,128)}, u32[]{:S(2)}) copy-start(f32[4,1024]{1,0:T(4,128)} %cv_ref.5) | copy-start | bytes 49156
  30.1 4.6 %copy-start.3 = (f32[4,512]{1,0:T(4,128)S(1)}, f32[4,512]{1,0:T(4,128)}, u32[]{:S(2)}) copy-start(f32[4,512]{1,0:T(4,128)} %cq_ref.3) | copy-start | bytes 24580
  32.5 4.7 %collective-permute-start = (bf16[272,128]{1,0:T(8,128)(2,1)S(1)}, bf16[272,128]{1,0:T(8,128)(2,1)S(1)}, u32[]{:S(2)}, u32[]{:S(2)}) collective-permute-start(bf16[272,128]{1,0:T(8,128)(2,1)S(1)} %get-tuple-element.24.hop_ref), channel_id=1, source_target_pairs={{0,16},{1,17},{2,18},{3,19},{4,20},{5,21},{6,22},{7,23},{8,24},{9,... | collective-permute-start | bytes 208904 | tf_op jit(solution)/shard_map/ppermute | solution.py:735
  34.6 2.5 %copy-start.4 = (f32[128]{0:T(128)S(1)}, f32[128]{0:T(128)}, u32[]{:S(2)}) copy-start(f32[128]{0:T(128)} %param.23) | copy-start | bytes 1540
  37.6 13.3 %copy-start = (bf16[64,4096]{1,0:T(8,128)(2,1)S(1)}, bf16[64,4096]{1,0:T(8,128)(2,1)}, u32[]{:S(2)}) copy-start(bf16[64,4096]{1,0:T(8,128)(2,1)} %z_ref.1) | copy-start | bytes 1572868

commit v12 on v11

--- a/solution.py
+++ b/solution.py
@@ -13,7 +13,6 @@
 KH = 16
 SUB = 16
 SPAN = 128
-GROUP = 4
 EDGE = CONV - 1
 EPS = 1e-06
 F32 = jnp.float32
@@ -134,10 +133,7 @@
         below = (block_of(row ^ col, 2 * width) == 0) & ((col & width) == 0)
         levels.append((width, jnp.where(below, 1.0, 0.0).astype(BF16)))
         width *= 2
-    grown = []
-    for i in range(0, count, GROUP):
-        grown += doubled(lows[i : i + GROUP], parts[i : i + GROUP], levels)
-    return grown
+    return doubled(lows, parts, levels)
 
 
 def doubled(lows, parts, levels):
@@ -203,7 +199,7 @@
             ].astype(F32)
 
 
-def keys_kernel(
+def keys_part(
     recv_ref,
     ck_ref,
     alog_ref,
@@ -232,7 +228,8 @@
     stacked.append(jnp.zeros((SPAN - spans * GATES, SPAN), F32))
     gates = jnp.concatenate(stacked, axis=0)
     decay, rate = gate_values(gates, sub, alog_ref, dt_ref)
-    early_ref[...] = jnp.where(iota((8, SPAN), 0) < 2, decay[0:8], rate[0:8])
+    if early_ref is not None:
+        early_ref[...] = jnp.where(iota((8, SPAN), 0) < 2, decay[0:8], rate[0:8])
     skipped = later & (iota(gates.shape, 0) < GATES) & (iota(gates.shape, 1) < EDGE)
     decay = jnp.where(skipped, 0.0, decay)
     rate = jnp.where(skipped, 0.0, rate)
@@ -355,7 +352,24 @@
 
 
 def opening_kernel(
-    recv_ref, cv_ref, keys_t_ref, t_ref, lin_ref, ends_ref, cols_ref, hop_ref, vs_ref, xs_ref, adds_ref, rows
+    recv_ref,
+    ck_ref,
+    cv_ref,
+    alog_ref,
+    dt_ref,
+    hop_ref,
+    keys_ref,
+    keys_t_ref,
+    t_ref,
+    lin_ref,
+    ends_ref,
+    within_ref,
+    cols_ref,
+    vs_ref,
+    xs_ref,
+    adds_ref,
+    key_rows,
+    rows,
 ):
     first = lax.axis_index("half") == 0
     peers = recv_ref.shape[0]
@@ -370,6 +384,21 @@
 
     @pl.when(first)
     def _():
+        keys_part(
+            recv_ref,
+            ck_ref,
+            alog_ref,
+            dt_ref,
+            keys_ref,
+            keys_t_ref,
+            t_ref,
+            lin_ref,
+            ends_ref,
+            within_ref,
+            cols_ref,
+            None,
+            key_rows,
+        )
         adds = values_part(recv_ref, cv_ref, keys_t_ref, t_ref, cols_ref, rows, vs_ref)
         for n in range(spans):
             for r in range(2):
@@ -398,21 +427,33 @@
 def output_kernel(
     recv_ref,
     cq_ref,
+    ck_ref,
     cv_ref,
-    keys_ref,
-    keys_t_ref,
-    t_ref,
-    lin_ref,
-    ends_ref,
-    within_ref,
-    cols_ref,
+    alog_ref,
+    dt_ref,
     hop_ref,
+    first_keys,
+    first_keys_t,
+    first_t,
+    first_lin,
+    first_ends,
+    first_within,
+    first_cols,
     vs_ref,
     xs_ref,
     adds_ref,
     oa_ref,
     om_ref,
     last_ref,
+    early_ref,
+    own_keys,
+    own_keys_t,
+    own_t,
+    own_lin,
+    own_ends,
+    own_within,
+    own_cols,
+    key_rows,
     rows,
     query_rows,
     values,
@@ -423,7 +464,7 @@
     sub = lax.axis_index("sub")
     first = lax.axis_index("half") == 0
     tokens = (recv_ref.shape[1] - GATES) // 4
-    spans = t_ref.shape[1]
+    spans = own_t.shape[1]
     both = [(n, r) for n in range(spans) for r in range(2)]
     tap = key_tap(sub, cq_ref)
     widened(query_rows, recv_ref, [3 * tokens], tokens)
@@ -431,10 +472,10 @@
     def span_rows(n):
         return slice(n * SPAN, (n + 1) * SPAN)
 
-    def growth(n, r):
-        return cols_ref[:, GATES * n + 2 + r : GATES * n + 3 + r]
-
-    def prepare():
+    def growing(cols_ref):
+        return lambda n, r: cols_ref[:, GATES * n + 2 + r : GATES * n + 3 + r]
+
+    def prepare(keys_ref, keys_t_ref, within_ref):
         queries = []
         for n in range(spans):
             at = n * SPAN + 8 - EDGE
@@ -452,7 +493,9 @@
 
     @pl.when(first)
     def _():
-        prepare()
+        t_ref, lin_ref, ends_ref = first_t, first_lin, first_ends
+        growth = growing(first_cols)
+        prepare(first_keys, first_keys_t, first_within)
         stacks, states = [], []
         for n in range(1, spans):
             if n == 1:
@@ -493,7 +536,24 @@
 
     @pl.when(jnp.logical_not(first))
     def _():
-        adds = values_part(recv_ref, cv_ref, keys_t_ref, t_ref, cols_ref, rows, values)
+        t_ref, lin_ref, ends_ref = own_t, own_lin, own_ends
+        growth = growing(own_cols)
+        keys_part(
+            recv_ref,
+            ck_ref,
+            alog_ref,
+            dt_ref,
+            own_keys,
+            own_keys_t,
+            own_t,
+            own_lin,
+            own_ends,
+            own_within,
+            own_cols,
+            early_ref,
+            key_rows,
+        )
+        adds = values_part(recv_ref, cv_ref, own_keys_t, own_t, own_cols, rows, values)
         zero_half = jnp.zeros((DK, DV), F32)
         identity = jnp.where(iota((DK, DK), 0) == iota((DK, DK), 1), 1.0, 0.0)
         states = [
@@ -513,7 +573,7 @@
                 states[r] = step(end, lin_ref[r, n], states[r], parts) + add
         for r in range(2):
             last_ref[r] = states[r]
-        prepare()
+        prepare(own_keys, own_keys_t, own_within)
         reads = [
             dot(
                 twice(readers[n], 1),
@@ -701,49 +761,45 @@
         flops=1 << 20,
     )(*inputs)
     blocks = near(lax.all_to_all(packed, group, 0, 0, tiled=True))
-    keys, keys_t, inverses, lins, ends, within, cols, early = call(
-        keys_kernel,
-        (
-            pltpu.VMEM((total, DK), BF16),
-            pltpu.VMEM((spans, DK, SPAN), BF16),
-            pltpu.VMEM((2, spans, 2, SPAN, SPAN), BF16),
-            pltpu.VMEM((2, spans, DK, DK), BF16),
-            pltpu.VMEM((SPAN, DK), F32),
-            pltpu.VMEM((2, total, SPAN), BF16),
-            pltpu.VMEM((SPAN, SPAN), F32),
-            pltpu.VMEM((8, SPAN), F32),
-        ),
-        [VMEM, VMEM, SMEM, SMEM],
-        [pltpu.VMEM((8 + total, DK), F32)],
-        flops=1 << 32,
-    )(blocks, conv_k, a_log, dt_bias)
-    keys, keys_t, inverses, lins, ends, within, cols, early = (
-        near(x) for x in (keys, keys_t, inverses, lins, ends, within, cols, early)
+    made = (
+        pltpu.VMEM((total, DK), BF16),
+        pltpu.VMEM((spans, DK, SPAN), BF16),
+        pltpu.VMEM((2, spans, 2, SPAN, SPAN), BF16),
+        pltpu.VMEM((2, spans, DK, DK), BF16),
+        pltpu.VMEM((SPAN, DK), F32),
+        pltpu.VMEM((2, total, SPAN), BF16),
+        pltpu.VMEM((SPAN, SPAN), F32),
     )
-    hop, values, starts, adds = call(
+    long_rows = [pltpu.VMEM((8 + total, DK), F32), pltpu.VMEM((8 + total, 2 * DV), F32)]
+    params = (conv_k, conv_v, a_log, dt_bias)
+    hop, *opened = call(
         opening_kernel,
         (
             pltpu.VMEM((2 * DK + 16, 128), BF16),
+            *made,
             pltpu.VMEM((2, total, DV), BF16),
             pltpu.VMEM((2, spans, 2 * DK, DV), BF16),
             pltpu.VMEM((2, spans, DK, DV), F32),
         ),
-        [VMEM] * 7,
-        [pltpu.VMEM((8 + total, 2 * DV), F32)],
+        [VMEM] * 3 + [SMEM] * 2,
+        long_rows,
         flops=1 << 32,
-    )(blocks, conv_v, keys_t, inverses, lins, ends, cols)
+    )(blocks, *params)
     entering = near(lax.ppermute(hop, "half", route))
-    hop, values, starts, adds = (near(x) for x in (hop, values, starts, adds))
-    out_a, out_m, last = call(
+    hop = near(hop)
+    opened = [near(x) for x in opened]
+    out_a, out_m, last, early = call(
         output_kernel,
         (
             pltpu.VMEM((2, total, DV), F32),
             pltpu.VMEM((2, total, DV), BF16),
             pltpu.VMEM((2, DK, 2 * DV), F32),
+            pltpu.VMEM((8, SPAN), F32),
         ),
-        [VMEM] * 14,
+        [VMEM] * 4 + [SMEM] * 2 + [VMEM] * (1 + len(opened)),
         [
-            pltpu.VMEM((8 + total, 2 * DV), F32),
+            *made,
+            *long_rows,
             pltpu.VMEM((8 + total, DK), F32),
             pltpu.VMEM((2, total, DV), BF16),
             pltpu.VMEM((2, spans, SPAN, SPAN), BF16),
@@ -751,22 +807,8 @@
             pltpu.VMEM((2, 2, spans, 2 * DK, DV), BF16),
         ],
         flops=1 << 32,
-    )(
-        blocks,
-        conv_q,
-        conv_v,
-        keys,
-        keys_t,
-        inverses,
-        lins,
-        ends,
-        within,
-        cols,
-        hop,
-        values,
-        starts,
-        adds,
-    )
+    )(blocks, conv_q, *params, hop, *opened)
+    early = near(early)
     for _ in range(shards - 2):
         moved = call(
             advance_kernel,

time: 52.3 us -> 51.2 us (0.979)
  starting transfers between devices: 2.18 us -> 1.29 us
    ppermute x1, starting transfers between devices: 2.18 us -> 1.29 us  [local(): entering = near(lax.ppermute(hop, 'half', route))]
    pallas_call x2 -> x1, Pallas kernels: 8.28 us -> 7.51 us  [local(): call(opening_kernel, (pltpu.VMEM((2 * DK + 16, 128), BF16), *made, pltpu....]
    pallas_call x1, Pallas kernels: 2.53 us -> 3.07 us  [local(): call(output_kernel, (pltpu.VMEM((2, total, DV), F32), pltpu.VMEM((2, tota...]
  transfers between devices with their start and end apart: 1 -> 1, of which waited for: 0 -> 0; matrix products, arithmetic and copies ran while one was open for 0% -> 0% of each run, Pallas kernels for 5% -> 6%
where the time goes in v12:
time: 51.2 us; the launch traced here: 50.9 us
  blocking collectives  36 us (70%)
  Pallas kernels  13.2 us (26%)
  starting transfers between devices  1.29 us (3%)
    all_to_all x1, blocking collectives, local(): blocks = near(lax.all_to_all(packed, group, 0, 0, tiled=True))  22.7 us
    all_to_all x1, blocking collectives, local(): returned = near(lax.all_to_all(normed, group, 0, 0, tiled=True))  13.3 us
    pallas_call x1, Pallas kernels, local(): call(opening_kernel, (pltpu.VMEM((2 * DK + 16, 128), BF16), *made, pltpu....  7.51 us
    pallas_call x1, Pallas kernels, local(): call(output_kernel, (pltpu.VMEM((2, total, DV), F32), pltpu.VMEM((2, tota...  3.07 us
    pallas_call x1, Pallas kernels, local(): call(functools.partial(pack_kernel, heads_axis), pltpu.VMEM((peers, GATES...  1.34 us
    ppermute x1, starting transfers between devices, local(): entering = near(lax.ppermute(hop, 'half', route))  1.29 us
  transfers between devices with their start and end apart: 1, of which 0 were waited for; matrix products, arithmetic and copies ran while one was open for 0% of the time, Pallas kernels for 6%

profile of v12, /device:TPU:0, one launch (start us, length us, event | category | flops | bytes accessed | tf_op | source)
XLA Modules:
  0.0 50.9 jit_solution(5372945820740550561)
XLA Ops:
  0.0 1.3 %shard_map.118 = bf16[16,264,128]{2,1,0:T(8,128)(2,1)S(1)} custom-call(bf16[64,2048]{1,0:T(8,128)(2,1)} %q_in.1, bf16[64,2048]{1,0:T(8,128)(2,1)} %k_in.1, bf16[64,4096]{1,0:T(8,128)(2,1)} %v_in.1, bf16[32,64]{1,0:T(8,128)(2,1)} %bitcast.4, bf16[32,64]{1,0:T(8,128)(2,1)} %bitcast.5), custom_call_target="tpu_custom_call" | custom-call | flops 1048576 | bytes 2097152 | tf_op jit(solution)/shard_map/pallas_call | solution.py:756
  1.3 0.0 copy-start.1
  1.4 0.0 copy-start.2
  1.4 0.0 copy-start.5
  1.4 0.0 copy-start.6
  1.4 22.7 %all_to_all.10.recv_ref = bf16[16,264,128]{2,1,0:T(8,128)(2,1)S(1)} all-to-all(bf16[16,264,128]{2,1,0:T(8,128)(2,1)S(1)} %shard_map.118), channel_id=1, replica_groups=mesh['half'=2,'sub'=4,'head'=4] {'sub','head'}, dimensions={0} | all-to-all | bytes 2162688 | tf_op jit(solution)/shard_map/all_to_all | solution.py:763
  24.1 0.0 copy-done.1
  24.1 0.0 copy-done.2
  24.1 0.0 copy-done.5
  24.1 0.0 copy-done.6
  24.2 0.0 copy-start.3
  24.2 7.5 %shard_map.119 = (bf16[272,128]{1,0:T(8,128)(2,1)S(1)}, bf16[1024,128]{1,0:T(8,128)(2,1)S(1)}, bf16[8,128,128]{2,1,0:T(8,128)(2,1)S(1)}, bf16[2,8,2,128,128]{4,3...) custom-call(bf16[16,264,128]{2,1,0:T(8,128)(2,1)S(1)} %all_to_all.10, ...), custom_call_target="tpu_custom_call" | custom-call | flops 4294967296 | bytes 2097152 | tf_op jit(solution)/shard_map/pallas_call | solution.py:775
  31.7 1.3 %collective-permute-start = (bf16[272,128]{1,0:T(8,128)(2,1)S(1)}, bf16[272,128]{1,0:T(8,128)(2,1)S(1)}, u32[]{:S(2)}, u32[]{:S(2)}) collective-permute-start(bf16[272,128]{1,0:T(8,128)(2,1)S(1)} %get-tuple-element.19.hop_ref), channel_id=1, source_target_pairs={{0,16},{1,17},{2,18},{3,19},{4,20},{5,21},{6,22},{7,23},{8,24},{9,... | collective-permute-start | bytes 208904 | tf_op jit(solution)/shard_map/ppermute | solution.py:788
  33.0 0.0 copy-done.3
  33.0 0.0 copy-start.4
  33.0 3.1 %shard_map.120 = (f32[2,1024,128]{2,1,0:T(8,128)S(1)}, bf16[2,1024,128]{2,1,0:T(8,128)(2,1)S(1)}, f32[2,128,256]{2,1,0:T(8,128)}, f32[8,128]{1,0:T(8,128)S(1)}) custom-call(bf16[16,264,128]{2,1,0:T(8,128)(2,1)S(1)} %all_to_all.10.recv_ref, f32[4,512]{1,0:T(4,128)S(1)} %copy-done.3, f32[4,512]{1,0:T(4,128)S(1)} %copy-done.2, f32[4,1024]{1,0:T(4,128)S(1)} %copy-done.1, ...), custom_call_target="tpu_custom_call" | custom-call | flops 4294967296 | bytes 2097152 | tf_op jit(solution)/shard_map/pallas_call | solution.py:791
  36.1 0.0 collective-permute-done.hop_ref
  36.1 0.0 copy-done.4
  36.1 0.4 shard_map.121
  36.4 0.0 copy-start
  36.5 13.3 %all_to_all.11.normed_ref = bf16[16,128,128]{2,1,0:T(8,128)(2,1)S(1)} all-to-all(bf16[16,128,128]{2,1,0:T(8,128)(2,1)S(1)} %shard_map.121), channel_id=1, replica_groups=mesh['half'=2,'sub'=4,'head'=4] {'sub','head'}, dimensions={0} | all-to-all | bytes 1048576 | tf_op jit(solution)/shard_map/all_to_all | solution.py:836
  49.8 0.0 copy-done
  49.8 1.0 %shard_map.122 = bf16[64,4096]{1,0:T(8,128)(2,1)} custom-call(bf16[16,128,128]{2,1,0:T(8,128)(2,1)S(1)} %all_to_all.11.normed_ref, bf16[64,4096]{1,0:T(8,128)(2,1)S(1)} %copy-done), custom_call_target="tpu_custom_call" | custom-call | flops 67108864 | bytes 2097152 | tf_op jit(solution)/shard_map/pallas_call | solution.py:837
Async XLA Ops:
  1.3 22.8 %copy-start.1 = (f32[4,1024]{1,0:T(4,128)S(1)}, f32[4,1024]{1,0:T(4,128)}, u32[]{:S(2)}) copy-start(f32[4,1024]{1,0:T(4,128)} %cv_ref.5) | copy-start | bytes 49156
  1.4 22.8 %copy-start.2 = (f32[4,512]{1,0:T(4,128)S(1)}, f32[4,512]{1,0:T(4,128)}, u32[]{:S(2)}) copy-start(f32[4,512]{1,0:T(4,128)} %ck_ref.5) | copy-start | bytes 24580
  1.4 22.8 %copy-start.5 = (f32[8]{0:T(128)S(1)}, f32[8]{0:T(128)}, u32[]{:S(2)}) copy-start(f32[8]{0:T(128)} %alog_ref.3) | copy-start | bytes 100
  1.4 22.8 %copy-start.6 = (f32[8]{0:T(128)S(1)}, f32[8]{0:T(128)}, u32[]{:S(2)}) copy-start(f32[8]{0:T(128)} %dt_ref.3) | copy-start | bytes 100
  24.2 8.8 %copy-start.3 = (f32[4,512]{1,0:T(4,128)S(1)}, f32[4,512]{1,0:T(4,128)}, u32[]{:S(2)}) copy-start(f32[4,512]{1,0:T(4,128)} %cq_ref.3) | copy-start | bytes 24580
  31.7 4.4 %collective-permute-start = (bf16[272,128]{1,0:T(8,128)(2,1)S(1)}, bf16[272,128]{1,0:T(8,128)(2,1)S(1)}, u32[]{:S(2)}, u32[]{:S(2)}) collective-permute-start(bf16[272,128]{1,0:T(8,128)(2,1)S(1)} %get-tuple-element.19.hop_ref), channel_id=1, source_target_pairs={{0,16},{1,17},{2,18},{3,19},{4,20},{5,21},{6,22},{7,23},{8,24},{9,... | collective-permute-start | bytes 208904 | tf_op jit(solution)/shard_map/ppermute | solution.py:788
  33.0 3.1 %copy-start.4 = (f32[128]{0:T(128)S(1)}, f32[128]{0:T(128)}, u32[]{:S(2)}) copy-start(f32[128]{0:T(128)} %param.23) | copy-start | bytes 1540
  36.4 13.3 %copy-start = (bf16[64,4096]{1,0:T(8,128)(2,1)S(1)}, bf16[64,4096]{1,0:T(8,128)(2,1)}, u32[]{:S(2)}) copy-start(bf16[64,4096]{1,0:T(8,128)(2,1)} %z_ref.1) | copy-start | bytes 1572868

commit v13 on v11

--- a/solution.py
+++ b/solution.py
@@ -13,7 +13,7 @@
 KH = 16
 SUB = 16
 SPAN = 128
-GROUP = 4
+PASSES = 2
 EDGE = CONV - 1
 EPS = 1e-06
 F32 = jnp.float32
@@ -103,30 +103,31 @@
     laid(q_ref, lambda key_head: key_head, 3)
 
 
-def invert(systems):
-    size = systems[0].shape[0]
-    blocks = size // SUB
-    row, col = iota((size, size), 0), iota((size, size), 1)
-    diagonal = block_of(row, SUB) == block_of(col, SUB)
-    compact = jnp.concatenate(
-        [
-            jnp.sum(jnp.where(diagonal, n, 0.0).reshape(blocks, SUB, size), axis=0)
-            for n in systems
-        ],
-        axis=0,
-    )
-    count = len(systems)
-    lane, line = iota(compact.shape, 1), iota(compact.shape, 0)
+def compacted(system):
+    size = system.shape[0]
+    diagonal = block_of(iota((size, size), 0), SUB) == block_of(iota((size, size), 1), SUB)
+    return jnp.sum(jnp.where(diagonal, system, 0.0).reshape(size // SUB, SUB, size), axis=0)
+
+
+def substituted(compact):
+    count, _, size = compact.shape
+    flat = compact.reshape(count * SUB, size)
+    lane, line = iota(flat.shape, 1), iota(flat.shape, 0)
     solved = jnp.where(place_in(lane ^ line, SUB) == 0, 1.0, 0.0).reshape(count, SUB, size)
     for m in range(SUB - 1):
         source = (lane & ~(SUB - 1)) | m
-        spread = jnp.take_along_axis(compact, source, axis=1, mode="promise_in_bounds")
+        spread = jnp.take_along_axis(flat, source, axis=1, mode="promise_in_bounds")
         solved = solved - spread.reshape(count, SUB, size) * solved[:, m : m + 1, :]
-    lows = [halves(n) for n in systems]
-    placed = jnp.where(diagonal, 1.0, 0.0).astype(BF16)
+    return solved
+
+
+def inverted(lows, small):
+    size = lows[0][0].shape[0]
+    row, col = iota((size, size), 0), iota((size, size), 1)
+    placed = jnp.where(block_of(row, SUB) == block_of(col, SUB), 1.0, 0.0).astype(BF16)
     parts = [
-        tuple(jnp.concatenate([x] * blocks, axis=0) * placed for x in halves(solved[i]))
-        for i in range(count)
+        tuple(jnp.concatenate([x] * (size // SUB), axis=0) * placed for x in halves(block))
+        for block in small
     ]
     levels = []
     width = SUB
@@ -134,10 +135,7 @@
         below = (block_of(row ^ col, 2 * width) == 0) & ((col & width) == 0)
         levels.append((width, jnp.where(below, 1.0, 0.0).astype(BF16)))
         width *= 2
-    grown = []
-    for i in range(0, count, GROUP):
-        grown += doubled(lows[i : i + GROUP], parts[i : i + GROUP], levels)
-    return grown
+    return doubled(lows, parts, levels)
 
 
 def doubled(lows, parts, levels):
@@ -217,6 +215,11 @@
     cols_ref,
     early_ref,
     rows,
+    col_parts,
+    cum_parts,
+    here_parts,
+    systems_ref,
+    small_ref,
 ):
     sub = lax.axis_index("sub")
     later = lax.axis_index("half") > 0
@@ -224,7 +227,14 @@
     tokens = (recv_ref.shape[1] - GATES) // 4
     spans = peers * tokens // SPAN
     tap = key_tap(sub, ck_ref)
-    widened(rows, recv_ref, [0], tokens)
+    part = spans // PASSES
+    part_rows = part * SPAN
+    rows[0, 0:8, :] = jnp.zeros((8, DK), F32)
+    for s in range(peers):
+        p, at = divmod(s * tokens, part_rows)
+        rows[p, 8 + at : 8 + at + tokens, :] = recv_ref[s, 0:tokens, :].astype(F32)
+        if at + tokens == part_rows and p + 1 < PASSES:
+            rows[p + 1, 0:8, :] = recv_ref[s, tokens - 16 : tokens, :].astype(F32)[8:]
     stacked = [
         sum(recv_ref[s, 4 * tokens :, :].astype(F32) for s in range(n, n + SPAN // tokens))
         for n in range(0, peers, SPAN // tokens)
@@ -248,46 +258,69 @@
     mixed = jnp.where(which < 2, cum, pltpu.roll(growth, 2, 0))
     columns = jnp.transpose(jnp.where(which < 4, mixed, pltpu.roll(rest, 4, 0)))
     cols_ref[...] = columns
+    ends_ref[...] = jnp.broadcast_to(growth[:, SPAN - 1 :], ends_ref.shape)
+    lines = part * GATES
+    for p in range(PASSES):
+        cum_parts[p] = cum[p * lines : (p + 1) * lines]
+        here_parts[p] = here[p * lines : (p + 1) * lines]
+        shift = (SPAN - p * lines) % SPAN
+        col_parts[p] = pltpu.roll(columns, shift, 1) if shift else columns
     lower = lane_r >= lane_c
     strict = lane_r > lane_c
-    both = [(n, r) for n in range(spans) for r in range(2)]
-    keys = []
-    for n in range(spans):
-        k_n = unit(convolved(rows, n * SPAN + 8 - EDGE, SPAN, slice(0, DK), tap), 1.0)
-        keys_ref[n * SPAN : (n + 1) * SPAN, :] = k_n
-        keys.append(k_n)
-    keys_t = []
-    for n in range(spans):
-        kt_n = jnp.transpose(keys[n].astype(F32)).astype(BF16)
-        keys_t_ref[n] = kt_n
-        keys_t.append(kt_n)
-    grams = [dot(keys[n], keys_t[n]) for n in range(spans)]
-    systems = []
-    for n, r in both:
-        at = GATES * n + r
-        gap = columns[:, at : at + 1] - cum[at : at + 1, :]
-        within = jnp.exp(jnp.where(lower, gap, 0.0)) * here[at : at + 1, :]
-        within_ref[r, n * SPAN : (n + 1) * SPAN, :] = jnp.where(lower, within, 0.0).astype(BF16)
-        systems.append(jnp.where(strict, within * grams[n], 0.0))
-    inverses = invert(systems)
-    for i, (n, r) in enumerate(both):
-        t_ref[r, n, 0], t_ref[r, n, 1] = inverses[i]
-    scaled = []
-    for n, r in both:
-        at = GATES * n + r
-        right = (columns[:, at + 2 : at + 3] * keys[n].astype(F32)).astype(BF16)
-        scaled.append(jnp.concatenate([right, right], axis=0))
-    w_mats = [dot(jnp.concatenate(t, axis=1), x) for t, x in zip(inverses, scaled)]
-    weighed = []
-    for (n, r), w_mat in zip(both, w_mats):
-        at = GATES * n + r
-        weighed.append((columns[:, at + 4 : at + 5] * w_mat).astype(BF16))
-    moved = [
-        dot(keys_t[n], jnp.concatenate(weighed[2 * n : 2 * n + 2], axis=1)) for n in range(spans)
-    ]
-    ends_ref[...] = jnp.broadcast_to(growth[:, SPAN - 1 :], ends_ref.shape)
-    for n, r in both:
-        lin_ref[r, n] = moved[n][:, r * DK : (r + 1) * DK].astype(BF16)
+    both = [(n, r) for n in range(part) for r in range(2)]
+
+    def first_pass(p, carry):
+        columns, cum, here = col_parts[p], cum_parts[p], here_parts[p]
+        keys = [
+            unit(convolved(rows.at[p], n * SPAN + 8 - EDGE, SPAN, slice(0, DK), tap), 1.0)
+            for n in range(part)
+        ]
+        keys_t = [jnp.transpose(k_n.astype(F32)).astype(BF16) for k_n in keys]
+        for n in range(part):
+            keys_ref[pl.ds(pl.multiple_of((p * part + n) * SPAN, SPAN), SPAN), :] = keys[n]
+            keys_t_ref[p * part + n] = keys_t[n]
+        grams = [dot(keys[n], keys_t[n]) for n in range(part)]
+        for i, (n, r) in enumerate(both):
+            at = GATES * n + r
+            gap = columns[:, at : at + 1] - cum[at : at + 1, :]
+            within = jnp.exp(jnp.where(lower, gap, 0.0)) * here[at : at + 1, :]
+            here_rows = pl.ds(pl.multiple_of((p * part + n) * SPAN, SPAN), SPAN)
+            within_ref[r, here_rows, :] = jnp.where(lower, within, 0.0).astype(BF16)
+            system = jnp.where(strict, within * grams[n], 0.0)
+            systems_ref[p, i, 0], systems_ref[p, i, 1] = halves(system)
+            small_ref[p, i] = compacted(system)
+        return carry
+
+    lax.fori_loop(0, PASSES, first_pass, 0)
+    count = PASSES * len(both)
+    small = substituted(small_ref[...].reshape(count, SUB, SPAN))
+    small_ref[...] = small.reshape(small_ref.shape)
+
+    def second_pass(p, carry):
+        columns = col_parts[p]
+        lows = [(systems_ref[p, i, 0], systems_ref[p, i, 1]) for i in range(len(both))]
+        inverses = inverted(lows, [small_ref[p, i] for i in range(len(both))])
+        scaled = []
+        for i, (n, r) in enumerate(both):
+            t_ref[r, p * part + n, 0], t_ref[r, p * part + n, 1] = inverses[i]
+            at = GATES * n + r
+            here_rows = pl.ds(pl.multiple_of((p * part + n) * SPAN, SPAN), SPAN)
+            right = columns[:, at + 2 : at + 3] * keys_ref[here_rows, :].astype(F32)
+            scaled.append(jnp.concatenate([right.astype(BF16)] * 2, axis=0))
+        w_mats = [dot(jnp.concatenate(t, axis=1), x) for t, x in zip(inverses, scaled)]
+        weighed = []
+        for (n, r), w_mat in zip(both, w_mats):
+            at = GATES * n + r
+            weighed.append((columns[:, at + 4 : at + 5] * w_mat).astype(BF16))
+        moved = [
+            dot(keys_t_ref[p * part + n], jnp.concatenate(weighed[2 * n : 2 * n + 2], axis=1))
+            for n in range(part)
+        ]
+        for n, r in both:
+            lin_ref[r, p * part + n] = moved[n][:, r * DK : (r + 1) * DK].astype(BF16)
+        return carry
+
+    lax.fori_loop(0, PASSES, second_pass, 0)
 
 
 def unwound(t_ref, n, r, x):
@@ -714,7 +747,14 @@
             pltpu.VMEM((8, SPAN), F32),
         ),
         [VMEM, VMEM, SMEM, SMEM],
-        [pltpu.VMEM((8 + total, DK), F32)],
+        [
+            pltpu.VMEM((PASSES, 8 + total // PASSES, DK), F32),
+            pltpu.VMEM((PASSES, SPAN, SPAN), F32),
+            pltpu.VMEM((PASSES, spans // PASSES * GATES, SPAN), F32),
+            pltpu.VMEM((PASSES, spans // PASSES * GATES, SPAN), F32),
+            pltpu.VMEM((PASSES, 2 * spans // PASSES, 2, SPAN, SPAN), BF16),
+            pltpu.VMEM((PASSES, 2 * spans // PASSES, SUB, SPAN), F32),
+        ],
         flops=1 << 32,
     )(blocks, conv_k, a_log, dt_bias)
     keys, keys_t, inverses, lins, ends, within, cols, early = (

time: 52.3 us -> 51.5 us (0.985)
  Pallas kernels: 13.5 us -> 12.8 us
where the time goes in v13:
time: 51.5 us; the launch traced here: 51.3 us
  blocking collectives  36.1 us (70%)
  Pallas kernels  12.8 us (25%)
  starting transfers between devices  2.18 us (4%)
    all_to_all x1, blocking collectives, local(): blocks = near(lax.all_to_all(packed, group, 0, 0, tiled=True))  22.7 us
    all_to_all x1, blocking collectives, local(): returned = near(lax.all_to_all(normed, group, 0, 0, tiled=True))  13.4 us
    pallas_call x1, Pallas kernels, local(): call(keys_kernel, (pltpu.VMEM((total, DK), BF16), pltpu.VMEM((spans, DK,...  5.44 us
    pallas_call x1, Pallas kernels, local(): call(output_kernel, (pltpu.VMEM((2, total, DV), F32), pltpu.VMEM((2, tota...  2.35 us
    pallas_call x1, Pallas kernels, local(): call(opening_kernel, (pltpu.VMEM((2 * DK + 16, 128), BF16), pltpu.VMEM((2...  2.34 us
    ppermute x1, starting transfers between devices, local(): entering = near(lax.ppermute(hop, 'half', route))  2.18 us
    pallas_call x1, Pallas kernels, local(): call(functools.partial(pack_kernel, heads_axis), pltpu.VMEM((peers, GATES...  1.34 us
  transfers between devices with their start and end apart: 1, of which 0 were waited for; matrix products, arithmetic and copies ran while one was open for 0% of the time, Pallas kernels for 5%

profile of v13, /device:TPU:0, one launch (start us, length us, event | category | flops | bytes accessed | tf_op | source)
XLA Modules:
  0.0 51.3 jit_solution(13975505048094387236)
XLA Ops:
  0.0 1.3 %shard_map.118 = bf16[16,264,128]{2,1,0:T(8,128)(2,1)S(1)} custom-call(bf16[64,2048]{1,0:T(8,128)(2,1)} %q_in.1, bf16[64,2048]{1,0:T(8,128)(2,1)} %k_in.1, bf16[64,4096]{1,0:T(8,128)(2,1)} %v_in.1, bf16[32,64]{1,0:T(8,128)(2,1)} %bitcast.4, bf16[32,64]{1,0:T(8,128)(2,1)} %bitcast.5), custom_call_target="tpu_custom_call" | custom-call | flops 1048576 | bytes 2097152 | tf_op jit(solution)/shard_map/pallas_call | solution.py:729
  1.3 0.0 copy-start.2
  1.4 0.0 copy-start.5
  1.4 0.0 copy-start.6
  1.4 22.7 %all_to_all.10.recv_ref = bf16[16,264,128]{2,1,0:T(8,128)(2,1)S(1)} all-to-all(bf16[16,264,128]{2,1,0:T(8,128)(2,1)S(1)} %shard_map.118), channel_id=1, replica_groups=mesh['half'=2,'sub'=4,'head'=4] {'sub','head'}, dimensions={0} | all-to-all | bytes 2162688 | tf_op jit(solution)/shard_map/all_to_all | solution.py:736
  24.1 0.0 copy-done.2
  24.1 0.0 copy-done.5
  24.1 0.0 copy-done.6
  24.1 0.0 copy-start.1
  24.1 5.4 %shard_map.119 = (bf16[1024,128]{1,0:T(8,128)(2,1)S(1)}, bf16[8,128,128]{2,1,0:T(8,128)(2,1)S(1)}, bf16[2,8,2,128,128]{4,3,2,1,0:T(8,128)(2,1)S(1)}, bf16[2,8,12...) custom-call(bf16[16,264,128]{2,1,0:T(8,128)(2,1)S(1)} %all_to_all.10, ...), custom_call_target="tpu_custom_call" | custom-call | flops 4294967296 | bytes 2097152 | tf_op jit(solution)/shard_map/pallas_call | solution.py:737
  29.6 0.0 copy-done.1
  29.6 0.0 copy-start.3
  29.6 2.3 %shard_map.120 = (bf16[272,128]{1,0:T(8,128)(2,1)S(1)}, bf16[2,1024,128]{2,1,0:T(8,128)(2,1)S(1)}, bf16[2,8,256,128]{3,2,1,0:T(8,128)(2,1)S(1)}, f32[2,8,128,128]{3,2,1,0:T(8,128)S(1)}) custom-call(bf16[16,264,128]{2,1,0:T(8,128)(2,1)S(1)} %all_to_all.10.recv_ref, f32[4,1024]{1,0:T(4,128)S(1)} %copy-done.1, ...), custom_call_target="tpu_custom_call" | custom-call | flops 4294967296 | bytes 2097152 | tf_op jit(solution)/shard_map/pallas_call | solution.py:763
  32.0 2.2 %collective-permute-start = (bf16[272,128]{1,0:T(8,128)(2,1)S(1)}, bf16[272,128]{1,0:T(8,128)(2,1)S(1)}, u32[]{:S(2)}, u32[]{:S(2)}) collective-permute-start(bf16[272,128]{1,0:T(8,128)(2,1)S(1)} %get-tuple-element.24.hop_ref), channel_id=1, source_target_pairs={{0,16},{1,17},{2,18},{3,19},{4,20},{5,21},{6,22},{7,23},{8,24},{9,... | collective-permute-start | bytes 208904 | tf_op jit(solution)/shard_map/ppermute | solution.py:775
  34.1 0.0 copy-done.3
  34.2 0.0 copy-start.4
  34.2 2.3 %shard_map.121 = (f32[2,1024,128]{2,1,0:T(8,128)S(1)}, bf16[2,1024,128]{2,1,0:T(8,128)(2,1)S(1)}, f32[2,128,256]{2,1,0:T(8,128)}) custom-call(bf16[16,264,128]{2,1,0:T(8,128)(2,1)S(1)} %all_to_all.10.recv_ref, f32[4,512]{1,0:T(4,128)S(1)} %copy-done.3, f32[4,1024]{1,0:T(4,128)S(1)} %copy-done.1, bf16[1024,128]{1,0:T(8,128)(2,1)S(1)} %get-tuple-element.26.keys_ref, ...), custom_call_target="tpu_custom_call" | custom-call | flops 4294967296 | bytes 2097152 | tf_op jit(solution)/shard_map/pallas_call | solution.py:777
  36.5 0.0 collective-permute-done.hop_ref
  36.5 0.0 copy-done.4
  36.5 0.4 shard_map.122
  36.9 0.0 copy-start
  36.9 13.4 %all_to_all.11.normed_ref = bf16[16,128,128]{2,1,0:T(8,128)(2,1)S(1)} all-to-all(bf16[16,128,128]{2,1,0:T(8,128)(2,1)S(1)} %shard_map.122), channel_id=1, replica_groups=mesh['half'=2,'sub'=4,'head'=4] {'sub','head'}, dimensions={0} | all-to-all | bytes 1048576 | tf_op jit(solution)/shard_map/all_to_all | solution.py:834
  50.3 0.0 copy-done
  50.3 1.0 %shard_map.123 = bf16[64,4096]{1,0:T(8,128)(2,1)} custom-call(bf16[16,128,128]{2,1,0:T(8,128)(2,1)S(1)} %all_to_all.11.normed_ref, bf16[64,4096]{1,0:T(8,128)(2,1)S(1)} %copy-done), custom_call_target="tpu_custom_call" | custom-call | flops 67108864 | bytes 2097152 | tf_op jit(solution)/shard_map/pallas_call | solution.py:835
Async XLA Ops:
  1.3 22.8 %copy-start.2 = (f32[4,512]{1,0:T(4,128)S(1)}, f32[4,512]{1,0:T(4,128)}, u32[]{:S(2)}) copy-start(f32[4,512]{1,0:T(4,128)} %ck_ref.3) | copy-start | bytes 24580
  1.4 22.8 %copy-start.5 = (f32[8]{0:T(128)S(1)}, f32[8]{0:T(128)}, u32[]{:S(2)}) copy-start(f32[8]{0:T(128)} %alog_ref.1) | copy-start | bytes 100
  1.4 22.8 %copy-start.6 = (f32[8]{0:T(128)S(1)}, f32[8]{0:T(128)}, u32[]{:S(2)}) copy-start(f32[8]{0:T(128)} %dt_ref.1) | copy-start | bytes 100
  24.1 5.5 %copy-start.1 = (f32[4,1024]{1,0:T(4,128)S(1)}, f32[4,1024]{1,0:T(4,128)}, u32[]{:S(2)}) copy-start(f32[4,1024]{1,0:T(4,128)} %cv_ref.5) | copy-start | bytes 49156
  29.6 4.6 %copy-start.3 = (f32[4,512]{1,0:T(4,128)S(1)}, f32[4,512]{1,0:T(4,128)}, u32[]{:S(2)}) copy-start(f32[4,512]{1,0:T(4,128)} %cq_ref.3) | copy-start | bytes 24580
  32.0 4.6 %collective-permute-start = (bf16[272,128]{1,0:T(8,128)(2,1)S(1)}, bf16[272,128]{1,0:T(8,128)(2,1)S(1)}, u32[]{:S(2)}, u32[]{:S(2)}) collective-permute-start(bf16[272,128]{1,0:T(8,128)(2,1)S(1)} %get-tuple-element.24.hop_ref), channel_id=1, source_target_pairs={{0,16},{1,17},{2,18},{3,19},{4,20},{5,21},{6,22},{7,23},{8,24},{9,... | collective-permute-start | bytes 208904 | tf_op jit(solution)/shard_map/ppermute | solution.py:775
  34.2 2.4 %copy-start.4 = (f32[128]{0:T(128)S(1)}, f32[128]{0:T(128)}, u32[]{:S(2)}) copy-start(f32[128]{0:T(128)} %param.23) | copy-start | bytes 1540
  36.9 13.4 %copy-start = (bf16[64,4096]{1,0:T(8,128)(2,1)S(1)}, bf16[64,4096]{1,0:T(8,128)(2,1)}, u32[]{:S(2)}) copy-start(bf16[64,4096]{1,0:T(8,128)(2,1)} %z_ref.1) | copy-start | bytes 1572868

commit v14 on v11

--- a/solution.py
+++ b/solution.py
@@ -13,7 +13,6 @@
 KH = 16
 SUB = 16
 SPAN = 128
-GROUP = 4
 EDGE = CONV - 1
 EPS = 1e-06
 F32 = jnp.float32
@@ -103,47 +102,35 @@
     laid(q_ref, lambda key_head: key_head, 3)
 
 
-def invert(systems):
-    size = systems[0].shape[0]
-    blocks = size // SUB
-    row, col = iota((size, size), 0), iota((size, size), 1)
-    diagonal = block_of(row, SUB) == block_of(col, SUB)
-    compact = jnp.concatenate(
-        [
-            jnp.sum(jnp.where(diagonal, n, 0.0).reshape(blocks, SUB, size), axis=0)
-            for n in systems
-        ],
-        axis=0,
-    )
-    count = len(systems)
-    lane, line = iota(compact.shape, 1), iota(compact.shape, 0)
+def compacted(system):
+    size = system.shape[0]
+    diagonal = block_of(iota((size, size), 0), SUB) == block_of(iota((size, size), 1), SUB)
+    return jnp.sum(jnp.where(diagonal, system, 0.0).reshape(size // SUB, SUB, size), axis=0)
+
+
+def substituted(compact):
+    count, _, size = compact.shape
+    flat = compact.reshape(count * SUB, size)
+    lane, line = iota(flat.shape, 1), iota(flat.shape, 0)
     solved = jnp.where(place_in(lane ^ line, SUB) == 0, 1.0, 0.0).reshape(count, SUB, size)
     for m in range(SUB - 1):
         source = (lane & ~(SUB - 1)) | m
-        spread = jnp.take_along_axis(compact, source, axis=1, mode="promise_in_bounds")
-        solved = solved - spread.reshape(count, SUB, size) * solved[:, m : m + 1, :]
-    lows = [halves(n) for n in systems]
-    placed = jnp.where(diagonal, 1.0, 0.0).astype(BF16)
+        spread = jnp.take_along_axis(flat, source, axis=1, mode="promise_in_bounds")
+        solved = solved + spread.reshape(count, SUB, size) * solved[:, m : m + 1, :]
+    return solved
+
+
+def inverted(systems, small):
+    size = systems[0][0].shape[0]
+    row, col = iota((size, size), 0), iota((size, size), 1)
+    placed = jnp.where(block_of(row, SUB) == block_of(col, SUB), 1.0, 0.0).astype(BF16)
     parts = [
-        tuple(jnp.concatenate([x] * blocks, axis=0) * placed for x in halves(solved[i]))
-        for i in range(count)
+        tuple(jnp.concatenate([x] * (size // SUB), axis=0) * placed for x in halves(block))
+        for block in small
     ]
-    levels = []
+    blank = jnp.zeros((size, size), BF16)
     width = SUB
     while width < size:
-        below = (block_of(row ^ col, 2 * width) == 0) & ((col & width) == 0)
-        levels.append((width, jnp.where(below, 1.0, 0.0).astype(BF16)))
-        width *= 2
-    grown = []
-    for i in range(0, count, GROUP):
-        grown += doubled(lows[i : i + GROUP], parts[i : i + GROUP], levels)
-    return grown
-
-
-def doubled(lows, parts, levels):
-    size = levels[0][1].shape[0]
-    blank = jnp.zeros((size, size), BF16)
-    for width, below in levels:
         odd = [(j, j + width) for j in range(width, size, 2 * width)]
 
         def rows_of(x):
@@ -155,17 +142,19 @@
                 pieces += [even[lo - width : lo], x[j * width : (j + 1) * width]]
             return jnp.concatenate(pieces, axis=0)
 
-        mask = rows_of(below)
+        below = rows_of(block_of(row ^ col, 2 * width)) + rows_of(col & width) == 0
+        identity = rows_of(jnp.where(row == col, 1.0, 0.0))
         firsts = [
-            mm_parts((rows_of(n[0]) * mask, rows_of(n[1]) * mask), t) for n, t in zip(lows, parts)
+            mm_parts((rows_of(n[0]), rows_of(n[1])), t) for n, t in zip(systems, parts)
         ]
-        spreads = [tuple(woven(blank, x) for x in halves(first)) for first in firsts]
+        rights = [
+            tuple(woven(blank, x) for x in halves(jnp.where(below, first, identity)))
+            for first in firsts
+        ]
         odds = [(rows_of(t[0]), rows_of(t[1])) for t in parts]
-        seconds = [halves(-mm_parts(o, spread)) for o, spread in zip(odds, spreads)]
-        parts = [
-            tuple(woven(t[i], o[i] + second[i]) for i in range(2))
-            for t, o, second in zip(parts, odds, seconds)
-        ]
+        grown = [halves(mm_parts(o, right)) for o, right in zip(odds, rights)]
+        parts = [tuple(woven(t[i], g[i]) for i in range(2)) for t, g in zip(parts, grown)]
+        width *= 2
     return parts
 
 
@@ -203,15 +192,15 @@
             ].astype(F32)
 
 
-def keys_kernel(
+def systems_kernel(
     recv_ref,
     ck_ref,
     alog_ref,
     dt_ref,
     keys_ref,
     keys_t_ref,
-    t_ref,
-    lin_ref,
+    systems_ref,
+    small_ref,
     ends_ref,
     within_ref,
     cols_ref,
@@ -262,32 +251,48 @@
         keys_t_ref[n] = kt_n
         keys_t.append(kt_n)
     grams = [dot(keys[n], keys_t[n]) for n in range(spans)]
-    systems = []
     for n, r in both:
         at = GATES * n + r
         gap = columns[:, at : at + 1] - cum[at : at + 1, :]
         within = jnp.exp(jnp.where(lower, gap, 0.0)) * here[at : at + 1, :]
         within_ref[r, n * SPAN : (n + 1) * SPAN, :] = jnp.where(lower, within, 0.0).astype(BF16)
-        systems.append(jnp.where(strict, within * grams[n], 0.0))
-    inverses = invert(systems)
-    for i, (n, r) in enumerate(both):
-        t_ref[r, n, 0], t_ref[r, n, 1] = inverses[i]
-    scaled = []
-    for n, r in both:
-        at = GATES * n + r
-        right = (columns[:, at + 2 : at + 3] * keys[n].astype(F32)).astype(BF16)
-        scaled.append(jnp.concatenate([right, right], axis=0))
-    w_mats = [dot(jnp.concatenate(t, axis=1), x) for t, x in zip(inverses, scaled)]
-    weighed = []
-    for (n, r), w_mat in zip(both, w_mats):
-        at = GATES * n + r
-        weighed.append((columns[:, at + 4 : at + 5] * w_mat).astype(BF16))
-    moved = [
-        dot(keys_t[n], jnp.concatenate(weighed[2 * n : 2 * n + 2], axis=1)) for n in range(spans)
-    ]
+        system = jnp.where(strict, within * -grams[n], 0.0)
+        systems_ref[r, n, 0], systems_ref[r, n, 1] = halves(system)
+        small_ref[r, n] = compacted(system)
     ends_ref[...] = jnp.broadcast_to(growth[:, SPAN - 1 :], ends_ref.shape)
-    for n, r in both:
-        lin_ref[r, n] = moved[n][:, r * DK : (r + 1) * DK].astype(BF16)
+
+
+def inverse_kernel(
+    on_first, hop_ref, keys_ref, keys_t_ref, systems_ref, small_ref, cols_ref, t_ref, lin_ref
+):
+    del hop_ref
+    spans = keys_t_ref.shape[0]
+    both = [(n, r) for n in range(spans) for r in range(2)]
+
+    @pl.when((lax.axis_index("half") == 0) == on_first)
+    def _():
+        compact = jnp.concatenate([small_ref[r, n] for n, r in both], axis=0)
+        small = substituted(compact.reshape(len(both), SUB, SPAN))
+        systems = [(systems_ref[r, n, 0], systems_ref[r, n, 1]) for n, r in both]
+        inverses = inverted(systems, [small[i] for i in range(len(both))])
+        scaled = []
+        for i, (n, r) in enumerate(both):
+            t_ref[r, n, 0], t_ref[r, n, 1] = inverses[i]
+            at = GATES * n + r
+            key = keys_ref[n * SPAN : (n + 1) * SPAN, :].astype(F32)
+            right = (cols_ref[:, at + 2 : at + 3] * key).astype(BF16)
+            scaled.append(jnp.concatenate([right, right], axis=0))
+        w_mats = [dot(jnp.concatenate(t, axis=1), x) for t, x in zip(inverses, scaled)]
+        weighed = []
+        for (n, r), w_mat in zip(both, w_mats):
+            at = GATES * n + r
+            weighed.append((cols_ref[:, at + 4 : at + 5] * w_mat).astype(BF16))
+        moved = [
+            dot(keys_t_ref[n], jnp.concatenate(weighed[2 * n : 2 * n + 2], axis=1))
+            for n in range(spans)
+        ]
+        for n, r in both:
+            lin_ref[r, n] = moved[n][:, r * DK : (r + 1) * DK].astype(BF16)
 
 
 def unwound(t_ref, n, r, x):
@@ -395,10 +400,76 @@
         hop_ref[0 : 2 * DK, :] = jnp.zeros((2 * DK, DV), BF16)
 
 
-def output_kernel(
+def states_kernel(
+    recv_ref,
+    cv_ref,
+    keys_t_ref,
+    t_ref,
+    lin_ref,
+    ends_ref,
+    cols_ref,
+    values_ref,
+    states_ref,
+    last_ref,
+    rows,
+):
+    @pl.when(lax.axis_index("half") > 0)
+    def _():
+        spans = t_ref.shape[1]
+        adds = values_part(recv_ref, cv_ref, keys_t_ref, t_ref, cols_ref, rows, values_ref)
+        zero_half = jnp.zeros((DK, DV), F32)
+        identity = jnp.where(iota((DK, DK), 0) == iota((DK, DK), 1), 1.0, 0.0)
+        states = [
+            jnp.concatenate(
+                [adds[r], ends_ref[r : r + 1, :] * identity - lin_ref[r, 0].astype(F32)], axis=1
+            )
+            for r in range(2)
+        ]
+        for n in range(1, spans):
+            for r in range(2):
+                parts = halves(states[r])
+                for i in range(2):
+                    both_parts = [x[:, i * DV : (i + 1) * DV] for x in parts]
+                    states_ref[i, r, n] = jnp.concatenate(both_parts, axis=0)
+                add = jnp.concatenate([adds[2 * n + r], zero_half], axis=1)
+                end = jnp.concatenate([end_of(ends_ref, n, r)] * 2, axis=1)
+                states[r] = step(end, lin_ref[r, n], states[r], parts) + add
+        for r in range(2):
+            last_ref[r] = states[r]
+
+
+def span_rows(n):
+    return slice(n * SPAN, (n + 1) * SPAN)
+
+
+def twice(x, axis):
+    return jnp.concatenate([x, x], axis=axis)
+
+
+def asked(recv_ref, cq_ref, keys_ref, keys_t_ref, within_ref, query_rows):
+    tokens = (recv_ref.shape[1] - GATES) // 4
+    spans = keys_t_ref.shape[0]
+    tap = key_tap(lax.axis_index("sub"), cq_ref)
+    widened(query_rows, recv_ref, [3 * tokens], tokens)
+    queries = [
+        unit(convolved(query_rows, n * SPAN + 8 - EDGE, SPAN, slice(0, DK), tap), DK**-0.5)
+        for n in range(spans)
+    ]
+    readers = [
+        jnp.concatenate([keys_ref[span_rows(n), :], queries[n]], axis=0) for n in range(spans)
+    ]
+    scores = [dot(queries[n], keys_t_ref[n]) for n in range(spans)]
+    inner = [
+        (within_ref[r, span_rows(n), :].astype(F32) * scores[n]).astype(BF16)
+        for n in range(spans)
+        for r in range(2)
+    ]
+    return readers, inner
+
+
+def first_outputs_kernel(
     recv_ref,
     cq_ref,
-    cv_ref,
     keys_ref,
     keys_t_ref,
     t_ref,
@@ -406,53 +477,17 @@
     ends_ref,
     within_ref,
     cols_ref,
-    hop_ref,
-    vs_ref,
+    values_ref,
     xs_ref,
     adds_ref,
     oa_ref,
-    om_ref,
-    last_ref,
-    rows,
     query_rows,
-    values,
-    inner,
-    readers,
-    states_ref,
-):
-    sub = lax.axis_index("sub")
-    first = lax.axis_index("half") == 0
-    tokens = (recv_ref.shape[1] - GATES) // 4
-    spans = t_ref.shape[1]
-    both = [(n, r) for n in range(spans) for r in range(2)]
-    tap = key_tap(sub, cq_ref)
-    widened(query_rows, recv_ref, [3 * tokens], tokens)
-
-    def span_rows(n):
-        return slice(n * SPAN, (n + 1) * SPAN)
-
-    def growth(n, r):
-        return cols_ref[:, GATES * n + 2 + r : GATES * n + 3 + r]
-
-    def prepare():
-        queries = []
-        for n in range(spans):
-            at = n * SPAN + 8 - EDGE
-            q_n = unit(convolved(query_rows, at, SPAN, slice(0, DK), tap), DK**-0.5)
-            queries.append(q_n)
-            readers[n, 0:SPAN, :] = keys_ref[span_rows(n), :]
-            readers[n, SPAN:, :] = q_n
-        scores = [dot(queries[n], keys_t_ref[n]) for n in range(spans)]
-        for n, r in both:
-            weight = within_ref[r, span_rows(n), :].astype(F32)
-            inner[r, n] = (weight * scores[n]).astype(BF16)
-
-    def twice(x, axis):
-        return jnp.concatenate([x, x], axis=axis)
-
-    @pl.when(first)
+):
+    @pl.when(lax.axis_index("half") == 0)
     def _():
-        prepare()
+        spans = t_ref.shape[1]
+        both = [(n, r) for n in range(spans) for r in range(2)]
+        readers, inner = asked(recv_ref, cq_ref, keys_ref, keys_t_ref, within_ref, query_rows)
         stacks, states = [], []
         for n in range(1, spans):
             if n == 1:
@@ -475,45 +510,41 @@
         rests, seen = [], []
         for n, r in both:
             lanes = slice(r * DV, (r + 1) * DV)
-            value = vs_ref[r, span_rows(n), :]
+            value = values_ref[r, span_rows(n), :]
             if n == 0:
                 rests.append(value)
                 seen.append(None)
             else:
-                read = growth(n, r) * reads[n - 1][:SPAN, lanes]
+                growth = cols_ref[:, GATES * n + 2 + r : GATES * n + 3 + r]
+                read = growth * reads[n - 1][:SPAN, lanes]
                 rests.append((value.astype(F32) - read).astype(BF16))
-                seen.append(growth(n, r) * reads[n - 1][SPAN:, lanes])
+                seen.append(growth * reads[n - 1][SPAN:, lanes])
         fresh = [unwound(t_ref, n, r, x).astype(BF16) for (n, r), x in zip(both, rests)]
-        spreads = [dot(inner[r, n], x) for (n, r), x in zip(both, fresh)]
+        spreads = [dot(w, x) for w, x in zip(inner, fresh)]
         for (n, r), x, y in zip(both, spreads, seen):
             oa_ref[r, span_rows(n), :] = x if y is None else x + y
-        for r in range(2):
-            last_ref[r, :, 0:DV] = hop_ref[r * DK : (r + 1) * DK, :].astype(F32)
-            last_ref[r, :, DV:] = jnp.zeros((DK, DV), F32)
-
-    @pl.when(jnp.logical_not(first))
+
+
+def later_outputs_kernel(
+    recv_ref,
+    cq_ref,
+    keys_ref,
+    keys_t_ref,
+    t_ref,
+    within_ref,
+    cols_ref,
+    values_ref,
+    states_ref,
+    oa_ref,
+    om_ref,
+    query_rows,
+):
+    @pl.when(lax.axis_index("half") > 0)
     def _():
-        adds = values_part(recv_ref, cv_ref, keys_t_ref, t_ref, cols_ref, rows, values)
-        zero_half = jnp.zeros((DK, DV), F32)
-        identity = jnp.where(iota((DK, DK), 0) == iota((DK, DK), 1), 1.0, 0.0)
-        states = [
-            jnp.concatenate(
-                [adds[r], ends_ref[r : r + 1, :] * identity - lin_ref[r, 0].astype(F32)], axis=1
-            )
-            for r in range(2)
-        ]
-        for n in range(1, spans):
-            for r in range(2):
-                parts = halves(states[r])
-                for i in range(2):
-                    both_parts = [x[:, i * DV : (i + 1) * DV] for x in parts]
-                    states_ref[i, r, n] = jnp.concatenate(both_parts, axis=0)
-                add = jnp.concatenate([adds[2 * n + r], zero_half], axis=1)
-                end = jnp.concatenate([end_of(ends_ref, n, r)] * 2, axis=1)
-                states[r] = step(end, lin_ref[r, n], states[r], parts) + add
-        for r in range(2):
-            last_ref[r] = states[r]
-        prepare()
+        spans = t_ref.shape[1]
+        both = [(n, r) for n in range(spans) for r in range(2)]
+        readers, inner = asked(recv_ref, cq_ref, keys_ref, keys_t_ref, within_ref, query_rows)
+        zero_half = jnp.zeros((SPAN, DV), F32)
         reads = [
             dot(
                 twice(readers[n], 1),
@@ -525,18 +556,18 @@
         ]
         rests, seen = [], []
         for (n, r), read in zip(both, reads):
-            value = values[r, span_rows(n), :].astype(F32)
+            value = values_ref[r, span_rows(n), :].astype(F32)
+            growth = cols_ref[:, GATES * n + 2 + r : GATES * n + 3 + r]
             if n == 0:
-                known = growth(n, r) * readers[n].astype(F32)[:SPAN]
-                asked = growth(n, r) * readers[n].astype(F32)[SPAN:]
-                rest = jnp.concatenate([value, -known], axis=1)
-                seen.append(jnp.concatenate([zero_half, asked], axis=1))
+                reader = readers[n].astype(F32)
+                rest = jnp.concatenate([value, -(growth * reader[:SPAN])], axis=1)
+                seen.append(jnp.concatenate([zero_half, growth * reader[SPAN:]], axis=1))
             else:
-                rest = jnp.concatenate([value, zero_half], axis=1) - growth(n, r) * read[:SPAN]
-                seen.append(growth(n, r) * read[SPAN:])
+                rest = jnp.concatenate([value, zero_half], axis=1) - growth * read[:SPAN]
+                seen.append(growth * read[SPAN:])
             rests.append(rest.astype(BF16))
         fresh = [unwound(t_ref, n, r, x).astype(BF16) for (n, r), x in zip(both, rests)]
-        spreads = [dot(inner[r, n], x) for (n, r), x in zip(both, fresh)]
+        spreads = [dot(w, x) for w, x in zip(inner, fresh)]
         for (n, r), x, y in zip(both, spreads, seen):
             out = x + y
             oa_ref[r, span_rows(n), :] = out[:, :DV]
@@ -578,7 +609,18 @@
 
 
 def finish_kernel(
-    hop_ref, recv_ref, early_ref, cq_ref, ck_ref, cv_ref, gain_ref, oa_ref, om_ref, out_ref, rows
+    hop_ref,
+    recv_ref,
+    early_ref,
+    cq_ref,
+    ck_ref,
+    cv_ref,
+    gain_ref,
+    first_oa,
+    oa_ref,
+    om_ref,
+    out_ref,
+    rows,
 ):
     peers, tokens = out_ref.shape[0], out_ref.shape[1] // 2
     first = lax.axis_index("half") == 0
@@ -596,7 +638,7 @@
     def _():
         for c in range(chunks):
             for r in range(2):
-                put(c, r, oa_ref[r, c * part : (c + 1) * part, :])
+                put(c, r, first_oa[r, c * part : (c + 1) * part, :])
 
     @pl.when(jnp.logical_not(first))
     def _():
@@ -622,7 +664,8 @@
     for r in range(2):
         last = last_ref[r]
         through = mm_parts(halves(last[:, DV:]), halves(finals[r]))
-        moved = jnp.where(first, 0.0, through) + last[:, :DV]
+        own = hop_own[r * DK : (r + 1) * DK, :].astype(F32)
+        moved = jnp.where(first, own, through + last[:, :DV])
         next_ref[r * DK : (r + 1) * DK, :] = moved.astype(BF16)
     next_ref[2 * DK :, :] = hop_own[2 * DK :, :]
 
@@ -701,13 +744,13 @@
         flops=1 << 20,
     )(*inputs)
     blocks = near(lax.all_to_all(packed, group, 0, 0, tiled=True))
-    keys, keys_t, inverses, lins, ends, within, cols, early = call(
-        keys_kernel,
+    made = call(
+        systems_kernel,
         (
             pltpu.VMEM((total, DK), BF16),
             pltpu.VMEM((spans, DK, SPAN), BF16),
             pltpu.VMEM((2, spans, 2, SPAN, SPAN), BF16),
-            pltpu.VMEM((2, spans, DK, DK), BF16),
+            pltpu.VMEM((2, spans, SUB, SPAN), F32),
             pltpu.VMEM((SPAN, DK), F32),
             pltpu.VMEM((2, total, SPAN), BF16),
             pltpu.VMEM((SPAN, SPAN), F32),
@@ -717,9 +760,19 @@
         [pltpu.VMEM((8 + total, DK), F32)],
         flops=1 << 32,
     )(blocks, conv_k, a_log, dt_bias)
-    keys, keys_t, inverses, lins, ends, within, cols, early = (
-        near(x) for x in (keys, keys_t, inverses, lins, ends, within, cols, early)
+    keys, keys_t, systems, small, ends, within, cols, early = (near(x) for x in made)
+    map_shapes = (
+        pltpu.VMEM((2, spans, 2, SPAN, SPAN), BF16),
+        pltpu.VMEM((2, spans, DK, DK), BF16),
     )
+
+    def inverses_of(on_first, after):
+        solved = call(
+            functools.partial(inverse_kernel, on_first), map_shapes, [VMEM] * 6, flops=1 << 32
+        )(after, keys, keys_t, systems, small, cols)
+        return [near(x) for x in solved]
+
+    inverses, lins = inverses_of(True, early)
     hop, values, starts, adds = call(
         opening_kernel,
         (
@@ -734,27 +787,15 @@
     )(blocks, conv_v, keys_t, inverses, lins, ends, cols)
     entering = near(lax.ppermute(hop, "half", route))
     hop, values, starts, adds = (near(x) for x in (hop, values, starts, adds))
-    out_a, out_m, last = call(
-        output_kernel,
-        (
-            pltpu.VMEM((2, total, DV), F32),
-            pltpu.VMEM((2, total, DV), BF16),
-            pltpu.VMEM((2, DK, 2 * DV), F32),
-        ),
-        [VMEM] * 14,
-        [
-            pltpu.VMEM((8 + total, 2 * DV), F32),
-            pltpu.VMEM((8 + total, DK), F32),
-            pltpu.VMEM((2, total, DV), BF16),
-            pltpu.VMEM((2, spans, SPAN, SPAN), BF16),
-            pltpu.VMEM((spans, 2 * SPAN, DK), BF16),
-            pltpu.VMEM((2, 2, spans, 2 * DK, DV), BF16),
-        ],
+    first_out = call(
+        first_outputs_kernel,
+        pltpu.VMEM((2, total, DV), F32),
+        [VMEM] * 12,
+        [pltpu.VMEM((8 + total, DK), F32)],
         flops=1 << 32,
     )(
         blocks,
         conv_q,
-        conv_v,
         keys,
         keys_t,
         inverses,
@@ -762,10 +803,38 @@
         ends,
         within,
         cols,
-        hop,
         values,
         starts,
         adds,
+    )
+    later_inverses, later_lins = inverses_of(False, hop)
+    later_values, states, last = call(
+        states_kernel,
+        (
+            pltpu.VMEM((2, total, DV), BF16),
+            pltpu.VMEM((2, 2, spans, 2 * DK, DV), BF16),
+            pltpu.VMEM((2, DK, 2 * DV), F32),
+        ),
+        [VMEM] * 7,
+        [pltpu.VMEM((8 + total, 2 * DV), F32)],
+        flops=1 << 32,
+    )(blocks, conv_v, keys_t, later_inverses, later_lins, ends, cols)
+    out_a, out_m = call(
+        later_outputs_kernel,
+        (pltpu.VMEM((2, total, DV), F32), pltpu.VMEM((2, total, DV), BF16)),
+        [VMEM] * 9,
+        [pltpu.VMEM((8 + total, DK), F32)],
+        flops=1 << 32,
+    )(
+        blocks,
+        conv_q,
+        keys,
+        keys_t,
+        later_inverses,
+        within,
+        cols,
+        near(later_values),
+        near(states),
     )
     for _ in range(shards - 2):
         moved = call(
@@ -778,7 +847,7 @@
     normed = call(
         finish_kernel,
         pltpu.VMEM((peers, 2 * tokens, DV), BF16),
-        [VMEM] * 9,
+        [VMEM] * 10,
         [pltpu.VMEM((32, 512), F32)],
     )(
         entering,
@@ -788,6 +857,7 @@
         conv_k,
         conv_v,
         norm_gain.reshape(1, DV),
+        near(first_out),
         near(out_a),
         near(out_m),
     )

time: 52.3 us -> 51.9 us (level)
  the two profiles are of different devices: /device:TPU:0 before, /device:TPU:16 now
where the time goes in v14:
time: 51.9 us; the launch traced here: 51.6 us
  blocking collectives  34.6 us (67%)
  Pallas kernels  14.1 us (27%)
  local copies, waits for them, and re-layouts  1.33 us (3%)
  starting transfers between devices  1.29 us (2%)
    all_to_all x1, blocking collectives, local(): blocks = near(lax.all_to_all(packed, group, 0, 0, tiled=True))  21.3 us
    all_to_all x1, blocking collectives, local(): returned = near(lax.all_to_all(normed, group, 0, 0, tiled=True))  13.3 us
    pallas_call x1, Pallas kernels, local(): call(states_kernel, (pltpu.VMEM((2, total, DV), BF16), pltpu.VMEM((2, 2,...  3.75 us
    pallas_call x2, Pallas kernels, inverses_of(): call(functools.partial(inverse_kernel, on_first), map_shapes, [VMEM] * 6,...  3.53 us
    pallas_call x1, Pallas kernels, local(): call(systems_kernel, (pltpu.VMEM((total, DK), BF16), pltpu.VMEM((spans, D...  1.87 us
    pallas_call x1, Pallas kernels, local(): call(later_outputs_kernel, (pltpu.VMEM((2, total, DV), F32), pltpu.VMEM((...  1.63 us
    pallas_call x1, Pallas kernels, local(): call(functools.partial(pack_kernel, heads_axis), pltpu.VMEM((peers, GATES...  1.34 us
    unnamed x14, local copies, waits for them, and re-layouts  1.33 us
  transfers between devices with their start and end apart: 1, of which 0 were waited for; matrix products, arithmetic and copies ran while one was open for 0% of the time, Pallas kernels for 17%

profile of v14, /device:TPU:16, one launch (start us, length us, event | category | flops | bytes accessed | tf_op | source)
XLA Modules:
  0.0 51.6 jit_solution(777886385038082698)
XLA Ops:
  0.0 1.3 %shard_map.118 = bf16[16,264,128]{2,1,0:T(8,128)(2,1)S(1)} custom-call(bf16[64,2048]{1,0:T(8,128)(2,1)} %q_in.1, bf16[64,2048]{1,0:T(8,128)(2,1)} %k_in.1, bf16[64,4096]{1,0:T(8,128)(2,1)} %v_in.1, bf16[32,64]{1,0:T(8,128)(2,1)} %bitcast.4, bf16[32,64]{1,0:T(8,128)(2,1)} %bitcast.5), custom_call_target="tpu_custom_call" | custom-call | flops 1048576 | bytes 2097152 | tf_op jit(solution)/shard_map/pallas_call | solution.py:739
  1.3 0.0 copy-start.2
  1.4 0.0 copy-start.5
  1.4 0.0 copy-start.6
  1.4 21.3 %all_to_all.10.recv_ref = bf16[16,264,128]{2,1,0:T(8,128)(2,1)S(1)} all-to-all(bf16[16,264,128]{2,1,0:T(8,128)(2,1)S(1)} %shard_map.118), channel_id=1, replica_groups=mesh['half'=2,'sub'=4,'head'=4] {'sub','head'}, dimensions={0} | all-to-all | bytes 2162688 | tf_op jit(solution)/shard_map/all_to_all | solution.py:746
  22.7 0.0 copy-done.2
  22.7 0.0 copy-done.5
  22.7 0.0 copy-done.6
  22.7 1.9 %shard_map.119 = (bf16[1024,128]{1,0:T(8,128)(2,1)S(1)}, bf16[8,128,128]{2,1,0:T(8,128)(2,1)S(1)}, bf16[2,8,2,128,128]{4,3,2,1,0:T(8,128)(2,1)S(1)}, f32[2,8,16,...) custom-call(bf16[16,264,128]{2,1,0:T(8,128)(2,1)S(1)} %all_to_all.10, ...), custom_call_target="tpu_custom_call" | custom-call | flops 4294967296 | bytes 2097152 | tf_op jit(solution)/shard_map/pallas_call | solution.py:747
  24.6 0.0 copy-start.1
  24.6 0.7 %copy-done.1 = f32[4,1024]{1,0:T(4,128)S(1)} copy-done((f32[4,1024]{1,0:T(4,128)S(1)}, f32[4,1024]{1,0:T(4,128)}, u32[]{:S(2)}) %copy-start.1) | copy-done | bytes 16408
  25.3 1.3 %collective-permute-start = (bf16[272,128]{1,0:T(8,128)(2,1)S(1)}, bf16[272,128]{1,0:T(8,128)(2,1)S(1)}, u32[]{:S(2)}, u32[]{:S(2)}) collective-permute-start(bf16[272,128]{1,0:T(8,128)(2,1)S(1)} %get-tuple-element.34.hop_ref), channel_id=1, source_target_pairs={{0,16},{1,17},{2,18},{3,19},{4,20},{5,21},{6,22},{7,23},{8,24},{9,... | collective-permute-start | bytes 208904 | tf_op jit(solution)/shard_map/ppermute | solution.py:788
  26.6 3.5 %shard_map.123 = (bf16[2,8,2,128,128]{4,3,2,1,0:T(8,128)(2,1)S(1)}, bf16[2,8,128,128]{3,2,1,0:T(8,128)(2,1)S(1)}) custom-call(bf16[272,128]{1,0:T(8,128)(2,1)S(1)} %get-tuple-element.34.hop_ref, bf16[1024,128]{1,0:T(8,128)(2,1)S(1)} %get-tuple-element.27.keys_ref, bf16[8,128,128]{2,1,0:T(8,128)(2,1)S(1)} %get-tuple-element.25.keys_t_ref, ...), custom_call_target="tpu_custom_call" | custom-call | flops 4294967296 | bytes 2097152 | tf_op jit(solution)/shard_map/pallas_call | solution.py:770
  30.1 0.0 copy-start.3
  30.1 3.7 %shard_map.124 = (bf16[2,1024,128]{2,1,0:T(8,128)(2,1)S(1)}, bf16[2,2,8,256,128]{4,3,2,1,0:T(8,128)(2,1)S(1)}, f32[2,128,256]{2,1,0:T(8,128)}) custom-call(bf16[16,264,128]{2,1,0:T(8,128)(2,1)S(1)} %all_to_all.10.recv_ref, f32[4,1024]{1,0:T(4,128)S(1)} %copy-done.1, bf16[8,128,128]{2,1,0:T(8,128)(2,1)S(1)} %get-tuple-element.25.keys_t_ref, ...), custom_call_target="tpu_custom_call" | custom-call | flops 4294967296 | bytes 2097152 | tf_op jit(solution)/shard_map/pallas_call | solution.py:811
  33.9 0.0 copy-done.3
  33.9 1.6 %shard_map.125 = (f32[2,1024,128]{2,1,0:T(8,128)S(1)}, bf16[2,1024,128]{2,1,0:T(8,128)(2,1)S(1)}) custom-call(bf16[16,264,128]{2,1,0:T(8,128)(2,1)S(1)} %all_to_all.10.recv_ref, f32[4,512]{1,0:T(4,128)S(1)} %copy-done.3, bf16[1024,128]{1,0:T(8,128)(2,1)S(1)} %get-tuple-element.27.keys_ref, bf16[8,128,128]{2,1,0:T(8,128)(2,1)S(1)} %get-tuple-element.25.keys_t_ref, ...), custom_call_target="tpu_custom_call" | custom-call | flops 4294967296 | bytes 2097152 | tf_op jit(solution)/shard_map/pallas_call | solution.py:822
  35.5 0.0 copy-start.4
  35.6 0.0 collective-permute-done.hop_ref
  35.6 0.6 %copy-done.4 = f32[128]{0:T(128)S(1)} copy-done((f32[128]{0:T(128)S(1)}, f32[128]{0:T(128)}, u32[]{:S(2)}) %copy-start.4) | copy-done | bytes 536
  36.2 0.9 %shard_map.126 = bf16[16,128,128]{2,1,0:T(8,128)(2,1)S(1)} custom-call(bf16[272,128]{1,0:T(8,128)(2,1)S(1)} %collective-permute-done.hop_ref, bf16[16,264,128]{2,1,0:T(8,128)(2,1)S(1)} %all_to_all.10.recv_ref, f32[8,128]{1,0:T(8,128)S(1)} %get-tuple-element.26.hop_ref.early_ref, f32[4,512]{1,0:T(4,128)S(1)} %copy-done.3, f32[4,512]{1,0:T(4,128)S(1)} %copy-done.2, ...), custom_call_target="tpu_custom_call" | custom-call | flops 67108864 | bytes 2097152 | tf_op jit(solution)/shard_map/pallas_call | solution.py:847
  37.1 0.0 copy-start
  37.1 13.3 %all_to_all.11.normed_ref = bf16[16,128,128]{2,1,0:T(8,128)(2,1)S(1)} all-to-all(bf16[16,128,128]{2,1,0:T(8,128)(2,1)S(1)} %shard_map.126), channel_id=1, replica_groups=mesh['half'=2,'sub'=4,'head'=4] {'sub','head'}, dimensions={0} | all-to-all | bytes 1048576 | tf_op jit(solution)/shard_map/all_to_all | solution.py:864
  50.4 0.0 copy-done
  50.4 1.0 %shard_map.127 = bf16[64,4096]{1,0:T(8,128)(2,1)} custom-call(bf16[16,128,128]{2,1,0:T(8,128)(2,1)S(1)} %all_to_all.11.normed_ref, bf16[64,4096]{1,0:T(8,128)(2,1)S(1)} %copy-done), custom_call_target="tpu_custom_call" | custom-call | flops 67108864 | bytes 2097152 | tf_op jit(solution)/shard_map/pallas_call | solution.py:865
  (3 shorter events, 0.1 us)
Async XLA Ops:
  1.3 21.3 %copy-start.2 = (f32[4,512]{1,0:T(4,128)S(1)}, f32[4,512]{1,0:T(4,128)}, u32[]{:S(2)}) copy-start(f32[4,512]{1,0:T(4,128)} %ck_ref.3) | copy-start | bytes 24580
  1.4 21.3 %copy-start.5 = (f32[8]{0:T(128)S(1)}, f32[8]{0:T(128)}, u32[]{:S(2)}) copy-start(f32[8]{0:T(128)} %alog_ref.1) | copy-start | bytes 100
  1.4 21.3 %copy-start.6 = (f32[8]{0:T(128)S(1)}, f32[8]{0:T(128)}, u32[]{:S(2)}) copy-start(f32[8]{0:T(128)} %dt_ref.1) | copy-start | bytes 100
  24.6 0.7 %copy-start.1 = (f32[4,1024]{1,0:T(4,128)S(1)}, f32[4,1024]{1,0:T(4,128)}, u32[]{:S(2)}) copy-start(f32[4,1024]{1,0:T(4,128)} %cv_ref.5) | copy-start | bytes 49156
  25.3 10.3 %collective-permute-start = (bf16[272,128]{1,0:T(8,128)(2,1)S(1)}, bf16[272,128]{1,0:T(8,128)(2,1)S(1)}, u32[]{:S(2)}, u32[]{:S(2)}) collective-permute-start(bf16[272,128]{1,0:T(8,128)(2,1)S(1)} %get-tuple-element.34.hop_ref), channel_id=1, source_target_pairs={{0,16},{1,17},{2,18},{3,19},{4,20},{5,21},{6,22},{7,23},{8,24},{9,... | collective-permute-start | bytes 208904 | tf_op jit(solution)/shard_map/ppermute | solution.py:788
  30.1 3.8 %copy-start.3 = (f32[4,512]{1,0:T(4,128)S(1)}, f32[4,512]{1,0:T(4,128)}, u32[]{:S(2)}) copy-start(f32[4,512]{1,0:T(4,128)} %cq_ref.5) | copy-start | bytes 24580
  35.5 0.7 %copy-start.4 = (f32[128]{0:T(128)S(1)}, f32[128]{0:T(128)}, u32[]{:S(2)}) copy-start(f32[128]{0:T(128)} %param.23) | copy-start | bytes 1540
  37.1 13.3 %copy-start = (bf16[64,4096]{1,0:T(8,128)(2,1)S(1)}, bf16[64,4096]{1,0:T(8,128)(2,1)}, u32[]{:S(2)}) copy-start(bf16[64,4096]{1,0:T(8,128)(2,1)} %z_ref.1) | copy-start | bytes 1572868

commit v15 on v14

--- a/solution.py
+++ b/solution.py
@@ -31,8 +31,8 @@
 
 
 def mm_parts(a, b):
-    both = jnp.concatenate(a, axis=1)
-    return dot(both, jnp.concatenate([b[0], b[0]], axis=0)) + dot(a[0], b[1])
+    left = jnp.concatenate([a[0], a[1], a[0]], axis=1)
+    return dot(left, jnp.concatenate([b[0], b[0], b[1]], axis=0))
 
 
 def silu(x):
@@ -193,6 +193,16 @@
 
 
 def systems_kernel(
+    recv_ref,
+    ck_ref,
+    alog_ref,
+    dt_ref,
+    *refs,
+):
+    systems_of(recv_ref, ck_ref, alog_ref, dt_ref, *refs[3:])
+
+
+def systems_of(
     recv_ref,
     ck_ref,
     alog_ref,
@@ -410,9 +420,10 @@
     cols_ref,
     values_ref,
     states_ref,
-    last_ref,
-    rows,
-):
+    *rest,
+):
+    *last_ref, rows = rest
+
     @pl.when(lax.axis_index("half") > 0)
     def _():
         spans = t_ref.shape[1]
@@ -434,8 +445,9 @@
                 add = jnp.concatenate([adds[2 * n + r], zero_half], axis=1)
                 end = jnp.concatenate([end_of(ends_ref, n, r)] * 2, axis=1)
                 states[r] = step(end, lin_ref[r, n], states[r], parts) + add
-        for r in range(2):
-            last_ref[r] = states[r]
+        for ref in last_ref:
+            for r in range(2):
+                ref[r] = states[r]
 
 
 def span_rows(n):
@@ -735,6 +747,8 @@
     spans = total // SPAN
     group = ("sub", "head")
     route = [(i, i + 1) for i in range(shards - 1)]
+    conv_q, conv_k, conv_v = near(conv_q), near(conv_k), near(conv_v)
+    gain = near(norm_gain.reshape(1, DV))
     inputs = [far(x) for x in (q_rows, k_rows, v_rows, a_rows.T, b_rows.T)]
     packed = call(
         functools.partial(pack_kernel, heads_axis),
@@ -756,10 +770,10 @@
             pltpu.VMEM((SPAN, SPAN), F32),
             pltpu.VMEM((8, SPAN), F32),
         ),
-        [VMEM, VMEM, SMEM, SMEM],
+        [VMEM, VMEM, SMEM, SMEM, VMEM, VMEM, VMEM],
         [pltpu.VMEM((8 + total, DK), F32)],
         flops=1 << 32,
-    )(blocks, conv_k, a_log, dt_bias)
+    )(blocks, conv_k, a_log, dt_bias, conv_q, conv_v, gain)
     keys, keys_t, systems, small, ends, within, cols, early = (near(x) for x in made)
     map_shapes = (
         pltpu.VMEM((2, spans, 2, SPAN, SPAN), BF16),
@@ -808,12 +822,13 @@
         adds,
     )
     later_inverses, later_lins = inverses_of(False, hop)
-    later_values, states, last = call(
+    read_on = [pltpu.VMEM((2, DK, 2 * DV), F32)] if shards > 2 else []
+    later_values, states, *last = call(
         states_kernel,
         (
             pltpu.VMEM((2, total, DV), BF16),
             pltpu.VMEM((2, 2, spans, 2 * DK, DV), BF16),
-            pltpu.VMEM((2, DK, 2 * DV), F32),
+            *read_on,
         ),
         [VMEM] * 7,
         [pltpu.VMEM((8 + total, 2 * DV), F32)],
@@ -842,7 +857,7 @@
             pltpu.VMEM(hop.shape, BF16),
             [VMEM] * 8,
             [pltpu.VMEM((32, 512), F32)],
-        )(entering, blocks, early, conv_q, conv_k, conv_v, hop, near(last))
+        )(entering, blocks, early, conv_q, conv_k, conv_v, hop, near(last[0]))
         entering = near(lax.ppermute(moved, "half", route))
     normed = call(
         finish_kernel,
@@ -856,7 +871,7 @@
         conv_q,
         conv_k,
         conv_v,
-        norm_gain.reshape(1, DV),
+        gain,
         near(first_out),
         near(out_a),
         near(out_m),

time: 51.9 us -> 51 us (0.983)
  the two profiles are of different devices: /device:TPU:16 before, /device:TPU:0 now
where the time goes in v15:
time: 51 us; the launch traced here: 50.7 us
  blocking collectives  36.7 us (72%)
  Pallas kernels  12.3 us (24%)
  starting transfers between devices  1.29 us (3%)
    all_to_all x1, blocking collectives, local(): blocks = near(lax.all_to_all(packed, group, 0, 0, tiled=True))  22.7 us
    all_to_all x1, blocking collectives, local(): returned = near(lax.all_to_all(normed, group, 0, 0, tiled=True))  14 us
    pallas_call x2, Pallas kernels, inverses_of(): call(functools.partial(inverse_kernel, on_first), map_shapes, [VMEM] * 6,...  3.55 us
    pallas_call x1, Pallas kernels, local(): call(opening_kernel, (pltpu.VMEM((2 * DK + 16, 128), BF16), pltpu.VMEM((2...  2.35 us
    pallas_call x1, Pallas kernels, local(): call(systems_kernel, (pltpu.VMEM((total, DK), BF16), pltpu.VMEM((spans, D...  1.88 us
    pallas_call x1, Pallas kernels, local(): call(first_outputs_kernel, pltpu.VMEM((2, total, DV), F32), [VMEM] * 12,...  1.68 us
    pallas_call x1, Pallas kernels, local(): call(functools.partial(pack_kernel, heads_axis), pltpu.VMEM((peers, GATES...  1.34 us
    ppermute x1, starting transfers between devices, local(): entering = near(lax.ppermute(hop, 'half', route))  1.29 us
  transfers between devices with their start and end apart: 1, of which 0 were waited for; matrix products, arithmetic and copies ran while one was open for 0% of the time, Pallas kernels for 4%

profile of v15, /device:TPU:0, one launch (start us, length us, event | category | flops | bytes accessed | tf_op | source)
XLA Modules:
  0.0 50.7 jit_solution(3752203061834633024)
XLA Ops:
  0.0 1.3 %shard_map.118 = bf16[16,264,128]{2,1,0:T(8,128)(2,1)S(1)} custom-call(bf16[64,2048]{1,0:T(8,128)(2,1)} %q_in.1, bf16[64,2048]{1,0:T(8,128)(2,1)} %k_in.1, bf16[64,4096]{1,0:T(8,128)(2,1)} %v_in.1, bf16[32,64]{1,0:T(8,128)(2,1)} %bitcast.5, bf16[32,64]{1,0:T(8,128)(2,1)} %bitcast.6), custom_call_target="tpu_custom_call" | custom-call | flops 1048576 | bytes 2097152 | tf_op jit(solution)/shard_map/pallas_call | solution.py:753
  1.3 0.0 copy-start.1
  1.4 0.0 copy-start.2
  1.4 0.0 copy-start.3
  1.4 0.0 copy-start.4
  1.4 0.0 copy-start.5
  1.4 0.0 copy-start.6
  1.4 22.7 %all_to_all.10.recv_ref = bf16[16,264,128]{2,1,0:T(8,128)(2,1)S(1)} all-to-all(bf16[16,264,128]{2,1,0:T(8,128)(2,1)S(1)} %shard_map.118), channel_id=1, replica_groups=mesh['half'=2,'sub'=4,'head'=4] {'sub','head'}, dimensions={0} | all-to-all | bytes 2162688 | tf_op jit(solution)/shard_map/all_to_all | solution.py:760
  24.2 0.0 copy-done.1
  24.2 0.0 copy-done.2
  24.2 0.0 copy-done.3
  24.2 0.0 copy-done.4
  24.2 0.0 copy-done.5
  24.2 0.0 copy-done.6
  24.2 1.9 %shard_map.119 = (bf16[1024,128]{1,0:T(8,128)(2,1)S(1)}, bf16[8,128,128]{2,1,0:T(8,128)(2,1)S(1)}, bf16[2,8,2,128,128]{4,3,2,1,0:T(8,128)(2,1)S(1)}, f32[2,8,16,...) custom-call(bf16[16,264,128]{2,1,0:T(8,128)(2,1)S(1)} %all_to_all.10, ...), custom_call_target="tpu_custom_call" | custom-call | flops 4294967296 | bytes 2097152 | tf_op jit(solution)/shard_map/pallas_call | solution.py:761
  26.1 3.5 %shard_map.120 = (bf16[2,8,2,128,128]{4,3,2,1,0:T(8,128)(2,1)S(1)}, bf16[2,8,128,128]{3,2,1,0:T(8,128)(2,1)S(1)}) custom-call(f32[8,128]{1,0:T(8,128)S(1)} %get-tuple-element.26.hop_ref.early_ref, bf16[1024,128]{1,0:T(8,128)(2,1)S(1)} %get-tuple-element.27.keys_ref, bf16[8,128,128]{2,1,0:T(8,128)(2,1)S(1)} %get-tuple-element.25.keys_t_ref, ...), custom_call_target="tpu_custom_call" | custom-call | flops 4294967296 | bytes 2097152 | tf_op jit(solution)/shard_map/pallas_call | solution.py:784
  29.6 2.4 %shard_map.121 = (bf16[272,128]{1,0:T(8,128)(2,1)S(1)}, bf16[2,1024,128]{2,1,0:T(8,128)(2,1)S(1)}, bf16[2,8,256,128]{3,2,1,0:T(8,128)(2,1)S(1)}, f32[2,8,128,128]{3,2,1,0:T(8,128)S(1)}) custom-call(bf16[16,264,128]{2,1,0:T(8,128)(2,1)S(1)} %all_to_all.10.recv_ref, f32[4,1024]{1,0:T(4,128)S(1)} %copy-done.1, ...), custom_call_target="tpu_custom_call" | custom-call | flops 4294967296 | bytes 2097152 | tf_op jit(solution)/shard_map/pallas_call | solution.py:790
  32.0 1.3 %collective-permute-start = (bf16[272,128]{1,0:T(8,128)(2,1)S(1)}, bf16[272,128]{1,0:T(8,128)(2,1)S(1)}, u32[]{:S(2)}, u32[]{:S(2)}) collective-permute-start(bf16[272,128]{1,0:T(8,128)(2,1)S(1)} %get-tuple-element.34.hop_ref), channel_id=1, source_target_pairs={{0,16},{1,17},{2,18},{3,19},{4,20},{5,21},{6,22},{7,23},{8,24},{9,... | collective-permute-start | bytes 208904 | tf_op jit(solution)/shard_map/ppermute | solution.py:802
  33.3 0.2 shard_map.124
  33.5 1.7 %shard_map.122.first_oa = f32[2,1024,128]{2,1,0:T(8,128)S(1)} custom-call(bf16[16,264,128]{2,1,0:T(8,128)(2,1)S(1)} %all_to_all.10.recv_ref, f32[4,512]{1,0:T(4,128)S(1)} %copy-done.3, bf16[1024,128]{1,0:T(8,128)(2,1)S(1)} %get-tuple-element.27.keys_ref, bf16[8,128,128]{2,1,0:T(8,128)(2,1)S(1)} %get-tuple-element.25.keys_t_ref, ...), custom_call_target="tpu_custom_call" | custom-call | flops 4294967296 | bytes 2097152 | tf_op jit(solution)/shard_map/pallas_call | solution.py:804
  35.2 0.0 collective-permute-done.hop_ref
  35.2 0.4 shard_map.126
  35.6 0.0 copy-start
  35.6 14.0 %all_to_all.11.normed_ref = bf16[16,128,128]{2,1,0:T(8,128)(2,1)S(1)} all-to-all(bf16[16,128,128]{2,1,0:T(8,128)(2,1)S(1)} %shard_map.126), channel_id=1, replica_groups=mesh['half'=2,'sub'=4,'head'=4] {'sub','head'}, dimensions={0} | all-to-all | bytes 1048576 | tf_op jit(solution)/shard_map/all_to_all | solution.py:879
  49.6 0.0 copy-done
  49.6 1.0 %shard_map.127 = bf16[64,4096]{1,0:T(8,128)(2,1)} custom-call(bf16[16,128,128]{2,1,0:T(8,128)(2,1)S(1)} %all_to_all.11.normed_ref, bf16[64,4096]{1,0:T(8,128)(2,1)S(1)} %copy-done), custom_call_target="tpu_custom_call" | custom-call | flops 67108864 | bytes 2097152 | tf_op jit(solution)/shard_map/pallas_call | solution.py:880
  (2 shorter events, 0.0 us)
Async XLA Ops:
  1.3 22.8 %copy-start.1 = (f32[4,1024]{1,0:T(4,128)S(1)}, f32[4,1024]{1,0:T(4,128)}, u32[]{:S(2)}) copy-start(f32[4,1024]{1,0:T(4,128)} %cv_ref.5) | copy-start | bytes 49156
  1.4 22.8 %copy-start.2 = (f32[4,512]{1,0:T(4,128)S(1)}, f32[4,512]{1,0:T(4,128)}, u32[]{:S(2)}) copy-start(f32[4,512]{1,0:T(4,128)} %ck_ref.3) | copy-start | bytes 24580
  1.4 22.8 %copy-start.3 = (f32[4,512]{1,0:T(4,128)S(1)}, f32[4,512]{1,0:T(4,128)}, u32[]{:S(2)}) copy-start(f32[4,512]{1,0:T(4,128)} %cq_ref.5) | copy-start | bytes 24580
  1.4 22.8 %copy-start.4 = (f32[128]{0:T(128)S(1)}, f32[128]{0:T(128)}, u32[]{:S(2)}) copy-start(f32[128]{0:T(128)} %param.23) | copy-start | bytes 1540
  1.4 22.8 %copy-start.5 = (f32[8]{0:T(128)S(1)}, f32[8]{0:T(128)}, u32[]{:S(2)}) copy-start(f32[8]{0:T(128)} %alog_ref.1) | copy-start | bytes 100
  1.4 22.8 %copy-start.6 = (f32[8]{0:T(128)S(1)}, f32[8]{0:T(128)}, u32[]{:S(2)}) copy-start(f32[8]{0:T(128)} %dt_ref.1) | copy-start | bytes 100
  32.0 3.2 %collective-permute-start = (bf16[272,128]{1,0:T(8,128)(2,1)S(1)}, bf16[272,128]{1,0:T(8,128)(2,1)S(1)}, u32[]{:S(2)}, u32[]{:S(2)}) collective-permute-start(bf16[272,128]{1,0:T(8,128)(2,1)S(1)} %get-tuple-element.34.hop_ref), channel_id=1, source_target_pairs={{0,16},{1,17},{2,18},{3,19},{4,20},{5,21},{6,22},{7,23},{8,24},{9,... | collective-permute-start | bytes 208904 | tf_op jit(solution)/shard_map/ppermute | solution.py:802
  35.6 14.0 %copy-start = (bf16[64,4096]{1,0:T(8,128)(2,1)S(1)}, bf16[64,4096]{1,0:T(8,128)(2,1)}, u32[]{:S(2)}) copy-start(bf16[64,4096]{1,0:T(8,128)(2,1)} %z_ref.1) | copy-start | bytes 1572868

commit v16 on v15

--- a/solution.py
+++ b/solution.py
@@ -124,9 +124,9 @@
     size = systems[0][0].shape[0]
     row, col = iota((size, size), 0), iota((size, size), 1)
     placed = jnp.where(block_of(row, SUB) == block_of(col, SUB), 1.0, 0.0).astype(BF16)
-    parts = [
-        tuple(jnp.concatenate([x] * (size // SUB), axis=0) * placed for x in halves(block))
-        for block in small
+    identity = jnp.where(row == col, 1.0, 0.0)
+    rough = [
+        jnp.concatenate([block.astype(BF16)] * (size // SUB), axis=0) * placed for block in small
     ]
     blank = jnp.zeros((size, size), BF16)
     width = SUB
@@ -143,19 +143,22 @@
             return jnp.concatenate(pieces, axis=0)
 
         below = rows_of(block_of(row ^ col, 2 * width)) + rows_of(col & width) == 0
-        identity = rows_of(jnp.where(row == col, 1.0, 0.0))
-        firsts = [
-            mm_parts((rows_of(n[0]), rows_of(n[1])), t) for n, t in zip(systems, parts)
+        own = rows_of(identity)
+        firsts = [dot(rows_of(n[0]), t) for n, t in zip(systems, rough)]
+        rights = [
+            woven(blank, jnp.where(below, first, own).astype(BF16)) for first in firsts
         ]
-        rights = [
-            tuple(woven(blank, x) for x in halves(jnp.where(below, first, identity)))
-            for first in firsts
-        ]
-        odds = [(rows_of(t[0]), rows_of(t[1])) for t in parts]
-        grown = [halves(mm_parts(o, right)) for o, right in zip(odds, rights)]
-        parts = [tuple(woven(t[i], g[i]) for i in range(2)) for t, g in zip(parts, grown)]
+        grown = [dot(rows_of(t), right).astype(BF16) for t, right in zip(rough, rights)]
+        rough = [woven(t, g) for t, g in zip(rough, grown)]
         width *= 2
-    return parts
+    products = [
+        dot(jnp.concatenate(n, axis=1), jnp.concatenate([t, t], axis=0))
+        for n, t in zip(systems, rough)
+    ]
+    rests = [
+        (identity - t.astype(F32) + product).astype(BF16) for t, product in zip(rough, products)
+    ]
+    return [halves(t.astype(F32) + dot(t, rest)) for t, rest in zip(rough, rests)]
 
 
 def gate_values(gates, sub, alog_ref, dt_ref):

time: 51 us -> 50.4 us (0.988)
  Pallas kernels: 12.3 us -> 11.7 us
    pallas_call x2, Pallas kernels: 3.55 us -> 2.95 us  [inverses_of(): call(functools.partial(inverse_kernel, on_first), map_shapes, [VMEM] * 6,...]
where the time goes in v16:
time: 50.4 us; the launch traced here: 50.1 us
  blocking collectives  36.7 us (73%)
  Pallas kernels  11.7 us (23%)
  starting transfers between devices  1.29 us (3%)
    all_to_all x1, blocking collectives, local(): blocks = near(lax.all_to_all(packed, group, 0, 0, tiled=True))  22.7 us
    all_to_all x1, blocking collectives, local(): returned = near(lax.all_to_all(normed, group, 0, 0, tiled=True))  14 us
    pallas_call x2, Pallas kernels, inverses_of(): call(functools.partial(inverse_kernel, on_first), map_shapes, [VMEM] * 6,...  2.95 us
    pallas_call x1, Pallas kernels, local(): call(opening_kernel, (pltpu.VMEM((2 * DK + 16, 128), BF16), pltpu.VMEM((2...  2.35 us
    pallas_call x1, Pallas kernels, local(): call(systems_kernel, (pltpu.VMEM((total, DK), BF16), pltpu.VMEM((spans, D...  1.88 us
    pallas_call x1, Pallas kernels, local(): call(first_outputs_kernel, pltpu.VMEM((2, total, DV), F32), [VMEM] * 12,...  1.68 us
    pallas_call x1, Pallas kernels, local(): call(functools.partial(pack_kernel, heads_axis), pltpu.VMEM((peers, GATES...  1.34 us
    ppermute x1, starting transfers between devices, local(): entering = near(lax.ppermute(hop, 'half', route))  1.29 us
  transfers between devices with their start and end apart: 1, of which 0 were waited for; matrix products, arithmetic and copies ran while one was open for 0% of the time, Pallas kernels for 4%

profile of v16, /device:TPU:0, one launch (start us, length us, event | category | flops | bytes accessed | tf_op | source)
XLA Modules:
  0.0 50.1 jit_solution(90396321485196246)
XLA Ops:
  0.0 1.3 %shard_map.118 = bf16[16,264,128]{2,1,0:T(8,128)(2,1)S(1)} custom-call(bf16[64,2048]{1,0:T(8,128)(2,1)} %q_in.1, bf16[64,2048]{1,0:T(8,128)(2,1)} %k_in.1, bf16[64,4096]{1,0:T(8,128)(2,1)} %v_in.1, bf16[32,64]{1,0:T(8,128)(2,1)} %bitcast.5, bf16[32,64]{1,0:T(8,128)(2,1)} %bitcast.6), custom_call_target="tpu_custom_call" | custom-call | flops 1048576 | bytes 2097152 | tf_op jit(solution)/shard_map/pallas_call | solution.py:756
  1.3 0.0 copy-start.1
  1.4 0.0 copy-start.2
  1.4 0.0 copy-start.3
  1.4 0.0 copy-start.4
  1.4 0.0 copy-start.5
  1.4 0.0 copy-start.6
  1.4 22.7 %all_to_all.10.recv_ref = bf16[16,264,128]{2,1,0:T(8,128)(2,1)S(1)} all-to-all(bf16[16,264,128]{2,1,0:T(8,128)(2,1)S(1)} %shard_map.118), channel_id=1, replica_groups=mesh['half'=2,'sub'=4,'head'=4] {'sub','head'}, dimensions={0} | all-to-all | bytes 2162688 | tf_op jit(solution)/shard_map/all_to_all | solution.py:763
  24.2 0.0 copy-done.1
  24.2 0.0 copy-done.2
  24.2 0.0 copy-done.3
  24.2 0.0 copy-done.4
  24.2 0.0 copy-done.5
  24.2 0.0 copy-done.6
  24.2 1.9 %shard_map.119 = (bf16[1024,128]{1,0:T(8,128)(2,1)S(1)}, bf16[8,128,128]{2,1,0:T(8,128)(2,1)S(1)}, bf16[2,8,2,128,128]{4,3,2,1,0:T(8,128)(2,1)S(1)}, f32[2,8,16,...) custom-call(bf16[16,264,128]{2,1,0:T(8,128)(2,1)S(1)} %all_to_all.10, ...), custom_call_target="tpu_custom_call" | custom-call | flops 4294967296 | bytes 2097152 | tf_op jit(solution)/shard_map/pallas_call | solution.py:764
  26.1 2.9 %shard_map.120 = (bf16[2,8,2,128,128]{4,3,2,1,0:T(8,128)(2,1)S(1)}, bf16[2,8,128,128]{3,2,1,0:T(8,128)(2,1)S(1)}) custom-call(f32[8,128]{1,0:T(8,128)S(1)} %get-tuple-element.26.hop_ref.early_ref, bf16[1024,128]{1,0:T(8,128)(2,1)S(1)} %get-tuple-element.27.keys_ref, bf16[8,128,128]{2,1,0:T(8,128)(2,1)S(1)} %get-tuple-element.25.keys_t_ref, ...), custom_call_target="tpu_custom_call" | custom-call | flops 4294967296 | bytes 2097152 | tf_op jit(solution)/shard_map/pallas_call | solution.py:787
  29.0 2.4 %shard_map.121 = (bf16[272,128]{1,0:T(8,128)(2,1)S(1)}, bf16[2,1024,128]{2,1,0:T(8,128)(2,1)S(1)}, bf16[2,8,256,128]{3,2,1,0:T(8,128)(2,1)S(1)}, f32[2,8,128,128]{3,2,1,0:T(8,128)S(1)}) custom-call(bf16[16,264,128]{2,1,0:T(8,128)(2,1)S(1)} %all_to_all.10.recv_ref, f32[4,1024]{1,0:T(4,128)S(1)} %copy-done.1, ...), custom_call_target="tpu_custom_call" | custom-call | flops 4294967296 | bytes 2097152 | tf_op jit(solution)/shard_map/pallas_call | solution.py:793
  31.4 1.3 %collective-permute-start = (bf16[272,128]{1,0:T(8,128)(2,1)S(1)}, bf16[272,128]{1,0:T(8,128)(2,1)S(1)}, u32[]{:S(2)}, u32[]{:S(2)}) collective-permute-start(bf16[272,128]{1,0:T(8,128)(2,1)S(1)} %get-tuple-element.34.hop_ref), channel_id=1, source_target_pairs={{0,16},{1,17},{2,18},{3,19},{4,20},{5,21},{6,22},{7,23},{8,24},{9,... | collective-permute-start | bytes 208904 | tf_op jit(solution)/shard_map/ppermute | solution.py:805
  32.7 0.2 shard_map.125
  32.9 1.7 %shard_map.122.first_oa = f32[2,1024,128]{2,1,0:T(8,128)S(1)} custom-call(bf16[16,264,128]{2,1,0:T(8,128)(2,1)S(1)} %all_to_all.10.recv_ref, f32[4,512]{1,0:T(4,128)S(1)} %copy-done.3, bf16[1024,128]{1,0:T(8,128)(2,1)S(1)} %get-tuple-element.27.keys_ref, bf16[8,128,128]{2,1,0:T(8,128)(2,1)S(1)} %get-tuple-element.25.keys_t_ref, ...), custom_call_target="tpu_custom_call" | custom-call | flops 4294967296 | bytes 2097152 | tf_op jit(solution)/shard_map/pallas_call | solution.py:807
  34.6 0.0 collective-permute-done.hop_ref
  34.6 0.4 shard_map.126
  35.0 0.0 copy-start
  35.0 14.0 %all_to_all.11.normed_ref = bf16[16,128,128]{2,1,0:T(8,128)(2,1)S(1)} all-to-all(bf16[16,128,128]{2,1,0:T(8,128)(2,1)S(1)} %shard_map.126), channel_id=1, replica_groups=mesh['half'=2,'sub'=4,'head'=4] {'sub','head'}, dimensions={0} | all-to-all | bytes 1048576 | tf_op jit(solution)/shard_map/all_to_all | solution.py:882
  49.0 0.0 copy-done
  49.0 1.0 %shard_map.127 = bf16[64,4096]{1,0:T(8,128)(2,1)} custom-call(bf16[16,128,128]{2,1,0:T(8,128)(2,1)S(1)} %all_to_all.11.normed_ref, bf16[64,4096]{1,0:T(8,128)(2,1)S(1)} %copy-done), custom_call_target="tpu_custom_call" | custom-call | flops 67108864 | bytes 2097152 | tf_op jit(solution)/shard_map/pallas_call | solution.py:883
  (2 shorter events, 0.0 us)
Async XLA Ops:
  1.3 22.8 %copy-start.1 = (f32[4,1024]{1,0:T(4,128)S(1)}, f32[4,1024]{1,0:T(4,128)}, u32[]{:S(2)}) copy-start(f32[4,1024]{1,0:T(4,128)} %cv_ref.5) | copy-start | bytes 49156
  1.4 22.8 %copy-start.2 = (f32[4,512]{1,0:T(4,128)S(1)}, f32[4,512]{1,0:T(4,128)}, u32[]{:S(2)}) copy-start(f32[4,512]{1,0:T(4,128)} %ck_ref.3) | copy-start | bytes 24580
  1.4 22.8 %copy-start.3 = (f32[4,512]{1,0:T(4,128)S(1)}, f32[4,512]{1,0:T(4,128)}, u32[]{:S(2)}) copy-start(f32[4,512]{1,0:T(4,128)} %cq_ref.5) | copy-start | bytes 24580
  1.4 22.8 %copy-start.4 = (f32[128]{0:T(128)S(1)}, f32[128]{0:T(128)}, u32[]{:S(2)}) copy-start(f32[128]{0:T(128)} %param.23) | copy-start | bytes 1540
  1.4 22.8 %copy-start.5 = (f32[8]{0:T(128)S(1)}, f32[8]{0:T(128)}, u32[]{:S(2)}) copy-start(f32[8]{0:T(128)} %alog_ref.1) | copy-start | bytes 100
  1.4 22.8 %copy-start.6 = (f32[8]{0:T(128)S(1)}, f32[8]{0:T(128)}, u32[]{:S(2)}) copy-start(f32[8]{0:T(128)} %dt_ref.1) | copy-start | bytes 100
  31.4 3.2 %collective-permute-start = (bf16[272,128]{1,0:T(8,128)(2,1)S(1)}, bf16[272,128]{1,0:T(8,128)(2,1)S(1)}, u32[]{:S(2)}, u32[]{:S(2)}) collective-permute-start(bf16[272,128]{1,0:T(8,128)(2,1)S(1)} %get-tuple-element.34.hop_ref), channel_id=1, source_target_pairs={{0,16},{1,17},{2,18},{3,19},{4,20},{5,21},{6,22},{7,23},{8,24},{9,... | collective-permute-start | bytes 208904 | tf_op jit(solution)/shard_map/ppermute | solution.py:805
  35.0 14.0 %copy-start = (bf16[64,4096]{1,0:T(8,128)(2,1)S(1)}, bf16[64,4096]{1,0:T(8,128)(2,1)}, u32[]{:S(2)}) copy-start(bf16[64,4096]{1,0:T(8,128)(2,1)} %z_ref.1) | copy-start | bytes 1572868

commit v17 on v16

--- a/solution.py
+++ b/solution.py
@@ -120,7 +120,7 @@
     return solved
 
 
-def inverted(systems, small):
+def inverted(systems, small, meanwhile=lambda: None):
     size = systems[0][0].shape[0]
     row, col = iota((size, size), 0), iota((size, size), 1)
     placed = jnp.where(block_of(row, SUB) == block_of(col, SUB), 1.0, 0.0).astype(BF16)
@@ -145,6 +145,7 @@
         below = rows_of(block_of(row ^ col, 2 * width)) + rows_of(col & width) == 0
         own = rows_of(identity)
         firsts = [dot(rows_of(n[0]), t) for n, t in zip(systems, rough)]
+        meanwhile()
         rights = [
             woven(blank, jnp.where(below, first, own).astype(BF16)) for first in firsts
         ]
@@ -276,13 +277,13 @@
 
 
 def inverse_kernel(
-    on_first, hop_ref, keys_ref, keys_t_ref, systems_ref, small_ref, cols_ref, t_ref, lin_ref
+    hop_ref, keys_ref, keys_t_ref, systems_ref, small_ref, cols_ref, t_ref, lin_ref
 ):
     del hop_ref
     spans = keys_t_ref.shape[0]
     both = [(n, r) for n in range(spans) for r in range(2)]
 
-    @pl.when((lax.axis_index("half") == 0) == on_first)
+    @pl.when(lax.axis_index("half") > 0)
     def _():
         compact = jnp.concatenate([small_ref[r, n] for n, r in both], axis=0)
         small = substituted(compact.reshape(len(both), SUB, SPAN))
@@ -373,12 +374,26 @@
 
 
 def opening_kernel(
-    recv_ref, cv_ref, keys_t_ref, t_ref, lin_ref, ends_ref, cols_ref, hop_ref, vs_ref, xs_ref, adds_ref, rows
+    recv_ref,
+    cv_ref,
+    keys_ref,
+    keys_t_ref,
+    systems_ref,
+    small_ref,
+    ends_ref,
+    cols_ref,
+    hop_ref,
+    t_ref,
+    lin_ref,
+    vs_ref,
+    xs_ref,
+    adds_ref,
+    rows,
 ):
     first = lax.axis_index("half") == 0
     peers = recv_ref.shape[0]
     tokens = (recv_ref.shape[1] - GATES) // 4
-    spans = t_ref.shape[1]
+    spans = keys_t_ref.shape[0]
     edges = []
     for which in (3, 0, 1, 2):
         end = (which + 1) * tokens
@@ -388,10 +403,47 @@
 
     @pl.when(first)
     def _():
-        adds = values_part(recv_ref, cv_ref, keys_t_ref, t_ref, cols_ref, rows, vs_ref)
-        for n in range(spans):
-            for r in range(2):
-                adds_ref[r, n] = adds[2 * n + r]
+        both = [(n, r) for n in range(spans) for r in range(2)]
+        taps = value_taps(lax.axis_index("sub"), cv_ref)
+        widened(rows, recv_ref, [tokens, 2 * tokens], tokens)
+        waiting = list(both)
+
+        def meanwhile():
+            for n, r in waiting[:6]:
+                lanes = slice(r * DV, (r + 1) * DV)
+                value = convolved(rows, n * SPAN + 8 - EDGE, SPAN, lanes, taps[r])
+                vs_ref[r, n * SPAN : (n + 1) * SPAN, :] = value.astype(BF16)
+            del waiting[:6]
+
+        compact = jnp.concatenate([small_ref[r, n] for n, r in both], axis=0)
+        small = substituted(compact.reshape(len(both), SUB, SPAN))
+        systems = [(systems_ref[r, n, 0], systems_ref[r, n, 1]) for n, r in both]
+        inverses = inverted(systems, [small[i] for i in range(len(both))], meanwhile)
+        while waiting:
+            meanwhile()
+        rights = []
+        for i, (n, r) in enumerate(both):
+            t_ref[r, n, 0], t_ref[r, n, 1] = inverses[i]
+            at = GATES * n + r
+            here = slice(n * SPAN, (n + 1) * SPAN)
+            key = (cols_ref[:, at + 2 : at + 3] * keys_ref[here, :].astype(F32)).astype(BF16)
+            right = jnp.concatenate([key, vs_ref[r, here, :]], axis=1)
+            rights.append(jnp.concatenate([right, right], axis=0))
+        solved = [dot(jnp.concatenate(t, axis=1), x) for t, x in zip(inverses, rights)]
+        weighed = []
+        for (n, r), x in zip(both, solved):
+            at = GATES * n + r
+            weighed.append((cols_ref[:, at + 4 : at + 5] * x).astype(BF16))
+        moved = [
+            dot(keys_t_ref[n], jnp.concatenate(weighed[2 * n : 2 * n + 2], axis=1))
+            for n in range(spans)
+        ]
+        adds = []
+        for n, r in both:
+            at = 2 * r * DK
+            lin_ref[r, n] = moved[n][:, at : at + DK].astype(BF16)
+            adds.append(moved[n][:, at + DK : at + 2 * DK])
+            adds_ref[r, n] = adds[-1]
         maps = [
             [(end_of(ends_ref, n, r), lin_ref[r, n], adds[2 * n + r]) for n in range(spans)]
             for r in range(2)
@@ -783,27 +835,23 @@
         pltpu.VMEM((2, spans, DK, DK), BF16),
     )
 
-    def inverses_of(on_first, after):
-        solved = call(
-            functools.partial(inverse_kernel, on_first), map_shapes, [VMEM] * 6, flops=1 << 32
-        )(after, keys, keys_t, systems, small, cols)
-        return [near(x) for x in solved]
-
-    inverses, lins = inverses_of(True, early)
-    hop, values, starts, adds = call(
+    hop, inverses, lins, values, starts, adds = call(
         opening_kernel,
         (
             pltpu.VMEM((2 * DK + 16, 128), BF16),
+            *map_shapes,
             pltpu.VMEM((2, total, DV), BF16),
             pltpu.VMEM((2, spans, 2 * DK, DV), BF16),
             pltpu.VMEM((2, spans, DK, DV), F32),
         ),
-        [VMEM] * 7,
+        [VMEM] * 8,
         [pltpu.VMEM((8 + total, 2 * DV), F32)],
         flops=1 << 32,
-    )(blocks, conv_v, keys_t, inverses, lins, ends, cols)
+    )(blocks, conv_v, keys, keys_t, systems, small, ends, cols)
     entering = near(lax.ppermute(hop, "half", route))
-    hop, values, starts, adds = (near(x) for x in (hop, values, starts, adds))
+    hop, inverses, lins, values, starts, adds = (
+        near(x) for x in (hop, inverses, lins, values, starts, adds)
+    )
     first_out = call(
         first_outputs_kernel,
         pltpu.VMEM((2, total, DV), F32),
@@ -824,7 +872,10 @@
         starts,
         adds,
     )
-    later_inverses, later_lins = inverses_of(False, hop)
+    later_solved = call(inverse_kernel, map_shapes, [VMEM] * 6, flops=1 << 32)(
+        hop, keys, keys_t, systems, small, cols
+    )
+    later_inverses, later_lins = (near(x) for x in later_solved)
     read_on = [pltpu.VMEM((2, DK, 2 * DV), F32)] if shards > 2 else []
     later_values, states, *last = call(
         states_kernel,

time: 50.4 us -> 50.3 us (level)
    pallas_call x3 -> x2, Pallas kernels: 5.3 us -> 5.19 us  [the longest x1 5.17 us: local(): call(opening_kernel, (pltpu.VMEM((2 * DK + 16, 128), BF16), *map_shapes,...]
where the time goes in v17:
time: 50.3 us; the launch traced here: 50 us
  blocking collectives  36.7 us (73%)
  Pallas kernels  11.6 us (23%)
  starting transfers between devices  1.29 us (3%)
    all_to_all x1, blocking collectives, local(): blocks = near(lax.all_to_all(packed, group, 0, 0, tiled=True))  22.7 us
    all_to_all x1, blocking collectives, local(): returned = near(lax.all_to_all(normed, group, 0, 0, tiled=True))  14 us
    pallas_call x1, Pallas kernels, local(): call(opening_kernel, (pltpu.VMEM((2 * DK + 16, 128), BF16), *map_shapes,...  5.17 us
    pallas_call x1, Pallas kernels, local(): call(systems_kernel, (pltpu.VMEM((total, DK), BF16), pltpu.VMEM((spans, D...  1.88 us
    pallas_call x1, Pallas kernels, local(): call(first_outputs_kernel, pltpu.VMEM((2, total, DV), F32), [VMEM] * 12,...  1.68 us
    pallas_call x1, Pallas kernels, local(): call(functools.partial(pack_kernel, heads_axis), pltpu.VMEM((peers, GATES...  1.34 us
    ppermute x1, starting transfers between devices, local(): entering = near(lax.ppermute(hop, 'half', route))  1.29 us
  transfers between devices with their start and end apart: 1, of which 0 were waited for; matrix products, arithmetic and copies ran while one was open for 0% of the time, Pallas kernels for 4%

profile of v17, /device:TPU:0, one launch (start us, length us, event | category | flops | bytes accessed | tf_op | source)
XLA Modules:
  0.0 50.0 jit_solution(9643272235760968669)
XLA Ops:
  0.0 1.3 %shard_map.118 = bf16[16,264,128]{2,1,0:T(8,128)(2,1)S(1)} custom-call(bf16[64,2048]{1,0:T(8,128)(2,1)} %q_in.1, bf16[64,2048]{1,0:T(8,128)(2,1)} %k_in.1, bf16[64,4096]{1,0:T(8,128)(2,1)} %v_in.1, bf16[32,64]{1,0:T(8,128)(2,1)} %bitcast.5, bf16[32,64]{1,0:T(8,128)(2,1)} %bitcast.6), custom_call_target="tpu_custom_call" | custom-call | flops 1048576 | bytes 2097152 | tf_op jit(solution)/shard_map/pallas_call | solution.py:808
  1.3 0.0 copy-start.1
  1.4 0.0 copy-start.2
  1.4 0.0 copy-start.3
  1.4 0.0 copy-start.4
  1.4 0.0 copy-start.5
  1.4 0.0 copy-start.6
  1.4 22.7 %all_to_all.10.recv_ref = bf16[16,264,128]{2,1,0:T(8,128)(2,1)S(1)} all-to-all(bf16[16,264,128]{2,1,0:T(8,128)(2,1)S(1)} %shard_map.118), channel_id=1, replica_groups=mesh['half'=2,'sub'=4,'head'=4] {'sub','head'}, dimensions={0} | all-to-all | bytes 2162688 | tf_op jit(solution)/shard_map/all_to_all | solution.py:815
  24.2 0.0 copy-done.1
  24.2 0.0 copy-done.2
  24.2 0.0 copy-done.3
  24.2 0.0 copy-done.4
  24.2 0.0 copy-done.5
  24.2 0.0 copy-done.6
  24.2 1.9 %shard_map.119 = (bf16[1024,128]{1,0:T(8,128)(2,1)S(1)}, bf16[8,128,128]{2,1,0:T(8,128)(2,1)S(1)}, bf16[2,8,2,128,128]{4,3,2,1,0:T(8,128)(2,1)S(1)}, f32[2,8,16,...) custom-call(bf16[16,264,128]{2,1,0:T(8,128)(2,1)S(1)} %all_to_all.10, ...), custom_call_target="tpu_custom_call" | custom-call | flops 4294967296 | bytes 2097152 | tf_op jit(solution)/shard_map/pallas_call | solution.py:816
  26.1 5.2 %shard_map.120 = (bf16[272,128]{1,0:T(8,128)(2,1)S(1)}, bf16[2,8,2,128,128]{4,3,2,1,0:T(8,128)(2,1)S(1)}, bf16[2,8,128,128]{3,2,1,0:T(8,128)(2,1)S(1)}, bf16[2,1...) custom-call(bf16[16,264,128]{2,1,0:T(8,128)(2,1)S(1)} %all_to_all.10.recv_ref, ...), custom_call_target="tpu_custom_call" | custom-call | flops 4294967296 | bytes 2097152 | tf_op jit(solution)/shard_map/pallas_call | solution.py:838
  31.3 1.3 %collective-permute-start = (bf16[272,128]{1,0:T(8,128)(2,1)S(1)}, bf16[272,128]{1,0:T(8,128)(2,1)S(1)}, u32[]{:S(2)}, u32[]{:S(2)}) collective-permute-start(bf16[272,128]{1,0:T(8,128)(2,1)S(1)} %get-tuple-element.31.hop_ref), channel_id=1, source_target_pairs={{0,16},{1,17},{2,18},{3,19},{4,20},{5,21},{6,22},{7,23},{8,24},{9,... | collective-permute-start | bytes 208904 | tf_op jit(solution)/shard_map/ppermute | solution.py:851
  32.6 0.2 shard_map.124
  32.8 1.7 %shard_map.121.first_oa = f32[2,1024,128]{2,1,0:T(8,128)S(1)} custom-call(bf16[16,264,128]{2,1,0:T(8,128)(2,1)S(1)} %all_to_all.10.recv_ref, f32[4,512]{1,0:T(4,128)S(1)} %copy-done.3, bf16[1024,128]{1,0:T(8,128)(2,1)S(1)} %get-tuple-element.25.keys_ref, bf16[8,128,128]{2,1,0:T(8,128)(2,1)S(1)} %get-tuple-element.26.keys_t_ref, ...), custom_call_target="tpu_custom_call" | custom-call | flops 4294967296 | bytes 2097152 | tf_op jit(solution)/shard_map/pallas_call | solution.py:855
  34.5 0.0 collective-permute-done.hop_ref
  34.5 0.4 shard_map.125
  34.9 0.0 copy-start
  34.9 14.0 %all_to_all.11.normed_ref = bf16[16,128,128]{2,1,0:T(8,128)(2,1)S(1)} all-to-all(bf16[16,128,128]{2,1,0:T(8,128)(2,1)S(1)} %shard_map.125), channel_id=1, replica_groups=mesh['half'=2,'sub'=4,'head'=4] {'sub','head'}, dimensions={0} | all-to-all | bytes 1048576 | tf_op jit(solution)/shard_map/all_to_all | solution.py:933
  48.9 0.0 copy-done
  48.9 1.0 %shard_map.126 = bf16[64,4096]{1,0:T(8,128)(2,1)} custom-call(bf16[16,128,128]{2,1,0:T(8,128)(2,1)S(1)} %all_to_all.11.normed_ref, bf16[64,4096]{1,0:T(8,128)(2,1)S(1)} %copy-done), custom_call_target="tpu_custom_call" | custom-call | flops 67108864 | bytes 2097152 | tf_op jit(solution)/shard_map/pallas_call | solution.py:934
  (2 shorter events, 0.0 us)
Async XLA Ops:
  1.3 22.8 %copy-start.1 = (f32[4,1024]{1,0:T(4,128)S(1)}, f32[4,1024]{1,0:T(4,128)}, u32[]{:S(2)}) copy-start(f32[4,1024]{1,0:T(4,128)} %cv_ref.5) | copy-start | bytes 49156
  1.4 22.8 %copy-start.2 = (f32[4,512]{1,0:T(4,128)S(1)}, f32[4,512]{1,0:T(4,128)}, u32[]{:S(2)}) copy-start(f32[4,512]{1,0:T(4,128)} %ck_ref.3) | copy-start | bytes 24580
  1.4 22.8 %copy-start.3 = (f32[4,512]{1,0:T(4,128)S(1)}, f32[4,512]{1,0:T(4,128)}, u32[]{:S(2)}) copy-start(f32[4,512]{1,0:T(4,128)} %cq_ref.5) | copy-start | bytes 24580
  1.4 22.8 %copy-start.4 = (f32[128]{0:T(128)S(1)}, f32[128]{0:T(128)}, u32[]{:S(2)}) copy-start(f32[128]{0:T(128)} %param.23) | copy-start | bytes 1540
  1.4 22.8 %copy-start.5 = (f32[8]{0:T(128)S(1)}, f32[8]{0:T(128)}, u32[]{:S(2)}) copy-start(f32[8]{0:T(128)} %alog_ref.1) | copy-start | bytes 100
  1.4 22.8 %copy-start.6 = (f32[8]{0:T(128)S(1)}, f32[8]{0:T(128)}, u32[]{:S(2)}) copy-start(f32[8]{0:T(128)} %dt_ref.1) | copy-start | bytes 100
  31.3 3.2 %collective-permute-start = (bf16[272,128]{1,0:T(8,128)(2,1)S(1)}, bf16[272,128]{1,0:T(8,128)(2,1)S(1)}, u32[]{:S(2)}, u32[]{:S(2)}) collective-permute-start(bf16[272,128]{1,0:T(8,128)(2,1)S(1)} %get-tuple-element.31.hop_ref), channel_id=1, source_target_pairs={{0,16},{1,17},{2,18},{3,19},{4,20},{5,21},{6,22},{7,23},{8,24},{9,... | collective-permute-start | bytes 208904 | tf_op jit(solution)/shard_map/ppermute | solution.py:851
  34.9 14.0 %copy-start = (bf16[64,4096]{1,0:T(8,128)(2,1)S(1)}, bf16[64,4096]{1,0:T(8,128)(2,1)}, u32[]{:S(2)}) copy-start(bf16[64,4096]{1,0:T(8,128)(2,1)} %z_ref.1) | copy-start | bytes 1572868

commit v18 on v17

--- a/solution.py
+++ b/solution.py
@@ -196,14 +196,12 @@
             ].astype(F32)
 
 
-def systems_kernel(
-    recv_ref,
-    ck_ref,
-    alog_ref,
-    dt_ref,
-    *refs,
-):
-    systems_of(recv_ref, ck_ref, alog_ref, dt_ref, *refs[3:])
+def systems_kernel(hop_ref, recv_ref, ck_ref, alog_ref, dt_ref, *refs):
+    del hop_ref
+
+    @pl.when(lax.axis_index("half") > 0)
+    def _():
+        systems_of(recv_ref, ck_ref, alog_ref, dt_ref, *refs)
 
 
 def systems_of(
@@ -235,7 +233,8 @@
     stacked.append(jnp.zeros((SPAN - spans * GATES, SPAN), F32))
     gates = jnp.concatenate(stacked, axis=0)
     decay, rate = gate_values(gates, sub, alog_ref, dt_ref)
-    early_ref[...] = jnp.where(iota((8, SPAN), 0) < 2, decay[0:8], rate[0:8])
+    if early_ref is not None:
+        early_ref[...] = jnp.where(iota((8, SPAN), 0) < 2, decay[0:8], rate[0:8])
     skipped = later & (iota(gates.shape, 0) < GATES) & (iota(gates.shape, 1) < EDGE)
     decay = jnp.where(skipped, 0.0, decay)
     rate = jnp.where(skipped, 0.0, rate)
@@ -375,20 +374,27 @@
 
 def opening_kernel(
     recv_ref,
+    ck_ref,
     cv_ref,
+    alog_ref,
+    dt_ref,
+    cq_ref,
+    gain_ref,
+    hop_ref,
     keys_ref,
     keys_t_ref,
-    systems_ref,
-    small_ref,
     ends_ref,
+    within_ref,
     cols_ref,
-    hop_ref,
     t_ref,
     lin_ref,
     vs_ref,
     xs_ref,
     adds_ref,
+    key_rows,
     rows,
+    systems_ref,
+    small_ref,
 ):
     first = lax.axis_index("half") == 0
     peers = recv_ref.shape[0]
@@ -404,6 +410,21 @@
     @pl.when(first)
     def _():
         both = [(n, r) for n in range(spans) for r in range(2)]
+        systems_of(
+            recv_ref,
+            ck_ref,
+            alog_ref,
+            dt_ref,
+            keys_ref,
+            keys_t_ref,
+            systems_ref,
+            small_ref,
+            ends_ref,
+            within_ref,
+            cols_ref,
+            None,
+            key_rows,
+        )
         taps = value_taps(lax.axis_index("sub"), cv_ref)
         widened(rows, recv_ref, [tokens, 2 * tokens], tokens)
         waiting = list(both)
@@ -737,15 +758,21 @@
     next_ref[2 * DK :, :] = hop_own[2 * DK :, :]
 
 
-def gate_kernel(heads_axis, normed_ref, z_ref, out_ref, made, sems):
-    subs, tokens = normed_ref.shape[0] // heads_axis, z_ref.shape[0]
+def open_gate_kernel(hop_ref, z_ref, gate_ref):
+    del hop_ref
+    for at in range(0, z_ref.shape[1], DV):
+        gate_ref[:, at : at + DV] = silu(z_ref[:, at : at + DV].astype(F32))
+
+
+def gate_kernel(heads_axis, normed_ref, gate_ref, out_ref, made, sems):
+    subs, tokens = normed_ref.shape[0] // heads_axis, gate_ref.shape[0]
     width = subs * 2 * DV
     copies = []
     for head in range(heads_axis):
         for sub in range(subs):
             for r in range(2):
                 at = (2 * (head * subs + sub) + r) * DV
-                gate = silu(z_ref[:, at : at + DV].astype(F32))
+                gate = gate_ref[:, at : at + DV]
                 here = slice(r * tokens, (r + 1) * tokens)
                 value = normed_ref[sub * heads_axis + head, here, :].astype(F32)
                 made[:, at : at + DV] = (value * gate).astype(BF16)
@@ -813,44 +840,43 @@
         flops=1 << 20,
     )(*inputs)
     blocks = near(lax.all_to_all(packed, group, 0, 0, tiled=True))
-    made = call(
-        systems_kernel,
-        (
-            pltpu.VMEM((total, DK), BF16),
-            pltpu.VMEM((spans, DK, SPAN), BF16),
-            pltpu.VMEM((2, spans, 2, SPAN, SPAN), BF16),
-            pltpu.VMEM((2, spans, SUB, SPAN), F32),
-            pltpu.VMEM((SPAN, DK), F32),
-            pltpu.VMEM((2, total, SPAN), BF16),
-            pltpu.VMEM((SPAN, SPAN), F32),
-            pltpu.VMEM((8, SPAN), F32),
-        ),
-        [VMEM, VMEM, SMEM, SMEM, VMEM, VMEM, VMEM],
-        [pltpu.VMEM((8 + total, DK), F32)],
-        flops=1 << 32,
-    )(blocks, conv_k, a_log, dt_bias, conv_q, conv_v, gain)
-    keys, keys_t, systems, small, ends, within, cols, early = (near(x) for x in made)
+    key_shapes = (pltpu.VMEM((total, DK), BF16), pltpu.VMEM((spans, DK, SPAN), BF16))
+    system_shapes = (
+        pltpu.VMEM((2, spans, 2, SPAN, SPAN), BF16),
+        pltpu.VMEM((2, spans, SUB, SPAN), F32),
+    )
+    decay_shapes = (
+        pltpu.VMEM((SPAN, DK), F32),
+        pltpu.VMEM((2, total, SPAN), BF16),
+        pltpu.VMEM((SPAN, SPAN), F32),
+    )
     map_shapes = (
         pltpu.VMEM((2, spans, 2, SPAN, SPAN), BF16),
         pltpu.VMEM((2, spans, DK, DK), BF16),
     )
-
-    hop, inverses, lins, values, starts, adds = call(
+    opened = call(
         opening_kernel,
         (
             pltpu.VMEM((2 * DK + 16, 128), BF16),
+            *key_shapes,
+            *decay_shapes,
             *map_shapes,
             pltpu.VMEM((2, total, DV), BF16),
             pltpu.VMEM((2, spans, 2 * DK, DV), BF16),
             pltpu.VMEM((2, spans, DK, DV), F32),
         ),
-        [VMEM] * 8,
-        [pltpu.VMEM((8 + total, 2 * DV), F32)],
+        [VMEM, VMEM, VMEM, SMEM, SMEM, VMEM, VMEM],
+        [
+            pltpu.VMEM((8 + total, DK), F32),
+            pltpu.VMEM((8 + total, 2 * DV), F32),
+            *system_shapes,
+        ],
         flops=1 << 32,
-    )(blocks, conv_v, keys, keys_t, systems, small, ends, cols)
+    )(blocks, conv_k, conv_v, a_log, dt_bias, conv_q, gain)
+    hop = opened[0]
     entering = near(lax.ppermute(hop, "half", route))
-    hop, inverses, lins, values, starts, adds = (
-        near(x) for x in (hop, inverses, lins, values, starts, adds)
+    hop, keys, keys_t, ends, within, cols, inverses, lins, values, starts, adds = (
+        near(x) for x in opened
     )
     first_out = call(
         first_outputs_kernel,
@@ -872,6 +898,17 @@
         starts,
         adds,
     )
+    open_gate = call(
+        open_gate_kernel, pltpu.VMEM(z_rows.shape, F32), [VMEM] * 2, flops=1 << 30
+    )(hop, near(z_rows))
+    made = call(
+        systems_kernel,
+        (*key_shapes, *system_shapes, *decay_shapes, pltpu.VMEM((8, SPAN), F32)),
+        [VMEM, VMEM, VMEM, SMEM, SMEM],
+        [pltpu.VMEM((8 + total, DK), F32)],
+        flops=1 << 32,
+    )(hop, blocks, conv_k, a_log, dt_bias)
+    keys, keys_t, systems, small, ends, within, cols, early = (near(x) for x in made)
     later_solved = call(inverse_kernel, map_shapes, [VMEM] * 6, flops=1 << 32)(
         hop, keys, keys_t, systems, small, cols
     )
@@ -937,7 +974,7 @@
         [VMEM] * 2,
         [pltpu.VMEM(z_rows.shape, BF16), pltpu.SemaphoreType.DMA((heads_axis,))],
         ANY,
-    )(returned, z_rows)
+    )(returned, near(open_gate))
 
 
 def solution(mesh):

time: 50.3 us -> 51.6 us (1.026)
  blocking collectives: 36.7 us -> 22.7 us
  waiting for transfers between devices: 0.01 us -> 10.3 us
  starting transfers between devices: 1.29 us -> 4.87 us
  Pallas kernels: 11.6 us -> 12.9 us
    all_to_all x1 -> x0, blocking collectives: 14 us -> none  [local(): returned = near(lax.all_to_all(normed, group, 0, 0, tiled=True))]
    all_to_all x0 -> x1, waiting for transfers between devices: none -> 10.3 us  [local(): returned = near(lax.all_to_all(normed, group, 0, 0, tiled=True))]
    all_to_all x0 -> x1, starting transfers between devices: none -> 3.57 us  [local(): returned = near(lax.all_to_all(normed, group, 0, 0, tiled=True))]
    pallas_call x1, Pallas kernels: 0.37 us -> 1.16 us  [local(): call(finish_kernel, pltpu.VMEM((peers, 2 * tokens, DV), BF16), [VMEM] * 1...]
    pallas_call x2 -> x3, Pallas kernels: 7.05 us -> 7.67 us  [the longest x1 6.93 us: local(): call(opening_kernel, (pltpu.VMEM((2 * DK + 16, 128), BF16), *key_shapes,...]
  transfers between devices with their start and end apart: 1 -> 2, of which waited for: 0 -> 1; matrix products, arithmetic and copies ran while one was open for 0% -> 0% of each run, Pallas kernels for 4% -> 5%
where the time goes in v18:
time: 51.6 us; the launch traced here: 51.2 us
  blocking collectives  22.7 us (44%)
  Pallas kernels  12.9 us (25%)
  waiting for transfers between devices  10.3 us (20%)
  starting transfers between devices  4.87 us (9%)
    all_to_all x1, blocking collectives, local(): blocks = near(lax.all_to_all(packed, group, 0, 0, tiled=True))  22.7 us
    all_to_all x1, waiting for transfers between devices, local(): returned = near(lax.all_to_all(normed, group, 0, 0, tiled=True))  10.3 us
    pallas_call x1, Pallas kernels, local(): call(opening_kernel, (pltpu.VMEM((2 * DK + 16, 128), BF16), *key_shapes,...  6.93 us
    all_to_all x1, starting transfers between devices, local(): returned = near(lax.all_to_all(normed, group, 0, 0, tiled=True))  3.57 us
    pallas_call x1, Pallas kernels, local(): call(first_outputs_kernel, pltpu.VMEM((2, total, DV), F32), [VMEM] * 12,...  1.67 us
    pallas_call x1, Pallas kernels, local(): call(functools.partial(pack_kernel, heads_axis), pltpu.VMEM((peers, GATES...  1.34 us
    ppermute x1, starting transfers between devices, local(): entering = near(lax.ppermute(hop, 'half', route))  1.29 us
    pallas_call x1, Pallas kernels, local(): call(finish_kernel, pltpu.VMEM((peers, 2 * tokens, DV), BF16), [VMEM] * 1...  1.16 us
  transfers between devices with their start and end apart: 2, of which 1 were waited for; matrix products, arithmetic and copies ran while one was open for 0% of the time, Pallas kernels for 5%

profile of v18, /device:TPU:0, one launch (start us, length us, event | category | flops | bytes accessed | tf_op | source)
XLA Modules:
  0.0 51.2 jit_solution(4642458285985055407)
XLA Ops:
  0.0 1.3 %shard_map.118 = bf16[16,264,128]{2,1,0:T(8,128)(2,1)S(1)} custom-call(bf16[64,2048]{1,0:T(8,128)(2,1)} %q_in.1, bf16[64,2048]{1,0:T(8,128)(2,1)} %k_in.1, bf16[64,4096]{1,0:T(8,128)(2,1)} %v_in.1, bf16[32,64]{1,0:T(8,128)(2,1)} %bitcast.5, bf16[32,64]{1,0:T(8,128)(2,1)} %bitcast.6), custom_call_target="tpu_custom_call" | custom-call | flops 1048576 | bytes 2097152 | tf_op jit(solution)/shard_map/pallas_call | solution.py:835
  1.3 0.0 copy-start
  1.4 0.0 copy-start.1
  1.4 0.0 copy-start.2
  1.4 0.0 copy-start.3
  1.4 0.0 copy-start.5
  1.4 0.0 copy-start.6
  1.4 22.7 %all_to_all.10.recv_ref = bf16[16,264,128]{2,1,0:T(8,128)(2,1)S(1)} all-to-all(bf16[16,264,128]{2,1,0:T(8,128)(2,1)S(1)} %shard_map.118), channel_id=1, replica_groups=mesh['half'=2,'sub'=4,'head'=4] {'sub','head'}, dimensions={0} | all-to-all | bytes 2162688 | tf_op jit(solution)/shard_map/all_to_all | solution.py:842
  24.2 0.0 copy-done
  24.2 0.0 copy-done.1
  24.2 0.0 copy-done.2
  24.2 0.0 copy-done.3
  24.2 0.0 copy-done.5
  24.2 0.0 copy-done.6
  24.2 6.9 %shard_map.119 = (bf16[272,128]{1,0:T(8,128)(2,1)S(1)}, bf16[1024,128]{1,0:T(8,128)(2,1)S(1)}, bf16[8,128,128]{2,1,0:T(8,128)(2,1)S(1)}, f32[128,128]{1,0:T(8,12...) custom-call(bf16[16,264,128]{2,1,0:T(8,128)(2,1)S(1)} %all_to_all.10, ...), custom_call_target="tpu_custom_call" | custom-call | flops 4294967296 | bytes 2097152 | tf_op jit(solution)/shard_map/pallas_call | solution.py:857
  31.1 1.3 %collective-permute-start = (bf16[272,128]{1,0:T(8,128)(2,1)S(1)}, bf16[272,128]{1,0:T(8,128)(2,1)S(1)}, u32[]{:S(2)}, u32[]{:S(2)}) collective-permute-start(bf16[272,128]{1,0:T(8,128)(2,1)S(1)} %get-tuple-element.30.hop_ref), channel_id=1, source_target_pairs={{0,16},{1,17},{2,18},{3,19},{4,20},{5,21},{6,22},{7,23},{8,24},{9,... | collective-permute-start | bytes 208904 | tf_op jit(solution)/shard_map/ppermute | solution.py:877
  32.4 0.6 %shard_map.120 = (bf16[1024,128]{1,0:T(8,128)(2,1)S(1)}, bf16[8,128,128]{2,1,0:T(8,128)(2,1)S(1)}, bf16[2,8,2,128,128]{4,3,2,1,0:T(8,128)(2,1)S(1)}, f32[2,8,16,...) custom-call(bf16[272,128]{1,0:T(8,128)(2,1)S(1)} %get-tuple-element., ...), custom_call_target="tpu_custom_call" | custom-call | flops 4294967296 | bytes 2097152 | tf_op jit(solution)/shard_map/pallas_call | solution.py:904
  33.0 0.2 shard_map.123
  33.3 1.7 %shard_map.121.first_oa = f32[2,1024,128]{2,1,0:T(8,128)S(1)} custom-call(bf16[16,264,128]{2,1,0:T(8,128)(2,1)S(1)} %all_to_all.10.recv_ref, f32[4,512]{1,0:T(4,128)S(1)} %copy-done.2, bf16[1024,128]{1,0:T(8,128)(2,1)S(1)} %get-tuple-element.32.keys_ref, bf16[8,128,128]{2,1,0:T(8,128)(2,1)S(1)} %get-tuple-element.33.keys_t_ref, ...), custom_call_target="tpu_custom_call" | custom-call | flops 4294967296 | bytes 2097152 | tf_op jit(solution)/shard_map/pallas_call | solution.py:881
  34.9 0.0 collective-permute-done.hop_ref
  35.0 0.0 copy-start.4
  35.0 1.2 %shard_map.125 = bf16[16,128,128]{2,1,0:T(8,128)(2,1)} custom-call(bf16[272,128]{1,0:T(8,128)(2,1)S(1)} %collective-permute-done.hop_ref, bf16[16,264,128]{2,1,0:T(8,128)(2,1)S(1)} %all_to_all.10.recv_ref, f32[8,128]{1,0:T(8,128)S(1)} %get-tuple-element.31.early_ref, f32[4,512]{1,0:T(4,128)S(1)} %copy-done.2, f32[4,512]{1,0:T(4,128)S(1)} %copy-done.1, ...), custom_call_target="tpu_custom_call" | custom-call | flops 67108864 | bytes 2097152 | tf_op jit(solution)/shard_map/pallas_call | solution.py:953
  36.1 3.6 %all-to-all-start.1 = ((bf16[16,128,128]{2,1,0:T(8,128)(2,1)}), bf16[16,128,128]{2,1,0:T(8,128)(2,1)S(1)}, u32[]{:S(2)}, u32[]{:S(2)}) async-start(bf16[16,128,128]{2,1,0:T(8,128)(2,1)} %shard_map.125), calls=%async_computation.1 | async-start | bytes 1048576 | tf_op jit(solution)/shard_map/all_to_all | solution.py:970
  39.7 0.0 copy-done.4
  39.7 0.2 shard_map.126.gate_ref
  39.9 10.3 %all-to-all-done.1.normed_ref = bf16[16,128,128]{2,1,0:T(8,128)(2,1)S(1)} async-done(((bf16[16,128,128]{2,1,0:T(8,128)(2,1)}), bf16[16,128,128]{2,1,0:T(8,128)(2,1)S(1)}, u32[]{:S(2)}, u32[]{:S(2)}) %all-to-all-start.1) | async-done | bytes 524320 | tf_op jit(solution)/shard_map/all_to_all | solution.py:970
  50.2 0.8 %shard_map.127 = bf16[64,4096]{1,0:T(8,128)(2,1)} custom-call(bf16[16,128,128]{2,1,0:T(8,128)(2,1)S(1)} %all-to-all-done.1.normed_ref, f32[64,4096]{1,0:T(8,128)S(1)} %shard_map.126.gate_ref), custom_call_target="tpu_custom_call" | custom-call | flops 67108864 | bytes 2097152 | tf_op jit(solution)/shard_map/pallas_call | solution.py:971
  (2 shorter events, 0.0 us)
Async XLA Ops:
  1.3 22.8 %copy-start = (f32[4,1024]{1,0:T(4,128)S(1)}, f32[4,1024]{1,0:T(4,128)}, u32[]{:S(2)}) copy-start(f32[4,1024]{1,0:T(4,128)} %cv_ref.5) | copy-start | bytes 49156
  1.4 22.8 %copy-start.1 = (f32[4,512]{1,0:T(4,128)S(1)}, f32[4,512]{1,0:T(4,128)}, u32[]{:S(2)}) copy-start(f32[4,512]{1,0:T(4,128)} %ck_ref.5) | copy-start | bytes 24580
  1.4 22.8 %copy-start.2 = (f32[4,512]{1,0:T(4,128)S(1)}, f32[4,512]{1,0:T(4,128)}, u32[]{:S(2)}) copy-start(f32[4,512]{1,0:T(4,128)} %cq_ref.7) | copy-start | bytes 24580
  1.4 22.8 %copy-start.3 = (f32[128]{0:T(128)S(1)}, f32[128]{0:T(128)}, u32[]{:S(2)}) copy-start(f32[128]{0:T(128)} %param.23) | copy-start | bytes 1540
  1.4 22.8 %copy-start.5 = (f32[8]{0:T(128)S(1)}, f32[8]{0:T(128)}, u32[]{:S(2)}) copy-start(f32[8]{0:T(128)} %alog_ref.3) | copy-start | bytes 100
  1.4 22.8 %copy-start.6 = (f32[8]{0:T(128)S(1)}, f32[8]{0:T(128)}, u32[]{:S(2)}) copy-start(f32[8]{0:T(128)} %dt_ref.3) | copy-start | bytes 100
  31.1 3.8 %collective-permute-start = (bf16[272,128]{1,0:T(8,128)(2,1)S(1)}, bf16[272,128]{1,0:T(8,128)(2,1)S(1)}, u32[]{:S(2)}, u32[]{:S(2)}) collective-permute-start(bf16[272,128]{1,0:T(8,128)(2,1)S(1)} %get-tuple-element.30.hop_ref), channel_id=1, source_target_pairs={{0,16},{1,17},{2,18},{3,19},{4,20},{5,21},{6,22},{7,23},{8,24},{9,... | collective-permute-start | bytes 208904 | tf_op jit(solution)/shard_map/ppermute | solution.py:877
  35.0 4.8 %copy-start.4 = (bf16[64,4096]{1,0:T(8,128)(2,1)S(1)}, bf16[64,4096]{1,0:T(8,128)(2,1)}, u32[]{:S(2)}) copy-start(bf16[64,4096]{1,0:T(8,128)(2,1)} %z_ref.1) | copy-start | bytes 1572868
  36.1 14.1 %all-to-all-start.1 = ((bf16[16,128,128]{2,1,0:T(8,128)(2,1)}), bf16[16,128,128]{2,1,0:T(8,128)(2,1)S(1)}, u32[]{:S(2)}, u32[]{:S(2)}) async-start(bf16[16,128,128]{2,1,0:T(8,128)(2,1)} %shard_map.125), calls=%async_computation.1 | async-start | bytes 1048576 | tf_op jit(solution)/shard_map/all_to_all | solution.py:970

commit v19 on v18

--- a/solution.py
+++ b/solution.py
@@ -162,10 +162,17 @@
     return [halves(t.astype(F32) + dot(t, rest)) for t, rest in zip(rough, rests)]
 
 
+def own_entry(ref, index):
+    row = ref[...]
+    return jnp.sum(jnp.where(iota(row.shape, 1) == index, row, 0.0), axis=1, keepdims=True)
+
+
 def gate_values(gates, sub, alog_ref, dt_ref):
     second = place_in(iota(gates.shape, 0), GATES) == 1
-    a_log = jnp.where(second, alog_ref[2 * sub + 1], alog_ref[2 * sub])
-    dt_bias = jnp.where(second, dt_ref[2 * sub + 1], dt_ref[2 * sub])
+    a_log, dt_bias = (
+        jnp.where(second, own_entry(ref, 2 * sub + 1), own_entry(ref, 2 * sub))
+        for ref in (alog_ref, dt_ref)
+    )
     shifted = gates + dt_bias
     soft = jnp.maximum(shifted, 0.0) + jnp.log1p(jnp.exp(-jnp.abs(shifted)))
     return -jnp.exp(a_log) * soft, 1.0 / (1.0 + jnp.exp(-gates))
@@ -758,21 +765,15 @@
     next_ref[2 * DK :, :] = hop_own[2 * DK :, :]
 
 
-def open_gate_kernel(hop_ref, z_ref, gate_ref):
-    del hop_ref
-    for at in range(0, z_ref.shape[1], DV):
-        gate_ref[:, at : at + DV] = silu(z_ref[:, at : at + DV].astype(F32))
-
-
-def gate_kernel(heads_axis, normed_ref, gate_ref, out_ref, made, sems):
-    subs, tokens = normed_ref.shape[0] // heads_axis, gate_ref.shape[0]
+def gate_kernel(heads_axis, normed_ref, z_ref, out_ref, made, sems):
+    subs, tokens = normed_ref.shape[0] // heads_axis, z_ref.shape[0]
     width = subs * 2 * DV
     copies = []
     for head in range(heads_axis):
         for sub in range(subs):
             for r in range(2):
                 at = (2 * (head * subs + sub) + r) * DV
-                gate = gate_ref[:, at : at + DV]
+                gate = silu(z_ref[:, at : at + DV].astype(F32))
                 here = slice(r * tokens, (r + 1) * tokens)
                 value = normed_ref[sub * heads_axis + head, here, :].astype(F32)
                 made[:, at : at + DV] = (value * gate).astype(BF16)
@@ -785,7 +786,6 @@
 
 
 VMEM = pl.BlockSpec(memory_space=pltpu.VMEM)
-SMEM = pl.BlockSpec(memory_space=pltpu.SMEM)
 ANY = pl.BlockSpec(memory_space=pl.ANY)
 
 
@@ -831,6 +831,7 @@
     route = [(i, i + 1) for i in range(shards - 1)]
     conv_q, conv_k, conv_v = near(conv_q), near(conv_k), near(conv_v)
     gain = near(norm_gain.reshape(1, DV))
+    a_log, dt_bias = near(a_log.reshape(1, -1)), near(dt_bias.reshape(1, -1))
     inputs = [far(x) for x in (q_rows, k_rows, v_rows, a_rows.T, b_rows.T)]
     packed = call(
         functools.partial(pack_kernel, heads_axis),
@@ -865,7 +866,7 @@
             pltpu.VMEM((2, spans, 2 * DK, DV), BF16),
             pltpu.VMEM((2, spans, DK, DV), F32),
         ),
-        [VMEM, VMEM, VMEM, SMEM, SMEM, VMEM, VMEM],
+        [VMEM] * 7,
         [
             pltpu.VMEM((8 + total, DK), F32),
             pltpu.VMEM((8 + total, 2 * DV), F32),
@@ -898,13 +899,10 @@
         starts,
         adds,
     )
-    open_gate = call(
-        open_gate_kernel, pltpu.VMEM(z_rows.shape, F32), [VMEM] * 2, flops=1 << 30
-    )(hop, near(z_rows))
     made = call(
         systems_kernel,
         (*key_shapes, *system_shapes, *decay_shapes, pltpu.VMEM((8, SPAN), F32)),
-        [VMEM, VMEM, VMEM, SMEM, SMEM],
+        [VMEM] * 5,
         [pltpu.VMEM((8 + total, DK), F32)],
         flops=1 << 32,
     )(hop, blocks, conv_k, a_log, dt_bias)
@@ -974,7 +972,7 @@
         [VMEM] * 2,
         [pltpu.VMEM(z_rows.shape, BF16), pltpu.SemaphoreType.DMA((heads_axis,))],
         ANY,
-    )(returned, near(open_gate))
+    )(returned, z_rows)
 
 
 def solution(mesh):

time: 51.6 us -> 49.7 us (0.963)
  blocking collectives: 22.7 us -> 36.7 us
  waiting for transfers between devices: 10.3 us -> 0.01 us
  starting transfers between devices: 4.87 us -> 1.29 us
  Pallas kernels: 12.9 us -> 11.1 us
    all_to_all x0 -> x1, blocking collectives: none -> 13.9 us  [local(): returned = near(lax.all_to_all(normed, group, 0, 0, tiled=True))]
    all_to_all x1 -> x0, waiting for transfers between devices: 10.3 us -> none  [local(): returned = near(lax.all_to_all(normed, group, 0, 0, tiled=True))]
    all_to_all x1 -> x0, starting transfers between devices: 3.57 us -> none  [local(): returned = near(lax.all_to_all(normed, group, 0, 0, tiled=True))]
    pallas_call x1, Pallas kernels: 1.16 us -> 0.37 us  [local(): call(finish_kernel, pltpu.VMEM((peers, 2 * tokens, DV), BF16), [VMEM] * 1...]
    pallas_call x1, Pallas kernels: 0.56 us -> 0.02 us  [local(): call(systems_kernel, (*key_shapes, *system_shapes, *decay_shapes, pltpu.V...]
  transfers between devices with their start and end apart: 2 -> 1, of which waited for: 1 -> 0; matrix products, arithmetic and copies ran while one was open for 0% -> 0% of each run, Pallas kernels for 5% -> 4%
where the time goes in v19:
time: 49.7 us; the launch traced here: 49.4 us
  blocking collectives  36.7 us (74%)
  Pallas kernels  11.1 us (22%)
  starting transfers between devices  1.29 us (3%)
    all_to_all x1, blocking collectives, local(): blocks = near(lax.all_to_all(packed, group, 0, 0, tiled=True))  22.7 us
    all_to_all x1, blocking collectives, local(): returned = near(lax.all_to_all(normed, group, 0, 0, tiled=True))  13.9 us
    pallas_call x1, Pallas kernels, local(): call(opening_kernel, (pltpu.VMEM((2 * DK + 16, 128), BF16), *key_shapes,...  6.49 us
    pallas_call x1, Pallas kernels, local(): call(first_outputs_kernel, pltpu.VMEM((2, total, DV), F32), [VMEM] * 12,...  1.68 us
    pallas_call x1, Pallas kernels, local(): call(functools.partial(pack_kernel, heads_axis), pltpu.VMEM((peers, GATES...  1.34 us
    ppermute x1, starting transfers between devices, local(): entering = near(lax.ppermute(hop, 'half', route))  1.29 us
  transfers between devices with their start and end apart: 1, of which 0 were waited for; matrix products, arithmetic and copies ran while one was open for 0% of the time, Pallas kernels for 4%

profile of v19, /device:TPU:0, one launch (start us, length us, event | category | flops | bytes accessed | tf_op | source)
XLA Modules:
  0.0 49.4 jit_solution(9277971472377468261)
XLA Ops:
  0.0 1.3 %shard_map.118 = bf16[16,264,128]{2,1,0:T(8,128)(2,1)S(1)} custom-call(bf16[64,2048]{1,0:T(8,128)(2,1)} %q_in.1, bf16[64,2048]{1,0:T(8,128)(2,1)} %k_in.1, bf16[64,4096]{1,0:T(8,128)(2,1)} %v_in.1, bf16[32,64]{1,0:T(8,128)(2,1)} %bitcast.11, bf16[32,64]{1,0:T(8,128)(2,1)} %bitcast.12), custom_call_target="tpu_custom_call" | custom-call | flops 1048576 | bytes 2097152 | tf_op jit(solution)/shard_map/pallas_call | solution.py:836
  1.3 0.0 copy-start.1
  1.4 0.0 copy-start.2
  1.4 0.0 copy-start.3
  1.4 0.0 copy-start.4
  1.4 0.0 copy-start.5
  1.4 0.0 copy-start.6
  1.4 22.7 %all_to_all.10.recv_ref = bf16[16,264,128]{2,1,0:T(8,128)(2,1)S(1)} all-to-all(bf16[16,264,128]{2,1,0:T(8,128)(2,1)S(1)} %shard_map.118), channel_id=1, replica_groups=mesh['half'=2,'sub'=4,'head'=4] {'sub','head'}, dimensions={0} | all-to-all | bytes 2162688 | tf_op jit(solution)/shard_map/all_to_all | solution.py:843
  24.2 0.0 copy-done.1
  24.2 0.0 copy-done.2
  24.2 0.0 copy-done.3
  24.2 0.0 copy-done.4
  24.2 0.0 copy-done.5
  24.2 0.0 copy-done.6
  24.2 6.5 %shard_map.119 = (bf16[272,128]{1,0:T(8,128)(2,1)S(1)}, bf16[1024,128]{1,0:T(8,128)(2,1)S(1)}, bf16[8,128,128]{2,1,0:T(8,128)(2,1)S(1)}, f32[128,128]{1,0:T(8,12...) custom-call(bf16[16,264,128]{2,1,0:T(8,128)(2,1)S(1)} %all_to_all.10, ...), custom_call_target="tpu_custom_call" | custom-call | flops 4294967296 | bytes 2097152 | tf_op jit(solution)/shard_map/pallas_call | solution.py:858
  30.7 1.3 %collective-permute-start = (bf16[272,128]{1,0:T(8,128)(2,1)S(1)}, bf16[272,128]{1,0:T(8,128)(2,1)S(1)}, u32[]{:S(2)}, u32[]{:S(2)}) collective-permute-start(bf16[272,128]{1,0:T(8,128)(2,1)S(1)} %get-tuple-element.30.hop_ref), channel_id=1, source_target_pairs={{0,16},{1,17},{2,18},{3,19},{4,20},{5,21},{6,22},{7,23},{8,24},{9,... | collective-permute-start | bytes 208904 | tf_op jit(solution)/shard_map/ppermute | solution.py:878
  32.0 0.2 shard_map.123
  32.3 1.7 %shard_map.121.first_oa = f32[2,1024,128]{2,1,0:T(8,128)S(1)} custom-call(bf16[16,264,128]{2,1,0:T(8,128)(2,1)S(1)} %all_to_all.10.recv_ref, f32[4,512]{1,0:T(4,128)S(1)} %copy-done.3, bf16[1024,128]{1,0:T(8,128)(2,1)S(1)} %get-tuple-element.32.keys_ref, bf16[8,128,128]{2,1,0:T(8,128)(2,1)S(1)} %get-tuple-element.33.keys_t_ref, ...), custom_call_target="tpu_custom_call" | custom-call | flops 4294967296 | bytes 2097152 | tf_op jit(solution)/shard_map/pallas_call | solution.py:882
  34.0 0.0 collective-permute-done.hop_ref
  34.0 0.4 shard_map.125
  34.4 0.0 copy-start
  34.4 13.9 %all_to_all.11.normed_ref = bf16[16,128,128]{2,1,0:T(8,128)(2,1)S(1)} all-to-all(bf16[16,128,128]{2,1,0:T(8,128)(2,1)S(1)} %shard_map.125), channel_id=1, replica_groups=mesh['half'=2,'sub'=4,'head'=4] {'sub','head'}, dimensions={0} | all-to-all | bytes 1048576 | tf_op jit(solution)/shard_map/all_to_all | solution.py:968
  48.3 0.0 copy-done
  48.3 1.0 %shard_map.126 = bf16[64,4096]{1,0:T(8,128)(2,1)} custom-call(bf16[16,128,128]{2,1,0:T(8,128)(2,1)S(1)} %all_to_all.11.normed_ref, bf16[64,4096]{1,0:T(8,128)(2,1)S(1)} %copy-done), custom_call_target="tpu_custom_call" | custom-call | flops 67108864 | bytes 2097152 | tf_op jit(solution)/shard_map/pallas_call | solution.py:969
  (3 shorter events, 0.1 us)
Async XLA Ops:
  1.3 22.8 %copy-start.1 = (f32[4,1024]{1,0:T(4,128)S(1)}, f32[4,1024]{1,0:T(4,128)}, u32[]{:S(2)}) copy-start(f32[4,1024]{1,0:T(4,128)} %cv_ref.5) | copy-start | bytes 49156
  1.4 22.8 %copy-start.2 = (f32[4,512]{1,0:T(4,128)S(1)}, f32[4,512]{1,0:T(4,128)}, u32[]{:S(2)}) copy-start(f32[4,512]{1,0:T(4,128)} %ck_ref.5) | copy-start | bytes 24580
  1.4 22.8 %copy-start.3 = (f32[4,512]{1,0:T(4,128)S(1)}, f32[4,512]{1,0:T(4,128)}, u32[]{:S(2)}) copy-start(f32[4,512]{1,0:T(4,128)} %cq_ref.7) | copy-start | bytes 24580
  1.4 22.8 %copy-start.4 = (f32[128]{0:T(128)S(1)}, f32[128]{0:T(128)}, u32[]{:S(2)}) copy-start(f32[128]{0:T(128)} %param.23) | copy-start | bytes 1540
  1.4 22.8 %copy-start.5 = (f32[8]{0:T(128)S(1)}, f32[8]{0:T(128)}, u32[]{:S(2)}) copy-start(f32[8]{0:T(128)} %param.21) | copy-start | bytes 100
  1.4 22.8 %copy-start.6 = (f32[8]{0:T(128)S(1)}, f32[8]{0:T(128)}, u32[]{:S(2)}) copy-start(f32[8]{0:T(128)} %param.22) | copy-start | bytes 100
  30.7 3.3 %collective-permute-start = (bf16[272,128]{1,0:T(8,128)(2,1)S(1)}, bf16[272,128]{1,0:T(8,128)(2,1)S(1)}, u32[]{:S(2)}, u32[]{:S(2)}) collective-permute-start(bf16[272,128]{1,0:T(8,128)(2,1)S(1)} %get-tuple-element.30.hop_ref), channel_id=1, source_target_pairs={{0,16},{1,17},{2,18},{3,19},{4,20},{5,21},{6,22},{7,23},{8,24},{9,... | collective-permute-start | bytes 208904 | tf_op jit(solution)/shard_map/ppermute | solution.py:878
  34.4 13.9 %copy-start = (bf16[64,4096]{1,0:T(8,128)(2,1)S(1)}, bf16[64,4096]{1,0:T(8,128)(2,1)}, u32[]{:S(2)}) copy-start(bf16[64,4096]{1,0:T(8,128)(2,1)} %z_ref.1) | copy-start | bytes 1572868

commit v20 on v19

--- a/solution.py
+++ b/solution.py
@@ -13,6 +13,7 @@
 KH = 16
 SUB = 16
 SPAN = 128
+CHUNKS = 4
 EDGE = CONV - 1
 EPS = 1e-06
 F32 = jnp.float32
@@ -685,25 +686,45 @@
     k_cols = jnp.transpose(unit(results[1], 1.0).astype(F32))
     gates = early_ref[...]
     line = iota((8, DV), 0)
-    finals, outputs = [], []
-    for r in range(2):
-        values = results[2 + r].astype(BF16).astype(F32)
-        entering = hop_ref[r * DK : (r + 1) * DK, :].astype(F32)
-        state, out = entering, jnp.zeros((8, DV), F32)
-        for t in range(EDGE):
-            k_t, q_t = k_cols[:, t : t + 1], q_cols[:, t : t + 1]
-            state = jnp.exp(gates[r : r + 1, t : t + 1]) * state
-            held = jnp.sum(k_t * state, axis=0, keepdims=True)
-            state = state + k_t * (
-                gates[2 + r : 3 + r, t : t + 1] * (values[t : t + 1, :] - held)
-            )
-            out = jnp.where(line == t, jnp.sum(q_t * state, axis=0, keepdims=True), out)
-        finals.append(state)
-        outputs.append(out)
-    return finals, outputs
-
-
-def finish_kernel(
+    values = [x.astype(BF16).astype(F32) for x in results[2:]]
+    states = [hop_ref[r * DK : (r + 1) * DK, :].astype(F32) for r in range(2)]
+    outputs = [jnp.zeros((8, DV), F32) for r in range(2)]
+    for t in range(EDGE):
+        k_t, q_t = k_cols[:, t : t + 1], q_cols[:, t : t + 1]
+        states = [jnp.exp(gates[r : r + 1, t : t + 1]) * states[r] for r in range(2)]
+        held = [jnp.sum(k_t * x, axis=0, keepdims=True) for x in states]
+        fresh = [
+            gates[2 + r : 3 + r, t : t + 1] * (values[r][t : t + 1, :] - held[r])
+            for r in range(2)
+        ]
+        states = [x + k_t * y for x, y in zip(states, fresh)]
+        outputs = [
+            jnp.where(line == t, jnp.sum(q_t * x, axis=0, keepdims=True), y)
+            for x, y in zip(states, outputs)
+        ]
+    return states, outputs
+
+
+def put(out_ref, gain, c, r, core):
+    peer_part, tokens = out_ref.shape[0] // CHUNKS, out_ref.shape[1] // 2
+    scale = lax.rsqrt(jnp.mean(core * core, axis=-1, keepdims=True) + EPS)
+    normed = (core * scale * gain).astype(BF16)
+    here = slice(c * peer_part, (c + 1) * peer_part)
+    out_ref[here, r * tokens : (r + 1) * tokens, :] = normed.reshape(peer_part, tokens, DV)
+
+
+def first_finish_kernel(gain_ref, oa_ref, out_ref):
+    @pl.when(lax.axis_index("half") == 0)
+    def _():
+        gain = gain_ref[...]
+        part = oa_ref.shape[1] // CHUNKS
+        for c in range(CHUNKS):
+            for r in range(2):
+                put(out_ref, gain, c, r, oa_ref[r, c * part : (c + 1) * part, :])
+
+
+def later_finish_kernel(
+    normed_ref,
     hop_ref,
     recv_ref,
     early_ref,
@@ -711,36 +732,21 @@
     ck_ref,
     cv_ref,
     gain_ref,
-    first_oa,
     oa_ref,
     om_ref,
     out_ref,
     rows,
 ):
-    peers, tokens = out_ref.shape[0], out_ref.shape[1] // 2
-    first = lax.axis_index("half") == 0
-    gain = gain_ref[...]
-    chunks = 4
-    part, peer_part = peers * tokens // chunks, peers // chunks
-
-    def put(c, r, core):
-        scale = lax.rsqrt(jnp.mean(core * core, axis=-1, keepdims=True) + EPS)
-        normed = (core * scale * gain).astype(BF16)
-        here = slice(c * peer_part, (c + 1) * peer_part)
-        out_ref[here, r * tokens : (r + 1) * tokens, :] = normed.reshape(peer_part, tokens, DV)
-
-    @pl.when(first)
+    del normed_ref
+
+    @pl.when(lax.axis_index("half") > 0)
     def _():
-        for c in range(chunks):
-            for r in range(2):
-                put(c, r, first_oa[r, c * part : (c + 1) * part, :])
-
-    @pl.when(jnp.logical_not(first))
-    def _():
+        gain = gain_ref[...]
+        part = oa_ref.shape[1] // CHUNKS
         finals, outputs = first_tokens(hop_ref, recv_ref, early_ref, cq_ref, ck_ref, cv_ref, rows)
         replaced = iota((8, DV), 0) < EDGE
         passed = [dot(om_ref[r], finals[r].astype(BF16)) for r in range(2)]
-        for c in range(chunks):
+        for c in range(CHUNKS):
             at = c * part
             for r in range(2):
                 core = oa_ref[r, at : at + part, :] + passed[r][at : at + part]
@@ -748,7 +754,7 @@
                     core = jnp.concatenate(
                         [jnp.where(replaced, outputs[r], core[0:8]), core[8:]], axis=0
                     )
-                put(c, r, core)
+                put(out_ref, gain, c, r, core)
 
 
 def advance_kernel(
@@ -797,13 +803,16 @@
     return pltpu.with_memory_space_constraint(x, pltpu.HBM)
 
 
-def call(kernel, outs, in_specs, scratch=(), out_spec=VMEM, flops=1 << 26, moved=1 << 21):
+def call(
+    kernel, outs, in_specs, scratch=(), out_spec=VMEM, flops=1 << 26, moved=1 << 21, aliases=()
+):
     return pl.pallas_call(
         kernel,
         out_shape=outs,
         in_specs=in_specs,
         out_specs=jax.tree.map(lambda _: out_spec, outs),
         scratch_shapes=list(scratch),
+        input_output_aliases=dict(aliases),
         compiler_params=pltpu.CompilerParams(vmem_limit_bytes=VMEM_BYTES),
         cost_estimate=pl.CostEstimate(flops=flops, bytes_accessed=moved, transcendentals=0),
     )
@@ -948,12 +957,18 @@
             [pltpu.VMEM((32, 512), F32)],
         )(entering, blocks, early, conv_q, conv_k, conv_v, hop, near(last[0]))
         entering = near(lax.ppermute(moved, "half", route))
+    normed_shape = pltpu.VMEM((peers, 2 * tokens, DV), BF16)
+    first_normed = call(first_finish_kernel, normed_shape, [VMEM] * 2, flops=1 << 30)(
+        gain, near(first_out)
+    )
     normed = call(
-        finish_kernel,
-        pltpu.VMEM((peers, 2 * tokens, DV), BF16),
+        later_finish_kernel,
+        normed_shape,
         [VMEM] * 10,
         [pltpu.VMEM((32, 512), F32)],
+        aliases=((0, 0),),
     )(
+        near(first_normed),
         entering,
         blocks,
         early,
@@ -961,7 +976,6 @@
         conv_k,
         conv_v,
         gain,
-        near(first_out),
         near(out_a),
         near(out_m),
     )

time: 49.7 us -> 49.6 us (level)
  transfers between devices with their start and end apart: 1 -> 1, of which waited for: 0 -> 0; matrix products, arithmetic and copies ran while one was open for 0% -> 0% of each run, Pallas kernels for 4% -> 5%
where the time goes in v20:
time: 49.6 us; the launch traced here: 49 us
  blocking collectives  36.3 us (73%)
  Pallas kernels  11.1 us (22%)
  starting transfers between devices  1.29 us (3%)
    all_to_all x1, blocking collectives, local(): blocks = near(lax.all_to_all(packed, group, 0, 0, tiled=True))  22.7 us
    all_to_all x1, blocking collectives, local(): returned = near(lax.all_to_all(normed, group, 0, 0, tiled=True))  13.5 us
    pallas_call x1, Pallas kernels, local(): call(opening_kernel, (pltpu.VMEM((2 * DK + 16, 128), BF16), *key_shapes,...  6.49 us
    pallas_call x1, Pallas kernels, local(): call(first_outputs_kernel, pltpu.VMEM((2, total, DV), F32), [VMEM] * 12,...  1.68 us
    pallas_call x1, Pallas kernels, local(): call(functools.partial(pack_kernel, heads_axis), pltpu.VMEM((peers, GATES...  1.34 us
    ppermute x1, starting transfers between devices, local(): entering = near(lax.ppermute(hop, 'half', route))  1.29 us
  transfers between devices with their start and end apart: 1, of which 0 were waited for; matrix products, arithmetic and copies ran while one was open for 0% of the time, Pallas kernels for 5%

profile of v20, /device:TPU:0, one launch (start us, length us, event | category | flops | bytes accessed | tf_op | source)
XLA Modules:
  0.0 49.0 jit_solution(12629400176134272874)
XLA Ops:
  0.0 1.3 %shard_map.118 = bf16[16,264,128]{2,1,0:T(8,128)(2,1)S(1)} custom-call(bf16[64,2048]{1,0:T(8,128)(2,1)} %q_in.1, bf16[64,2048]{1,0:T(8,128)(2,1)} %k_in.1, bf16[64,4096]{1,0:T(8,128)(2,1)} %v_in.1, bf16[32,64]{1,0:T(8,128)(2,1)} %bitcast.12, bf16[32,64]{1,0:T(8,128)(2,1)} %bitcast.13), custom_call_target="tpu_custom_call" | custom-call | flops 1048576 | bytes 2097152 | tf_op jit(solution)/shard_map/pallas_call | solution.py:845
  1.3 0.0 copy-start.1
  1.4 0.0 copy-start.2
  1.4 0.0 copy-start.3
  1.4 0.0 copy-start.4
  1.4 0.0 copy-start.5
  1.4 0.0 copy-start.6
  1.4 22.7 %all_to_all.10.recv_ref = bf16[16,264,128]{2,1,0:T(8,128)(2,1)S(1)} all-to-all(bf16[16,264,128]{2,1,0:T(8,128)(2,1)S(1)} %shard_map.118), channel_id=1, replica_groups=mesh['half'=2,'sub'=4,'head'=4] {'sub','head'}, dimensions={0} | all-to-all | bytes 2162688 | tf_op jit(solution)/shard_map/all_to_all | solution.py:852
  24.2 0.0 copy-done.1
  24.2 0.0 copy-done.2
  24.2 0.0 copy-done.3
  24.2 0.0 copy-done.4
  24.2 0.0 copy-done.5
  24.2 0.0 copy-done.6
  24.2 6.5 %shard_map.119 = (bf16[272,128]{1,0:T(8,128)(2,1)S(1)}, bf16[1024,128]{1,0:T(8,128)(2,1)S(1)}, bf16[8,128,128]{2,1,0:T(8,128)(2,1)S(1)}, f32[128,128]{1,0:T(8,12...) custom-call(bf16[16,264,128]{2,1,0:T(8,128)(2,1)S(1)} %all_to_all.10, ...), custom_call_target="tpu_custom_call" | custom-call | flops 4294967296 | bytes 2097152 | tf_op jit(solution)/shard_map/pallas_call | solution.py:867
  30.7 1.3 %collective-permute-start = (bf16[272,128]{1,0:T(8,128)(2,1)S(1)}, bf16[272,128]{1,0:T(8,128)(2,1)S(1)}, u32[]{:S(2)}, u32[]{:S(2)}) collective-permute-start(bf16[272,128]{1,0:T(8,128)(2,1)S(1)} %get-tuple-element.40.hop_ref), channel_id=1, source_target_pairs={{0,16},{1,17},{2,18},{3,19},{4,20},{5,21},{6,22},{7,23},{8,24},{9,... | collective-permute-start | bytes 208904 | tf_op jit(solution)/shard_map/ppermute | solution.py:887
  32.0 0.2 shard_map.124
  32.3 1.7 %shard_map.120.oa_ref = f32[2,1024,128]{2,1,0:T(8,128)S(1)} custom-call(bf16[16,264,128]{2,1,0:T(8,128)(2,1)S(1)} %all_to_all.10.recv_ref, f32[4,512]{1,0:T(4,128)S(1)} %copy-done.2, bf16[1024,128]{1,0:T(8,128)(2,1)S(1)} %get-tuple-element.30.keys_ref, bf16[8,128,128]{2,1,0:T(8,128)(2,1)S(1)} %get-tuple-element.31.keys_t_ref, ...), custom_call_target="tpu_custom_call" | custom-call | flops 4294967296 | bytes 2097152 | tf_op jit(solution)/shard_map/pallas_call | solution.py:891
  34.0 0.4 shard_map.121.normed_ref
  34.3 0.0 collective-permute-done.hop_ref
  34.4 0.0 copy-start
  34.4 13.5 %all_to_all.11.normed_ref = bf16[16,128,128]{2,1,0:T(8,128)(2,1)S(1)} all-to-all(bf16[16,128,128]{2,1,0:T(8,128)(2,1)S(1)} %shard_map.126), channel_id=1, replica_groups=mesh['half'=2,'sub'=4,'head'=4] {'sub','head'}, dimensions={0} | all-to-all | bytes 1048576 | tf_op jit(solution)/shard_map/all_to_all | solution.py:982
  47.9 0.0 copy-done
  47.9 1.0 %shard_map.127 = bf16[64,4096]{1,0:T(8,128)(2,1)} custom-call(bf16[16,128,128]{2,1,0:T(8,128)(2,1)S(1)} %all_to_all.11.normed_ref, bf16[64,4096]{1,0:T(8,128)(2,1)S(1)} %copy-done), custom_call_target="tpu_custom_call" | custom-call | flops 67108864 | bytes 2097152 | tf_op jit(solution)/shard_map/pallas_call | solution.py:983
  (4 shorter events, 0.1 us)
Async XLA Ops:
  1.3 22.8 %copy-start.1 = (f32[4,1024]{1,0:T(4,128)S(1)}, f32[4,1024]{1,0:T(4,128)}, u32[]{:S(2)}) copy-start(f32[4,1024]{1,0:T(4,128)} %cv_ref.5) | copy-start | bytes 49156
  1.4 22.8 %copy-start.2 = (f32[4,512]{1,0:T(4,128)S(1)}, f32[4,512]{1,0:T(4,128)}, u32[]{:S(2)}) copy-start(f32[4,512]{1,0:T(4,128)} %cq_ref.7) | copy-start | bytes 24580
  1.4 22.8 %copy-start.3 = (f32[4,512]{1,0:T(4,128)S(1)}, f32[4,512]{1,0:T(4,128)}, u32[]{:S(2)}) copy-start(f32[4,512]{1,0:T(4,128)} %ck_ref.5) | copy-start | bytes 24580
  1.4 22.8 %copy-start.4 = (f32[128]{0:T(128)S(1)}, f32[128]{0:T(128)}, u32[]{:S(2)}) copy-start(f32[128]{0:T(128)} %param.23) | copy-start | bytes 1540
  1.4 22.8 %copy-start.5 = (f32[8]{0:T(128)S(1)}, f32[8]{0:T(128)}, u32[]{:S(2)}) copy-start(f32[8]{0:T(128)} %param.21) | copy-start | bytes 100
  1.4 22.8 %copy-start.6 = (f32[8]{0:T(128)S(1)}, f32[8]{0:T(128)}, u32[]{:S(2)}) copy-start(f32[8]{0:T(128)} %param.22) | copy-start | bytes 100
  30.7 3.6 %collective-permute-start = (bf16[272,128]{1,0:T(8,128)(2,1)S(1)}, bf16[272,128]{1,0:T(8,128)(2,1)S(1)}, u32[]{:S(2)}, u32[]{:S(2)}) collective-permute-start(bf16[272,128]{1,0:T(8,128)(2,1)S(1)} %get-tuple-element.40.hop_ref), channel_id=1, source_target_pairs={{0,16},{1,17},{2,18},{3,19},{4,20},{5,21},{6,22},{7,23},{8,24},{9,... | collective-permute-start | bytes 208904 | tf_op jit(solution)/shard_map/ppermute | solution.py:887
  34.4 13.5 %copy-start = (bf16[64,4096]{1,0:T(8,128)(2,1)S(1)}, bf16[64,4096]{1,0:T(8,128)(2,1)}, u32[]{:S(2)}) copy-start(bf16[64,4096]{1,0:T(8,128)(2,1)} %z_ref.1) | copy-start | bytes 1572868

commit v21 on v20

--- a/solution.py
+++ b/solution.py
@@ -62,7 +62,12 @@
     heads_axis, q_in, k_in, v_in, at_in, bt_in, out_ref, q_ref, k_ref, v_ref, at_ref, bt_ref, sems
 ):
     peers, tokens = out_ref.shape[0], q_ref.shape[0]
-    pairs = ((at_in, at_ref), (bt_in, bt_ref), (k_in, k_ref), (v_in, v_ref), (q_in, q_ref))
+    pairs = [(at_in, at_ref), (bt_in, bt_ref)]
+    for source, target, pieces in ((k_in, k_ref, 2), (v_in, v_ref, 4), (q_in, q_ref, 2)):
+        width = source.shape[1] // pieces
+        for i in range(pieces):
+            lanes = pl.ds(i * width, width)
+            pairs.append((source.at[:, lanes], target.at[:, lanes]))
     copies = [pltpu.make_async_copy(a, b, sems.at[i]) for i, (a, b) in enumerate(pairs)]
     for copy in copies:
         copy.start()
@@ -87,20 +92,22 @@
     for dest in range(peers):
         out_ref[dest, 4 * tokens :, :] = gates[GATES * dest : GATES * (dest + 1), :]
 
-    def laid(ref, lane, start):
+    def laid(ref, lane, start, piece, pieces):
         for dest, key_head in enumerate(key_heads):
-            at = lane(key_head) * 128
-            out_ref[dest, start * tokens : (start + 1) * tokens, :] = ref[
-                :, at : at + 128
-            ]
-
-    copies[2].wait()
-    laid(k_ref, lambda key_head: key_head, 0)
-    copies[3].wait()
-    laid(v_ref, lambda key_head: 2 * key_head, 1)
-    laid(v_ref, lambda key_head: 2 * key_head + 1, 2)
-    copies[4].wait()
-    laid(q_ref, lambda key_head: key_head, 3)
+            if key_head * pieces // peers == piece:
+                at = lane(key_head) * 128
+                out_ref[dest, start * tokens : (start + 1) * tokens, :] = ref[:, at : at + 128]
+
+    for i in range(2):
+        copies[2 + i].wait()
+        laid(k_ref, lambda key_head: key_head, 0, i, 2)
+    for i in range(4):
+        copies[4 + i].wait()
+        laid(v_ref, lambda key_head: 2 * key_head, 1, i, 4)
+        laid(v_ref, lambda key_head: 2 * key_head + 1, 2, i, 4)
+    for i in range(2):
+        copies[8 + i].wait()
+        laid(q_ref, lambda key_head: key_head, 3, i, 2)
 
 
 def compacted(system):
@@ -258,6 +265,8 @@
     mixed = jnp.where(which < 2, cum, pltpu.roll(growth, 2, 0))
     columns = jnp.transpose(jnp.where(which < 4, mixed, pltpu.roll(rest, 4, 0)))
     cols_ref[...] = columns
+    if early_ref is None:
+        within_ref[0], within_ref[1] = cum, here
     lower = lane_r >= lane_c
     strict = lane_r > lane_c
     both = [(n, r) for n in range(spans) for r in range(2)]
@@ -276,7 +285,9 @@
         at = GATES * n + r
         gap = columns[:, at : at + 1] - cum[at : at + 1, :]
         within = jnp.exp(jnp.where(lower, gap, 0.0)) * here[at : at + 1, :]
-        within_ref[r, n * SPAN : (n + 1) * SPAN, :] = jnp.where(lower, within, 0.0).astype(BF16)
+        if early_ref is not None:
+            kept = jnp.where(lower, within, 0.0).astype(BF16)
+            within_ref[r, n * SPAN : (n + 1) * SPAN, :] = kept
         system = jnp.where(strict, within * -grams[n], 0.0)
         systems_ref[r, n, 0], systems_ref[r, n, 1] = halves(system)
         small_ref[r, n] = compacted(system)
@@ -472,7 +483,8 @@
             at = 2 * r * DK
             lin_ref[r, n] = moved[n][:, at : at + DK].astype(BF16)
             adds.append(moved[n][:, at + DK : at + 2 * DK])
-            adds_ref[r, n] = adds[-1]
+            if n == 0 or (n + 1) & n:
+                adds_ref[r, n] = adds[-1]
         maps = [
             [(end_of(ends_ref, n, r), lin_ref[r, n], adds[2 * n + r]) for n in range(spans)]
             for r in range(2)
@@ -542,7 +554,7 @@
     return jnp.concatenate([x, x], axis=axis)
 
 
-def asked(recv_ref, cq_ref, keys_ref, keys_t_ref, within_ref, query_rows):
+def asked(recv_ref, cq_ref, keys_ref, keys_t_ref, within, query_rows):
     tokens = (recv_ref.shape[1] - GATES) // 4
     spans = keys_t_ref.shape[0]
     tap = key_tap(lax.axis_index("sub"), cq_ref)
@@ -556,7 +568,7 @@
     ]
     scores = [dot(queries[n], keys_t_ref[n]) for n in range(spans)]
     inner = [
-        (within_ref[r, span_rows(n), :].astype(F32) * scores[n]).astype(BF16)
+        (within(n, r) * scores[n]).astype(BF16)
         for n in range(spans)
         for r in range(2)
     ]
@@ -583,7 +595,15 @@
     def _():
         spans = t_ref.shape[1]
         both = [(n, r) for n in range(spans) for r in range(2)]
-        readers, inner = asked(recv_ref, cq_ref, keys_ref, keys_t_ref, within_ref, query_rows)
+        lower = iota((SPAN, SPAN), 0) >= iota((SPAN, SPAN), 1)
+
+        def within(n, r):
+            line = slice(GATES * n + r, GATES * n + r + 1)
+            gap = cols_ref[:, line] - within_ref[0, line, :]
+            decayed = jnp.exp(jnp.where(lower, gap, 0.0)) * within_ref[1, line, :]
+            return jnp.where(lower, decayed, 0.0)
+
+        readers, inner = asked(recv_ref, cq_ref, keys_ref, keys_t_ref, within, query_rows)
         stacks, states = [], []
         for n in range(1, spans):
             if n == 1:
@@ -639,7 +659,14 @@
     def _():
         spans = t_ref.shape[1]
         both = [(n, r) for n in range(spans) for r in range(2)]
-        readers, inner = asked(recv_ref, cq_ref, keys_ref, keys_t_ref, within_ref, query_rows)
+        readers, inner = asked(
+            recv_ref,
+            cq_ref,
+            keys_ref,
+            keys_t_ref,
+            lambda n, r: within_ref[r, span_rows(n), :].astype(F32),
+            query_rows,
+        )
         zero_half = jnp.zeros((SPAN, DV), F32)
         reads = [
             dot(
@@ -783,10 +810,13 @@
                 here = slice(r * tokens, (r + 1) * tokens)
                 value = normed_ref[sub * heads_axis + head, here, :].astype(F32)
                 made[:, at : at + DV] = (value * gate).astype(BF16)
-        lanes = pl.ds(head * width, width)
-        copy = pltpu.make_async_copy(made.at[:, lanes], out_ref.at[:, lanes], sems.at[head])
-        copy.start()
-        copies.append(copy)
+            if sub % 2 == 1:
+                lanes = pl.ds(head * width + (sub - 1) * 2 * DV, 4 * DV)
+                copy = pltpu.make_async_copy(
+                    made.at[:, lanes], out_ref.at[:, lanes], sems.at[len(copies)]
+                )
+                copy.start()
+                copies.append(copy)
     for copy in copies:
         copy.wait()
 
@@ -846,7 +876,7 @@
         functools.partial(pack_kernel, heads_axis),
         pltpu.VMEM((peers, GATES + 4 * tokens, 128), BF16),
         [ANY] * 5,
-        [pltpu.VMEM(x.shape, BF16) for x in inputs] + [pltpu.SemaphoreType.DMA((5,))],
+        [pltpu.VMEM(x.shape, BF16) for x in inputs] + [pltpu.SemaphoreType.DMA((10,))],
         flops=1 << 20,
     )(*inputs)
     blocks = near(lax.all_to_all(packed, group, 0, 0, tiled=True))
@@ -869,7 +899,9 @@
         (
             pltpu.VMEM((2 * DK + 16, 128), BF16),
             *key_shapes,
-            *decay_shapes,
+            decay_shapes[0],
+            pltpu.VMEM((2, SPAN, SPAN), F32),
+            decay_shapes[2],
             *map_shapes,
             pltpu.VMEM((2, total, DV), BF16),
             pltpu.VMEM((2, spans, 2 * DK, DV), BF16),
@@ -984,7 +1016,7 @@
         functools.partial(gate_kernel, heads_axis),
         jax.ShapeDtypeStruct(z_rows.shape, BF16),
         [VMEM] * 2,
-        [pltpu.VMEM(z_rows.shape, BF16), pltpu.SemaphoreType.DMA((heads_axis,))],
+        [pltpu.VMEM(z_rows.shape, BF16), pltpu.SemaphoreType.DMA((peers // 2,))],
         ANY,
     )(returned, z_rows)
 

time: 49.6 us -> 49.6 us (level)
  no operation moved by 1% of the time
where the time goes in v21:
time: 49.6 us; the launch traced here: 49.1 us
  blocking collectives  36.1 us (73%)
  Pallas kernels  11.3 us (23%)
  starting transfers between devices  1.29 us (3%)
    all_to_all x1, blocking collectives, local(): blocks = near(lax.all_to_all(packed, group, 0, 0, tiled=True))  22.7 us
    all_to_all x1, blocking collectives, local(): returned = near(lax.all_to_all(normed, group, 0, 0, tiled=True))  13.4 us
    pallas_call x1, Pallas kernels, local(): call(opening_kernel, (pltpu.VMEM((2 * DK + 16, 128), BF16), *key_shapes,...  6.48 us
    pallas_call x1, Pallas kernels, local(): call(first_outputs_kernel, pltpu.VMEM((2, total, DV), F32), [VMEM] * 12,...  1.8 us
    pallas_call x1, Pallas kernels, local(): call(functools.partial(pack_kernel, heads_axis), pltpu.VMEM((peers, GATES...  1.42 us
    ppermute x1, starting transfers between devices, local(): entering = near(lax.ppermute(hop, 'half', route))  1.29 us
  transfers between devices with their start and end apart: 1, of which 0 were waited for; matrix products, arithmetic and copies ran while one was open for 0% of the time, Pallas kernels for 5%

profile of v21, /device:TPU:0, one launch (start us, length us, event | category | flops | bytes accessed | tf_op | source)
XLA Modules:
  0.0 49.1 jit_solution(8759723895193832469)
XLA Ops:
  0.0 1.4 %shard_map.118 = bf16[16,264,128]{2,1,0:T(8,128)(2,1)S(1)} custom-call(bf16[64,2048]{1,0:T(8,128)(2,1)} %q_in.1, bf16[64,2048]{1,0:T(8,128)(2,1)} %k_in.1, bf16[64,4096]{1,0:T(8,128)(2,1)} %v_in.1, bf16[32,64]{1,0:T(8,128)(2,1)} %bitcast.12, bf16[32,64]{1,0:T(8,128)(2,1)} %bitcast.13), custom_call_target="tpu_custom_call" | custom-call | flops 1048576 | bytes 2097152 | tf_op jit(solution)/shard_map/pallas_call | solution.py:875
  1.4 0.0 copy-start.1
  1.4 0.0 copy-start.2
  1.4 0.0 copy-start.3
  1.5 0.0 copy-start.4
  1.5 0.0 copy-start.5
  1.5 0.0 copy-start.6
  1.5 22.7 %all_to_all.10.recv_ref = bf16[16,264,128]{2,1,0:T(8,128)(2,1)S(1)} all-to-all(bf16[16,264,128]{2,1,0:T(8,128)(2,1)S(1)} %shard_map.118), channel_id=1, replica_groups=mesh['half'=2,'sub'=4,'head'=4] {'sub','head'}, dimensions={0} | all-to-all | bytes 2162688 | tf_op jit(solution)/shard_map/all_to_all | solution.py:882
  24.2 0.0 copy-done.1
  24.2 0.0 copy-done.2
  24.2 0.0 copy-done.3
  24.2 0.0 copy-done.4
  24.3 0.0 copy-done.5
  24.3 0.0 copy-done.6
  24.3 6.5 %shard_map.119 = (bf16[272,128]{1,0:T(8,128)(2,1)S(1)}, bf16[1024,128]{1,0:T(8,128)(2,1)S(1)}, bf16[8,128,128]{2,1,0:T(8,128)(2,1)S(1)}, f32[128,128]{1,0:T(8,12...) custom-call(bf16[16,264,128]{2,1,0:T(8,128)(2,1)S(1)} %all_to_all.10, ...), custom_call_target="tpu_custom_call" | custom-call | flops 4294967296 | bytes 2097152 | tf_op jit(solution)/shard_map/pallas_call | solution.py:897
  30.8 1.3 %collective-permute-start = (bf16[272,128]{1,0:T(8,128)(2,1)S(1)}, bf16[272,128]{1,0:T(8,128)(2,1)S(1)}, u32[]{:S(2)}, u32[]{:S(2)}) collective-permute-start(bf16[272,128]{1,0:T(8,128)(2,1)S(1)} %get-tuple-element.40.hop_ref), channel_id=1, source_target_pairs={{0,16},{1,17},{2,18},{3,19},{4,20},{5,21},{6,22},{7,23},{8,24},{9,... | collective-permute-start | bytes 208904 | tf_op jit(solution)/shard_map/ppermute | solution.py:919
  32.1 0.2 shard_map.124
  32.3 1.8 %shard_map.120.oa_ref = f32[2,1024,128]{2,1,0:T(8,128)S(1)} custom-call(bf16[16,264,128]{2,1,0:T(8,128)(2,1)S(1)} %all_to_all.10.recv_ref, f32[4,512]{1,0:T(4,128)S(1)} %copy-done.2, bf16[1024,128]{1,0:T(8,128)(2,1)S(1)} %get-tuple-element.30.keys_ref, bf16[8,128,128]{2,1,0:T(8,128)(2,1)S(1)} %get-tuple-element.31.keys_t_ref, ...), custom_call_target="tpu_custom_call" | custom-call | flops 4294967296 | bytes 2097152 | tf_op jit(solution)/shard_map/pallas_call | solution.py:923
  34.2 0.4 shard_map.121.normed_ref
  34.5 0.0 collective-permute-done.hop_ref
  34.6 0.0 copy-start
  34.6 13.4 %all_to_all.11.normed_ref = bf16[16,128,128]{2,1,0:T(8,128)(2,1)S(1)} all-to-all(bf16[16,128,128]{2,1,0:T(8,128)(2,1)S(1)} %shard_map.126), channel_id=1, replica_groups=mesh['half'=2,'sub'=4,'head'=4] {'sub','head'}, dimensions={0} | all-to-all | bytes 1048576 | tf_op jit(solution)/shard_map/all_to_all | solution.py:1014
  48.0 0.0 copy-done
  48.0 1.0 %shard_map.127 = bf16[64,4096]{1,0:T(8,128)(2,1)} custom-call(bf16[16,128,128]{2,1,0:T(8,128)(2,1)S(1)} %all_to_all.11.normed_ref, bf16[64,4096]{1,0:T(8,128)(2,1)S(1)} %copy-done), custom_call_target="tpu_custom_call" | custom-call | flops 67108864 | bytes 2097152 | tf_op jit(solution)/shard_map/pallas_call | solution.py:1015
  (4 shorter events, 0.1 us)
Async XLA Ops:
  1.4 22.8 %copy-start.1 = (f32[4,1024]{1,0:T(4,128)S(1)}, f32[4,1024]{1,0:T(4,128)}, u32[]{:S(2)}) copy-start(f32[4,1024]{1,0:T(4,128)} %cv_ref.5) | copy-start | bytes 49156
  1.4 22.8 %copy-start.2 = (f32[4,512]{1,0:T(4,128)S(1)}, f32[4,512]{1,0:T(4,128)}, u32[]{:S(2)}) copy-start(f32[4,512]{1,0:T(4,128)} %cq_ref.7) | copy-start | bytes 24580
  1.4 22.8 %copy-start.3 = (f32[4,512]{1,0:T(4,128)S(1)}, f32[4,512]{1,0:T(4,128)}, u32[]{:S(2)}) copy-start(f32[4,512]{1,0:T(4,128)} %ck_ref.5) | copy-start | bytes 24580
  1.5 22.8 %copy-start.4 = (f32[128]{0:T(128)S(1)}, f32[128]{0:T(128)}, u32[]{:S(2)}) copy-start(f32[128]{0:T(128)} %param.23) | copy-start | bytes 1540
  1.5 22.8 %copy-start.5 = (f32[8]{0:T(128)S(1)}, f32[8]{0:T(128)}, u32[]{:S(2)}) copy-start(f32[8]{0:T(128)} %param.21) | copy-start | bytes 100
  1.5 22.8 %copy-start.6 = (f32[8]{0:T(128)S(1)}, f32[8]{0:T(128)}, u32[]{:S(2)}) copy-start(f32[8]{0:T(128)} %param.22) | copy-start | bytes 100
  30.8 3.8 %collective-permute-start = (bf16[272,128]{1,0:T(8,128)(2,1)S(1)}, bf16[272,128]{1,0:T(8,128)(2,1)S(1)}, u32[]{:S(2)}, u32[]{:S(2)}) collective-permute-start(bf16[272,128]{1,0:T(8,128)(2,1)S(1)} %get-tuple-element.40.hop_ref), channel_id=1, source_target_pairs={{0,16},{1,17},{2,18},{3,19},{4,20},{5,21},{6,22},{7,23},{8,24},{9,... | collective-permute-start | bytes 208904 | tf_op jit(solution)/shard_map/ppermute | solution.py:919
  34.6 13.4 %copy-start = (bf16[64,4096]{1,0:T(8,128)(2,1)S(1)}, bf16[64,4096]{1,0:T(8,128)(2,1)}, u32[]{:S(2)}) copy-start(bf16[64,4096]{1,0:T(8,128)(2,1)} %z_ref.1) | copy-start | bytes 1572868

commit v22 on v20

--- a/solution.py
+++ b/solution.py
@@ -418,6 +418,18 @@
     @pl.when(first)
     def _():
         both = [(n, r) for n in range(spans) for r in range(2)]
+        taps = value_taps(lax.axis_index("sub"), cv_ref)
+        widened(rows, recv_ref, [tokens, 2 * tokens], tokens)
+        waiting = list(both)
+
+        def meanwhile():
+            for n, r in waiting[:6]:
+                lanes = slice(r * DV, (r + 1) * DV)
+                value = convolved(rows, n * SPAN + 8 - EDGE, SPAN, lanes, taps[r])
+                vs_ref[r, n * SPAN : (n + 1) * SPAN, :] = value.astype(BF16)
+            del waiting[:6]
+
+        meanwhile()
         systems_of(
             recv_ref,
             ck_ref,
@@ -433,17 +445,6 @@
             None,
             key_rows,
         )
-        taps = value_taps(lax.axis_index("sub"), cv_ref)
-        widened(rows, recv_ref, [tokens, 2 * tokens], tokens)
-        waiting = list(both)
-
-        def meanwhile():
-            for n, r in waiting[:6]:
-                lanes = slice(r * DV, (r + 1) * DV)
-                value = convolved(rows, n * SPAN + 8 - EDGE, SPAN, lanes, taps[r])
-                vs_ref[r, n * SPAN : (n + 1) * SPAN, :] = value.astype(BF16)
-            del waiting[:6]
-
         compact = jnp.concatenate([small_ref[r, n] for n, r in both], axis=0)
         small = substituted(compact.reshape(len(both), SUB, SPAN))
         systems = [(systems_ref[r, n, 0], systems_ref[r, n, 1]) for n, r in both]

time: 49.6 us -> 49.6 us (level)
  no operation moved by 1% of the time
where the time goes in v22:
time: 49.6 us; the launch traced here: 49 us
  blocking collectives  36.3 us (73%)
  Pallas kernels  11.1 us (22%)
  starting transfers between devices  1.29 us (3%)
    all_to_all x1, blocking collectives, local(): blocks = near(lax.all_to_all(packed, group, 0, 0, tiled=True))  22.7 us
    all_to_all x1, blocking collectives, local(): returned = near(lax.all_to_all(normed, group, 0, 0, tiled=True))  13.5 us
    pallas_call x1, Pallas kernels, local(): call(opening_kernel, (pltpu.VMEM((2 * DK + 16, 128), BF16), *key_shapes,...  6.49 us
    pallas_call x1, Pallas kernels, local(): call(first_outputs_kernel, pltpu.VMEM((2, total, DV), F32), [VMEM] * 12,...  1.68 us
    pallas_call x1, Pallas kernels, local(): call(functools.partial(pack_kernel, heads_axis), pltpu.VMEM((peers, GATES...  1.34 us
    ppermute x1, starting transfers between devices, local(): entering = near(lax.ppermute(hop, 'half', route))  1.29 us
  transfers between devices with their start and end apart: 1, of which 0 were waited for; matrix products, arithmetic and copies ran while one was open for 0% of the time, Pallas kernels for 5%

profile of v22, /device:TPU:0, one launch (start us, length us, event | category | flops | bytes accessed | tf_op | source)
XLA Modules:
  0.0 49.0 jit_solution(12629400176134272874)
XLA Ops:
  0.0 1.3 %shard_map.118 = bf16[16,264,128]{2,1,0:T(8,128)(2,1)S(1)} custom-call(bf16[64,2048]{1,0:T(8,128)(2,1)} %q_in.1, bf16[64,2048]{1,0:T(8,128)(2,1)} %k_in.1, bf16[64,4096]{1,0:T(8,128)(2,1)} %v_in.1, bf16[32,64]{1,0:T(8,128)(2,1)} %bitcast.12, bf16[32,64]{1,0:T(8,128)(2,1)} %bitcast.13), custom_call_target="tpu_custom_call" | custom-call | flops 1048576 | bytes 2097152 | tf_op jit(solution)/shard_map/pallas_call | solution.py:846
  1.3 0.0 copy-start.1
  1.4 0.0 copy-start.2
  1.4 0.0 copy-start.3
  1.4 0.0 copy-start.4
  1.4 0.0 copy-start.5
  1.4 0.0 copy-start.6
  1.4 22.7 %all_to_all.10.recv_ref = bf16[16,264,128]{2,1,0:T(8,128)(2,1)S(1)} all-to-all(bf16[16,264,128]{2,1,0:T(8,128)(2,1)S(1)} %shard_map.118), channel_id=1, replica_groups=mesh['half'=2,'sub'=4,'head'=4] {'sub','head'}, dimensions={0} | all-to-all | bytes 2162688 | tf_op jit(solution)/shard_map/all_to_all | solution.py:853
  24.2 0.0 copy-done.1
  24.2 0.0 copy-done.2
  24.2 0.0 copy-done.3
  24.2 0.0 copy-done.4
  24.2 0.0 copy-done.5
  24.2 0.0 copy-done.6
  24.2 6.5 %shard_map.119 = (bf16[272,128]{1,0:T(8,128)(2,1)S(1)}, bf16[1024,128]{1,0:T(8,128)(2,1)S(1)}, bf16[8,128,128]{2,1,0:T(8,128)(2,1)S(1)}, f32[128,128]{1,0:T(8,12...) custom-call(bf16[16,264,128]{2,1,0:T(8,128)(2,1)S(1)} %all_to_all.10, ...), custom_call_target="tpu_custom_call" | custom-call | flops 4294967296 | bytes 2097152 | tf_op jit(solution)/shard_map/pallas_call | solution.py:868
  30.7 1.3 %collective-permute-start = (bf16[272,128]{1,0:T(8,128)(2,1)S(1)}, bf16[272,128]{1,0:T(8,128)(2,1)S(1)}, u32[]{:S(2)}, u32[]{:S(2)}) collective-permute-start(bf16[272,128]{1,0:T(8,128)(2,1)S(1)} %get-tuple-element.40.hop_ref), channel_id=1, source_target_pairs={{0,16},{1,17},{2,18},{3,19},{4,20},{5,21},{6,22},{7,23},{8,24},{9,... | collective-permute-start | bytes 208904 | tf_op jit(solution)/shard_map/ppermute | solution.py:888
  32.0 0.2 shard_map.124
  32.3 1.7 %shard_map.120.oa_ref = f32[2,1024,128]{2,1,0:T(8,128)S(1)} custom-call(bf16[16,264,128]{2,1,0:T(8,128)(2,1)S(1)} %all_to_all.10.recv_ref, f32[4,512]{1,0:T(4,128)S(1)} %copy-done.2, bf16[1024,128]{1,0:T(8,128)(2,1)S(1)} %get-tuple-element.30.keys_ref, bf16[8,128,128]{2,1,0:T(8,128)(2,1)S(1)} %get-tuple-element.31.keys_t_ref, ...), custom_call_target="tpu_custom_call" | custom-call | flops 4294967296 | bytes 2097152 | tf_op jit(solution)/shard_map/pallas_call | solution.py:892
  34.0 0.4 shard_map.121.normed_ref
  34.3 0.0 collective-permute-done.hop_ref
  34.4 0.0 copy-start
  34.4 13.5 %all_to_all.11.normed_ref = bf16[16,128,128]{2,1,0:T(8,128)(2,1)S(1)} all-to-all(bf16[16,128,128]{2,1,0:T(8,128)(2,1)S(1)} %shard_map.126), channel_id=1, replica_groups=mesh['half'=2,'sub'=4,'head'=4] {'sub','head'}, dimensions={0} | all-to-all | bytes 1048576 | tf_op jit(solution)/shard_map/all_to_all | solution.py:983
  47.9 0.0 copy-done
  47.9 1.0 %shard_map.127 = bf16[64,4096]{1,0:T(8,128)(2,1)} custom-call(bf16[16,128,128]{2,1,0:T(8,128)(2,1)S(1)} %all_to_all.11.normed_ref, bf16[64,4096]{1,0:T(8,128)(2,1)S(1)} %copy-done), custom_call_target="tpu_custom_call" | custom-call | flops 67108864 | bytes 2097152 | tf_op jit(solution)/shard_map/pallas_call | solution.py:984
  (4 shorter events, 0.1 us)
Async XLA Ops:
  1.3 22.8 %copy-start.1 = (f32[4,1024]{1,0:T(4,128)S(1)}, f32[4,1024]{1,0:T(4,128)}, u32[]{:S(2)}) copy-start(f32[4,1024]{1,0:T(4,128)} %cv_ref.5) | copy-start | bytes 49156
  1.4 22.8 %copy-start.2 = (f32[4,512]{1,0:T(4,128)S(1)}, f32[4,512]{1,0:T(4,128)}, u32[]{:S(2)}) copy-start(f32[4,512]{1,0:T(4,128)} %cq_ref.7) | copy-start | bytes 24580
  1.4 22.8 %copy-start.3 = (f32[4,512]{1,0:T(4,128)S(1)}, f32[4,512]{1,0:T(4,128)}, u32[]{:S(2)}) copy-start(f32[4,512]{1,0:T(4,128)} %ck_ref.5) | copy-start | bytes 24580
  1.4 22.8 %copy-start.4 = (f32[128]{0:T(128)S(1)}, f32[128]{0:T(128)}, u32[]{:S(2)}) copy-start(f32[128]{0:T(128)} %param.23) | copy-start | bytes 1540
  1.4 22.8 %copy-start.5 = (f32[8]{0:T(128)S(1)}, f32[8]{0:T(128)}, u32[]{:S(2)}) copy-start(f32[8]{0:T(128)} %param.21) | copy-start | bytes 100
  1.4 22.8 %copy-start.6 = (f32[8]{0:T(128)S(1)}, f32[8]{0:T(128)}, u32[]{:S(2)}) copy-start(f32[8]{0:T(128)} %param.22) | copy-start | bytes 100
  30.7 3.6 %collective-permute-start = (bf16[272,128]{1,0:T(8,128)(2,1)S(1)}, bf16[272,128]{1,0:T(8,128)(2,1)S(1)}, u32[]{:S(2)}, u32[]{:S(2)}) collective-permute-start(bf16[272,128]{1,0:T(8,128)(2,1)S(1)} %get-tuple-element.40.hop_ref), channel_id=1, source_target_pairs={{0,16},{1,17},{2,18},{3,19},{4,20},{5,21},{6,22},{7,23},{8,24},{9,... | collective-permute-start | bytes 208904 | tf_op jit(solution)/shard_map/ppermute | solution.py:888
  34.4 13.5 %copy-start = (bf16[64,4096]{1,0:T(8,128)(2,1)S(1)}, bf16[64,4096]{1,0:T(8,128)(2,1)}, u32[]{:S(2)}) copy-start(bf16[64,4096]{1,0:T(8,128)(2,1)} %z_ref.1) | copy-start | bytes 1572868
